TPU v7x, 32 devices: a whole 2x2x4 slice. The times are simulated.
32 devices in a mesh: gx: 4 (over z), gy: 2 (over x), gz: 4 (over y, core).
Axes of the slice: x: 2, y: 2, z: 4, core: 2. Of those that a mesh axis runs over, the one named last changes fastest.
Arguments:
- old_fields: float32 [2, 4, 64, 16, 1024], P(None, 'gy', 'gz', None, 'gx'), may hold values from -6 to 6
- old_coef: bfloat16 [4, 4, 64, 16, 1024], P(None, 'gy', 'gz', None, 'gx'), may hold values from 0.25 to 4
- held_slabs: int32 [4, 4, 4], P('gy', 'gz', 'gx'), may hold values from 0 to 3, as said below
Outputs:
- solution: float32 [64, 48, 1024], P('gz', 'gy', 'gx')
- residual: float32 [64, 48, 1024], P('gz', 'gy', 'gx')
Inputs may be any that keep to these rules, and one draw needn't show every extreme that they name: `held_slabs`: in every column of bricks and for every p below 1, rows 4p to 4p + 3 hold the old slabs 3p, 3p + 1, 3p + 2 once each and one entry 3, which marks an empty slot.
All inputs are finite; a program needn't handle non-finite values.
Results may differ from a plain program's by a relative error of at most 0.0003.
Values may be sent and summed in bfloat16 or wider, within the bound.
No kernel may reach another device: no remote copies, remote signals or barrier semaphores. Data moves between devices by JAX's collectives and lax.ppermute only.
A program may use at most 64 MiB of HBM per device.

v0:
```python
import jax
import jax.numpy as jnp
from jax import lax
from jax.sharding import PartitionSpec as P

SWEEPS = 4


def from_partner(x, axis, distance):
    return lax.ppermute(x, axis, [(i, i ^ 1 << distance) for i in range(lax.axis_size(axis))])


def passed_along(value, axis, steps):
    count = lax.axis_size(axis)
    pairs = [(source, (source + steps) % count) for source in range(count)]
    return lax.ppermute(value, axis, pairs)


def extended(cells, sides, width):
    for axis, dim in sides:
        count = lax.axis_size(axis)
        head = lax.slice_in_dim(cells, 0, width, axis=dim)
        tail = lax.slice_in_dim(cells, cells.shape[dim] - width, cells.shape[dim], axis=dim)
        cells = jnp.concatenate(
            [
                lax.ppermute(tail, axis, [(i, (i + 1) % count) for i in range(count)]),
                cells,
                lax.ppermute(head, axis, [((i + 1) % count, i) for i in range(count)]),
            ],
            axis=dim,
        )
    return cells


def chebyshev_weights(count):
    low_bound = 0.25
    high_bound = 2.0
    centre_value = 0.5 * (high_bound + low_bound)
    half_width = 0.5 * (high_bound - low_bound)
    ratio_value = centre_value / half_width
    damping = 1.0 / ratio_value
    first_list = [0.0]
    second_list = [1.0 / centre_value]
    for step_index in range(1, count):
        damping_next = 1.0 / (2.0 * ratio_value - damping)
        first_list.append(damping_next * damping)
        second_list.append(2.0 * damping_next / half_width)
        damping = damping_next
    return (first_list, second_list)


def pick_slab(slot_data, slot_ids, target):
    chosen = jnp.zeros_like(slot_data[0])
    for data_piece, slab_id in zip(slot_data, slot_ids):
        chosen = jnp.where(slab_id == target, data_piece, chosen)
    return chosen


def apply_box(field_ext, face_terms):
    cell_alpha, beta_x, upper_x, beta_y, upper_y, beta_z, upper_z = face_terms
    centre = field_ext[1:-1, 1:-1, 1:-1]
    result = cell_alpha * centre
    result = (
        result
        + beta_x * (centre - field_ext[1:-1, 1:-1, :-2])
        + upper_x * (centre - field_ext[1:-1, 1:-1, 2:])
    )
    result = (
        result
        + beta_y * (centre - field_ext[1:-1, :-2, 1:-1])
        + upper_y * (centre - field_ext[1:-1, 2:, 1:-1])
    )
    result = (
        result
        + beta_z * (centre - field_ext[:-2, 1:-1, 1:-1])
        + upper_z * (centre - field_ext[2:, 1:-1, 1:-1])
    )
    return result


def inverse_diagonal(face_terms):
    cell_alpha, beta_x, upper_x, beta_y, upper_y, beta_z, upper_z = face_terms
    return 1.0 / (cell_alpha + beta_x + upper_x + beta_y + upper_y + beta_z + upper_z)


def local(old_fields, old_coef, held_slabs):
    group_index = lax.axis_index("gy")
    pair_first = 3 * (group_index // 2)
    own_half = group_index % 2
    unit_rows = old_fields.shape[3] // 2
    brick_rows = 3 * unit_rows
    own_ids = held_slabs[:, 0, 0]
    partner_fields, partner_ids = from_partner((old_fields, own_ids.astype(jnp.float32)), "gy", 0)
    partner_coef = from_partner(old_coef, "gy", 0)
    field_slots = [old_fields[:, 0], old_fields[:, 1], partner_fields[:, 0], partner_fields[:, 1]]
    coef_slots = [old_coef[:, 0], old_coef[:, 1], partner_coef[:, 0], partner_coef[:, 1]]
    slot_ids = [
        own_ids[0].astype(jnp.float32),
        own_ids[1].astype(jnp.float32),
        partner_ids[0],
        partner_ids[1],
    ]
    targets = [(pair_first + offset).astype(jnp.float32) for offset in range(3)]
    region_fields = jnp.concatenate(
        [pick_slab(field_slots, slot_ids, target) for target in targets], axis=2
    )
    region_coef = jnp.concatenate(
        [pick_slab(coef_slots, slot_ids, target) for target in targets], axis=2
    )
    grid_fields = lax.dynamic_slice_in_dim(region_fields, own_half * brick_rows, brick_rows, 2)
    grid_coef = lax.dynamic_slice_in_dim(region_coef, own_half * brick_rows, brick_rows, 2)
    solution = grid_fields[0]
    rhs_field = grid_fields[1]
    first_list, second_list = chebyshev_weights(SWEEPS)
    rim_x = passed_along(grid_coef[1][:, :, :1], "gx", -1)
    rim_y = passed_along(grid_coef[2][:, :1, :], "gy", -1)
    rim_z = passed_along(grid_coef[3][:1], "gz", -1)
    upper_x = jnp.concatenate([grid_coef[1][:, :, 1:], rim_x], axis=2)
    upper_y = jnp.concatenate([grid_coef[2][:, 1:, :], rim_y], axis=1)
    upper_z = jnp.concatenate([grid_coef[3][1:], rim_z], axis=0)
    face_terms = tuple(
        (
            member.astype(jnp.float32)
            for member in (
                grid_coef[0],
                grid_coef[1],
                upper_x,
                grid_coef[2],
                upper_y,
                grid_coef[3],
                upper_z,
            )
        )
    )
    inverse = inverse_diagonal(face_terms)

    def extend(field):
        return extended(field, (("gx", 2), ("gy", 1), ("gz", 0)), 1)

    residual = rhs_field - apply_box(extend(solution), face_terms)
    direction = jnp.zeros_like(solution)
    for sweep_index in range(SWEEPS):
        direction = first_list[sweep_index] * direction + second_list[sweep_index] * (
            inverse * residual
        )
        solution = solution + direction
        residual = residual - apply_box(extend(direction), face_terms)
    return (solution, residual)


def solution(mesh):
    in_specs = (
        P(None, "gy", "gz", None, "gx"),
        P(None, "gy", "gz", None, "gx"),
        P("gy", "gz", "gx"),
    )
    out_specs = (P("gz", "gy", "gx"), P("gz", "gy", "gx"))
    return jax.shard_map(local, mesh=mesh, in_specs=in_specs, out_specs=out_specs, check_vma=False)
```

profile of v0, /device:TPU:1, one launch (start us, length us, event | category | flops | bytes accessed | tf_op | source)
XLA Modules:
  0.0 156.7 jit_solution(17873356044824081380)
XLA Ops:
  0.6 2.4 %copy.5 = f32[2,2,16,16,256]{4,3,2,0,1:T(8,128)} copy(f32[2,2,16,16,256]{4,3,2,1,0:T(8,128)} %param.3) | data formatting | bytes 2097152 | tf_op args[0]
  3.1 2.0 %collective-permute-start.1 = (f32[2,2,16,16,256]{4,3,2,0,1:T(8,128)}, f32[2,2,16,16,256]{4,3,2,0,1:T(8,128)}, u32[]{:S(2)}, u32[]{:S(2)}) collective-permute-start(f32[2,2,16,16,256]{4,3,2,0,1:T(8,128)} %copy.5), channel_id=1, source_target_pairs={{0,4},{4,0},{1,5},{5,1},{2,6},{6,2},{3,7},{7,3},{8,12},{12,8},{9,1... | collective-permute-start | bytes 3145736 | tf_op jit(solution)/shard_map/ppermute | solution.py:10
  9.6 18.7 %collective-permute-done = f32[2]{0:T(128)S(1)} collective-permute-done((f32[2]{0:T(128)S(1)}, f32[2]{0:T(128)S(1)}, u32[]{:S(2)}, u32[]{:S(2)}) %collective-permute-start) | collective-permute-done | bytes 40 | tf_op jit(solution)/shard_map/ppermute | solution.py:10
  37.4 2.1 %collective-permute-start.7 = (f32[16,24,1]{2,1,0:T(8,128)S(1)}, f32[16,24,1]{2,1,0:T(8,128)S(1)}, u32[]{:S(2)}, u32[]{:S(2)}) collective-permute-start(f32[16,24,1]{2,1,0:T(8,128)S(1)} %get-tuple-element.47), channel_id=1, source_target_pairs={{8,0},{16,8},{24,16},{0,24},{9,1},{17,9},{25,17},{1,25},{10,2},{18... | collective-permute-start | bytes 4616 | tf_op jit(solution)/shard_map/ppermute | solution.py:28
  39.5 11.2 %collective-permute-done.2 = bf16[4,2,16,16,256]{4,3,2,0,1:T(8,128)(2,1)S(1)} collective-permute-done((bf16[4,2,16,16,256]{4,3,2,0,1:T(8,128)(2,1)}, bf16[4,2,16,16,256]{4,3,2,0,1:T(8,128)(2,1)S(1)}, u32[]{:S(2)}, u32[]{:S(2)}) %collective-permute-start.2) | collective-permute-done | bytes 1048608 | tf_op jit(solution)/shard_map/ppermute | solution.py:10
  53.7 1.8 %collective-permute-start.5 = (bf16[1,24,256]{2,1,0:T(8,128)(2,1)S(1)}, bf16[1,24,256]{2,1,0:T(8,128)(2,1)S(1)}, u32[]{:S(2)}, u32[]{:S(2)}) collective-permute-start(bf16[1,24,256]{2,1,0:T(8,128)(2,1)S(1)} %slice_bitcast_fusion.7), channel_id=1, source_target_pairs={{0,3},{1,0},{2,1},{3,2},{4,7},{5,4},{6,5},{7,6},{8,11},{9,8},{10,9... | collective-permute-start | bytes 36872 | tf_op jit(solution)/shard_map/ppermute | solution.py:16
  55.5 1.5 collective-permute-start.4
  57.0 3.4 %collective-permute-start.3 = (bf16[16,24,1]{2,1,0:T(8,128)(2,1)S(1)}, bf16[16,24,1]{2,1,0:T(8,128)(2,1)S(1)}, u32[]{:S(2)}, u32[]{:S(2)}) collective-permute-start(bf16[16,24,1]{2,1,0:T(8,128)(2,1)S(1)} %slice.396), channel_id=1, source_target_pairs={{0,24},{8,0},{16,8},{24,16},{1,25},{9,1},{17,9},{25,17},{2,26},{10... | collective-permute-start | bytes 2312 | tf_op jit(solution)/shard_map/ppermute | solution.py:16
  60.5 1.7 %collective-permute-start.10 = (f32[1,26,258]{2,1,0:T(8,128)S(1)}, f32[1,26,258]{2,1,0:T(8,128)S(1)}, u32[]{:S(2)}, u32[]{:S(2)}) collective-permute-start(f32[1,26,258]{2,1,0:T(8,128)S(1)} %get-tuple-element.24), channel_id=1, source_target_pairs={{0,1},{1,2},{2,3},{3,0},{4,5},{5,6},{6,7},{7,4},{8,9},{9,10},{10,1... | collective-permute-start | bytes 80504 | tf_op jit(solution)/shard_map/ppermute | solution.py:26
  63.4 2.3 %collective-permute-done.11 = f32[1,26,258]{2,1,0:T(8,128)S(1)} collective-permute-done((f32[1,26,258]{2,1,0:T(8,128)S(1)}, f32[1,26,258]{2,1,0:T(8,128)S(1)}, u32[]{:S(2)}, u32[]{:S(2)}) %collective-permute-start.11) | collective-permute-done | bytes 26864 | tf_op jit(solution)/shard_map/ppermute | solution.py:28
  67.0 3.3 %collective-permute-start.13 = (f32[16,24,1]{2,1,0:T(8,128)S(1)}, f32[16,24,1]{2,1,0:T(8,128)S(1)}, u32[]{:S(2)}, u32[]{:S(2)}) collective-permute-start(f32[16,24,1]{2,1,0:T(8,128)S(1)} %get-tuple-element.45), channel_id=1, source_target_pairs={{8,0},{16,8},{24,16},{0,24},{9,1},{17,9},{25,17},{1,25},{10,2},{18... | collective-permute-start | bytes 4616 | tf_op jit(solution)/shard_map/ppermute | solution.py:28
  70.2 5.2 %collective-permute-done.12 = f32[16,24,1]{2,1,0:T(8,128)S(1)} collective-permute-done((f32[16,24,1]{2,1,0:T(8,128)S(1)}, f32[16,24,1]{2,1,0:T(8,128)S(1)}, u32[]{:S(2)}, u32[]{:S(2)}) %collective-permute-start.12) | collective-permute-done | bytes 1568 | tf_op jit(solution)/shard_map/ppermute | solution.py:26
  75.4 1.8 %collective-permute-done.13 = f32[16,24,1]{2,1,0:T(8,128)S(1)} collective-permute-done((f32[16,24,1]{2,1,0:T(8,128)S(1)}, f32[16,24,1]{2,1,0:T(8,128)S(1)}, u32[]{:S(2)}, u32[]{:S(2)}) %collective-permute-start.13) | collective-permute-done | bytes 1568 | tf_op jit(solution)/shard_map/ppermute | solution.py:28
  80.5 2.9 %collective-permute-start.16 = (f32[1,26,258]{2,1,0:T(8,128)S(1)}, f32[1,26,258]{2,1,0:T(8,128)S(1)}, u32[]{:S(2)}, u32[]{:S(2)}) collective-permute-start(f32[1,26,258]{2,1,0:T(8,128)S(1)} %get-tuple-element.22), channel_id=1, source_target_pairs={{0,1},{1,2},{2,3},{3,0},{4,5},{5,6},{6,7},{7,4},{8,9},{9,10},{10,1... | collective-permute-start | bytes 80504 | tf_op jit(solution)/shard_map/ppermute | solution.py:26
  84.6 2.3 %collective-permute-done.17 = f32[1,26,258]{2,1,0:T(8,128)S(1)} collective-permute-done((f32[1,26,258]{2,1,0:T(8,128)S(1)}, f32[1,26,258]{2,1,0:T(8,128)S(1)}, u32[]{:S(2)}, u32[]{:S(2)}) %collective-permute-start.17) | collective-permute-done | bytes 26864 | tf_op jit(solution)/shard_map/ppermute | solution.py:28
  88.7 2.6 %collective-permute-start.19 = (f32[16,24,1]{2,1,0:T(8,128)S(1)}, f32[16,24,1]{2,1,0:T(8,128)S(1)}, u32[]{:S(2)}, u32[]{:S(2)}) collective-permute-start(f32[16,24,1]{2,1,0:T(8,128)S(1)} %get-tuple-element.43), channel_id=1, source_target_pairs={{8,0},{16,8},{24,16},{0,24},{9,1},{17,9},{25,17},{1,25},{10,2},{18... | collective-permute-start | bytes 4616 | tf_op jit(solution)/shard_map/ppermute | solution.py:28
  91.3 5.2 %collective-permute-done.18 = f32[16,24,1]{2,1,0:T(8,128)S(1)} collective-permute-done((f32[16,24,1]{2,1,0:T(8,128)S(1)}, f32[16,24,1]{2,1,0:T(8,128)S(1)}, u32[]{:S(2)}, u32[]{:S(2)}) %collective-permute-start.18) | collective-permute-done | bytes 1568 | tf_op jit(solution)/shard_map/ppermute | solution.py:26
  96.5 3.5 %collective-permute-done.19 = f32[16,24,1]{2,1,0:T(8,128)S(1)} collective-permute-done((f32[16,24,1]{2,1,0:T(8,128)S(1)}, f32[16,24,1]{2,1,0:T(8,128)S(1)}, u32[]{:S(2)}, u32[]{:S(2)}) %collective-permute-start.19) | collective-permute-done | bytes 1568 | tf_op jit(solution)/shard_map/ppermute | solution.py:28
  104.3 2.4 %collective-permute-start.22 = (f32[1,26,258]{2,1,0:T(8,128)S(1)}, f32[1,26,258]{2,1,0:T(8,128)S(1)}, u32[]{:S(2)}, u32[]{:S(2)}) collective-permute-start(f32[1,26,258]{2,1,0:T(8,128)S(1)} %get-tuple-element.20), channel_id=1, source_target_pairs={{0,1},{1,2},{2,3},{3,0},{4,5},{5,6},{6,7},{7,4},{8,9},{9,10},{10,1... | collective-permute-start | bytes 80504 | tf_op jit(solution)/shard_map/ppermute | solution.py:26
  107.8 2.3 %collective-permute-done.23 = f32[1,26,258]{2,1,0:T(8,128)S(1)} collective-permute-done((f32[1,26,258]{2,1,0:T(8,128)S(1)}, f32[1,26,258]{2,1,0:T(8,128)S(1)}, u32[]{:S(2)}, u32[]{:S(2)}) %collective-permute-start.23) | collective-permute-done | bytes 26864 | tf_op jit(solution)/shard_map/ppermute | solution.py:28
  111.8 2.7 %collective-permute-start.25 = (f32[16,24,1]{2,1,0:T(8,128)S(1)}, f32[16,24,1]{2,1,0:T(8,128)S(1)}, u32[]{:S(2)}, u32[]{:S(2)}) collective-permute-start(f32[16,24,1]{2,1,0:T(8,128)S(1)} %get-tuple-element.41), channel_id=1, source_target_pairs={{8,0},{16,8},{24,16},{0,24},{9,1},{17,9},{25,17},{1,25},{10,2},{18... | collective-permute-start | bytes 4616 | tf_op jit(solution)/shard_map/ppermute | solution.py:28
  114.5 5.5 %collective-permute-done.24 = f32[16,24,1]{2,1,0:T(8,128)S(1)} collective-permute-done((f32[16,24,1]{2,1,0:T(8,128)S(1)}, f32[16,24,1]{2,1,0:T(8,128)S(1)}, u32[]{:S(2)}, u32[]{:S(2)}) %collective-permute-start.24) | collective-permute-done | bytes 1568 | tf_op jit(solution)/shard_map/ppermute | solution.py:26
  120.0 2.8 %collective-permute-done.25 = f32[16,24,1]{2,1,0:T(8,128)S(1)} collective-permute-done((f32[16,24,1]{2,1,0:T(8,128)S(1)}, f32[16,24,1]{2,1,0:T(8,128)S(1)}, u32[]{:S(2)}, u32[]{:S(2)}) %collective-permute-start.25) | collective-permute-done | bytes 1568 | tf_op jit(solution)/shard_map/ppermute | solution.py:28
  126.1 2.4 %collective-permute-start.28 = (f32[1,26,258]{2,1,0:T(8,128)S(1)}, f32[1,26,258]{2,1,0:T(8,128)S(1)}, u32[]{:S(2)}, u32[]{:S(2)}) collective-permute-start(f32[1,26,258]{2,1,0:T(8,128)S(1)} %get-tuple-element.18), channel_id=1, source_target_pairs={{0,1},{1,2},{2,3},{3,0},{4,5},{5,6},{6,7},{7,4},{8,9},{9,10},{10,1... | collective-permute-start | bytes 80504 | tf_op jit(solution)/shard_map/ppermute | solution.py:26
  129.7 2.3 %collective-permute-done.29 = f32[1,26,258]{2,1,0:T(8,128)S(1)} collective-permute-done((f32[1,26,258]{2,1,0:T(8,128)S(1)}, f32[1,26,258]{2,1,0:T(8,128)S(1)}, u32[]{:S(2)}, u32[]{:S(2)}) %collective-permute-start.29) | collective-permute-done | bytes 26864 | tf_op jit(solution)/shard_map/ppermute | solution.py:28
  133.6 2.8 %collective-permute-start.31 = (f32[16,24,1]{2,1,0:T(8,128)S(1)}, f32[16,24,1]{2,1,0:T(8,128)S(1)}, u32[]{:S(2)}, u32[]{:S(2)}) collective-permute-start(f32[16,24,1]{2,1,0:T(8,128)S(1)} %get-tuple-element.39), channel_id=1, source_target_pairs={{8,0},{16,8},{24,16},{0,24},{9,1},{17,9},{25,17},{1,25},{10,2},{18... | collective-permute-start | bytes 4616 | tf_op jit(solution)/shard_map/ppermute | solution.py:28
  136.3 5.2 %collective-permute-done.30 = f32[16,24,1]{2,1,0:T(8,128)S(1)} collective-permute-done((f32[16,24,1]{2,1,0:T(8,128)S(1)}, f32[16,24,1]{2,1,0:T(8,128)S(1)}, u32[]{:S(2)}, u32[]{:S(2)}) %collective-permute-start.30) | collective-permute-done | bytes 1568 | tf_op jit(solution)/shard_map/ppermute | solution.py:26
  141.6 2.6 %collective-permute-done.31 = f32[16,24,1]{2,1,0:T(8,128)S(1)} collective-permute-done((f32[16,24,1]{2,1,0:T(8,128)S(1)}, f32[16,24,1]{2,1,0:T(8,128)S(1)}, u32[]{:S(2)}, u32[]{:S(2)}) %collective-permute-start.31) | collective-permute-done | bytes 1568 | tf_op jit(solution)/shard_map/ppermute | solution.py:28
  144.4 1.6 %collective-permute-start.32 = (f32[16,1,258]{2,1,0:T(1,128)S(1)}, f32[16,1,258]{2,1,0:T(1,128)S(1)}, u32[]{:S(2)}, u32[]{:S(2)}) collective-permute-start(f32[16,1,258]{2,1,0:T(1,128)S(1)} %get-tuple-element.26), channel_id=1, source_target_pairs={{0,4},{4,0},{1,5},{5,1},{2,6},{6,2},{3,7},{7,3},{8,12},{12,8},{9,1... | collective-permute-start | bytes 49544 | tf_op jit(solution)/shard_map/ppermute | solution.py:26
  148.9 2.7 %collective-permute-start.34 = (f32[1,26,258]{2,1,0:T(8,128)S(1)}, f32[1,26,258]{2,1,0:T(8,128)S(1)}, u32[]{:S(2)}, u32[]{:S(2)}) collective-permute-start(f32[1,26,258]{2,1,0:T(8,128)S(1)} %get-tuple-element.16), channel_id=1, source_target_pairs={{0,1},{1,2},{2,3},{3,0},{4,5},{5,6},{6,7},{7,4},{8,9},{9,10},{10,1... | collective-permute-start | bytes 80504 | tf_op jit(solution)/shard_map/ppermute | solution.py:26
  152.7 2.3 %collective-permute-done.35 = f32[1,26,258]{2,1,0:T(8,128)S(1)} collective-permute-done((f32[1,26,258]{2,1,0:T(8,128)S(1)}, f32[1,26,258]{2,1,0:T(8,128)S(1)}, u32[]{:S(2)}, u32[]{:S(2)}) %collective-permute-start.35) | collective-permute-done | bytes 26864 | tf_op jit(solution)/shard_map/ppermute | solution.py:28
  155.1 1.7 %fusion.38 = f32[16,24,256]{2,1,0:T(8,128)} fusion(f32[16,24,256]{2,1,0:T(8,128)S(1)} %get-tuple-element.3, bf16[16,24,256]{2,1,0:T(8,128)(2,1)S(1)} %get-tuple-element.11, f32[16,24,256]{2,1,0:T(8,128)S(1)} %get-tuple-element.2, f32[1,26,258]{2,1,0:T(8,128)S(1)} %collective-permute-done.35, f32[16,1,258]{2,1,0:T(1,128)S(1)} %collective-permute-done.33, ...), kind=kLoop, calls=%fused_computation.91 | loop fusion | flops 5013504 | bytes 2645664 | tf_op jit(solution)/shard_map/sub | solution.py:147
  (86 shorter events, 37.1 us)
Async XLA Ops:
  3.1 29.7 %collective-permute-start.1 = (f32[2,2,16,16,256]{4,3,2,0,1:T(8,128)}, f32[2,2,16,16,256]{4,3,2,0,1:T(8,128)}, u32[]{:S(2)}, u32[]{:S(2)}) collective-permute-start(f32[2,2,16,16,256]{4,3,2,0,1:T(8,128)} %copy.5), channel_id=1, source_target_pairs={{0,4},{4,0},{1,5},{5,1},{2,6},{6,2},{3,7},{7,3},{8,12},{12,8},{9,1... | collective-permute-start | bytes 3145736 | tf_op jit(solution)/shard_map/ppermute | solution.py:10
  5.1 23.2 %collective-permute-start = (f32[2]{0:T(128)S(1)}, f32[2]{0:T(128)S(1)}, u32[]{:S(2)}, u32[]{:S(2)}) collective-permute-start(f32[2]{0:T(128)S(1)} %convert_bitcast_fusion), channel_id=1, source_target_pairs={{0,4},{4,0},{1,5},{5,1},{2,6},{6,2},{3,7},{7,3},{8,12},{12,8},{9,1... | collective-permute-start | bytes 32 | tf_op jit(solution)/shard_map/ppermute | solution.py:10
  6.3 44.4 %collective-permute-start.2 = (bf16[4,2,16,16,256]{4,3,2,0,1:T(8,128)(2,1)}, bf16[4,2,16,16,256]{4,3,2,0,1:T(8,128)(2,1)S(1)}, u32[]{:S(2)}, u32[]{:S(2)}) collective-permute-start(bf16[4,2,16,16,256]{4,3,2,0,1:T(8,128)(2,1)} %copy.8), channel_id=1, source_target_pairs={{0,4},{4,0},{1,5},{5,1},{2,6},{6,2},{3,7},{7,3},{8,12},{12,8},{9,1... | collective-permute-start | bytes 3145736 | tf_op jit(solution)/shard_map/ppermute | solution.py:10
  36.1 15.8 %collective-permute-start.6 = (f32[16,24,1]{2,1,0:T(8,128)S(1)}, f32[16,24,1]{2,1,0:T(8,128)S(1)}, u32[]{:S(2)}, u32[]{:S(2)}) collective-permute-start(f32[16,24,1]{2,1,0:T(8,128)S(1)} %get-tuple-element.46), channel_id=1, source_target_pairs={{0,8},{8,16},{16,24},{24,0},{1,9},{9,17},{17,25},{25,1},{2,10},{10... | collective-permute-start | bytes 4616 | tf_op jit(solution)/shard_map/ppermute | solution.py:26
  37.4 14.5 %collective-permute-start.7 = (f32[16,24,1]{2,1,0:T(8,128)S(1)}, f32[16,24,1]{2,1,0:T(8,128)S(1)}, u32[]{:S(2)}, u32[]{:S(2)}) collective-permute-start(f32[16,24,1]{2,1,0:T(8,128)S(1)} %get-tuple-element.47), channel_id=1, source_target_pairs={{8,0},{16,8},{24,16},{0,24},{9,1},{17,9},{25,17},{1,25},{10,2},{18... | collective-permute-start | bytes 4616 | tf_op jit(solution)/shard_map/ppermute | solution.py:28
  52.1 8.3 %collective-permute-start.8 = (f32[16,1,258]{2,1,0:T(1,128)S(1)}, f32[16,1,258]{2,1,0:T(1,128)S(1)}, u32[]{:S(2)}, u32[]{:S(2)}) collective-permute-start(f32[16,1,258]{2,1,0:T(1,128)S(1)} %get-tuple-element.36), channel_id=1, source_target_pairs={{0,4},{4,0},{1,5},{5,1},{2,6},{6,2},{3,7},{7,3},{8,12},{12,8},{9,1... | collective-permute-start | bytes 49544 | tf_op jit(solution)/shard_map/ppermute | solution.py:26
  53.4 7.1 %collective-permute-start.9 = (f32[16,1,258]{2,1,0:T(1,128)S(1)}, f32[16,1,258]{2,1,0:T(1,128)S(1)}, u32[]{:S(2)}, u32[]{:S(2)}) collective-permute-start(f32[16,1,258]{2,1,0:T(1,128)S(1)} %get-tuple-element.37), channel_id=1, source_target_pairs={{4,0},{0,4},{5,1},{1,5},{6,2},{2,6},{7,3},{3,7},{12,8},{8,12},{13,... | collective-permute-start | bytes 49544 | tf_op jit(solution)/shard_map/ppermute | solution.py:28
  53.7 8.8 %collective-permute-start.5 = (bf16[1,24,256]{2,1,0:T(8,128)(2,1)S(1)}, bf16[1,24,256]{2,1,0:T(8,128)(2,1)S(1)}, u32[]{:S(2)}, u32[]{:S(2)}) collective-permute-start(bf16[1,24,256]{2,1,0:T(8,128)(2,1)S(1)} %slice_bitcast_fusion.7), channel_id=1, source_target_pairs={{0,3},{1,0},{2,1},{3,2},{4,7},{5,4},{6,5},{7,6},{8,11},{9,8},{10,9... | collective-permute-start | bytes 36872 | tf_op jit(solution)/shard_map/ppermute | solution.py:16
  55.5 7.0 %collective-permute-start.4 = (bf16[16,1,256]{2,1,0:T(2,128)(2,1)S(1)}, bf16[16,1,256]{2,1,0:T(2,128)(2,1)S(1)}, u32[]{:S(2)}, u32[]{:S(2)}) collective-permute-start(bf16[16,1,256]{2,1,0:T(2,128)(2,1)S(1)} %slice.399), channel_id=1, source_target_pairs={{0,4},{4,0},{1,5},{5,1},{2,6},{6,2},{3,7},{7,3},{8,12},{12,8},{9,1... | collective-permute-start | bytes 24584 | tf_op jit(solution)/shard_map/ppermute | solution.py:16
  57.0 5.4 %collective-permute-start.3 = (bf16[16,24,1]{2,1,0:T(8,128)(2,1)S(1)}, bf16[16,24,1]{2,1,0:T(8,128)(2,1)S(1)}, u32[]{:S(2)}, u32[]{:S(2)}) collective-permute-start(bf16[16,24,1]{2,1,0:T(8,128)(2,1)S(1)} %slice.396), channel_id=1, source_target_pairs={{0,24},{8,0},{16,8},{24,16},{1,25},{9,1},{17,9},{25,17},{2,26},{10... | collective-permute-start | bytes 2312 | tf_op jit(solution)/shard_map/ppermute | solution.py:16
  60.5 2.9 %collective-permute-start.10 = (f32[1,26,258]{2,1,0:T(8,128)S(1)}, f32[1,26,258]{2,1,0:T(8,128)S(1)}, u32[]{:S(2)}, u32[]{:S(2)}) collective-permute-start(f32[1,26,258]{2,1,0:T(8,128)S(1)} %get-tuple-element.24), channel_id=1, source_target_pairs={{0,1},{1,2},{2,3},{3,0},{4,5},{5,6},{6,7},{7,4},{8,9},{9,10},{10,1... | collective-permute-start | bytes 80504 | tf_op jit(solution)/shard_map/ppermute | solution.py:26
  62.3 3.5 %collective-permute-start.11 = (f32[1,26,258]{2,1,0:T(8,128)S(1)}, f32[1,26,258]{2,1,0:T(8,128)S(1)}, u32[]{:S(2)}, u32[]{:S(2)}) collective-permute-start(f32[1,26,258]{2,1,0:T(8,128)S(1)} %get-tuple-element.25), channel_id=1, source_target_pairs={{1,0},{2,1},{3,2},{0,3},{5,4},{6,5},{7,6},{4,7},{9,8},{10,9},{11,1... | collective-permute-start | bytes 80504 | tf_op jit(solution)/shard_map/ppermute | solution.py:28
  66.9 8.5 %collective-permute-start.12 = (f32[16,24,1]{2,1,0:T(8,128)S(1)}, f32[16,24,1]{2,1,0:T(8,128)S(1)}, u32[]{:S(2)}, u32[]{:S(2)}) collective-permute-start(f32[16,24,1]{2,1,0:T(8,128)S(1)} %get-tuple-element.44), channel_id=1, source_target_pairs={{0,8},{8,16},{16,24},{24,0},{1,9},{9,17},{17,25},{25,1},{2,10},{10... | collective-permute-start | bytes 4616 | tf_op jit(solution)/shard_map/ppermute | solution.py:26
  67.0 10.2 %collective-permute-start.13 = (f32[16,24,1]{2,1,0:T(8,128)S(1)}, f32[16,24,1]{2,1,0:T(8,128)S(1)}, u32[]{:S(2)}, u32[]{:S(2)}) collective-permute-start(f32[16,24,1]{2,1,0:T(8,128)S(1)} %get-tuple-element.45), channel_id=1, source_target_pairs={{8,0},{16,8},{24,16},{0,24},{9,1},{17,9},{25,17},{1,25},{10,2},{18... | collective-permute-start | bytes 4616 | tf_op jit(solution)/shard_map/ppermute | solution.py:28
  77.4 2.7 %collective-permute-start.14 = (f32[16,1,258]{2,1,0:T(1,128)S(1)}, f32[16,1,258]{2,1,0:T(1,128)S(1)}, u32[]{:S(2)}, u32[]{:S(2)}) collective-permute-start(f32[16,1,258]{2,1,0:T(1,128)S(1)} %get-tuple-element.32), channel_id=1, source_target_pairs={{0,4},{4,0},{1,5},{5,1},{2,6},{6,2},{3,7},{7,3},{8,12},{12,8},{9,1... | collective-permute-start | bytes 49544 | tf_op jit(solution)/shard_map/ppermute | solution.py:26
  80.5 4.1 %collective-permute-start.16 = (f32[1,26,258]{2,1,0:T(8,128)S(1)}, f32[1,26,258]{2,1,0:T(8,128)S(1)}, u32[]{:S(2)}, u32[]{:S(2)}) collective-permute-start(f32[1,26,258]{2,1,0:T(8,128)S(1)} %get-tuple-element.22), channel_id=1, source_target_pairs={{0,1},{1,2},{2,3},{3,0},{4,5},{5,6},{6,7},{7,4},{8,9},{9,10},{10,1... | collective-permute-start | bytes 80504 | tf_op jit(solution)/shard_map/ppermute | solution.py:26
  83.5 3.5 %collective-permute-start.17 = (f32[1,26,258]{2,1,0:T(8,128)S(1)}, f32[1,26,258]{2,1,0:T(8,128)S(1)}, u32[]{:S(2)}, u32[]{:S(2)}) collective-permute-start(f32[1,26,258]{2,1,0:T(8,128)S(1)} %get-tuple-element.23), channel_id=1, source_target_pairs={{1,0},{2,1},{3,2},{0,3},{5,4},{6,5},{7,6},{4,7},{9,8},{10,9},{11,1... | collective-permute-start | bytes 80504 | tf_op jit(solution)/shard_map/ppermute | solution.py:28
  88.0 8.5 %collective-permute-start.18 = (f32[16,24,1]{2,1,0:T(8,128)S(1)}, f32[16,24,1]{2,1,0:T(8,128)S(1)}, u32[]{:S(2)}, u32[]{:S(2)}) collective-permute-start(f32[16,24,1]{2,1,0:T(8,128)S(1)} %get-tuple-element.42), channel_id=1, source_target_pairs={{0,8},{8,16},{16,24},{24,0},{1,9},{9,17},{17,25},{25,1},{2,10},{10... | collective-permute-start | bytes 4616 | tf_op jit(solution)/shard_map/ppermute | solution.py:26
  88.7 11.3 %collective-permute-start.19 = (f32[16,24,1]{2,1,0:T(8,128)S(1)}, f32[16,24,1]{2,1,0:T(8,128)S(1)}, u32[]{:S(2)}, u32[]{:S(2)}) collective-permute-start(f32[16,24,1]{2,1,0:T(8,128)S(1)} %get-tuple-element.43), channel_id=1, source_target_pairs={{8,0},{16,8},{24,16},{0,24},{9,1},{17,9},{25,17},{1,25},{10,2},{18... | collective-permute-start | bytes 4616 | tf_op jit(solution)/shard_map/ppermute | solution.py:28
  100.2 2.7 %collective-permute-start.20 = (f32[16,1,258]{2,1,0:T(1,128)S(1)}, f32[16,1,258]{2,1,0:T(1,128)S(1)}, u32[]{:S(2)}, u32[]{:S(2)}) collective-permute-start(f32[16,1,258]{2,1,0:T(1,128)S(1)} %get-tuple-element.30), channel_id=1, source_target_pairs={{0,4},{4,0},{1,5},{5,1},{2,6},{6,2},{3,7},{7,3},{8,12},{12,8},{9,1... | collective-permute-start | bytes 49544 | tf_op jit(solution)/shard_map/ppermute | solution.py:26
  104.3 3.6 %collective-permute-start.22 = (f32[1,26,258]{2,1,0:T(8,128)S(1)}, f32[1,26,258]{2,1,0:T(8,128)S(1)}, u32[]{:S(2)}, u32[]{:S(2)}) collective-permute-start(f32[1,26,258]{2,1,0:T(8,128)S(1)} %get-tuple-element.20), channel_id=1, source_target_pairs={{0,1},{1,2},{2,3},{3,0},{4,5},{5,6},{6,7},{7,4},{8,9},{9,10},{10,1... | collective-permute-start | bytes 80504 | tf_op jit(solution)/shard_map/ppermute | solution.py:26
  106.7 3.5 %collective-permute-start.23 = (f32[1,26,258]{2,1,0:T(8,128)S(1)}, f32[1,26,258]{2,1,0:T(8,128)S(1)}, u32[]{:S(2)}, u32[]{:S(2)}) collective-permute-start(f32[1,26,258]{2,1,0:T(8,128)S(1)} %get-tuple-element.21), channel_id=1, source_target_pairs={{1,0},{2,1},{3,2},{0,3},{5,4},{6,5},{7,6},{4,7},{9,8},{10,9},{11,1... | collective-permute-start | bytes 80504 | tf_op jit(solution)/shard_map/ppermute | solution.py:28
  111.2 8.8 %collective-permute-start.24 = (f32[16,24,1]{2,1,0:T(8,128)S(1)}, f32[16,24,1]{2,1,0:T(8,128)S(1)}, u32[]{:S(2)}, u32[]{:S(2)}) collective-permute-start(f32[16,24,1]{2,1,0:T(8,128)S(1)} %get-tuple-element.40), channel_id=1, source_target_pairs={{0,8},{8,16},{16,24},{24,0},{1,9},{9,17},{17,25},{25,1},{2,10},{10... | collective-permute-start | bytes 4616 | tf_op jit(solution)/shard_map/ppermute | solution.py:26
  111.8 11.0 %collective-permute-start.25 = (f32[16,24,1]{2,1,0:T(8,128)S(1)}, f32[16,24,1]{2,1,0:T(8,128)S(1)}, u32[]{:S(2)}, u32[]{:S(2)}) collective-permute-start(f32[16,24,1]{2,1,0:T(8,128)S(1)} %get-tuple-element.41), channel_id=1, source_target_pairs={{8,0},{16,8},{24,16},{0,24},{9,1},{17,9},{25,17},{1,25},{10,2},{18... | collective-permute-start | bytes 4616 | tf_op jit(solution)/shard_map/ppermute | solution.py:28
  123.0 2.7 %collective-permute-start.26 = (f32[16,1,258]{2,1,0:T(1,128)S(1)}, f32[16,1,258]{2,1,0:T(1,128)S(1)}, u32[]{:S(2)}, u32[]{:S(2)}) collective-permute-start(f32[16,1,258]{2,1,0:T(1,128)S(1)} %get-tuple-element.28), channel_id=1, source_target_pairs={{0,4},{4,0},{1,5},{5,1},{2,6},{6,2},{3,7},{7,3},{8,12},{12,8},{9,1... | collective-permute-start | bytes 49544 | tf_op jit(solution)/shard_map/ppermute | solution.py:26
  126.1 3.6 %collective-permute-start.28 = (f32[1,26,258]{2,1,0:T(8,128)S(1)}, f32[1,26,258]{2,1,0:T(8,128)S(1)}, u32[]{:S(2)}, u32[]{:S(2)}) collective-permute-start(f32[1,26,258]{2,1,0:T(8,128)S(1)} %get-tuple-element.18), channel_id=1, source_target_pairs={{0,1},{1,2},{2,3},{3,0},{4,5},{5,6},{6,7},{7,4},{8,9},{9,10},{10,1... | collective-permute-start | bytes 80504 | tf_op jit(solution)/shard_map/ppermute | solution.py:26
  128.5 3.5 %collective-permute-start.29 = (f32[1,26,258]{2,1,0:T(8,128)S(1)}, f32[1,26,258]{2,1,0:T(8,128)S(1)}, u32[]{:S(2)}, u32[]{:S(2)}) collective-permute-start(f32[1,26,258]{2,1,0:T(8,128)S(1)} %get-tuple-element.19), channel_id=1, source_target_pairs={{1,0},{2,1},{3,2},{0,3},{5,4},{6,5},{7,6},{4,7},{9,8},{10,9},{11,1... | collective-permute-start | bytes 80504 | tf_op jit(solution)/shard_map/ppermute | solution.py:28
  133.0 8.6 %collective-permute-start.30 = (f32[16,24,1]{2,1,0:T(8,128)S(1)}, f32[16,24,1]{2,1,0:T(8,128)S(1)}, u32[]{:S(2)}, u32[]{:S(2)}) collective-permute-start(f32[16,24,1]{2,1,0:T(8,128)S(1)} %get-tuple-element.38), channel_id=1, source_target_pairs={{0,8},{8,16},{16,24},{24,0},{1,9},{9,17},{17,25},{25,1},{2,10},{10... | collective-permute-start | bytes 4616 | tf_op jit(solution)/shard_map/ppermute | solution.py:26
  133.6 10.7 %collective-permute-start.31 = (f32[16,24,1]{2,1,0:T(8,128)S(1)}, f32[16,24,1]{2,1,0:T(8,128)S(1)}, u32[]{:S(2)}, u32[]{:S(2)}) collective-permute-start(f32[16,24,1]{2,1,0:T(8,128)S(1)} %get-tuple-element.39), channel_id=1, source_target_pairs={{8,0},{16,8},{24,16},{0,24},{9,1},{17,9},{25,17},{1,25},{10,2},{18... | collective-permute-start | bytes 4616 | tf_op jit(solution)/shard_map/ppermute | solution.py:28
  144.4 2.8 %collective-permute-start.32 = (f32[16,1,258]{2,1,0:T(1,128)S(1)}, f32[16,1,258]{2,1,0:T(1,128)S(1)}, u32[]{:S(2)}, u32[]{:S(2)}) collective-permute-start(f32[16,1,258]{2,1,0:T(1,128)S(1)} %get-tuple-element.26), channel_id=1, source_target_pairs={{0,4},{4,0},{1,5},{5,1},{2,6},{6,2},{3,7},{7,3},{8,12},{12,8},{9,1... | collective-permute-start | bytes 49544 | tf_op jit(solution)/shard_map/ppermute | solution.py:26
  148.9 3.9 %collective-permute-start.34 = (f32[1,26,258]{2,1,0:T(8,128)S(1)}, f32[1,26,258]{2,1,0:T(8,128)S(1)}, u32[]{:S(2)}, u32[]{:S(2)}) collective-permute-start(f32[1,26,258]{2,1,0:T(8,128)S(1)} %get-tuple-element.16), channel_id=1, source_target_pairs={{0,1},{1,2},{2,3},{3,0},{4,5},{5,6},{6,7},{7,4},{8,9},{9,10},{10,1... | collective-permute-start | bytes 80504 | tf_op jit(solution)/shard_map/ppermute | solution.py:26
  151.6 3.5 %collective-permute-start.35 = (f32[1,26,258]{2,1,0:T(8,128)S(1)}, f32[1,26,258]{2,1,0:T(8,128)S(1)}, u32[]{:S(2)}, u32[]{:S(2)}) collective-permute-start(f32[1,26,258]{2,1,0:T(8,128)S(1)} %get-tuple-element.17), channel_id=1, source_target_pairs={{1,0},{2,1},{3,2},{0,3},{5,4},{6,5},{7,6},{4,7},{9,8},{10,9},{11,1... | collective-permute-start | bytes 80504 | tf_op jit(solution)/shard_map/ppermute | solution.py:28
  (7 other events, 47.5 us)
where the time goes:
time: 157 us
  waiting for transfers between devices  86.2 us (55%)
  starting transfers between devices  46.9 us (30%)
  other arithmetic  12 us (8%)
  between operations  6.16 us (4%)
  local copies, waits for them, and re-layouts  5.5 us (4%)
    ppermute x15, waiting for transfers between devices, extended(): lax.ppermute(tail, axis, [(i, (i + 1) % count) for i in range(count)])  30.6 us
    ppermute x3, waiting for transfers between devices, from_partner(): lax.ppermute(x, axis, [(i, i ^ 1 << distance) for i in range(lax.axis_siz...  29.9 us
    ppermute x15, waiting for transfers between devices, extended(): lax.ppermute(head, axis, [((i + 1) % count, i) for i in range(count)])  25.7 us
    ppermute x15, starting transfers between devices, extended(): lax.ppermute(tail, axis, [(i, (i + 1) % count) for i in range(count)])  20.1 us
    ppermute x15, starting transfers between devices, extended(): lax.ppermute(head, axis, [((i + 1) % count, i) for i in range(count)])  16.5 us
    ppermute x3, starting transfers between devices, passed_along(): return lax.ppermute(value, axis, pairs)  6.7 us
    select_n x4, other arithmetic, pick_slab(): chosen = jnp.where(slab_id == target, data_piece, chosen)  3.63 us
    unnamed x8, local copies, waits for them, and re-layouts  3.52 us
  transfers between devices with their start and end apart: 36, of which 28 were waited for; matrix products, arithmetic and copies ran while one was open for 5% of the time, Pallas kernels for 0%

commit v1 on v0

v1 whole, which is shorter than its diff:
```python
import functools

import jax
import jax.numpy as jnp
from jax import lax
from jax.experimental import pallas as pl
from jax.experimental.pallas import tpu as pltpu
from jax.sharding import PartitionSpec as P

SWEEPS = 4
LANES = 128
STRIP = 8
SHIFT = 4096.0
VMEM_LIMIT = 24 * 1024 * 1024


def chebyshev_weights(count):
    low_bound = 0.25
    high_bound = 2.0
    centre_value = 0.5 * (high_bound + low_bound)
    half_width = 0.5 * (high_bound - low_bound)
    ratio_value = centre_value / half_width
    damping = 1.0 / ratio_value
    first_list = [0.0]
    second_list = [1.0 / centre_value]
    for step_index in range(1, count):
        damping_next = 1.0 / (2.0 * ratio_value - damping)
        first_list.append(damping_next * damping)
        second_list.append(2.0 * damping_next / half_width)
        damping = damping_next
    return (first_list, second_list)


def shifted(value, axis, steps):
    count = lax.axis_size(axis)
    return lax.ppermute(value, axis, [(i, (i + steps) % count) for i in range(count)])


def swapped(value):
    return lax.ppermute(value, "gy", [(i, i ^ 1) for i in range(lax.axis_size("gy"))])


def row_ghosts(rows):
    if lax.axis_size("gy") == 2:
        return swapped(rows)
    return jnp.concatenate([shifted(rows[:1], "gy", 1), shifted(rows[1:], "gy", -1)])


def f32(*shape):
    return jax.ShapeDtypeStruct(shape, jnp.float32)


def call(kernel, outs, *operands):
    specs = [pl.BlockSpec(memory_space=pltpu.VMEM) for _ in operands]
    specs[0] = pl.BlockSpec(memory_space=pltpu.SMEM)
    return pl.pallas_call(
        kernel,
        out_shape=outs,
        in_specs=specs,
        out_specs=[pl.BlockSpec(memory_space=pltpu.VMEM) for _ in outs],
        compiler_params=pltpu.CompilerParams(vmem_limit_bytes=VMEM_LIMIT),
    )(*operands)


def lane_of(shape):
    return lax.broadcasted_iota(jnp.int32, shape, 1)


def row_of(shape):
    return lax.broadcasted_iota(jnp.int32, shape, 0)


def units_of(ids, half):
    first = 3 * (lax.axis_index("gy") // 2)
    a, b = ids[0, 0, 0] - first, ids[1, 0, 0] - first
    found = []
    for k in range(3):
        unit = 3 * half + k
        slab = unit // 2
        found.append((jnp.logical_or(a == slab, b == slab), jnp.where(a == slab, 0, 1), unit % 2))
    return found


def field_unit(fields, item, place, z):
    rows = fields.shape[3] // 2
    _, slot, part = place
    return fields[item, slot, z, pl.ds(pl.multiple_of(part * rows, rows), rows), :]


def coef_unit(coef, item, place, z):
    rows = coef.shape[3] // 2
    _, slot, part = place
    both = coef[item, slot, z].astype(jnp.float32)
    return jnp.where(part == 0, both[:rows], both[rows:])


def strips(fields, coef, item, place, planes):
    columns, rows = fields.shape[4], fields.shape[3] // 2
    group = lane_of((rows, LANES)) // STRIP
    low = jnp.zeros((rows, LANES), jnp.float32)
    high = jnp.zeros((rows, LANES), jnp.float32)
    for z in range(planes):
        if item < 2:
            cells = field_unit(fields, item, place, z)
        else:
            cells = coef_unit(coef, 2 * item - 4, place, z) + SHIFT * coef_unit(coef, 2 * item - 3, place, z)
        first, last = cells[:, :LANES], cells[:, columns - LANES :]
        turn = STRIP * z
        low = jnp.where(group == z, pltpu.roll(first, turn, 1) if turn else first, low)
        turn = (STRIP * z + STRIP) % LANES
        high = jnp.where(group == z, pltpu.roll(last, turn, 1) if turn else last, high)
    return low, high


def pack_kernel(ids, fields, coef, strip_out, start_out, rhs_out, coef_out):
    planes = fields.shape[2]
    places = units_of(ids, 1 - lax.axis_index("gy") % 2)
    for k, place in enumerate(places):
        for item in range(4):
            low, high = strips(fields, coef, item, place, planes)
            strip_out[0, item, k] = low
            strip_out[1, item, k] = high
        for z in range(planes):
            start_out[k, z] = field_unit(fields, 0, place, z)
            rhs_out[k, z] = field_unit(fields, 1, place, z)
        for part in range(4):
            for z in range(0, planes, 2):
                both = [coef_unit(coef, part, place, z + j) for j in range(2)]
                coef_out[part, k, z // 2] = jnp.concatenate(both).astype(jnp.bfloat16)


def strip_kernel(ids, fields, coef, strip_in, left, right):
    planes = fields.shape[2]
    for k, place in enumerate(units_of(ids, lax.axis_index("gy") % 2)):
        for item in range(4):
            low, high = strips(fields, coef, item, place, planes)
            left[item, k] = jnp.where(place[0], low, strip_in[0, item, k])
            right[item, k] = jnp.where(place[0], high, strip_in[1, item, k])


def gather_kernel(
    ids, fields, coef, start_in, coef_in, from_left, from_right, start, rhs_ghost, wide, up, down, rows_out
):
    _, _, planes, rows, columns = fields.shape
    rows //= 2
    lane = lane_of((rows, LANES))
    for k, place in enumerate(units_of(ids, lax.axis_index("gy") % 2)):
        at = slice(k * rows, (k + 1) * rows)
        for item in range(4):
            low, high = from_left[item, k], from_right[item, k]
            for z in range(planes):
                turn = (LANES - STRIP * z) % LANES
                right = pltpu.roll(high, turn, 1) if turn else high
                turn = (LANES - STRIP - STRIP * z) % LANES
                left = pltpu.roll(low, turn, 1) if turn else low
                ghost = jnp.where(lane < LANES // 2, right, left)
                if item == 0:
                    start[z, at, :columns] = jnp.where(place[0], field_unit(fields, 0, place, z), start_in[k, z])
                    start[z, at, columns:] = ghost
                elif item == 1:
                    rhs_ghost[z, at] = ghost
                else:
                    b = jnp.floor(ghost * 0.125) * (8.0 / SHIFT)
                    a = ghost - SHIFT * b
                    for part, value in ((2 * item - 4, a), (2 * item - 3, b)):
                        got = coef_in[part, k, z // 2].astype(jnp.float32)
                        got = got[rows:] if z % 2 else got[:rows]
                        own = coef_unit(coef, part, place, z)
                        wide[part, z, at, :columns] = jnp.where(place[0], own, got)
                        wide[part, z, at, columns:] = value
    last = 3 * rows - 1
    up[...] = start[planes - 1]
    down[0] = start[0]
    down[1] = wide[3, 0]
    for z in range(planes):
        rows_out[0, z : z + 1] = start[z, last : last + 1]
        rows_out[1, z : z + 1] = start[z, 0:1]
        rows_out[2, z : z + 1] = wide[2, z, 0:1]


def apply_plane(value, low_row, high_row, lower_flux, upper_flux, alpha, beta_x, beta_y, rim_row):
    rows, width = value.shape
    flux_x = beta_x * (value - pltpu.roll(value, 1, 1))
    row = row_of(value.shape)
    before = jnp.where(row == 0, low_row, pltpu.roll(value, 1, 0))
    flux_y = beta_y * (value - before)
    top = rim_row * (high_row - value[rows - 1 : rows])
    after = jnp.where(row == rows - 1, top, pltpu.roll(flux_y, rows - 1, 0))
    return (
        alpha * value
        + (flux_x - pltpu.roll(flux_x, width - 1, 1))
        + (flux_y - after)
        + (lower_flux - upper_flux)
    )


def sweep_kernel(stage, first, second, ids, wide, field, low_face, high_face, low_high_rows, rim_face, rim_rows, *refs):
    if stage == 0:
        fields, rhs_in, rhs_ghost, residual, inverse, direction, total, up, down, rows_out = refs
        places = units_of(ids, lax.axis_index("gy") % 2)
    elif stage < SWEEPS:
        old, inverse, sum_in, residual, direction, total, up, down, rows_out = refs
    else:
        old, residual = refs
    planes, rows, width = field.shape
    columns = width - LANES
    value, beta_z = field[0], wide[3, 0]
    lower = beta_z * (value - low_face[...])
    for z in range(planes):
        at = slice(z, z + 1)
        if z + 1 < planes:
            following, next_z = field[z + 1], wide[3, z + 1]
        else:
            following, next_z = high_face[0], rim_face[1]
        upper = next_z * (following - value)
        alpha, beta_x, beta_y = wide[0, z], wide[1, z], wide[2, z]
        rim_row = rim_rows[2, at]
        image = apply_plane(
            value, low_high_rows[0, at], low_high_rows[1, at], lower, upper, alpha, beta_x, beta_y, rim_row
        )
        if stage == 0:
            parts = [
                jnp.where(place[0], field_unit(fields, 1, place, z), rhs_in[k, z]) for k, place in enumerate(places)
            ]
            rhs = jnp.concatenate([jnp.concatenate(parts), rhs_ghost[z]], axis=1)
            left = rhs - image
            next_y = jnp.where(row_of(value.shape) == rows - 1, rim_row, pltpu.roll(beta_y, rows - 1, 0))
            factor = 1.0 / (alpha + beta_x + pltpu.roll(beta_x, width - 1, 1) + beta_y + next_y + beta_z + next_z)
            inverse[z] = factor
            step = second * (factor * left)
            total[z] = value[:, :columns] + step[:, :columns]
        elif stage < SWEEPS:
            left = old[z] - image
            step = first * value + second * (inverse[z] * left)
            total[z] = sum_in[z] + step[:, :columns]
        else:
            residual[z] = (old[z] - image)[:, :columns]
        if stage < SWEEPS:
            residual[z] = left
            direction[z] = step
            rows_out[0, at] = step[rows - 1 : rows]
            rows_out[1, at] = step[0:1]
            if z == 0:
                down[0] = step
            if z == planes - 1:
                up[...] = step
        value, lower, beta_z = following, upper, next_z


def local(old_fields, old_coef, held_slabs):
    _, _, planes, rows, columns = old_fields.shape
    half = rows // 2
    rows = 3 * half
    width = columns + LANES
    full, own = f32(planes, rows, width), f32(planes, rows, columns)
    unit = f32(3, planes, half, columns)
    strip_out, start_out, rhs_out, coef_out = call(
        pack_kernel,
        [
            f32(2, 4, 3, half, LANES),
            unit,
            unit,
            jax.ShapeDtypeStruct((4, 3, planes // 2, 2 * half, columns), jnp.bfloat16),
        ],
        held_slabs,
        old_fields,
        old_coef,
    )
    strip_in = swapped(strip_out)
    start_in, coef_in, rhs_in = swapped(start_out), swapped(coef_out), swapped(rhs_out)
    strip = f32(4, 3, half, LANES)
    left, right = call(strip_kernel, [strip, strip], held_slabs, old_fields, old_coef, strip_in)
    from_left, from_right = shifted(right, "gx", 1), shifted(left, "gx", -1)
    field, rhs_ghost, wide, up, down, rows_out = call(
        gather_kernel,
        [
            full,
            f32(planes, rows, LANES),
            f32(4, planes, rows, width),
            f32(rows, width),
            f32(2, rows, width),
            f32(3, planes, width),
        ],
        held_slabs,
        old_fields,
        old_coef,
        start_in,
        coef_in,
        from_left,
        from_right,
    )
    first_list, second_list = chebyshev_weights(SWEEPS)
    faces = [f32(rows, width), f32(1, rows, width), f32(2, planes, width)]
    rim_face = rim_rows = None
    for stage in range(SWEEPS + 1):
        low_face, high_face, low_high_rows = shifted(up, "gz", 1), shifted(down, "gz", -1), row_ghosts(rows_out)
        if stage == 0:
            rim_face, rim_rows = high_face, low_high_rows
        common = (held_slabs, wide, field, low_face, high_face, low_high_rows, rim_face, rim_rows)
        if stage == 0:
            residual, inverse, field, total, up, down, rows_out = call(
                functools.partial(sweep_kernel, stage, first_list[stage], second_list[stage]),
                [full, full, full, own] + faces,
                *common,
                old_fields,
                rhs_in,
                rhs_ghost,
            )
        elif stage < SWEEPS:
            residual, field, total, up, down, rows_out = call(
                functools.partial(sweep_kernel, stage, first_list[stage], second_list[stage]),
                [full, full, own] + faces,
                *common,
                residual,
                inverse,
                total,
            )
        else:
            (residual,) = call(functools.partial(sweep_kernel, stage, 0.0, 0.0), [own], *common, residual)
    return total, residual


def solution(mesh):
    in_specs = (
        P(None, "gy", "gz", None, "gx"),
        P(None, "gy", "gz", None, "gx"),
        P("gy", "gz", "gx"),
    )
    out_specs = (P("gz", "gy", "gx"), P("gz", "gy", "gx"))
    return jax.shard_map(local, mesh=mesh, in_specs=in_specs, out_specs=out_specs, check_vma=False)
```

time: 157 us -> 87.5 us (0.56)
  waiting for transfers between devices: 86.2 us -> 50.3 us
  starting transfers between devices: 46.9 us -> 19.8 us
  Pallas kernels: 0 us -> 13.4 us
  other arithmetic: 12 us -> 0 us
  between operations: 6.16 us -> 0.7 us
  local copies, waits for them, and re-layouts: 5.5 us -> 3.19 us
    ppermute x36 -> x21, waiting for transfers between devices: 86.2 us -> 50.3 us  [the longest x9 34.8 us: swapped(): lax.ppermute(value, 'gy', [(i, i ^ 1) for i in range(lax.axis_size('gy'))])]
    ppermute x36 -> x21, starting transfers between devices: 46.9 us -> 19.8 us  [the longest x12 11.5 us: shifted(): lax.ppermute(value, axis, [(i, (i + steps) % count) for i in range(count)])]
    pallas_call x0 -> x8, Pallas kernels: none -> 13.4 us  [call(): pl.pallas_call(kernel, out_shape=outs, in_specs=specs, out_specs=[pl.Bloc...]
    select_n x4 -> x0, other arithmetic: 3.63 us -> none  [pick_slab(): chosen = jnp.where(slab_id == target, data_piece, chosen)]
    add x4 -> x0, other arithmetic: 3.53 us -> none  [the longest x3 2.63 us: local(): first_list[sweep_index] * direction]
    slice x13 -> x0, local copies, waits for them, and re-layouts: 1.92 us -> none  [the longest x1 0.58 us: local(): partner_ids[1]]
    sub x1 -> x0, other arithmetic: 1.67 us -> none  [local(): residual = residual - apply_box(extend(direction), face_terms)]
    unnamed x8 -> x5, local copies, waits for them, and re-layouts: 3.52 us -> 3.19 us
  transfers between devices with their start and end apart: 36 -> 21, of which waited for: 28 -> 13; matrix products, arithmetic and copies ran while one was open for 5% -> 0% of each run, Pallas kernels for 0% -> 2%
where the time goes in v1:
time: 87.5 us; the launch traced here: 87.3 us
  waiting for transfers between devices  50.3 us (57%)
  starting transfers between devices  19.8 us (23%)
  Pallas kernels  13.4 us (15%)
  local copies, waits for them, and re-layouts  3.19 us (4%)
    ppermute x9, waiting for transfers between devices, swapped(): lax.ppermute(value, 'gy', [(i, i ^ 1) for i in range(lax.axis_size('gy'))])  34.8 us
    ppermute x12, waiting for transfers between devices, shifted(): lax.ppermute(value, axis, [(i, (i + steps) % count) for i in range(count)])  15.5 us
    pallas_call x8, Pallas kernels, call(): pl.pallas_call(kernel, out_shape=outs, in_specs=specs, out_specs=[pl.Bloc...  13.4 us
    ppermute x12, starting transfers between devices, shifted(): lax.ppermute(value, axis, [(i, (i + steps) % count) for i in range(count)])  11.5 us
    ppermute x9, starting transfers between devices, swapped(): lax.ppermute(value, 'gy', [(i, i ^ 1) for i in range(lax.axis_size('gy'))])  8.34 us
    unnamed x5, local copies, waits for them, and re-layouts  3.19 us
  transfers between devices with their start and end apart: 21, of which 13 were waited for; matrix products, arithmetic and copies ran while one was open for 0% of the time, Pallas kernels for 2%

profile of v1, /device:TPU:1, one launch (start us, length us, event | category | flops | bytes accessed | tf_op | source)
XLA Modules:
  0.0 87.3 jit_solution(2854913671659923444)
XLA Ops:
  0.6 0.7 copy.11.ids
  1.4 1.2 %copy-done = f32[2,2,16,16,256]{4,3,2,1,0:T(8,128)S(1)} copy-done((f32[2,2,16,16,256]{4,3,2,1,0:T(8,128)S(1)}, f32[2,2,16,16,256]{4,3,2,1,0:T(8,128)}, u32[]{:S(2)}) %copy-start) | copy-done | bytes 1048600
  2.6 1.2 %copy-done.1 = bf16[4,2,16,16,256]{4,3,2,1,0:T(8,128)(2,1)S(1)} copy-done((bf16[4,2,16,16,256]{4,3,2,1,0:T(8,128)(2,1)S(1)}, bf16[4,2,16,16,256]{4,3,2,1,0:T(8,128)(2,1)}, u32[]{:S(2)}) %copy-start.1) | copy-done | bytes 1048600
  3.8 1.2 %shard_map.50 = (f32[2,4,3,8,128]{4,3,2,1,0:T(8,128)S(1)}, f32[3,16,8,256]{3,2,1,0:T(8,128)S(1)}, f32[3,16,8,256]{3,2,1,0:T(8,128)S(1)}, bf16[4,3,8,16,256]{4,3,2,1,0:T(8,128)(2,1)S(1)}) custom-call(s32[2,1,1]{2,1,0:T(1,128)S(1)} %copy.11.ids, f32[2,2,16,16,256]{4,3,2,1,0:T(8,128)S(1)} %copy-done, bf16[4,2,16,16,256]{4,3,2,1,0:T(8,128)(2,1)S(1)} %copy-done.1), custom_call_target="tpu_custom_call" | custom-call | tf_op jit(solution)/shard_map/pallas_call | solution.py:56
  5.0 2.1 %collective-permute-start.1 = (bf16[4,3,8,16,256]{4,3,2,1,0:T(8,128)(2,1)S(1)}, bf16[4,3,8,16,256]{4,3,2,1,0:T(8,128)(2,1)S(1)}, u32[]{:S(2)}, u32[]{:S(2)}) collective-permute-start(bf16[4,3,8,16,256]{4,3,2,1,0:T(8,128)(2,1)S(1)} %get-tuple-element.40), channel_id=1, source_target_pairs={{0,4},{4,0},{1,5},{5,1},{2,6},{6,2},{3,7},{7,3},{8,12},{12,8},{9,1... | collective-permute-start | bytes 2359304 | tf_op jit(solution)/shard_map/ppermute | solution.py:40
  7.2 1.4 %collective-permute-start.8 = (f32[3,16,8,256]{3,2,1,0:T(8,128)S(1)}, f32[3,16,8,256]{3,2,1,0:T(8,128)S(1)}, u32[]{:S(2)}, u32[]{:S(2)}) collective-permute-start(f32[3,16,8,256]{3,2,1,0:T(8,128)S(1)} %get-tuple-element.49), channel_id=1, source_target_pairs={{0,4},{4,0},{1,5},{5,1},{2,6},{6,2},{3,7},{7,3},{8,12},{12,8},{9,1... | collective-permute-start | bytes 1179656 | tf_op jit(solution)/shard_map/ppermute | solution.py:40
  8.6 34.7 %collective-permute-done.2.strip_in = f32[2,4,3,8,128]{4,3,2,1,0:T(8,128)S(1)} collective-permute-done((f32[2,4,3,8,128]{4,3,2,1,0:T(8,128)S(1)}, f32[2,4,3,8,128]{4,3,2,1,0:T(8,128)S(1)}, u32[]{:S(2)}, u32[]{:S(2)}) %collective-permute-start.2) | collective-permute-done | bytes 98336 | tf_op jit(solution)/shard_map/ppermute | solution.py:40
  43.3 1.0 %shard_map.51 = (f32[4,3,8,128]{3,2,1,0:T(8,128)S(1)}, f32[4,3,8,128]{3,2,1,0:T(8,128)S(1)}) custom-call(s32[2,1,1]{2,1,0:T(1,128)S(1)} %copy.11.ids, f32[2,2,16,16,256]{4,3,2,1,0:T(8,128)S(1)} %copy-done, bf16[4,2,16,16,256]{4,3,2,1,0:T(8,128)(2,1)S(1)} %copy-done.1, f32[2,4,3,8,128]{4,3,2,1,0:T(8,128)S(1)} %collective-permute-done.2.strip_in), custom_call_target="tpu_custom_call" | custom-call | tf_op jit(solution)/shard_map/pallas_call | solution.py:56
  44.4 1.3 %collective-permute-start.3 = (f32[4,3,8,128]{3,2,1,0:T(8,128)S(1)}, f32[4,3,8,128]{3,2,1,0:T(8,128)S(1)}, u32[]{:S(2)}, u32[]{:S(2)}) collective-permute-start(f32[4,3,8,128]{3,2,1,0:T(8,128)S(1)} %get-tuple-element.42), channel_id=1, source_target_pairs={{0,8},{8,16},{16,24},{24,0},{1,9},{9,17},{17,25},{25,1},{2,10},{10... | collective-permute-start | bytes 147464 | tf_op jit(solution)/shard_map/ppermute | solution.py:36
  45.6 2.1 %collective-permute-start.4 = (f32[4,3,8,128]{3,2,1,0:T(8,128)S(1)}, f32[4,3,8,128]{3,2,1,0:T(8,128)S(1)}, u32[]{:S(2)}, u32[]{:S(2)}) collective-permute-start(f32[4,3,8,128]{3,2,1,0:T(8,128)S(1)} %get-tuple-element.43), channel_id=1, source_target_pairs={{0,24},{8,0},{16,8},{24,16},{1,25},{9,1},{17,9},{25,17},{2,26},{10... | collective-permute-start | bytes 147464 | tf_op jit(solution)/shard_map/ppermute | solution.py:36
  47.7 1.4 %collective-permute-done.3.from_left = f32[4,3,8,128]{3,2,1,0:T(8,128)S(1)} collective-permute-done((f32[4,3,8,128]{3,2,1,0:T(8,128)S(1)}, f32[4,3,8,128]{3,2,1,0:T(8,128)S(1)}, u32[]{:S(2)}, u32[]{:S(2)}) %collective-permute-start.3) | collective-permute-done | bytes 49184 | tf_op jit(solution)/shard_map/ppermute | solution.py:36
  49.3 1.1 %shard_map.52 = (f32[16,24,384]{2,1,0:T(8,128)S(1)}, f32[16,24,128]{2,1,0:T(8,128)S(1)}, f32[4,16,24,384]{3,2,1,0:T(8,128)S(1)}, f32[24,384]{1,0:T(8,128)S(1)}, ...) custom-call(s32[2,1,1]{2,1,0:T(1,128)S(1)} %copy.11.ids, f32[2,2,16,16,256]{4,3,2,1,0:T(8,128)S(1)} %copy-done, ...), custom_call_target="tpu_custom_call" | custom-call | tf_op jit(solution)/shard_map/pallas_call | solution.py:56
  50.4 2.8 %collective-permute-start.6 = (f32[2,24,384]{2,1,0:T(8,128)S(1)}, f32[2,24,384]{2,1,0:T(8,128)S(1)}, u32[]{:S(2)}, u32[]{:S(2)}) collective-permute-start(f32[2,24,384]{2,1,0:T(8,128)S(1)} %get-tuple-element.47), channel_id=1, source_target_pairs={{0,3},{1,0},{2,1},{3,2},{4,7},{5,4},{6,5},{7,6},{8,11},{9,8},{10,9... | collective-permute-start | bytes 221192 | tf_op jit(solution)/shard_map/ppermute | solution.py:36
  53.3 1.2 %collective-permute-start.7 = (f32[3,16,384]{2,1,0:T(8,128)S(1)}, f32[3,16,384]{2,1,0:T(8,128)S(1)}, u32[]{:S(2)}, u32[]{:S(2)}) collective-permute-start(f32[3,16,384]{2,1,0:T(8,128)S(1)} %get-tuple-element.48), channel_id=1, source_target_pairs={{0,4},{4,0},{1,5},{5,1},{2,6},{6,2},{3,7},{7,3},{8,12},{12,8},{9,1... | collective-permute-start | bytes 221192 | tf_op jit(solution)/shard_map/ppermute | solution.py:40
  54.5 1.5 %collective-permute-start.5 = (f32[24,384]{1,0:T(8,128)S(1)}, f32[24,384]{1,0:T(8,128)S(1)}, u32[]{:S(2)}, u32[]{:S(2)}) collective-permute-start(f32[24,384]{1,0:T(8,128)S(1)} %get-tuple-element.46), channel_id=1, source_target_pairs={{0,1},{1,2},{2,3},{3,0},{4,5},{5,6},{6,7},{7,4},{8,9},{9,10},{10,1... | collective-permute-start | bytes 110600 | tf_op jit(solution)/shard_map/ppermute | solution.py:36
  56.0 1.1 %collective-permute-done.5.low_face = f32[24,384]{1,0:T(8,128)S(1)} collective-permute-done((f32[24,384]{1,0:T(8,128)S(1)}, f32[24,384]{1,0:T(8,128)S(1)}, u32[]{:S(2)}, u32[]{:S(2)}) %collective-permute-start.5) | collective-permute-done | bytes 36896 | tf_op jit(solution)/shard_map/ppermute | solution.py:36
  57.1 2.0 %shard_map.53 = (f32[16,24,384]{2,1,0:T(8,128)S(1)}, f32[16,24,384]{2,1,0:T(8,128)S(1)}, f32[16,24,384]{2,1,0:T(8,128)S(1)}, f32[16,24,256]{2,1,0:T(8,128)S(1)},...) custom-call(s32[2,1,1]{2,1,0:T(1,128)S(1)} %copy.11.ids, ...), custom_call_target="tpu_custom_call" | custom-call | tf_op jit(solution)/shard_map/pallas_call | solution.py:56
  59.1 1.3 %collective-permute-start.11 = (f32[2,16,384]{2,1,0:T(8,128)S(1)}, f32[2,16,384]{2,1,0:T(8,128)S(1)}, u32[]{:S(2)}, u32[]{:S(2)}) collective-permute-start(f32[2,16,384]{2,1,0:T(8,128)S(1)} %get-tuple-element.54), channel_id=1, source_target_pairs={{0,4},{4,0},{1,5},{5,1},{2,6},{6,2},{3,7},{7,3},{8,12},{12,8},{9,1... | collective-permute-start | bytes 147464 | tf_op jit(solution)/shard_map/ppermute | solution.py:40
  60.4 2.3 %collective-permute-start.9 = (f32[24,384]{1,0:T(8,128)S(1)}, f32[24,384]{1,0:T(8,128)S(1)}, u32[]{:S(2)}, u32[]{:S(2)}) collective-permute-start(f32[24,384]{1,0:T(8,128)S(1)} %get-tuple-element.52), channel_id=1, source_target_pairs={{0,1},{1,2},{2,3},{3,0},{4,5},{5,6},{6,7},{7,4},{8,9},{9,10},{10,1... | collective-permute-start | bytes 110600 | tf_op jit(solution)/shard_map/ppermute | solution.py:36
  62.7 1.1 %collective-permute-done.9.low_face = f32[24,384]{1,0:T(8,128)S(1)} collective-permute-done((f32[24,384]{1,0:T(8,128)S(1)}, f32[24,384]{1,0:T(8,128)S(1)}, u32[]{:S(2)}, u32[]{:S(2)}) %collective-permute-start.9) | collective-permute-done | bytes 36896 | tf_op jit(solution)/shard_map/ppermute | solution.py:36
  63.7 2.3 %collective-permute-done.10.high_face = f32[1,24,384]{2,1,0:T(8,128)S(1)} collective-permute-done((f32[1,24,384]{2,1,0:T(8,128)S(1)}, f32[1,24,384]{2,1,0:T(8,128)S(1)}, u32[]{:S(2)}, u32[]{:S(2)}) %collective-permute-start.10) | collective-permute-done | bytes 36896 | tf_op jit(solution)/shard_map/ppermute | solution.py:36
  66.0 1.7 %shard_map.54 = (f32[16,24,384]{2,1,0:T(8,128)S(1)}, f32[16,24,384]{2,1,0:T(8,128)S(1)}, f32[16,24,256]{2,1,0:T(8,128)S(1)}, f32[24,384]{1,0:T(8,128)S(1)}, f32[...) custom-call(s32[2,1,1]{2,1,0:T(1,128)S(1)} %copy.11.ids, f32[4,16,24,384]{3,2,1,0:T(8,128)S(1)} %get-tuple-element.44.wide, ...), custom_call_target="tpu_custom_call" | custom-call | tf_op jit(solution)/shard_map/pallas_call | solution.py:56
  68.8 0.8 collective-permute-done.12.low_face
  69.7 2.3 %collective-permute-done.13.high_face = f32[1,24,384]{2,1,0:T(8,128)S(1)} collective-permute-done((f32[1,24,384]{2,1,0:T(8,128)S(1)}, f32[1,24,384]{2,1,0:T(8,128)S(1)}, u32[]{:S(2)}, u32[]{:S(2)}) %collective-permute-start.13) | collective-permute-done | bytes 36896 | tf_op jit(solution)/shard_map/ppermute | solution.py:36
  72.0 1.7 %shard_map.55 = (f32[16,24,384]{2,1,0:T(8,128)S(1)}, f32[16,24,384]{2,1,0:T(8,128)S(1)}, f32[16,24,256]{2,1,0:T(8,128)S(1)}, f32[24,384]{1,0:T(8,128)S(1)}, f32[...) custom-call(s32[2,1,1]{2,1,0:T(1,128)S(1)} %copy.11.ids, f32[4,16,24,384]{3,2,1,0:T(8,128)S(1)} %get-tuple-element.44.wide, ...), custom_call_target="tpu_custom_call" | custom-call | tf_op jit(solution)/shard_map/pallas_call | solution.py:56
  73.7 1.0 %collective-permute-start.17 = (f32[2,16,384]{2,1,0:T(8,128)S(1)}, f32[2,16,384]{2,1,0:T(8,128)S(1)}, u32[]{:S(2)}, u32[]{:S(2)}) collective-permute-start(f32[2,16,384]{2,1,0:T(8,128)S(1)} %get-tuple-element.67), channel_id=1, source_target_pairs={{0,4},{4,0},{1,5},{5,1},{2,6},{6,2},{3,7},{7,3},{8,12},{12,8},{9,1... | collective-permute-start | bytes 147464 | tf_op jit(solution)/shard_map/ppermute | solution.py:40
  75.2 0.8 collective-permute-done.15.low_face
  76.0 2.3 %collective-permute-done.16.high_face = f32[1,24,384]{2,1,0:T(8,128)S(1)} collective-permute-done((f32[1,24,384]{2,1,0:T(8,128)S(1)}, f32[1,24,384]{2,1,0:T(8,128)S(1)}, u32[]{:S(2)}, u32[]{:S(2)}) %collective-permute-start.16) | collective-permute-done | bytes 36896 | tf_op jit(solution)/shard_map/ppermute | solution.py:36
  78.3 2.4 %shard_map.56 = (f32[16,24,384]{2,1,0:T(8,128)S(1)}, f32[16,24,384]{2,1,0:T(8,128)S(1)}, f32[16,24,256]{2,1,0:T(8,128)}, f32[24,384]{1,0:T(8,128)S(1)}, f32[1,24...) custom-call(s32[2,1,1]{2,1,0:T(1,128)S(1)} %copy.11.ids, f32[4,16,24,384]{3,2,1,0:T(8,128)S(1)} %get-tuple-element.44.wide, ...), custom_call_target="tpu_custom_call" | custom-call | tf_op jit(solution)/shard_map/pallas_call | solution.py:56
  81.9 0.8 collective-permute-done.18.low_face
  82.7 2.3 %collective-permute-done.19.high_face = f32[1,24,384]{2,1,0:T(8,128)S(1)} collective-permute-done((f32[1,24,384]{2,1,0:T(8,128)S(1)}, f32[1,24,384]{2,1,0:T(8,128)S(1)}, u32[]{:S(2)}, u32[]{:S(2)}) %collective-permute-start.19) | collective-permute-done | bytes 36896 | tf_op jit(solution)/shard_map/ppermute | solution.py:36
  85.0 2.3 %shard_map.57 = f32[16,24,256]{2,1,0:T(8,128)} custom-call(s32[2,1,1]{2,1,0:T(1,128)S(1)} %copy.11.ids, f32[4,16,24,384]{3,2,1,0:T(8,128)S(1)} %get-tuple-element.44.wide, f32[16,24,384]{2,1,0:T(8,128)S(1)} %get-tuple-element.71.field, f32[24,384]{1,0:T(8,128)S(1)} %collective-permute-done.18.low_face, f32[1,24,384]{2,1,0:T(8,128)S(1)} %collective-permute-done.19.high_face, ...), custom_call_target="tpu_custom_call" | custom-call | tf_op jit(solution)/shard_map/pallas_call | solution.py:56
  (23 shorter events, 3.1 us)
Async XLA Ops:
  1.4 1.2 %copy-start = (f32[2,2,16,16,256]{4,3,2,1,0:T(8,128)S(1)}, f32[2,2,16,16,256]{4,3,2,1,0:T(8,128)}, u32[]{:S(2)}) copy-start(f32[2,2,16,16,256]{4,3,2,1,0:T(8,128)} %refs_0_.1) | copy-start | bytes 3145732
  2.6 1.2 %copy-start.1 = (bf16[4,2,16,16,256]{4,3,2,1,0:T(8,128)(2,1)S(1)}, bf16[4,2,16,16,256]{4,3,2,1,0:T(8,128)(2,1)}, u32[]{:S(2)}) copy-start(bf16[4,2,16,16,256]{4,3,2,1,0:T(8,128)(2,1)} %coef.5) | copy-start | bytes 3145732
  5.0 44.3 %collective-permute-start.1 = (bf16[4,3,8,16,256]{4,3,2,1,0:T(8,128)(2,1)S(1)}, bf16[4,3,8,16,256]{4,3,2,1,0:T(8,128)(2,1)S(1)}, u32[]{:S(2)}, u32[]{:S(2)}) collective-permute-start(bf16[4,3,8,16,256]{4,3,2,1,0:T(8,128)(2,1)S(1)} %get-tuple-element.40), channel_id=1, source_target_pairs={{0,4},{4,0},{1,5},{5,1},{2,6},{6,2},{3,7},{7,3},{8,12},{12,8},{9,1... | collective-permute-start | bytes 2359304 | tf_op jit(solution)/shard_map/ppermute | solution.py:40
  7.1 42.2 %collective-permute-start = (f32[3,16,8,256]{3,2,1,0:T(8,128)S(1)}, f32[3,16,8,256]{3,2,1,0:T(8,128)S(1)}, u32[]{:S(2)}, u32[]{:S(2)}) collective-permute-start(f32[3,16,8,256]{3,2,1,0:T(8,128)S(1)} %get-tuple-element.39), channel_id=1, source_target_pairs={{0,4},{4,0},{1,5},{5,1},{2,6},{6,2},{3,7},{7,3},{8,12},{12,8},{9,1... | collective-permute-start | bytes 1179656 | tf_op jit(solution)/shard_map/ppermute | solution.py:40
  7.2 48.8 %collective-permute-start.8 = (f32[3,16,8,256]{3,2,1,0:T(8,128)S(1)}, f32[3,16,8,256]{3,2,1,0:T(8,128)S(1)}, u32[]{:S(2)}, u32[]{:S(2)}) collective-permute-start(f32[3,16,8,256]{3,2,1,0:T(8,128)S(1)} %get-tuple-element.49), channel_id=1, source_target_pairs={{0,4},{4,0},{1,5},{5,1},{2,6},{6,2},{3,7},{7,3},{8,12},{12,8},{9,1... | collective-permute-start | bytes 1179656 | tf_op jit(solution)/shard_map/ppermute | solution.py:40
  8.6 34.8 %collective-permute-start.2 = (f32[2,4,3,8,128]{4,3,2,1,0:T(8,128)S(1)}, f32[2,4,3,8,128]{4,3,2,1,0:T(8,128)S(1)}, u32[]{:S(2)}, u32[]{:S(2)}) collective-permute-start(f32[2,4,3,8,128]{4,3,2,1,0:T(8,128)S(1)} %get-tuple-element.41), channel_id=1, source_target_pairs={{0,4},{4,0},{1,5},{5,1},{2,6},{6,2},{3,7},{7,3},{8,12},{12,8},{9,1... | collective-permute-start | bytes 294920 | tf_op jit(solution)/shard_map/ppermute | solution.py:40
  44.4 4.8 %collective-permute-start.3 = (f32[4,3,8,128]{3,2,1,0:T(8,128)S(1)}, f32[4,3,8,128]{3,2,1,0:T(8,128)S(1)}, u32[]{:S(2)}, u32[]{:S(2)}) collective-permute-start(f32[4,3,8,128]{3,2,1,0:T(8,128)S(1)} %get-tuple-element.42), channel_id=1, source_target_pairs={{0,8},{8,16},{16,24},{24,0},{1,9},{9,17},{17,25},{25,1},{2,10},{10... | collective-permute-start | bytes 147464 | tf_op jit(solution)/shard_map/ppermute | solution.py:36
  45.6 3.7 %collective-permute-start.4 = (f32[4,3,8,128]{3,2,1,0:T(8,128)S(1)}, f32[4,3,8,128]{3,2,1,0:T(8,128)S(1)}, u32[]{:S(2)}, u32[]{:S(2)}) collective-permute-start(f32[4,3,8,128]{3,2,1,0:T(8,128)S(1)} %get-tuple-element.43), channel_id=1, source_target_pairs={{0,24},{8,0},{16,8},{24,16},{1,25},{9,1},{17,9},{25,17},{2,26},{10... | collective-permute-start | bytes 147464 | tf_op jit(solution)/shard_map/ppermute | solution.py:36
  50.4 6.6 %collective-permute-start.6 = (f32[2,24,384]{2,1,0:T(8,128)S(1)}, f32[2,24,384]{2,1,0:T(8,128)S(1)}, u32[]{:S(2)}, u32[]{:S(2)}) collective-permute-start(f32[2,24,384]{2,1,0:T(8,128)S(1)} %get-tuple-element.47), channel_id=1, source_target_pairs={{0,3},{1,0},{2,1},{3,2},{4,7},{5,4},{6,5},{7,6},{8,11},{9,8},{10,9... | collective-permute-start | bytes 221192 | tf_op jit(solution)/shard_map/ppermute | solution.py:36
  53.3 3.8 %collective-permute-start.7 = (f32[3,16,384]{2,1,0:T(8,128)S(1)}, f32[3,16,384]{2,1,0:T(8,128)S(1)}, u32[]{:S(2)}, u32[]{:S(2)}) collective-permute-start(f32[3,16,384]{2,1,0:T(8,128)S(1)} %get-tuple-element.48), channel_id=1, source_target_pairs={{0,4},{4,0},{1,5},{5,1},{2,6},{6,2},{3,7},{7,3},{8,12},{12,8},{9,1... | collective-permute-start | bytes 221192 | tf_op jit(solution)/shard_map/ppermute | solution.py:40
  54.5 2.5 %collective-permute-start.5 = (f32[24,384]{1,0:T(8,128)S(1)}, f32[24,384]{1,0:T(8,128)S(1)}, u32[]{:S(2)}, u32[]{:S(2)}) collective-permute-start(f32[24,384]{1,0:T(8,128)S(1)} %get-tuple-element.46), channel_id=1, source_target_pairs={{0,1},{1,2},{2,3},{3,0},{4,5},{5,6},{6,7},{7,4},{8,9},{9,10},{10,1... | collective-permute-start | bytes 110600 | tf_op jit(solution)/shard_map/ppermute | solution.py:36
  59.1 6.9 %collective-permute-start.11 = (f32[2,16,384]{2,1,0:T(8,128)S(1)}, f32[2,16,384]{2,1,0:T(8,128)S(1)}, u32[]{:S(2)}, u32[]{:S(2)}) collective-permute-start(f32[2,16,384]{2,1,0:T(8,128)S(1)} %get-tuple-element.54), channel_id=1, source_target_pairs={{0,4},{4,0},{1,5},{5,1},{2,6},{6,2},{3,7},{7,3},{8,12},{12,8},{9,1... | collective-permute-start | bytes 147464 | tf_op jit(solution)/shard_map/ppermute | solution.py:40
  60.4 3.3 %collective-permute-start.9 = (f32[24,384]{1,0:T(8,128)S(1)}, f32[24,384]{1,0:T(8,128)S(1)}, u32[]{:S(2)}, u32[]{:S(2)}) collective-permute-start(f32[24,384]{1,0:T(8,128)S(1)} %get-tuple-element.52), channel_id=1, source_target_pairs={{0,1},{1,2},{2,3},{3,0},{4,5},{5,6},{6,7},{7,4},{8,9},{9,10},{10,1... | collective-permute-start | bytes 110600 | tf_op jit(solution)/shard_map/ppermute | solution.py:36
  62.6 3.4 %collective-permute-start.10 = (f32[1,24,384]{2,1,0:T(8,128)S(1)}, f32[1,24,384]{2,1,0:T(8,128)S(1)}, u32[]{:S(2)}, u32[]{:S(2)}) collective-permute-start(f32[1,24,384]{2,1,0:T(8,128)S(1)} %get-tuple-element.53), channel_id=1, source_target_pairs={{0,3},{1,0},{2,1},{3,2},{4,7},{5,4},{6,5},{7,6},{8,11},{9,8},{10,9... | collective-permute-start | bytes 110600 | tf_op jit(solution)/shard_map/ppermute | solution.py:36
  67.7 4.3 %collective-permute-start.14 = (f32[2,16,384]{2,1,0:T(8,128)S(1)}, f32[2,16,384]{2,1,0:T(8,128)S(1)}, u32[]{:S(2)}, u32[]{:S(2)}) collective-permute-start(f32[2,16,384]{2,1,0:T(8,128)S(1)} %get-tuple-element.61), channel_id=1, source_target_pairs={{0,4},{4,0},{1,5},{5,1},{2,6},{6,2},{3,7},{7,3},{8,12},{12,8},{9,1... | collective-permute-start | bytes 147464 | tf_op jit(solution)/shard_map/ppermute | solution.py:40
  68.3 1.3 %collective-permute-start.12 = (f32[24,384]{1,0:T(8,128)S(1)}, f32[24,384]{1,0:T(8,128)S(1)}, u32[]{:S(2)}, u32[]{:S(2)}) collective-permute-start(f32[24,384]{1,0:T(8,128)S(1)} %get-tuple-element.59), channel_id=1, source_target_pairs={{0,1},{1,2},{2,3},{3,0},{4,5},{5,6},{6,7},{7,4},{8,9},{9,10},{10,1... | collective-permute-start | bytes 110600 | tf_op jit(solution)/shard_map/ppermute | solution.py:36
  68.6 3.4 %collective-permute-start.13 = (f32[1,24,384]{2,1,0:T(8,128)S(1)}, f32[1,24,384]{2,1,0:T(8,128)S(1)}, u32[]{:S(2)}, u32[]{:S(2)}) collective-permute-start(f32[1,24,384]{2,1,0:T(8,128)S(1)} %get-tuple-element.60), channel_id=1, source_target_pairs={{0,3},{1,0},{2,1},{3,2},{4,7},{5,4},{6,5},{7,6},{8,11},{9,8},{10,9... | collective-permute-start | bytes 110600 | tf_op jit(solution)/shard_map/ppermute | solution.py:36
  73.7 4.7 %collective-permute-start.17 = (f32[2,16,384]{2,1,0:T(8,128)S(1)}, f32[2,16,384]{2,1,0:T(8,128)S(1)}, u32[]{:S(2)}, u32[]{:S(2)}) collective-permute-start(f32[2,16,384]{2,1,0:T(8,128)S(1)} %get-tuple-element.67), channel_id=1, source_target_pairs={{0,4},{4,0},{1,5},{5,1},{2,6},{6,2},{3,7},{7,3},{8,12},{12,8},{9,1... | collective-permute-start | bytes 147464 | tf_op jit(solution)/shard_map/ppermute | solution.py:40
  74.7 1.3 %collective-permute-start.15 = (f32[24,384]{1,0:T(8,128)S(1)}, f32[24,384]{1,0:T(8,128)S(1)}, u32[]{:S(2)}, u32[]{:S(2)}) collective-permute-start(f32[24,384]{1,0:T(8,128)S(1)} %get-tuple-element.65), channel_id=1, source_target_pairs={{0,1},{1,2},{2,3},{3,0},{4,5},{5,6},{6,7},{7,4},{8,9},{9,10},{10,1... | collective-permute-start | bytes 110600 | tf_op jit(solution)/shard_map/ppermute | solution.py:36
  74.9 3.4 %collective-permute-start.16 = (f32[1,24,384]{2,1,0:T(8,128)S(1)}, f32[1,24,384]{2,1,0:T(8,128)S(1)}, u32[]{:S(2)}, u32[]{:S(2)}) collective-permute-start(f32[1,24,384]{2,1,0:T(8,128)S(1)} %get-tuple-element.66), channel_id=1, source_target_pairs={{0,3},{1,0},{2,1},{3,2},{4,7},{5,4},{6,5},{7,6},{8,11},{9,8},{10,9... | collective-permute-start | bytes 110600 | tf_op jit(solution)/shard_map/ppermute | solution.py:36
  80.7 4.3 %collective-permute-start.20 = (f32[2,16,384]{2,1,0:T(8,128)S(1)}, f32[2,16,384]{2,1,0:T(8,128)S(1)}, u32[]{:S(2)}, u32[]{:S(2)}) collective-permute-start(f32[2,16,384]{2,1,0:T(8,128)S(1)} %get-tuple-element.74), channel_id=1, source_target_pairs={{0,4},{4,0},{1,5},{5,1},{2,6},{6,2},{3,7},{7,3},{8,12},{12,8},{9,1... | collective-permute-start | bytes 147464 | tf_op jit(solution)/shard_map/ppermute | solution.py:40
  81.3 1.3 %collective-permute-start.18 = (f32[24,384]{1,0:T(8,128)S(1)}, f32[24,384]{1,0:T(8,128)S(1)}, u32[]{:S(2)}, u32[]{:S(2)}) collective-permute-start(f32[24,384]{1,0:T(8,128)S(1)} %get-tuple-element.72), channel_id=1, source_target_pairs={{0,1},{1,2},{2,3},{3,0},{4,5},{5,6},{6,7},{7,4},{8,9},{9,10},{10,1... | collective-permute-start | bytes 110600 | tf_op jit(solution)/shard_map/ppermute | solution.py:36
  81.6 3.4 %collective-permute-start.19 = (f32[1,24,384]{2,1,0:T(8,128)S(1)}, f32[1,24,384]{2,1,0:T(8,128)S(1)}, u32[]{:S(2)}, u32[]{:S(2)}) collective-permute-start(f32[1,24,384]{2,1,0:T(8,128)S(1)} %get-tuple-element.73), channel_id=1, source_target_pairs={{0,3},{1,0},{2,1},{3,2},{4,7},{5,4},{6,5},{7,6},{8,11},{9,8},{10,9... | collective-permute-start | bytes 110600 | tf_op jit(solution)/shard_map/ppermute | solution.py:36

commit v2 on v1

v2 whole, which is shorter than its diff:
```python
import functools

import jax
import jax.numpy as jnp
from jax import lax
from jax.experimental import pallas as pl
from jax.experimental.pallas import tpu as pltpu
from jax.sharding import PartitionSpec as P

SWEEPS = 4
LANES = 128
STRIP = 8
SHIFT = 4096.0
VMEM_LIMIT = 24 * 1024 * 1024


def chebyshev_weights(count):
    low_bound = 0.25
    high_bound = 2.0
    centre_value = 0.5 * (high_bound + low_bound)
    half_width = 0.5 * (high_bound - low_bound)
    ratio_value = centre_value / half_width
    damping = 1.0 / ratio_value
    first_list = [0.0]
    second_list = [1.0 / centre_value]
    for step_index in range(1, count):
        damping_next = 1.0 / (2.0 * ratio_value - damping)
        first_list.append(damping_next * damping)
        second_list.append(2.0 * damping_next / half_width)
        damping = damping_next
    return (first_list, second_list)


def shifted(value, axis, steps):
    count = lax.axis_size(axis)
    return lax.ppermute(value, axis, [(i, (i + steps) % count) for i in range(count)])


def swapped(value):
    return lax.ppermute(value, "gy", [(i, i ^ 1) for i in range(lax.axis_size("gy"))])


def row_ghosts(rows):
    if lax.axis_size("gy") == 2:
        return swapped(rows)
    return jnp.concatenate([shifted(rows[:1], "gy", 1), shifted(rows[1:], "gy", -1)])


def f32(*shape):
    return jax.ShapeDtypeStruct(shape, jnp.float32)


def call(kernel, outs, *operands, ids=False):
    specs = [pl.BlockSpec(memory_space=pltpu.VMEM) for _ in operands]
    if ids:
        specs[0] = pl.BlockSpec(memory_space=pltpu.SMEM)
    return pl.pallas_call(
        kernel,
        out_shape=outs,
        in_specs=specs,
        out_specs=[pl.BlockSpec(memory_space=pltpu.VMEM) for _ in outs],
        compiler_params=pltpu.CompilerParams(vmem_limit_bytes=VMEM_LIMIT),
    )(*operands)


def lane_of(shape):
    return lax.broadcasted_iota(jnp.int32, shape, 1)


def row_of(shape):
    return lax.broadcasted_iota(jnp.int32, shape, 0)


def units_of(ids, half):
    first = 3 * (lax.axis_index("gy") // 2)
    a, b = ids[0] - first, ids[1] - first
    found = []
    for k in range(3):
        unit = 3 * half + k
        slab = unit // 2
        found.append((jnp.logical_or(a == slab, b == slab), jnp.where(a == slab, 0, 1), unit % 2))
    return found


def field_unit(fields, item, place, z):
    rows = fields.shape[3] // 2
    _, slot, part = place
    return fields[item, slot, z, pl.ds(pl.multiple_of(part * rows, rows), rows), :]


def coef_unit(coef, item, place, z):
    rows = coef.shape[3] // 2
    _, slot, part = place
    both = coef[item, slot, z].astype(jnp.float32)
    return jnp.where(part == 0, both[:rows], both[rows:])


def strips(fields, coef, item, place, planes):
    columns, rows = fields.shape[4], fields.shape[3] // 2
    group = lane_of((rows, LANES)) // STRIP
    low = jnp.zeros((rows, LANES), jnp.float32)
    high = jnp.zeros((rows, LANES), jnp.float32)
    for z in range(planes):
        if item < 2:
            cells = field_unit(fields, item, place, z)
        else:
            cells = coef_unit(coef, 2 * item - 4, place, z) + SHIFT * coef_unit(coef, 2 * item - 3, place, z)
        first, last = cells[:, :LANES], cells[:, columns - LANES :]
        turn = STRIP * z
        low = jnp.where(group == z, pltpu.roll(first, turn, 1) if turn else first, low)
        turn = (STRIP * z + STRIP) % LANES
        high = jnp.where(group == z, pltpu.roll(last, turn, 1) if turn else last, high)
    return low, high


def take_kernel(ids, fields, start_out, sems):
    rows = fields.shape[3] // 2
    copies = []
    for k, (_, slot, part) in enumerate(units_of(ids, 1 - lax.axis_index("gy") % 2)):
        source = fields.at[0, slot, :, pl.ds(pl.multiple_of(part * rows, rows), rows), :]
        copies.append(pltpu.make_async_copy(source, start_out.at[k], sems.at[k]))
    for copy in copies:
        copy.start()
    for copy in copies:
        copy.wait()


def edge_kernel(ids, fields, coef, strip_out):
    planes = fields.shape[2]
    for k, place in enumerate(units_of(ids, 1 - lax.axis_index("gy") % 2)):
        for item in range(4):
            low, high = strips(fields, coef, item, place, planes)
            strip_out[0, item, k] = low
            strip_out[1, item, k] = high


def coef_kernel(first, ids, coef, _, out):
    planes = coef.shape[2]
    for k, place in enumerate(units_of(ids, 1 - lax.axis_index("gy") % 2)):
        for part in range(2):
            for z in range(0, planes, 2):
                both = [coef_unit(coef, first + part, place, z + j) for j in range(2)]
                out[part, k, z // 2] = jnp.concatenate(both).astype(jnp.bfloat16)


def rhs_kernel(ids, fields, _, out):
    for k, place in enumerate(units_of(ids, 1 - lax.axis_index("gy") % 2)):
        for z in range(fields.shape[2]):
            out[k, z] = field_unit(fields, 1, place, z)


def strip_kernel(ids, fields, coef, strip_in, left, right):
    planes = fields.shape[2]
    for k, place in enumerate(units_of(ids, lax.axis_index("gy") % 2)):
        for item in range(4):
            low, high = strips(fields, coef, item, place, planes)
            left[item, k] = jnp.where(place[0], low, strip_in[0, item, k])
            right[item, k] = jnp.where(place[0], high, strip_in[1, item, k])


def ghost_columns(from_left, from_right, item, k, z):
    low, high = from_left[item, k], from_right[item, k]
    turn = (LANES - STRIP * z) % LANES
    right = pltpu.roll(high, turn, 1) if turn else high
    turn = (LANES - STRIP - STRIP * z) % LANES
    left = pltpu.roll(low, turn, 1) if turn else low
    return jnp.where(lane_of(low.shape) < LANES // 2, right, left)


def coef_gather(coef, coef_in, item, place, k, z):
    rows = coef.shape[3] // 2
    got = coef_in[item % 2, k, z // 2].astype(jnp.float32)
    got = got[rows:] if z % 2 else got[:rows]
    return jnp.where(place[0], coef_unit(coef, item, place, z), got)


def gather_kernel(
    ids, fields, coef, start_in, coef_in, from_left, from_right, start, rhs_ghost, wide, ghosts, up, down, rows_out
):
    _, _, planes, rows, columns = fields.shape
    rows //= 2
    for k, place in enumerate(units_of(ids, lax.axis_index("gy") % 2)):
        at = slice(k * rows, (k + 1) * rows)
        for z in range(planes):
            start[z, at, :columns] = jnp.where(place[0], field_unit(fields, 0, place, z), start_in[k, z])
            start[z, at, columns:] = ghost_columns(from_left, from_right, 0, k, z)
            rhs_ghost[z, at] = ghost_columns(from_left, from_right, 1, k, z)
            for item in (2, 3):
                both = ghost_columns(from_left, from_right, item, k, z)
                b = jnp.floor(both * 0.125) * (8.0 / SHIFT)
                a = both - SHIFT * b
                if item == 2:
                    ghosts[0, z, at], ghosts[1, z, at] = a, b
                else:
                    wide[0, z, at, columns:], wide[1, z, at, columns:] = a, b
            for part in (0, 1):
                wide[part, z, at, :columns] = coef_gather(coef, coef_in, part + 2, place, k, z)
    last = 3 * rows - 1
    up[...] = start[planes - 1]
    down[0] = start[0]
    down[1] = wide[1, 0]
    for z in range(planes):
        rows_out[0, z : z + 1] = start[z, last : last + 1]
        rows_out[1, z : z + 1] = start[z, 0:1]
        rows_out[2, z : z + 1] = wide[0, z, 0:1]


def spread_kernel(ids, coef, coef_in, ghosts, wide):
    planes, columns, rows = coef.shape[2], coef.shape[4], coef.shape[3] // 2
    for part in (0, 1):
        wide[part, :, :, columns:] = ghosts[part]
        for k, place in enumerate(units_of(ids, lax.axis_index("gy") % 2)):
            at = slice(k * rows, (k + 1) * rows)
            for z in range(planes):
                wide[part, z, at, :columns] = coef_gather(coef, coef_in, part, place, k, z)


def image_plane(value, low_row, high_row, lower_flux, upper_flux, alpha, beta_x, beta_y, rim_row):
    rows, width = value.shape
    flux_x = beta_x * (value - pltpu.roll(value, 1, 1))
    row = row_of(value.shape)
    before = jnp.where(row == 0, 0.0 if low_row is None else low_row, pltpu.roll(value, 1, 0))
    flux_y = beta_y * (value - before)
    last = value[rows - 1 : rows]
    top = rim_row * (-last if high_row is None else high_row - last)
    after = jnp.where(row == rows - 1, top, pltpu.roll(flux_y, rows - 1, 0))
    return (
        alpha * value
        + (flux_x - pltpu.roll(flux_x, width - 1, 1))
        + (flux_y - after)
        + (lower_flux - upper_flux)
    )


def images(plane, wide_ax, wide_yz, rim_face, rim_rows, low_face=None, high_face=None, ghost_rows=None):
    planes = wide_ax.shape[1]
    (value, *others), beta_z = plane(0), wide_yz[1, 0]
    lower = beta_z * (value if low_face is None else value - low_face[...])
    for z in range(planes):
        at = slice(z, z + 1)
        if z + 1 < planes:
            (following, *next_others), next_z = plane(z + 1), wide_yz[1, z + 1]
            upper = next_z * (following - value)
        else:
            following, next_others, next_z = None, None, rim_face[1]
            upper = next_z * (-value if high_face is None else high_face[0] - value)
        low_row, high_row = (None, None) if ghost_rows is None else (ghost_rows[0, at], ghost_rows[1, at])
        image = image_plane(
            value, low_row, high_row, lower, upper, wide_ax[0, z], wide_ax[1, z], wide_yz[0, z], rim_rows[2, at]
        )
        yield z, (value, *others), image, beta_z, next_z
        value, others, lower, beta_z = following, next_others, upper, next_z


def first_kernel(
    wide_ax, wide_yz, field, low_face, high_face, ghost_rows, image_out, inverse
):
    _, rows, width = field.shape
    for z, (value,), image, beta_z, next_z in images(
        lambda z: (field[z],), wide_ax, wide_yz, high_face, ghost_rows, low_face, high_face, ghost_rows
    ):
        image_out[z] = image
        beta_x, beta_y = wide_ax[1, z], wide_yz[0, z]
        rim_row = ghost_rows[2, z : z + 1]
        next_y = jnp.where(row_of(value.shape) == rows - 1, rim_row, pltpu.roll(beta_y, rows - 1, 0))
        next_x = pltpu.roll(beta_x, width - 1, 1)
        inverse[z] = 1.0 / (wide_ax[0, z] + beta_x + next_x + beta_y + next_y + beta_z + next_z)


def store_faces(direction, up, down, rows_out):
    planes, rows, _ = direction.shape
    up[...] = direction[planes - 1]
    down[0] = direction[0]
    for z in range(planes):
        rows_out[0, z : z + 1] = direction[z, rows - 1 : rows]
        rows_out[1, z : z + 1] = direction[z, 0:1]


def start_kernel(
    second, ids, fields, rhs_in, rhs_ghost, image, inverse, start, residual, direction, total, up, down, rows_out
):
    planes, _, _ = start.shape
    columns = fields.shape[4]
    places = units_of(ids, lax.axis_index("gy") % 2)
    for z in range(planes):
        parts = [jnp.where(place[0], field_unit(fields, 1, place, z), rhs_in[k, z]) for k, place in enumerate(places)]
        left = jnp.concatenate([jnp.concatenate(parts), rhs_ghost[z]], axis=1) - image[z]
        step = second * (inverse[z] * left)
        residual[z] = left
        direction[z] = step
        total[z] = start[z, :, :columns] + step[:, :columns]
    store_faces(direction, up, down, rows_out)


def halo_flux(z, wide_yz, rim_face, rim_rows, low_face, high_face, ghost_rows):
    _, planes, rows, width = wide_yz.shape
    at, row = slice(z, z + 1), row_of((rows, width))
    top = jnp.where(row == rows - 1, rim_rows[2, at] * ghost_rows[1, at], 0.0)
    flux = jnp.where(row == 0, wide_yz[0, z, 0:1] * ghost_rows[0, at], top)
    if z == 0:
        flux = flux + wide_yz[1, 0] * low_face[...]
    if z == planes - 1:
        flux = flux + rim_face[1] * high_face[0]
    return flux


def inner_kernel(weights, wide_ax, wide_yz, rim_face, rim_rows, field, old, inverse, sum_in, *refs):
    before, first, second = weights
    rims = rim_face, rim_rows
    halo = refs[:3] if before else None
    if second:
        residual, direction, total = refs[-3:]
    else:
        residual, total = refs[-2:]
    columns = total.shape[2]

    def plane(z):
        if not before:
            return field[z], old[z], sum_in[z]
        flux = halo_flux(z, wide_yz, *rims, *halo)
        step = before * (inverse[z] * flux)
        return field[z] + step, old[z] + flux, sum_in[z] + step[:, :columns]

    for z, (value, left, done), image, _, _ in images(plane, wide_ax, wide_yz, *rims):
        left = left - image
        if second:
            step = first * value + second * (inverse[z] * left)
            residual[z] = left
            direction[z] = step
            total[z] = done + step[:, :columns]
        else:
            residual[z] = left[:, :columns]
            total[z] = done


def faces_kernel(second, wide_yz, rim_face, rim_rows, low_face, high_face, ghost_rows, inverse, direction, up, down, rows_out):
    halo = wide_yz, rim_face, rim_rows, low_face, high_face, ghost_rows
    planes, rows, _ = direction.shape
    for z, out in ((0, down.at[0]), (planes - 1, up)):
        out[...] = direction[z] + second * (inverse[z] * halo_flux(z, *halo))
    for z in range(planes):
        at = slice(z, z + 1)
        for edge, row, out in ((0, 0, 1), (1, rows - 1, 0)):
            line = slice(row, row + 1)
            if z == 0:
                rows_out[out, at] = down[0, line]
            elif z == planes - 1:
                rows_out[out, at] = up[line]
            else:
                beta = rim_rows[2, at] if edge else wide_yz[0, z, line]
                flux = beta * ghost_rows[edge, at]
                rows_out[out, at] = direction[z, line] + second * (inverse[z, line] * flux)


def last_kernel(wide_yz, rim_face, rim_rows, low_face, high_face, ghost_rows, partial, residual):
    planes, _, columns = residual.shape
    for z in range(planes):
        flux = halo_flux(z, wide_yz, rim_face, rim_rows, low_face, high_face, ghost_rows)
        residual[z] = partial[z] + flux[:, :columns]


def local(old_fields, old_coef, held_slabs):
    _, _, planes, rows, columns = old_fields.shape
    half = rows // 2
    rows = 3 * half
    width = columns + LANES
    full, own = f32(planes, rows, width), f32(planes, rows, columns)
    unit = f32(3, planes, half, columns)
    ids = held_slabs.reshape(2)
    start_out = pl.pallas_call(
        take_kernel,
        out_shape=unit,
        in_specs=[pl.BlockSpec(memory_space=pltpu.SMEM), pl.BlockSpec(memory_space=pl.ANY)],
        out_specs=pl.BlockSpec(memory_space=pltpu.VMEM),
        scratch_shapes=[pltpu.SemaphoreType.DMA((3,))],
    )(ids, old_fields)
    start_in = swapped(start_out)
    coef_units = jax.ShapeDtypeStruct((2, 3, planes // 2, 2 * half, columns), jnp.bfloat16)
    (strip_out,) = call(edge_kernel, [f32(2, 4, 3, half, LANES)], ids, old_fields, old_coef, ids=True)
    strip_in = swapped(strip_out)
    (coef_yz,) = call(functools.partial(coef_kernel, 2), [coef_units], ids, old_coef, strip_out, ids=True)
    yz_in = swapped(coef_yz)
    (coef_ax,) = call(functools.partial(coef_kernel, 0), [coef_units], ids, old_coef, coef_yz, ids=True)
    ax_in = swapped(coef_ax)
    strip = f32(4, 3, half, LANES)
    left, right = call(strip_kernel, [strip, strip], ids, old_fields, old_coef, strip_in, ids=True)
    from_left, from_right = shifted(right, "gx", 1), shifted(left, "gx", -1)
    coef_full = f32(2, planes, rows, width)
    field, rhs_ghost, wide_yz, ghosts, up, down, rows_out = call(
        gather_kernel,
        [
            full,
            f32(planes, rows, LANES),
            coef_full,
            f32(2, planes, rows, LANES),
            f32(rows, width),
            f32(2, rows, width),
            f32(3, planes, width),
        ],
        ids,
        old_fields,
        old_coef,
        start_in,
        yz_in,
        from_left,
        from_right,
        ids=True,
    )
    low_face, rim_face, rim_rows = shifted(up, "gz", 1), shifted(down, "gz", -1), row_ghosts(rows_out)
    (rhs_out,) = call(rhs_kernel, [unit], ids, old_fields, rows_out, ids=True)
    rhs_in = swapped(rhs_out)
    (wide_ax,) = call(spread_kernel, [coef_full], ids, old_coef, ax_in, ghosts, ids=True)
    image, inverse = call(first_kernel, [full, full], wide_ax, wide_yz, field, low_face, rim_face, rim_rows)
    first_list, second_list = chebyshev_weights(SWEEPS)
    faces = [f32(rows, width), f32(1, rows, width), f32(2, planes, width)]
    residual, direction, total, up, down, rows_out = call(
        functools.partial(start_kernel, second_list[0]),
        [full, full, own] + faces,
        ids,
        old_fields,
        rhs_in,
        rhs_ghost,
        image,
        inverse,
        field,
        ids=True,
    )
    rims, halo = (rim_face, rim_rows), ()
    for stage in range(1, SWEEPS + 1):
        before = second_list[stage - 1] if halo else 0.0
        last = stage == SWEEPS
        weights = (before, 0.0, 0.0) if last else (before, first_list[stage], second_list[stage])
        arrived = halo
        halo = shifted(up, "gz", 1), shifted(down, "gz", -1), row_ghosts(rows_out)
        state = call(
            functools.partial(inner_kernel, weights),
            [own, own] if last else [full, full, own],
            wide_ax,
            wide_yz,
            *rims,
            direction,
            residual,
            inverse,
            total,
            *arrived,
        )
        if last:
            residual, total = state
            (residual,) = call(last_kernel, [own], wide_yz, *rims, *halo, residual)
        else:
            residual, direction, total = state
            up, down, rows_out = call(
                functools.partial(faces_kernel, second_list[stage]), faces, wide_yz, *rims, *halo, inverse, direction
            )
    return total, residual


def solution(mesh):
    in_specs = (
        P(None, "gy", "gz", None, "gx"),
        P(None, "gy", "gz", None, "gx"),
        P("gy", "gz", "gx"),
    )
    out_specs = (P("gz", "gy", "gx"), P("gz", "gy", "gx"))
    return jax.shard_map(local, mesh=mesh, in_specs=in_specs, out_specs=out_specs, check_vma=False)
```

time: 87.5 us -> 74.3 us (0.85)
  waiting for transfers between devices: 50.3 us -> 32.6 us
  Pallas kernels: 13.4 us -> 16.5 us
  starting transfers between devices: 19.8 us -> 22.9 us
  local copies, waits for them, and re-layouts: 3.19 us -> 1.24 us
    ppermute x9 -> x10, waiting for transfers between devices: 34.8 us -> 23.5 us  [swapped(): lax.ppermute(value, 'gy', [(i, i ^ 1) for i in range(lax.axis_size('gy'))])]
    ppermute x12, waiting for transfers between devices: 15.5 us -> 9.16 us  [shifted(): lax.ppermute(value, axis, [(i, (i + steps) % count) for i in range(count)])]
    pallas_call x0 -> x1, Pallas kernels: none -> 2.63 us  [local(): pl.pallas_call(take_kernel, out_shape=unit, in_specs=[pl.BlockSpec(memory...]
    ppermute x12, starting transfers between devices: 11.5 us -> 13.7 us  [shifted(): lax.ppermute(value, axis, [(i, (i + steps) % count) for i in range(count)])]
    unnamed x5 -> x8, local copies, waits for them, and re-layouts: 3.19 us -> 1.24 us
    ppermute x9 -> x10, starting transfers between devices: 8.34 us -> 9.25 us  [swapped(): lax.ppermute(value, 'gy', [(i, i ^ 1) for i in range(lax.axis_size('gy'))])]
    pallas_call x8 -> x17, Pallas kernels: 13.4 us -> 13.9 us  [call(): pl.pallas_call(kernel, out_shape=outs, in_specs=specs, out_specs=[pl.Bloc...]
  transfers between devices with their start and end apart: 21 -> 22, of which waited for: 13 -> 9; matrix products, arithmetic and copies ran while one was open for 0% -> 0% of each run, Pallas kernels for 2% -> 16%
where the time goes in v2:
time: 74.3 us; the launch traced here: 74.1 us
  waiting for transfers between devices  32.6 us (44%)
  starting transfers between devices  22.9 us (31%)
  Pallas kernels  16.5 us (22%)
  local copies, waits for them, and re-layouts  1.24 us (2%)
  between operations  0.82 us (1%)
    ppermute x10, waiting for transfers between devices, swapped(): lax.ppermute(value, 'gy', [(i, i ^ 1) for i in range(lax.axis_size('gy'))])  23.5 us
    pallas_call x17, Pallas kernels, call(): pl.pallas_call(kernel, out_shape=outs, in_specs=specs, out_specs=[pl.Bloc...  13.9 us
    ppermute x12, starting transfers between devices, shifted(): lax.ppermute(value, axis, [(i, (i + steps) % count) for i in range(count)])  13.7 us
    ppermute x10, starting transfers between devices, swapped(): lax.ppermute(value, 'gy', [(i, i ^ 1) for i in range(lax.axis_size('gy'))])  9.25 us
    ppermute x12, waiting for transfers between devices, shifted(): lax.ppermute(value, axis, [(i, (i + steps) % count) for i in range(count)])  9.16 us
    pallas_call x1, Pallas kernels, local(): pl.pallas_call(take_kernel, out_shape=unit, in_specs=[pl.BlockSpec(memory...  2.63 us
  transfers between devices with their start and end apart: 22, of which 9 were waited for; matrix products, arithmetic and copies ran while one was open for 0% of the time, Pallas kernels for 16%

profile of v2, /device:TPU:1, one launch (start us, length us, event | category | flops | bytes accessed | tf_op | source)
XLA Modules:
  0.0 74.1 jit_solution(14506619888943851025)
XLA Ops:
  0.6 2.6 %shard_map.53 = f32[3,16,8,256]{3,2,1,0:T(8,128)} custom-call(s32[2]{0:T(128)} %bitcast.1, f32[2,2,16,16,256]{4,3,2,1,0:T(8,128)} %fields.11), custom_call_target="tpu_custom_call" | custom-call | tf_op jit(solution)/shard_map/pallas_call | solution.py:370
  3.3 2.1 %collective-permute-start.1 = (f32[3,16,8,256]{3,2,1,0:T(8,128)}, f32[3,16,8,256]{3,2,1,0:T(8,128)S(1)}, u32[]{:S(2)}, u32[]{:S(2)}) collective-permute-start(f32[3,16,8,256]{3,2,1,0:T(8,128)} %shard_map.53), channel_id=1, source_target_pairs={{0,4},{4,0},{1,5},{5,1},{2,6},{6,2},{3,7},{7,3},{8,12},{12,8},{9,1... | collective-permute-start | bytes 1179656 | tf_op jit(solution)/shard_map/ppermute | solution.py:40
  5.4 1.2 %copy-done.1 = f32[2,2,16,16,256]{4,3,2,1,0:T(8,128)S(1)} copy-done((f32[2,2,16,16,256]{4,3,2,1,0:T(8,128)S(1)}, f32[2,2,16,16,256]{4,3,2,1,0:T(8,128)}, u32[]{:S(2)}) %copy-start.1) | copy-done | bytes 1048600
  6.6 1.0 %shard_map.50._ = f32[2,4,3,8,128]{4,3,2,1,0:T(8,128)S(1)} custom-call(s32[2]{0:T(128)S(1)} %bitcast.2, f32[2,2,16,16,256]{4,3,2,1,0:T(8,128)S(1)} %copy-done.1, bf16[4,2,16,16,256]{4,3,2,1,0:T(8,128)(2,1)S(1)} %copy-done), custom_call_target="tpu_custom_call" | custom-call | tf_op jit(solution)/shard_map/pallas_call | solution.py:57
  7.6 0.7 shard_map.51._
  8.4 1.4 %collective-permute-start.3 = (f32[2,4,3,8,128]{4,3,2,1,0:T(8,128)S(1)}, f32[2,4,3,8,128]{4,3,2,1,0:T(8,128)S(1)}, u32[]{:S(2)}, u32[]{:S(2)}) collective-permute-start(f32[2,4,3,8,128]{4,3,2,1,0:T(8,128)S(1)} %shard_map.50._), channel_id=1, source_target_pairs={{0,4},{4,0},{1,5},{5,1},{2,6},{6,2},{3,7},{7,3},{8,12},{12,8},{9,1... | collective-permute-start | bytes 294920 | tf_op jit(solution)/shard_map/ppermute | solution.py:40
  9.8 15.1 %collective-permute-done.3.strip_in = f32[2,4,3,8,128]{4,3,2,1,0:T(8,128)S(1)} collective-permute-done((f32[2,4,3,8,128]{4,3,2,1,0:T(8,128)S(1)}, f32[2,4,3,8,128]{4,3,2,1,0:T(8,128)S(1)}, u32[]{:S(2)}, u32[]{:S(2)}) %collective-permute-start.3) | collective-permute-done | bytes 98336 | tf_op jit(solution)/shard_map/ppermute | solution.py:40
  25.0 1.0 %shard_map.54 = (f32[4,3,8,128]{3,2,1,0:T(8,128)S(1)}, f32[4,3,8,128]{3,2,1,0:T(8,128)S(1)}) custom-call(s32[2]{0:T(128)S(1)} %bitcast.4, f32[2,2,16,16,256]{4,3,2,1,0:T(8,128)S(1)} %copy-done.1, bf16[4,2,16,16,256]{4,3,2,1,0:T(8,128)(2,1)S(1)} %copy-done, f32[2,4,3,8,128]{4,3,2,1,0:T(8,128)S(1)} %collective-permute-done.3.strip_in), custom_call_target="tpu_custom_call" | custom-call | tf_op jit(solution)/shard_map/pallas_call | solution.py:57
  26.0 1.3 %collective-permute-start.4 = (f32[4,3,8,128]{3,2,1,0:T(8,128)S(1)}, f32[4,3,8,128]{3,2,1,0:T(8,128)S(1)}, u32[]{:S(2)}, u32[]{:S(2)}) collective-permute-start(f32[4,3,8,128]{3,2,1,0:T(8,128)S(1)} %get-tuple-element.39), channel_id=1, source_target_pairs={{0,8},{8,16},{16,24},{24,0},{1,9},{9,17},{17,25},{25,1},{2,10},{10... | collective-permute-start | bytes 147464 | tf_op jit(solution)/shard_map/ppermute | solution.py:36
  27.3 2.1 %collective-permute-start.5 = (f32[4,3,8,128]{3,2,1,0:T(8,128)S(1)}, f32[4,3,8,128]{3,2,1,0:T(8,128)S(1)}, u32[]{:S(2)}, u32[]{:S(2)}) collective-permute-start(f32[4,3,8,128]{3,2,1,0:T(8,128)S(1)} %get-tuple-element.40), channel_id=1, source_target_pairs={{0,24},{8,0},{16,8},{24,16},{1,25},{9,1},{17,9},{25,17},{2,26},{10... | collective-permute-start | bytes 147464 | tf_op jit(solution)/shard_map/ppermute | solution.py:36
  30.0 1.3 %collective-permute-start = (bf16[2,3,8,16,256]{4,3,2,1,0:T(8,128)(2,1)S(1)}, bf16[2,3,8,16,256]{4,3,2,1,0:T(8,128)(2,1)S(1)}, u32[]{:S(2)}, u32[]{:S(2)}) collective-permute-start(bf16[2,3,8,16,256]{4,3,2,1,0:T(8,128)(2,1)S(1)} %shard_map.52), channel_id=1, source_target_pairs={{0,4},{4,0},{1,5},{5,1},{2,6},{6,2},{3,7},{7,3},{8,12},{12,8},{9,1... | collective-permute-start | bytes 1179656 | tf_op jit(solution)/shard_map/ppermute | solution.py:40
  31.3 1.1 %shard_map.55 = (f32[16,24,384]{2,1,0:T(8,128)S(1)}, f32[16,24,128]{2,1,0:T(8,128)S(1)}, f32[2,16,24,384]{3,2,1,0:T(8,128)S(1)}, f32[2,16,24,128]{3,2,1,0:T(8,12...) custom-call(s32[2]{0:T(128)S(1)} %bitcast.6, ...), custom_call_target="tpu_custom_call" | custom-call | tf_op jit(solution)/shard_map/pallas_call | solution.py:57
  33.0 0.9 %collective-permute-start.8 = (f32[3,16,8,256]{3,2,1,0:T(8,128)S(1)}, f32[3,16,8,256]{3,2,1,0:T(8,128)S(1)}, u32[]{:S(2)}, u32[]{:S(2)}) collective-permute-start(f32[3,16,8,256]{3,2,1,0:T(8,128)S(1)} %shard_map.57), channel_id=1, source_target_pairs={{0,4},{4,0},{1,5},{5,1},{2,6},{6,2},{3,7},{7,3},{8,12},{12,8},{9,1... | collective-permute-start | bytes 1179656 | tf_op jit(solution)/shard_map/ppermute | solution.py:40
  33.9 3.1 %collective-permute-start.6 = (f32[2,24,384]{2,1,0:T(8,128)S(1)}, f32[2,24,384]{2,1,0:T(8,128)S(1)}, u32[]{:S(2)}, u32[]{:S(2)}) collective-permute-start(f32[2,24,384]{2,1,0:T(8,128)S(1)} %get-tuple-element.43), channel_id=1, source_target_pairs={{0,3},{1,0},{2,1},{3,2},{4,7},{5,4},{6,5},{7,6},{8,11},{9,8},{10,9... | collective-permute-start | bytes 221192 | tf_op jit(solution)/shard_map/ppermute | solution.py:36
  37.2 1.4 %collective-permute-start.9 = (f32[24,384]{1,0:T(8,128)S(1)}, f32[24,384]{1,0:T(8,128)S(1)}, u32[]{:S(2)}, u32[]{:S(2)}) collective-permute-start(f32[24,384]{1,0:T(8,128)S(1)} %get-tuple-element.47), channel_id=1, source_target_pairs={{0,1},{1,2},{2,3},{3,0},{4,5},{5,6},{6,7},{7,4},{8,9},{9,10},{10,1... | collective-permute-start | bytes 110600 | tf_op jit(solution)/shard_map/ppermute | solution.py:36
  38.9 0.7 shard_map.56.wide_ax
  39.7 1.1 %collective-permute-done.6.high_face.rim_face = f32[2,24,384]{2,1,0:T(8,128)S(1)} collective-permute-done((f32[2,24,384]{2,1,0:T(8,128)S(1)}, f32[2,24,384]{2,1,0:T(8,128)S(1)}, u32[]{:S(2)}, u32[]{:S(2)}) %collective-permute-start.6) | collective-permute-done | bytes 73760 | tf_op jit(solution)/shard_map/ppermute | solution.py:36
  40.8 8.1 %collective-permute-done.7.ghost_rows.rim_rows = f32[3,16,384]{2,1,0:T(8,128)S(1)} collective-permute-done((f32[3,16,384]{2,1,0:T(8,128)S(1)}, f32[3,16,384]{2,1,0:T(8,128)S(1)}, u32[]{:S(2)}, u32[]{:S(2)}) %collective-permute-start.7) | collective-permute-done | bytes 73760 | tf_op jit(solution)/shard_map/ppermute | solution.py:40
  48.9 1.3 %shard_map.58 = (f32[16,24,384]{2,1,0:T(8,128)S(1)}, f32[16,24,384]{2,1,0:T(8,128)S(1)}) custom-call(f32[2,16,24,384]{3,2,1,0:T(8,128)S(1)} %shard_map.56.wide_ax, f32[2,16,24,384]{3,2,1,0:T(8,128)S(1)} %get-tuple-element.42.wide_yz, f32[16,24,384]{2,1,0:T(8,128)S(1)} %get-tuple-element.46.field.start, f32[24,384]{1,0:T(8,128)S(1)} %collective-permute-done.9.low_face, ...), custom_call_target="tpu_custom_call" | custom-call | tf_op jit(solution)/shard_map/pallas_call | solution.py:57
  50.2 0.7 shard_map.59
  51.0 1.1 %collective-permute-start.12 = (f32[2,16,384]{2,1,0:T(8,128)S(1)}, f32[2,16,384]{2,1,0:T(8,128)S(1)}, u32[]{:S(2)}, u32[]{:S(2)}) collective-permute-start(f32[2,16,384]{2,1,0:T(8,128)S(1)} %get-tuple-element.58), channel_id=1, source_target_pairs={{0,4},{4,0},{1,5},{5,1},{2,6},{6,2},{3,7},{7,3},{8,12},{12,8},{9,1... | collective-permute-start | bytes 147464 | tf_op jit(solution)/shard_map/ppermute | solution.py:40
  52.1 4.3 %collective-permute-start.10 = (f32[24,384]{1,0:T(8,128)S(1)}, f32[24,384]{1,0:T(8,128)S(1)}, u32[]{:S(2)}, u32[]{:S(2)}) collective-permute-start(f32[24,384]{1,0:T(8,128)S(1)} %get-tuple-element.56), channel_id=1, source_target_pairs={{0,1},{1,2},{2,3},{3,0},{4,5},{5,6},{6,7},{7,4},{8,9},{9,10},{10,1... | collective-permute-start | bytes 110600 | tf_op jit(solution)/shard_map/ppermute | solution.py:36
  56.4 1.1 %shard_map.60 = (f32[16,24,384]{2,1,0:T(8,128)S(1)}, f32[16,24,384]{2,1,0:T(8,128)S(1)}, f32[16,24,256]{2,1,0:T(8,128)S(1)}) custom-call(f32[2,16,24,384]{3,2,1,0:T(8,128)S(1)} %shard_map.56.wide_ax, f32[2,16,24,384]{3,2,1,0:T(8,128)S(1)} %get-tuple-element.42.wide_yz, f32[2,24,384]{2,1,0:T(8,128)S(1)} %collective-permute-done.6.high_face.rim_face, ...), custom_call_target="tpu_custom_call" | custom-call | tf_op jit(solution)/shard_map/pallas_call | solution.py:57
  57.5 2.3 %collective-permute-done.11.refs_1_.high_face = f32[1,24,384]{2,1,0:T(8,128)S(1)} collective-permute-done((f32[1,24,384]{2,1,0:T(8,128)S(1)}, f32[1,24,384]{2,1,0:T(8,128)S(1)}, u32[]{:S(2)}, u32[]{:S(2)}) %collective-permute-start.11) | collective-permute-done | bytes 36896 | tf_op jit(solution)/shard_map/ppermute | solution.py:36
  60.7 1.1 %shard_map.61 = (f32[16,24,384]{2,1,0:T(8,128)S(1)}, f32[16,24,384]{2,1,0:T(8,128)S(1)}, f32[16,24,256]{2,1,0:T(8,128)S(1)}) custom-call(f32[2,16,24,384]{3,2,1,0:T(8,128)S(1)} %shard_map.56.wide_ax, f32[2,16,24,384]{3,2,1,0:T(8,128)S(1)} %get-tuple-element.42.wide_yz, f32[2,24,384]{2,1,0:T(8,128)S(1)} %collective-permute-done.6.high_face.rim_face, ...), custom_call_target="tpu_custom_call" | custom-call | tf_op jit(solution)/shard_map/pallas_call | solution.py:57
  61.9 2.2 %collective-permute-done.14.refs_1_.high_face = f32[1,24,384]{2,1,0:T(8,128)S(1)} collective-permute-done((f32[1,24,384]{2,1,0:T(8,128)S(1)}, f32[1,24,384]{2,1,0:T(8,128)S(1)}, u32[]{:S(2)}, u32[]{:S(2)}) %collective-permute-start.14) | collective-permute-done | bytes 36896 | tf_op jit(solution)/shard_map/ppermute | solution.py:36
  64.1 1.1 %collective-permute-start.18 = (f32[2,16,384]{2,1,0:T(8,128)S(1)}, f32[2,16,384]{2,1,0:T(8,128)S(1)}, u32[]{:S(2)}, u32[]{:S(2)}) collective-permute-start(f32[2,16,384]{2,1,0:T(8,128)S(1)} %get-tuple-element.70), channel_id=1, source_target_pairs={{0,4},{4,0},{1,5},{5,1},{2,6},{6,2},{3,7},{7,3},{8,12},{12,8},{9,1... | collective-permute-start | bytes 147464 | tf_op jit(solution)/shard_map/ppermute | solution.py:40
  65.7 1.1 %shard_map.63 = (f32[16,24,384]{2,1,0:T(8,128)S(1)}, f32[16,24,384]{2,1,0:T(8,128)S(1)}, f32[16,24,256]{2,1,0:T(8,128)S(1)}) custom-call(f32[2,16,24,384]{3,2,1,0:T(8,128)S(1)} %shard_map.56.wide_ax, f32[2,16,24,384]{3,2,1,0:T(8,128)S(1)} %get-tuple-element.42.wide_yz, f32[2,24,384]{2,1,0:T(8,128)S(1)} %collective-permute-done.6.high_face.rim_face, ...), custom_call_target="tpu_custom_call" | custom-call | tf_op jit(solution)/shard_map/pallas_call | solution.py:57
  66.9 2.0 %collective-permute-done.17.refs_1_.high_face = f32[1,24,384]{2,1,0:T(8,128)S(1)} collective-permute-done((f32[1,24,384]{2,1,0:T(8,128)S(1)}, f32[1,24,384]{2,1,0:T(8,128)S(1)}, u32[]{:S(2)}, u32[]{:S(2)}) %collective-permute-start.17) | collective-permute-done | bytes 36896 | tf_op jit(solution)/shard_map/ppermute | solution.py:36
  70.1 1.7 %shard_map.65 = (f32[16,24,256]{2,1,0:T(8,128)S(1)}, f32[16,24,256]{2,1,0:T(8,128)}) custom-call(f32[2,16,24,384]{3,2,1,0:T(8,128)S(1)} %shard_map.56.wide_ax, f32[2,16,24,384]{3,2,1,0:T(8,128)S(1)} %get-tuple-element.42.wide_yz, f32[2,24,384]{2,1,0:T(8,128)S(1)} %collective-permute-done.6.high_face.rim_face, ...), custom_call_target="tpu_custom_call" | custom-call | tf_op jit(solution)/shard_map/pallas_call | solution.py:57
  71.8 1.5 %collective-permute-done.20.high_face = f32[1,24,384]{2,1,0:T(8,128)S(1)} collective-permute-done((f32[1,24,384]{2,1,0:T(8,128)S(1)}, f32[1,24,384]{2,1,0:T(8,128)S(1)}, u32[]{:S(2)}, u32[]{:S(2)}) %collective-permute-start.20) | collective-permute-done | bytes 36896 | tf_op jit(solution)/shard_map/ppermute | solution.py:36
  73.3 0.8 %shard_map.67 = f32[16,24,256]{2,1,0:T(8,128)} custom-call(f32[2,16,24,384]{3,2,1,0:T(8,128)S(1)} %get-tuple-element.42.wide_yz, f32[2,24,384]{2,1,0:T(8,128)S(1)} %collective-permute-done.6.high_face.rim_face, f32[3,16,384]{2,1,0:T(8,128)S(1)} %collective-permute-done.7.ghost_rows.rim_rows, f32[24,384]{1,0:T(8,128)S(1)} %collective-permute-done.19.low_face, ...), custom_call_target="tpu_custom_call" | custom-call | tf_op jit(solution)/shard_map/pallas_call | solution.py:57
  (38 shorter events, 4.7 us)
Async XLA Ops:
  0.6 4.8 %copy-start.3 = (s32[2,1,1]{0,2,1:T(1,128)S(1)}, s32[2,1,1]{0,2,1:T(1,128)}, u32[]{:S(2)}) copy-start(s32[2,1,1]{0,2,1:T(1,128)} %param.5) | copy-start | bytes 28
  0.6 4.8 %copy-start = (bf16[4,2,16,16,256]{4,3,2,1,0:T(8,128)(2,1)S(1)}, bf16[4,2,16,16,256]{4,3,2,1,0:T(8,128)(2,1)}, u32[]{:S(2)}) copy-start(bf16[4,2,16,16,256]{4,3,2,1,0:T(8,128)(2,1)} %coef.11) | copy-start | bytes 3145732
  3.3 28.0 %collective-permute-start.1 = (f32[3,16,8,256]{3,2,1,0:T(8,128)}, f32[3,16,8,256]{3,2,1,0:T(8,128)S(1)}, u32[]{:S(2)}, u32[]{:S(2)}) collective-permute-start(f32[3,16,8,256]{3,2,1,0:T(8,128)} %shard_map.53), channel_id=1, source_target_pairs={{0,4},{4,0},{1,5},{5,1},{2,6},{6,2},{3,7},{7,3},{8,12},{12,8},{9,1... | collective-permute-start | bytes 1179656 | tf_op jit(solution)/shard_map/ppermute | solution.py:40
  5.4 1.2 %copy-start.1 = (f32[2,2,16,16,256]{4,3,2,1,0:T(8,128)S(1)}, f32[2,2,16,16,256]{4,3,2,1,0:T(8,128)}, u32[]{:S(2)}) copy-start(f32[2,2,16,16,256]{4,3,2,1,0:T(8,128)} %fields.11) | copy-start | bytes 3145732
  8.3 23.0 %collective-permute-start.2 = (bf16[2,3,8,16,256]{4,3,2,1,0:T(8,128)(2,1)S(1)}, bf16[2,3,8,16,256]{4,3,2,1,0:T(8,128)(2,1)S(1)}, u32[]{:S(2)}, u32[]{:S(2)}) collective-permute-start(bf16[2,3,8,16,256]{4,3,2,1,0:T(8,128)(2,1)S(1)} %shard_map.51._), channel_id=1, source_target_pairs={{0,4},{4,0},{1,5},{5,1},{2,6},{6,2},{3,7},{7,3},{8,12},{12,8},{9,1... | collective-permute-start | bytes 1179656 | tf_op jit(solution)/shard_map/ppermute | solution.py:40
  8.4 16.6 %collective-permute-start.3 = (f32[2,4,3,8,128]{4,3,2,1,0:T(8,128)S(1)}, f32[2,4,3,8,128]{4,3,2,1,0:T(8,128)S(1)}, u32[]{:S(2)}, u32[]{:S(2)}) collective-permute-start(f32[2,4,3,8,128]{4,3,2,1,0:T(8,128)S(1)} %shard_map.50._), channel_id=1, source_target_pairs={{0,4},{4,0},{1,5},{5,1},{2,6},{6,2},{3,7},{7,3},{8,12},{12,8},{9,1... | collective-permute-start | bytes 294920 | tf_op jit(solution)/shard_map/ppermute | solution.py:40
  26.0 5.3 %collective-permute-start.4 = (f32[4,3,8,128]{3,2,1,0:T(8,128)S(1)}, f32[4,3,8,128]{3,2,1,0:T(8,128)S(1)}, u32[]{:S(2)}, u32[]{:S(2)}) collective-permute-start(f32[4,3,8,128]{3,2,1,0:T(8,128)S(1)} %get-tuple-element.39), channel_id=1, source_target_pairs={{0,8},{8,16},{16,24},{24,0},{1,9},{9,17},{17,25},{25,1},{2,10},{10... | collective-permute-start | bytes 147464 | tf_op jit(solution)/shard_map/ppermute | solution.py:36
  27.3 4.0 %collective-permute-start.5 = (f32[4,3,8,128]{3,2,1,0:T(8,128)S(1)}, f32[4,3,8,128]{3,2,1,0:T(8,128)S(1)}, u32[]{:S(2)}, u32[]{:S(2)}) collective-permute-start(f32[4,3,8,128]{3,2,1,0:T(8,128)S(1)} %get-tuple-element.40), channel_id=1, source_target_pairs={{0,24},{8,0},{16,8},{24,16},{1,25},{9,1},{17,9},{25,17},{2,26},{10... | collective-permute-start | bytes 147464 | tf_op jit(solution)/shard_map/ppermute | solution.py:36
  30.0 8.8 %collective-permute-start = (bf16[2,3,8,16,256]{4,3,2,1,0:T(8,128)(2,1)S(1)}, bf16[2,3,8,16,256]{4,3,2,1,0:T(8,128)(2,1)S(1)}, u32[]{:S(2)}, u32[]{:S(2)}) collective-permute-start(bf16[2,3,8,16,256]{4,3,2,1,0:T(8,128)(2,1)S(1)} %shard_map.52), channel_id=1, source_target_pairs={{0,4},{4,0},{1,5},{5,1},{2,6},{6,2},{3,7},{7,3},{8,12},{12,8},{9,1... | collective-permute-start | bytes 1179656 | tf_op jit(solution)/shard_map/ppermute | solution.py:40
  33.0 17.2 %collective-permute-start.8 = (f32[3,16,8,256]{3,2,1,0:T(8,128)S(1)}, f32[3,16,8,256]{3,2,1,0:T(8,128)S(1)}, u32[]{:S(2)}, u32[]{:S(2)}) collective-permute-start(f32[3,16,8,256]{3,2,1,0:T(8,128)S(1)} %shard_map.57), channel_id=1, source_target_pairs={{0,4},{4,0},{1,5},{5,1},{2,6},{6,2},{3,7},{7,3},{8,12},{12,8},{9,1... | collective-permute-start | bytes 1179656 | tf_op jit(solution)/shard_map/ppermute | solution.py:40
  33.9 6.9 %collective-permute-start.6 = (f32[2,24,384]{2,1,0:T(8,128)S(1)}, f32[2,24,384]{2,1,0:T(8,128)S(1)}, u32[]{:S(2)}, u32[]{:S(2)}) collective-permute-start(f32[2,24,384]{2,1,0:T(8,128)S(1)} %get-tuple-element.43), channel_id=1, source_target_pairs={{0,3},{1,0},{2,1},{3,2},{4,7},{5,4},{6,5},{7,6},{8,11},{9,8},{10,9... | collective-permute-start | bytes 221192 | tf_op jit(solution)/shard_map/ppermute | solution.py:36
  37.0 11.9 %collective-permute-start.7 = (f32[3,16,384]{2,1,0:T(8,128)S(1)}, f32[3,16,384]{2,1,0:T(8,128)S(1)}, u32[]{:S(2)}, u32[]{:S(2)}) collective-permute-start(f32[3,16,384]{2,1,0:T(8,128)S(1)} %get-tuple-element.44._), channel_id=1, source_target_pairs={{0,4},{4,0},{1,5},{5,1},{2,6},{6,2},{3,7},{7,3},{8,12},{12,8},{9,1... | collective-permute-start | bytes 221192 | tf_op jit(solution)/shard_map/ppermute | solution.py:40
  37.2 2.5 %collective-permute-start.9 = (f32[24,384]{1,0:T(8,128)S(1)}, f32[24,384]{1,0:T(8,128)S(1)}, u32[]{:S(2)}, u32[]{:S(2)}) collective-permute-start(f32[24,384]{1,0:T(8,128)S(1)} %get-tuple-element.47), channel_id=1, source_target_pairs={{0,1},{1,2},{2,3},{3,0},{4,5},{5,6},{6,7},{7,4},{8,9},{9,10},{10,1... | collective-permute-start | bytes 110600 | tf_op jit(solution)/shard_map/ppermute | solution.py:36
  48.9 1.3 %copy-start.2 = (f32[2,2,16,16,256]{4,3,2,1,0:T(8,128)S(1)}, f32[2,2,16,16,256]{4,3,2,1,0:T(8,128)}, u32[]{:S(2)}) copy-start(f32[2,2,16,16,256]{4,3,2,1,0:T(8,128)} %fields.11) | copy-start | bytes 3145732
  51.0 8.8 %collective-permute-start.12 = (f32[2,16,384]{2,1,0:T(8,128)S(1)}, f32[2,16,384]{2,1,0:T(8,128)S(1)}, u32[]{:S(2)}, u32[]{:S(2)}) collective-permute-start(f32[2,16,384]{2,1,0:T(8,128)S(1)} %get-tuple-element.58), channel_id=1, source_target_pairs={{0,4},{4,0},{1,5},{5,1},{2,6},{6,2},{3,7},{7,3},{8,12},{12,8},{9,1... | collective-permute-start | bytes 147464 | tf_op jit(solution)/shard_map/ppermute | solution.py:40
  52.1 5.4 %collective-permute-start.10 = (f32[24,384]{1,0:T(8,128)S(1)}, f32[24,384]{1,0:T(8,128)S(1)}, u32[]{:S(2)}, u32[]{:S(2)}) collective-permute-start(f32[24,384]{1,0:T(8,128)S(1)} %get-tuple-element.56), channel_id=1, source_target_pairs={{0,1},{1,2},{2,3},{3,0},{4,5},{5,6},{6,7},{7,4},{8,9},{9,10},{10,1... | collective-permute-start | bytes 110600 | tf_op jit(solution)/shard_map/ppermute | solution.py:36
  56.4 3.4 %collective-permute-start.11 = (f32[1,24,384]{2,1,0:T(8,128)S(1)}, f32[1,24,384]{2,1,0:T(8,128)S(1)}, u32[]{:S(2)}, u32[]{:S(2)}) collective-permute-start(f32[1,24,384]{2,1,0:T(8,128)S(1)} %get-tuple-element.57), channel_id=1, source_target_pairs={{0,3},{1,0},{2,1},{3,2},{4,7},{5,4},{6,5},{7,6},{8,11},{9,8},{10,9... | collective-permute-start | bytes 110600 | tf_op jit(solution)/shard_map/ppermute | solution.py:36
  59.9 4.2 %collective-permute-start.15 = (f32[2,16,384]{2,1,0:T(8,128)S(1)}, f32[2,16,384]{2,1,0:T(8,128)S(1)}, u32[]{:S(2)}, u32[]{:S(2)}) collective-permute-start(f32[2,16,384]{2,1,0:T(8,128)S(1)} %get-tuple-element.64), channel_id=1, source_target_pairs={{0,4},{4,0},{1,5},{5,1},{2,6},{6,2},{3,7},{7,3},{8,12},{12,8},{9,1... | collective-permute-start | bytes 147464 | tf_op jit(solution)/shard_map/ppermute | solution.py:40
  60.2 1.7 %collective-permute-start.13 = (f32[24,384]{1,0:T(8,128)S(1)}, f32[24,384]{1,0:T(8,128)S(1)}, u32[]{:S(2)}, u32[]{:S(2)}) collective-permute-start(f32[24,384]{1,0:T(8,128)S(1)} %get-tuple-element.62), channel_id=1, source_target_pairs={{0,1},{1,2},{2,3},{3,0},{4,5},{5,6},{6,7},{7,4},{8,9},{9,10},{10,1... | collective-permute-start | bytes 110600 | tf_op jit(solution)/shard_map/ppermute | solution.py:36
  60.6 3.4 %collective-permute-start.14 = (f32[1,24,384]{2,1,0:T(8,128)S(1)}, f32[1,24,384]{2,1,0:T(8,128)S(1)}, u32[]{:S(2)}, u32[]{:S(2)}) collective-permute-start(f32[1,24,384]{2,1,0:T(8,128)S(1)} %get-tuple-element.63), channel_id=1, source_target_pairs={{0,3},{1,0},{2,1},{3,2},{4,7},{5,4},{6,5},{7,6},{8,11},{9,8},{10,9... | collective-permute-start | bytes 110600 | tf_op jit(solution)/shard_map/ppermute | solution.py:36
  64.1 4.8 %collective-permute-start.18 = (f32[2,16,384]{2,1,0:T(8,128)S(1)}, f32[2,16,384]{2,1,0:T(8,128)S(1)}, u32[]{:S(2)}, u32[]{:S(2)}) collective-permute-start(f32[2,16,384]{2,1,0:T(8,128)S(1)} %get-tuple-element.70), channel_id=1, source_target_pairs={{0,4},{4,0},{1,5},{5,1},{2,6},{6,2},{3,7},{7,3},{8,12},{12,8},{9,1... | collective-permute-start | bytes 147464 | tf_op jit(solution)/shard_map/ppermute | solution.py:40
  65.2 1.7 %collective-permute-start.16 = (f32[24,384]{1,0:T(8,128)S(1)}, f32[24,384]{1,0:T(8,128)S(1)}, u32[]{:S(2)}, u32[]{:S(2)}) collective-permute-start(f32[24,384]{1,0:T(8,128)S(1)} %get-tuple-element.68), channel_id=1, source_target_pairs={{0,1},{1,2},{2,3},{3,0},{4,5},{5,6},{6,7},{7,4},{8,9},{9,10},{10,1... | collective-permute-start | bytes 110600 | tf_op jit(solution)/shard_map/ppermute | solution.py:36
  65.5 3.4 %collective-permute-start.17 = (f32[1,24,384]{2,1,0:T(8,128)S(1)}, f32[1,24,384]{2,1,0:T(8,128)S(1)}, u32[]{:S(2)}, u32[]{:S(2)}) collective-permute-start(f32[1,24,384]{2,1,0:T(8,128)S(1)} %get-tuple-element.69), channel_id=1, source_target_pairs={{0,3},{1,0},{2,1},{3,2},{4,7},{5,4},{6,5},{7,6},{8,11},{9,8},{10,9... | collective-permute-start | bytes 110600 | tf_op jit(solution)/shard_map/ppermute | solution.py:36
  69.0 4.3 %collective-permute-start.21 = (f32[2,16,384]{2,1,0:T(8,128)S(1)}, f32[2,16,384]{2,1,0:T(8,128)S(1)}, u32[]{:S(2)}, u32[]{:S(2)}) collective-permute-start(f32[2,16,384]{2,1,0:T(8,128)S(1)} %get-tuple-element.74), channel_id=1, source_target_pairs={{0,4},{4,0},{1,5},{5,1},{2,6},{6,2},{3,7},{7,3},{8,12},{12,8},{9,1... | collective-permute-start | bytes 147464 | tf_op jit(solution)/shard_map/ppermute | solution.py:40
  69.6 2.2 %collective-permute-start.19 = (f32[24,384]{1,0:T(8,128)S(1)}, f32[24,384]{1,0:T(8,128)S(1)}, u32[]{:S(2)}, u32[]{:S(2)}) collective-permute-start(f32[24,384]{1,0:T(8,128)S(1)} %get-tuple-element.72), channel_id=1, source_target_pairs={{0,1},{1,2},{2,3},{3,0},{4,5},{5,6},{6,7},{7,4},{8,9},{9,10},{10,1... | collective-permute-start | bytes 110600 | tf_op jit(solution)/shard_map/ppermute | solution.py:36
  69.9 3.4 %collective-permute-start.20 = (f32[1,24,384]{2,1,0:T(8,128)S(1)}, f32[1,24,384]{2,1,0:T(8,128)S(1)}, u32[]{:S(2)}, u32[]{:S(2)}) collective-permute-start(f32[1,24,384]{2,1,0:T(8,128)S(1)} %get-tuple-element.73), channel_id=1, source_target_pairs={{0,3},{1,0},{2,1},{3,2},{4,7},{5,4},{6,5},{7,6},{8,11},{9,8},{10,9... | collective-permute-start | bytes 110600 | tf_op jit(solution)/shard_map/ppermute | solution.py:36

commit v3 on v2

--- a/solution.py
+++ b/solution.py
@@ -113,25 +113,56 @@
     return low, high
 
 
-def take_kernel(ids, fields, start_out, sems):
-    rows = fields.shape[3] // 2
+def brick_rows(ids, half, unit_rows):
+    first = 3 * (lax.axis_index("gy") // 2)
+    a, b = ids[0] - first, ids[1] - first
+    found = []
+    for j in range(3):
+        slab = jnp.where(half == 0, j // 2, 1 + (j + 1) // 2)
+        row = jnp.where((j + half) % 2 == 0, 0, 2 * unit_rows - 1)
+        found.append((jnp.logical_or(a == slab, b == slab), jnp.where(a == slab, 0, 1), row))
+    return found
+
+
+def field_row(fields, place, z):
+    last = fields.shape[3] - 1
+    _, slot, row = place
+    return jnp.where(row == 0, fields[0, slot, z, 0:1], fields[0, slot, z, last : last + 1])
+
+
+PLANES_AT, ROWS_AT = 12, 18
+
+
+def edge_kernel(ids, fields_in, coef_in, fields, coef, out, sems):
     copies = []
-    for k, (_, slot, part) in enumerate(units_of(ids, 1 - lax.axis_index("gy") % 2)):
-        source = fields.at[0, slot, :, pl.ds(pl.multiple_of(part * rows, rows), rows), :]
-        copies.append(pltpu.make_async_copy(source, start_out.at[k], sems.at[k]))
+    for item in range(2):
+        for slot in range(2):
+            at = len(copies)
+            copies.append(pltpu.make_async_copy(fields_in.at[item, slot], fields.at[item, slot], sems.at[at]))
+    for part in range(4):
+        at = len(copies)
+        copies.append(pltpu.make_async_copy(coef_in.at[part], coef.at[part], sems.at[at]))
     for copy in copies:
         copy.start()
     for copy in copies:
         copy.wait()
-
-
-def edge_kernel(ids, fields, coef, strip_out):
-    planes = fields.shape[2]
-    for k, place in enumerate(units_of(ids, 1 - lax.axis_index("gy") % 2)):
+    planes, unit_rows = fields.shape[2], fields.shape[3] // 2
+    half = 1 - lax.axis_index("gy") % 2
+    for k, place in enumerate(units_of(ids, half)):
         for item in range(4):
             low, high = strips(fields, coef, item, place, planes)
-            strip_out[0, item, k] = low
-            strip_out[1, item, k] = high
+            out[3 * item + k] = jnp.concatenate([low, high], axis=1)
+        for e, z in enumerate((0, planes - 1)):
+            out[PLANES_AT + 3 * e + k] = field_unit(fields, 0, place, z)
+    for j, place in enumerate(brick_rows(ids, half, unit_rows)):
+        for z in range(planes):
+            at = ROWS_AT + j * (planes // unit_rows) + z // unit_rows
+            line = z % unit_rows
+            out[at, line : line + 1] = field_row(fields, place, z)
+    at = ROWS_AT + 3 * (planes // unit_rows)
+    for k, place in enumerate(units_of(ids, half)):
+        for z in range(planes):
+            out[at + k * planes + z] = coef_unit(coef, 2, place, z) + SHIFT * coef_unit(coef, 3, place, z)
 
 
 def coef_kernel(first, ids, coef, _, out):
@@ -143,19 +174,57 @@
                 out[part, k, z // 2] = jnp.concatenate(both).astype(jnp.bfloat16)
 
 
-def rhs_kernel(ids, fields, _, out):
-    for k, place in enumerate(units_of(ids, 1 - lax.axis_index("gy") % 2)):
-        for z in range(fields.shape[2]):
-            out[k, z] = field_unit(fields, 1, place, z)
-
-
-def strip_kernel(ids, fields, coef, strip_in, left, right):
+def partial_kernel(ids, fields, coef, _, out, own, start_own, *refs):
+    start_out, partial = refs[:3], refs[3]
+    _, slots, planes, rows, columns = fields.shape
+    lane, row = lane_of((rows, columns)), row_of((rows, columns))
+    for slot in range(slots):
+        value, lower = fields[0, slot, 0], 0.0
+        for z in range(planes):
+            alpha, beta_x, beta_y = (coef[part, slot, z].astype(jnp.float32) for part in range(3))
+            flux_x = jnp.where(lane == 0, 0.0, beta_x * (value - pltpu.roll(value, 1, 1)))
+            flux_y = jnp.where(row == 0, 0.0, beta_y * (value - pltpu.roll(value, 1, 0)))
+            image = (
+                alpha * value
+                + (flux_x - pltpu.roll(flux_x, columns - 1, 1))
+                + (flux_y - pltpu.roll(flux_y, rows - 1, 0))
+                + lower
+            )
+            if z + 1 < planes:
+                following = fields[0, slot, z + 1]
+                lower = coef[3, slot, z + 1].astype(jnp.float32) * (following - value)
+                image = image - lower
+                value = following
+            partial[slot, z] = fields[1, slot, z] - image
+    half_rows = rows // 2
+    half = lax.axis_index("gy") % 2
+    for theirs, side in ((True, 1 - half), (False, half)):
+        for k, place in enumerate(units_of(ids, side)):
+            held, slot, part = place
+            at = pl.ds(pl.multiple_of(part * half_rows, half_rows), half_rows)
+            line = slice(k * half_rows, (k + 1) * half_rows)
+            for z in range(planes):
+                left = jnp.where(held, partial[slot, z, at, :], 0.0)
+                start = jnp.where(held, field_unit(fields, 0, place, z), 0.0)
+                if theirs:
+                    out[k, z], start_out[k][z] = left, start
+                else:
+                    own[z, line], start_own[z, line] = left, start
+
+
+def strip_kernel(ids, fields, coef, edge_in, left, right):
     planes = fields.shape[2]
     for k, place in enumerate(units_of(ids, lax.axis_index("gy") % 2)):
         for item in range(4):
             low, high = strips(fields, coef, item, place, planes)
-            left[item, k] = jnp.where(place[0], low, strip_in[0, item, k])
-            right[item, k] = jnp.where(place[0], high, strip_in[1, item, k])
+            got = edge_in[3 * item + k]
+            left[item, k] = jnp.where(place[0], low, got[:, :LANES])
+            right[item, k] = jnp.where(place[0], high, got[:, LANES:])
+
+
+def parted(both):
+    second = jnp.floor(both * 0.125) * (8.0 / SHIFT)
+    return both - SHIFT * second, second
 
 
 def ghost_columns(from_left, from_right, item, k, z):
@@ -175,34 +244,47 @@
 
 
 def gather_kernel(
-    ids, fields, coef, start_in, coef_in, from_left, from_right, start, rhs_ghost, wide, ghosts, up, down, rows_out
+    ids, fields, coef, edge_in, left, right, from_left, from_right,
+    edge_start, rhs_ghost, wide, ghosts, own_rows, up, down, rows_out,
 ):
     _, _, planes, rows, columns = fields.shape
     rows //= 2
-    for k, place in enumerate(units_of(ids, lax.axis_index("gy") % 2)):
+    half = lax.axis_index("gy") % 2
+    for k, place in enumerate(units_of(ids, half)):
         at = slice(k * rows, (k + 1) * rows)
         for z in range(planes):
-            start[z, at, :columns] = jnp.where(place[0], field_unit(fields, 0, place, z), start_in[k, z])
-            start[z, at, columns:] = ghost_columns(from_left, from_right, 0, k, z)
+            edge_start[z, at, :LANES] = ghost_columns(right, left, 0, k, z)
+            edge_start[z, at, LANES:] = ghost_columns(from_left, from_right, 0, k, z)
             rhs_ghost[z, at] = ghost_columns(from_left, from_right, 1, k, z)
             for item in (2, 3):
                 both = ghost_columns(from_left, from_right, item, k, z)
-                b = jnp.floor(both * 0.125) * (8.0 / SHIFT)
-                a = both - SHIFT * b
+                a, b = parted(both)
                 if item == 2:
                     ghosts[0, z, at], ghosts[1, z, at] = a, b
                 else:
                     wide[0, z, at, columns:], wide[1, z, at, columns:] = a, b
+            got = parted(edge_in[ROWS_AT + 3 * (planes // rows) + k * planes + z])
             for part in (0, 1):
-                wide[part, z, at, :columns] = coef_gather(coef, coef_in, part + 2, place, k, z)
+                wide[part, z, at, :columns] = jnp.where(place[0], coef_unit(coef, part + 2, place, z), got[part])
+        for e, (z, out) in enumerate(((0, down.at[0]), (planes - 1, up))):
+            own = field_unit(fields, 0, place, z)
+            out[at, :columns] = jnp.where(place[0], own, edge_in[PLANES_AT + 3 * e + k])
+            out[at, columns:] = edge_start[z, at, LANES:]
+    down[1] = wide[1, 0]
+    for j, place in enumerate(brick_rows(ids, half, rows)):
+        for z in range(planes):
+            at = ROWS_AT + j * (planes // rows) + z // rows
+            line = z % rows
+            own_rows[j, z : z + 1] = jnp.where(place[0], field_row(fields, place, z), edge_in[at, line : line + 1])
     last = 3 * rows - 1
-    up[...] = start[planes - 1]
-    down[0] = start[0]
-    down[1] = wide[1, 0]
     for z in range(planes):
-        rows_out[0, z : z + 1] = start[z, last : last + 1]
-        rows_out[1, z : z + 1] = start[z, 0:1]
-        rows_out[2, z : z + 1] = wide[0, z, 0:1]
+        line = slice(z, z + 1)
+        for out, row, j, known in ((0, last, 2, half == 1), (1, 0, 0, half == 0)):
+            edge = edge_start[z, row : row + 1]
+            middle = jnp.concatenate([edge[:, :LANES]] * (columns // LANES), axis=1)
+            rows_out[out, line, :columns] = jnp.where(known, own_rows[j, line], middle)
+            rows_out[out, line, columns:] = edge[:, LANES:]
+        rows_out[2, line] = wide[0, z, 0:1]
 
 
 def spread_kernel(ids, coef, coef_in, ghosts, wide):
@@ -221,8 +303,10 @@
     row = row_of(value.shape)
     before = jnp.where(row == 0, 0.0 if low_row is None else low_row, pltpu.roll(value, 1, 0))
     flux_y = beta_y * (value - before)
-    last = value[rows - 1 : rows]
-    top = rim_row * (-last if high_row is None else high_row - last)
+    top = 0.0
+    if rim_row is not None:
+        last = value[rows - 1 : rows]
+        top = rim_row * (-last if high_row is None else high_row - last)
     after = jnp.where(row == rows - 1, top, pltpu.roll(flux_y, rows - 1, 0))
     return (
         alpha * value
@@ -232,37 +316,74 @@
     )
 
 
-def images(plane, wide_ax, wide_yz, rim_face, rim_rows, low_face=None, high_face=None, ghost_rows=None):
-    planes = wide_ax.shape[1]
-    (value, *others), beta_z = plane(0), wide_yz[1, 0]
-    lower = beta_z * (value if low_face is None else value - low_face[...])
+def images(plane, coef, planes, rim_face, rim_row, low_face=None, high_face=None, ghost_row=None):
+    (value, *others), beta_z = plane(0), coef(3, 0)
+    lower = beta_z * (value if low_face is None else value - low_face)
     for z in range(planes):
-        at = slice(z, z + 1)
         if z + 1 < planes:
-            (following, *next_others), next_z = plane(z + 1), wide_yz[1, z + 1]
+            (following, *next_others), next_z = plane(z + 1), coef(3, z + 1)
             upper = next_z * (following - value)
         else:
-            following, next_others, next_z = None, None, rim_face[1]
-            upper = next_z * (-value if high_face is None else high_face[0] - value)
-        low_row, high_row = (None, None) if ghost_rows is None else (ghost_rows[0, at], ghost_rows[1, at])
-        image = image_plane(
-            value, low_row, high_row, lower, upper, wide_ax[0, z], wide_ax[1, z], wide_yz[0, z], rim_rows[2, at]
-        )
-        yield z, (value, *others), image, beta_z, next_z
+            following, next_others, next_z = None, None, rim_face
+            upper = next_z * (-value if high_face is None else high_face - value)
+        low_row, high_row = (None, None) if ghost_row is None else (ghost_row(0, z), ghost_row(1, z))
+        image = image_plane(value, low_row, high_row, lower, upper, coef(0, z), coef(1, z), coef(2, z), rim_row(z))
+        yield z, (value, *others), image
         value, others, lower, beta_z = following, next_others, upper, next_z
 
 
+def edges(value):
+    columns = value.shape[1] - LANES
+    own = jnp.where(lane_of((value.shape[0], LANES)) < LANES // 2, value[:, :LANES], value[:, columns - LANES : columns])
+    return jnp.concatenate([own, value[:, columns:]], axis=1)
+
+
 def first_kernel(
-    wide_ax, wide_yz, field, low_face, high_face, ghost_rows, image_out, inverse
+    wide_ax, wide_yz, edge_start, rhs_ghost, own_rows, up, down, partial, low_face, high_face, extra, inverse
 ):
-    _, rows, width = field.shape
-    for z, (value,), image, beta_z, next_z in images(
-        lambda z: (field[z],), wide_ax, wide_yz, high_face, ghost_rows, low_face, high_face, ghost_rows
+    planes, rows, width = extra.shape
+    columns = width - LANES
+    unit_rows = rows // 3
+    even = lax.axis_index("gy") % 2 == 0
+
+    def coef(part, z):
+        return wide_ax[part, z] if part < 2 else wide_yz[part - 2, z]
+
+    def ring(part, z):
+        return edges(coef(part, z))
+
+    lane, row = lane_of((rows, columns)), row_of((rows, columns))
+    inner = jnp.where(even, 2 * unit_rows, unit_rows)
+    for z, (value,), image in images(
+        lambda z: (edge_start[z],),
+        ring,
+        planes,
+        edges(high_face[1]),
+        lambda z: None,
+        edges(low_face[...]),
+        edges(high_face[0]),
     ):
-        image_out[z] = image
-        beta_x, beta_y = wide_ax[1, z], wide_yz[0, z]
-        rim_row = ghost_rows[2, z : z + 1]
-        next_y = jnp.where(row_of(value.shape) == rows - 1, rim_row, pltpu.roll(beta_y, rows - 1, 0))
+        flux = ring(1, z) * (value - pltpu.roll(value, 1, 1))
+        gain = jnp.where(lane == 0, -flux[:, :columns], 0.0)
+        far = jnp.where(lane == columns - 1, pltpu.roll(flux, LANES - 1, 1)[:, :columns], 0.0)
+        gain = gain + far
+        if z == 0:
+            gain = gain - (wide_yz[1, 0] * (down[0] - low_face[...]))[:, :columns]
+        if z == planes - 1:
+            gain = gain + (high_face[1] * (high_face[0] - up[...]))[:, :columns]
+        beta_y = wide_yz[0, z]
+        at = slice(z, z + 1)
+        between = jnp.where(even, own_rows[2, at] - own_rows[1, at], own_rows[1, at] - own_rows[0, at])
+        beta = jnp.where(even, beta_y[2 * unit_rows : 2 * unit_rows + 1], beta_y[unit_rows : unit_rows + 1])
+        between = beta[:, :columns] * between
+        gain = gain + jnp.where(row == inner, -between, jnp.where(row == inner - 1, between, 0.0))
+        low = jnp.where(even, beta_y[0:1, :columns] * own_rows[0, at], 0.0)
+        gain = gain - jnp.where(row == 0, low, 0.0)
+        extra[z, :, :columns] = gain + partial[z]
+        extra[z, :, columns:] = rhs_ghost[z] - image[:, LANES:]
+        beta_x, beta_z = wide_ax[1, z], wide_yz[1, z]
+        next_z = wide_yz[1, z + 1] if z + 1 < planes else high_face[1]
+        next_y = jnp.where(row_of((rows, width)) == rows - 1, 0.0, pltpu.roll(beta_y, rows - 1, 0))
         next_x = pltpu.roll(beta_x, width - 1, 1)
         inverse[z] = 1.0 / (wide_ax[0, z] + beta_x + next_x + beta_y + next_y + beta_z + next_z)
 
@@ -277,18 +398,31 @@
 
 
 def start_kernel(
-    second, ids, fields, rhs_in, rhs_ghost, image, inverse, start, residual, direction, total, up, down, rows_out
+    second, partial_in, extra, part_inverse, start, wide_yz, own_last, ghost_rows,
+    inverse, residual, direction, total, up, down, rows_out,
 ):
-    planes, _, _ = start.shape
-    columns = fields.shape[4]
-    places = units_of(ids, lax.axis_index("gy") % 2)
+    planes, rows, width = extra.shape
+    columns = total.shape[2]
+    even = lax.axis_index("gy") % 2 == 0
+    row = row_of((rows, width))
+    ghost = lane_of((1, width)) >= columns
     for z in range(planes):
-        parts = [jnp.where(place[0], field_unit(fields, 1, place, z), rhs_in[k, z]) for k, place in enumerate(places)]
-        left = jnp.concatenate([jnp.concatenate(parts), rhs_ghost[z]], axis=1) - image[z]
-        step = second * (inverse[z] * left)
+        at = slice(z, z + 1)
+        known = jnp.concatenate([partial_in[k, z] for k in range(3)])
+        left = extra[z] + jnp.concatenate([known, jnp.zeros((rows, width - columns), jnp.float32)], axis=1)
+        rim = ghost_rows[2, at]
+        low = jnp.where(jnp.logical_or(ghost, even), wide_yz[0, z, 0:1] * ghost_rows[0, at], 0.0)
+        high = rim * (ghost_rows[1, at] - own_last[0, at])
+        high = jnp.where(jnp.logical_and(jnp.logical_not(ghost), even), 0.0, high)
+        left = left + jnp.where(row == 0, low, jnp.where(row == rows - 1, high, 0.0))
+        factor = part_inverse[z]
+        last = factor[rows - 1 : rows]
+        factor = jnp.where(row == rows - 1, last / (1.0 + rim * last), factor)
+        step = second * (factor * left)
+        inverse[z] = factor
         residual[z] = left
         direction[z] = step
-        total[z] = start[z, :, :columns] + step[:, :columns]
+        total[z] = start[z] + step[:, :columns]
     store_faces(direction, up, down, rows_out)
 
 
@@ -304,24 +438,32 @@
     return flux
 
 
-def inner_kernel(weights, wide_ax, wide_yz, rim_face, rim_rows, field, old, inverse, sum_in, *refs):
+def inner_kernel(number, weights, wide_ax, wide_yz, rim_face, rim_rows, field, old, inverse, sum_in, *refs):
     before, first, second = weights
     rims = rim_face, rim_rows
-    halo = refs[:3] if before else None
+    halo, piece = (refs[:3], refs[3]) if before else (None, None)
     if second:
         residual, direction, total = refs[-3:]
     else:
         residual, total = refs[-2:]
-    columns = total.shape[2]
+    _, rows, columns = total.shape
 
     def plane(z):
         if not before:
             return field[z], old[z], sum_in[z]
         flux = halo_flux(z, wide_yz, *rims, *halo)
         step = before * (inverse[z] * flux)
-        return field[z] + step, old[z] + flux, sum_in[z] + step[:, :columns]
-
-    for z, (value, left, done), image, _, _ in images(plane, wide_ax, wide_yz, *rims):
+        got = [jnp.zeros_like(piece[z])] * 3
+        got[number - 2] = piece[z]
+        return field[z] + step, old[z] + flux, sum_in[z] + step[:, :columns] + jnp.concatenate(got)
+
+    def coef(part, z):
+        return wide_ax[part, z] if part < 2 else wide_yz[part - 2, z]
+
+    planes = wide_ax.shape[1]
+    for z, (value, left, done), image in images(
+        plane, coef, planes, rim_face[1], lambda z: rim_rows[2, z : z + 1]
+    ):
         left = left - image
         if second:
             step = first * value + second * (inverse[z] * left)
@@ -360,80 +502,105 @@
 
 
 def local(old_fields, old_coef, held_slabs):
-    _, _, planes, rows, columns = old_fields.shape
+    _, slots, planes, rows, columns = old_fields.shape
     half = rows // 2
     rows = 3 * half
     width = columns + LANES
     full, own = f32(planes, rows, width), f32(planes, rows, columns)
-    unit = f32(3, planes, half, columns)
     ids = held_slabs.reshape(2)
-    start_out = pl.pallas_call(
-        take_kernel,
-        out_shape=unit,
-        in_specs=[pl.BlockSpec(memory_space=pltpu.SMEM), pl.BlockSpec(memory_space=pl.ANY)],
-        out_specs=pl.BlockSpec(memory_space=pltpu.VMEM),
-        scratch_shapes=[pltpu.SemaphoreType.DMA((3,))],
-    )(ids, old_fields)
-    start_in = swapped(start_out)
+    vmem = pl.BlockSpec(memory_space=pltpu.VMEM)
+    fields, coef, edge_out = pl.pallas_call(
+        edge_kernel,
+        out_shape=[
+            f32(*old_fields.shape),
+            jax.ShapeDtypeStruct(old_coef.shape, old_coef.dtype),
+            f32(ROWS_AT + 3 * (planes // half) + 3 * planes, half, columns),
+        ],
+        in_specs=[pl.BlockSpec(memory_space=pltpu.SMEM)] + [pl.BlockSpec(memory_space=pltpu.HBM)] * 2,
+        out_specs=[vmem] * 3,
+        scratch_shapes=[pltpu.SemaphoreType.DMA((8,))],
+        compiler_params=pltpu.CompilerParams(vmem_limit_bytes=VMEM_LIMIT),
+    )(ids, *(pltpu.with_memory_space_constraint(array, pltpu.HBM) for array in (old_fields, old_coef)))
+    edge_in = swapped(edge_out)
     coef_units = jax.ShapeDtypeStruct((2, 3, planes // 2, 2 * half, columns), jnp.bfloat16)
-    (strip_out,) = call(edge_kernel, [f32(2, 4, 3, half, LANES)], ids, old_fields, old_coef, ids=True)
-    strip_in = swapped(strip_out)
-    (coef_yz,) = call(functools.partial(coef_kernel, 2), [coef_units], ids, old_coef, strip_out, ids=True)
-    yz_in = swapped(coef_yz)
-    (coef_ax,) = call(functools.partial(coef_kernel, 0), [coef_units], ids, old_coef, coef_yz, ids=True)
+    (coef_ax,) = call(functools.partial(coef_kernel, 0), [coef_units], ids, coef, edge_out, ids=True)
     ax_in = swapped(coef_ax)
+    third = f32(planes, half, columns)
+    partial_out, partial, start_own, *start_out, _ = call(
+        partial_kernel,
+        [f32(3, planes, half, columns), own, own, third, third, third, f32(slots, planes, 2 * half, columns)],
+        ids,
+        fields,
+        coef,
+        coef_ax,
+        ids=True,
+    )
+    partial_in = swapped(partial_out)
     strip = f32(4, 3, half, LANES)
-    left, right = call(strip_kernel, [strip, strip], ids, old_fields, old_coef, strip_in, ids=True)
+    left, right = call(strip_kernel, [strip, strip], ids, fields, coef, edge_in, ids=True)
     from_left, from_right = shifted(right, "gx", 1), shifted(left, "gx", -1)
     coef_full = f32(2, planes, rows, width)
-    field, rhs_ghost, wide_yz, ghosts, up, down, rows_out = call(
+    edge_start, rhs_ghost, wide_yz, ghosts, own_rows, up, down, rows_out = call(
         gather_kernel,
         [
-            full,
+            f32(planes, rows, 2 * LANES),
             f32(planes, rows, LANES),
             coef_full,
             f32(2, planes, rows, LANES),
+            f32(3, planes, columns),
             f32(rows, width),
             f32(2, rows, width),
             f32(3, planes, width),
         ],
         ids,
-        old_fields,
-        old_coef,
-        start_in,
-        yz_in,
+        fields,
+        coef,
+        edge_in,
+        left,
+        right,
         from_left,
         from_right,
         ids=True,
     )
     low_face, rim_face, rim_rows = shifted(up, "gz", 1), shifted(down, "gz", -1), row_ghosts(rows_out)
-    (rhs_out,) = call(rhs_kernel, [unit], ids, old_fields, rows_out, ids=True)
-    rhs_in = swapped(rhs_out)
-    (wide_ax,) = call(spread_kernel, [coef_full], ids, old_coef, ax_in, ghosts, ids=True)
-    image, inverse = call(first_kernel, [full, full], wide_ax, wide_yz, field, low_face, rim_face, rim_rows)
+    (wide_ax,) = call(spread_kernel, [coef_full], ids, coef, ax_in, ghosts, ids=True)
+    extra, part_inverse = call(
+        first_kernel,
+        [full, full],
+        wide_ax,
+        wide_yz,
+        edge_start,
+        rhs_ghost,
+        own_rows,
+        up,
+        down,
+        partial,
+        low_face,
+        rim_face,
+    )
+    pieces = [swapped(units) for units in start_out]
     first_list, second_list = chebyshev_weights(SWEEPS)
     faces = [f32(rows, width), f32(1, rows, width), f32(2, planes, width)]
-    residual, direction, total, up, down, rows_out = call(
+    inverse, residual, direction, total, up, down, rows_out = call(
         functools.partial(start_kernel, second_list[0]),
-        [full, full, own] + faces,
-        ids,
-        old_fields,
-        rhs_in,
-        rhs_ghost,
-        image,
-        inverse,
-        field,
-        ids=True,
+        [full, full, full, own] + faces,
+        partial_in,
+        extra,
+        part_inverse,
+        start_own,
+        wide_yz,
+        rows_out,
+        rim_rows,
     )
     rims, halo = (rim_face, rim_rows), ()
     for stage in range(1, SWEEPS + 1):
         before = second_list[stage - 1] if halo else 0.0
         last = stage == SWEEPS
         weights = (before, 0.0, 0.0) if last else (before, first_list[stage], second_list[stage])
-        arrived = halo
+        arrived = (*halo, pieces[stage - 2]) if halo else ()
         halo = shifted(up, "gz", 1), shifted(down, "gz", -1), row_ghosts(rows_out)
         state = call(
-            functools.partial(inner_kernel, weights),
+            functools.partial(inner_kernel, stage, weights),
             [own, own] if last else [full, full, own],
             wide_ax,
             wide_yz,

time: 74.3 us -> 61.9 us (0.83)
  waiting for transfers between devices: 32.6 us -> 19 us
  starting transfers between devices: 22.9 us -> 24.5 us
    ppermute x10 -> x11, waiting for transfers between devices: 23.5 us -> 9.68 us  [swapped(): lax.ppermute(value, 'gy', [(i, i ^ 1) for i in range(lax.axis_size('gy'))])]
    ppermute x12, starting transfers between devices: 13.7 us -> 16.2 us  [shifted(): lax.ppermute(value, axis, [(i, (i + steps) % count) for i in range(count)])]
    ppermute x10 -> x11, starting transfers between devices: 9.25 us -> 8.26 us  [swapped(): lax.ppermute(value, 'gy', [(i, i ^ 1) for i in range(lax.axis_size('gy'))])]
    pallas_call x17 -> x15, Pallas kernels: 13.9 us -> 14.3 us  [call(): pl.pallas_call(kernel, out_shape=outs, in_specs=specs, out_specs=[pl.Bloc...]
  transfers between devices with their start and end apart: 22 -> 23, of which waited for: 9 -> 9; matrix products, arithmetic and copies ran while one was open for 0% -> 0% of each run, Pallas kernels for 16% -> 22%
where the time goes in v3:
time: 61.9 us; the launch traced here: 61.8 us
  starting transfers between devices  24.5 us (40%)
  waiting for transfers between devices  19 us (31%)
  Pallas kernels  16.9 us (27%)
  between operations  0.76 us (1%)
  local copies, waits for them, and re-layouts  0.65 us (1%)
    ppermute x12, starting transfers between devices, shifted(): lax.ppermute(value, axis, [(i, (i + steps) % count) for i in range(count)])  16.2 us
    pallas_call x15, Pallas kernels, call(): pl.pallas_call(kernel, out_shape=outs, in_specs=specs, out_specs=[pl.Bloc...  14.3 us
    ppermute x11, waiting for transfers between devices, swapped(): lax.ppermute(value, 'gy', [(i, i ^ 1) for i in range(lax.axis_size('gy'))])  9.68 us
    ppermute x12, waiting for transfers between devices, shifted(): lax.ppermute(value, axis, [(i, (i + steps) % count) for i in range(count)])  9.28 us
    ppermute x11, starting transfers between devices, swapped(): lax.ppermute(value, 'gy', [(i, i ^ 1) for i in range(lax.axis_size('gy'))])  8.26 us
    pallas_call x1, Pallas kernels, local(): pl.pallas_call(edge_kernel, out_shape=[f32(*old_fields.shape), jax.ShapeD...  2.61 us
  transfers between devices with their start and end apart: 23, of which 9 were waited for; matrix products, arithmetic and copies ran while one was open for 0% of the time, Pallas kernels for 22%

profile of v3, /device:TPU:1, one launch (start us, length us, event | category | flops | bytes accessed | tf_op | source)
XLA Modules:
  0.0 61.8 jit_solution(13798041900613598679)
XLA Ops:
  0.6 0.6 %copy-done = s32[2,1,1]{0,2,1:T(1,128)S(1)} copy-done((s32[2,1,1]{0,2,1:T(1,128)S(1)}, s32[2,1,1]{0,2,1:T(1,128)}, u32[]{:S(2)}) %copy-start) | copy-done | bytes 32
  1.3 2.6 %shard_map.50 = (f32[2,2,16,16,256]{4,3,2,1,0:T(8,128)S(1)}, bf16[4,2,16,16,256]{4,3,2,1,0:T(8,128)(2,1)S(1)}, f32[72,8,256]{2,1,0:T(8,128)S(1)}) custom-call(s32[2]{0:T(128)S(1)} %bitcast.1, f32[2,2,16,16,256]{4,3,2,1,0:T(8,128)} %fields_in.1, bf16[4,2,16,16,256]{4,3,2,1,0:T(8,128)(2,1)} %coef_in.1), custom_call_target="tpu_custom_call" | custom-call | tf_op jit(solution)/shard_map/pallas_call | solution.py:512
  3.9 2.1 %collective-permute-start.1 = (f32[72,8,256]{2,1,0:T(8,128)S(1)}, f32[72,8,256]{2,1,0:T(8,128)S(1)}, u32[]{:S(2)}, u32[]{:S(2)}) collective-permute-start(f32[72,8,256]{2,1,0:T(8,128)S(1)} %get-tuple-element.51._), channel_id=1, source_target_pairs={{0,4},{4,0},{1,5},{5,1},{2,6},{6,2},{3,7},{7,3},{8,12},{12,8},{9,1... | collective-permute-start | bytes 1769480 | tf_op jit(solution)/shard_map/ppermute | solution.py:40
  6.0 0.7 %shard_map.51._ = bf16[2,3,8,16,256]{4,3,2,1,0:T(8,128)(2,1)S(1)} custom-call(s32[2]{0:T(128)S(1)} %bitcast.2, bf16[4,2,16,16,256]{4,3,2,1,0:T(8,128)(2,1)S(1)} %get-tuple-element.50.coef, f32[72,8,256]{2,1,0:T(8,128)S(1)} %get-tuple-element.51._), custom_call_target="tpu_custom_call" | custom-call | tf_op jit(solution)/shard_map/pallas_call | solution.py:57
  6.7 2.9 %shard_map.55 = (f32[3,16,8,256]{3,2,1,0:T(8,128)S(1)}, f32[16,24,256]{2,1,0:T(8,128)S(1)}, f32[16,24,256]{2,1,0:T(8,128)S(1)}, f32[16,8,256]{2,1,0:T(8,128)S(1)...) custom-call(s32[2]{0:T(128)S(1)} %bitcast.3, ...), custom_call_target="tpu_custom_call" | custom-call | tf_op jit(solution)/shard_map/pallas_call | solution.py:57
  9.6 1.4 %collective-permute-start.6 = (f32[3,16,8,256]{3,2,1,0:T(8,128)S(1)}, f32[3,16,8,256]{3,2,1,0:T(8,128)S(1)}, u32[]{:S(2)}, u32[]{:S(2)}) collective-permute-start(f32[3,16,8,256]{3,2,1,0:T(8,128)S(1)} %get-tuple-element.59), channel_id=1, source_target_pairs={{0,4},{4,0},{1,5},{5,1},{2,6},{6,2},{3,7},{7,3},{8,12},{12,8},{9,1... | collective-permute-start | bytes 1179656 | tf_op jit(solution)/shard_map/ppermute | solution.py:40
  11.1 8.0 %collective-permute-done.1.edge_in = f32[72,8,256]{2,1,0:T(8,128)S(1)} collective-permute-done((f32[72,8,256]{2,1,0:T(8,128)S(1)}, f32[72,8,256]{2,1,0:T(8,128)S(1)}, u32[]{:S(2)}, u32[]{:S(2)}) %collective-permute-start.1) | collective-permute-done | bytes 589856 | tf_op jit(solution)/shard_map/ppermute | solution.py:40
  19.1 1.0 %shard_map.52 = (f32[4,3,8,128]{3,2,1,0:T(8,128)S(1)}, f32[4,3,8,128]{3,2,1,0:T(8,128)S(1)}) custom-call(s32[2]{0:T(128)S(1)} %bitcast.4, f32[2,2,16,16,256]{4,3,2,1,0:T(8,128)S(1)} %get-tuple-element.52.fields, bf16[4,2,16,16,256]{4,3,2,1,0:T(8,128)(2,1)S(1)} %get-tuple-element.50.coef, f32[72,8,256]{2,1,0:T(8,128)S(1)} %collective-permute-done.1.edge_in), custom_call_target="tpu_custom_call" | custom-call | tf_op jit(solution)/shard_map/pallas_call | solution.py:57
  20.1 1.3 %collective-permute-start.2 = (f32[4,3,8,128]{3,2,1,0:T(8,128)S(1)}, f32[4,3,8,128]{3,2,1,0:T(8,128)S(1)}, u32[]{:S(2)}, u32[]{:S(2)}) collective-permute-start(f32[4,3,8,128]{3,2,1,0:T(8,128)S(1)} %get-tuple-element.54.right), channel_id=1, source_target_pairs={{0,8},{8,16},{16,24},{24,0},{1,9},{9,17},{17,25},{25,1},{2,10},{10... | collective-permute-start | bytes 147464 | tf_op jit(solution)/shard_map/ppermute | solution.py:36
  21.4 2.1 %collective-permute-start.3 = (f32[4,3,8,128]{3,2,1,0:T(8,128)S(1)}, f32[4,3,8,128]{3,2,1,0:T(8,128)S(1)}, u32[]{:S(2)}, u32[]{:S(2)}) collective-permute-start(f32[4,3,8,128]{3,2,1,0:T(8,128)S(1)} %get-tuple-element.53.left), channel_id=1, source_target_pairs={{0,24},{8,0},{16,8},{24,16},{1,25},{9,1},{17,9},{25,17},{2,26},{10... | collective-permute-start | bytes 147464 | tf_op jit(solution)/shard_map/ppermute | solution.py:36
  23.5 1.4 %collective-permute-done.2.from_left = f32[4,3,8,128]{3,2,1,0:T(8,128)S(1)} collective-permute-done((f32[4,3,8,128]{3,2,1,0:T(8,128)S(1)}, f32[4,3,8,128]{3,2,1,0:T(8,128)S(1)}, u32[]{:S(2)}, u32[]{:S(2)}) %collective-permute-start.2) | collective-permute-done | bytes 49184 | tf_op jit(solution)/shard_map/ppermute | solution.py:36
  24.9 1.2 %shard_map.53 = (f32[16,24,256]{2,1,0:T(8,128)S(1)}, f32[16,24,128]{2,1,0:T(8,128)S(1)}, f32[2,16,24,384]{3,2,1,0:T(8,128)S(1)}, f32[2,16,24,128]{3,2,1,0:T(8,12...) custom-call(s32[2]{0:T(128)S(1)} %bitcast.5, ...), custom_call_target="tpu_custom_call" | custom-call | tf_op jit(solution)/shard_map/pallas_call | solution.py:57
  26.1 4.1 %collective-permute-start.4 = (f32[2,24,384]{2,1,0:T(8,128)S(1)}, f32[2,24,384]{2,1,0:T(8,128)S(1)}, u32[]{:S(2)}, u32[]{:S(2)}) collective-permute-start(f32[2,24,384]{2,1,0:T(8,128)S(1)} %get-tuple-element.57.down), channel_id=1, source_target_pairs={{0,3},{1,0},{2,1},{3,2},{4,7},{5,4},{6,5},{7,6},{8,11},{9,8},{10,9... | collective-permute-start | bytes 221192 | tf_op jit(solution)/shard_map/ppermute | solution.py:36
  30.2 1.2 %collective-permute-start.5 = (f32[3,16,384]{2,1,0:T(8,128)S(1)}, f32[3,16,384]{2,1,0:T(8,128)S(1)}, u32[]{:S(2)}, u32[]{:S(2)}) collective-permute-start(f32[3,16,384]{2,1,0:T(8,128)S(1)} %get-tuple-element.58.own_last), channel_id=1, source_target_pairs={{0,4},{4,0},{1,5},{5,1},{2,6},{6,2},{3,7},{7,3},{8,12},{12,8},{9,1... | collective-permute-start | bytes 221192 | tf_op jit(solution)/shard_map/ppermute | solution.py:40
  31.7 1.7 %collective-permute-start.7 = (f32[24,384]{1,0:T(8,128)S(1)}, f32[24,384]{1,0:T(8,128)S(1)}, u32[]{:S(2)}, u32[]{:S(2)}) collective-permute-start(f32[24,384]{1,0:T(8,128)S(1)} %get-tuple-element.63.up), channel_id=1, source_target_pairs={{0,1},{1,2},{2,3},{3,0},{4,5},{5,6},{6,7},{7,4},{8,9},{9,10},{10,1... | collective-permute-start | bytes 110600 | tf_op jit(solution)/shard_map/ppermute | solution.py:36
  33.5 0.7 %shard_map.54.wide_ax = f32[2,16,24,384]{3,2,1,0:T(8,128)S(1)} custom-call(s32[2]{0:T(128)S(1)} %bitcast.6, bf16[4,2,16,16,256]{4,3,2,1,0:T(8,128)(2,1)S(1)} %get-tuple-element.50.coef, bf16[2,3,8,16,256]{4,3,2,1,0:T(8,128)(2,1)S(1)} %collective-permute-done.coef_in, f32[2,16,24,128]{3,2,1,0:T(8,128)S(1)} %get-tuple-element.55.ghosts), custom_call_target="tpu_custom_call" | custom-call | tf_op jit(solution)/shard_map/pallas_call | solution.py:57
  34.5 1.2 %shard_map.56 = (f32[16,24,384]{2,1,0:T(8,128)S(1)}, f32[16,24,384]{2,1,0:T(8,128)S(1)}) custom-call(f32[2,16,24,384]{3,2,1,0:T(8,128)S(1)} %shard_map.54.wide_ax, f32[2,16,24,384]{3,2,1,0:T(8,128)S(1)} %get-tuple-element.56.wide_yz, f32[16,24,256]{2,1,0:T(8,128)S(1)} %get-tuple-element.60.edge_start, f32[16,24,128]{2,1,0:T(8,128)S(1)} %get-tuple-element.61.rhs_ghost, ...), custom_call_target="tpu_custom_call" | custom-call | tf_op jit(solution)/shard_map/pallas_call | solution.py:57
  35.9 1.6 %collective-permute-done.5.ghost_rows.rim_rows = f32[3,16,384]{2,1,0:T(8,128)S(1)} collective-permute-done((f32[3,16,384]{2,1,0:T(8,128)S(1)}, f32[3,16,384]{2,1,0:T(8,128)S(1)}, u32[]{:S(2)}, u32[]{:S(2)}) %collective-permute-start.5) | collective-permute-done | bytes 73760 | tf_op jit(solution)/shard_map/ppermute | solution.py:40
  37.8 1.2 %collective-permute-start.10 = (f32[2,16,384]{2,1,0:T(8,128)S(1)}, f32[2,16,384]{2,1,0:T(8,128)S(1)}, u32[]{:S(2)}, u32[]{:S(2)}) collective-permute-start(f32[2,16,384]{2,1,0:T(8,128)S(1)} %get-tuple-element.77), channel_id=1, source_target_pairs={{0,4},{4,0},{1,5},{5,1},{2,6},{6,2},{3,7},{7,3},{8,12},{12,8},{9,1... | collective-permute-start | bytes 147464 | tf_op jit(solution)/shard_map/ppermute | solution.py:40
  39.0 4.1 %collective-permute-start.8 = (f32[24,384]{1,0:T(8,128)S(1)}, f32[24,384]{1,0:T(8,128)S(1)}, u32[]{:S(2)}, u32[]{:S(2)}) collective-permute-start(f32[24,384]{1,0:T(8,128)S(1)} %get-tuple-element.75), channel_id=1, source_target_pairs={{0,1},{1,2},{2,3},{3,0},{4,5},{5,6},{6,7},{7,4},{8,9},{9,10},{10,1... | collective-permute-start | bytes 110600 | tf_op jit(solution)/shard_map/ppermute | solution.py:36
  43.3 1.1 %shard_map.58 = (f32[16,24,384]{2,1,0:T(8,128)S(1)}, f32[16,24,384]{2,1,0:T(8,128)S(1)}, f32[16,24,256]{2,1,0:T(8,128)S(1)}) custom-call(f32[2,16,24,384]{3,2,1,0:T(8,128)S(1)} %shard_map.54.wide_ax, f32[2,16,24,384]{3,2,1,0:T(8,128)S(1)} %get-tuple-element.56.wide_yz, f32[2,24,384]{2,1,0:T(8,128)S(1)} %collective-permute-done.4.high_face.rim_face, ...), custom_call_target="tpu_custom_call" | custom-call | tf_op jit(solution)/shard_map/pallas_call | solution.py:57
  44.5 2.0 %collective-permute-done.9.refs_1_.high_face = f32[1,24,384]{2,1,0:T(8,128)S(1)} collective-permute-done((f32[1,24,384]{2,1,0:T(8,128)S(1)}, f32[1,24,384]{2,1,0:T(8,128)S(1)}, u32[]{:S(2)}, u32[]{:S(2)}) %collective-permute-start.9) | collective-permute-done | bytes 36896 | tf_op jit(solution)/shard_map/ppermute | solution.py:36
  46.5 0.6 %collective-permute-start.14 = (f32[2,16,384]{2,1,0:T(8,128)S(1)}, f32[2,16,384]{2,1,0:T(8,128)S(1)}, u32[]{:S(2)}, u32[]{:S(2)}) collective-permute-start(f32[2,16,384]{2,1,0:T(8,128)S(1)} %get-tuple-element.84), channel_id=1, source_target_pairs={{0,4},{4,0},{1,5},{5,1},{2,6},{6,2},{3,7},{7,3},{8,12},{12,8},{9,1... | collective-permute-start | bytes 147464 | tf_op jit(solution)/shard_map/ppermute | solution.py:40
  47.1 1.0 %collective-permute-start.12 = (f32[24,384]{1,0:T(8,128)S(1)}, f32[24,384]{1,0:T(8,128)S(1)}, u32[]{:S(2)}, u32[]{:S(2)}) collective-permute-start(f32[24,384]{1,0:T(8,128)S(1)} %get-tuple-element.82), channel_id=1, source_target_pairs={{0,1},{1,2},{2,3},{3,0},{4,5},{5,6},{6,7},{7,4},{8,9},{9,10},{10,1... | collective-permute-start | bytes 110600 | tf_op jit(solution)/shard_map/ppermute | solution.py:36
  48.6 1.2 %shard_map.59 = (f32[16,24,384]{2,1,0:T(8,128)S(1)}, f32[16,24,384]{2,1,0:T(8,128)S(1)}, f32[16,24,256]{2,1,0:T(8,128)S(1)}) custom-call(f32[2,16,24,384]{3,2,1,0:T(8,128)S(1)} %shard_map.54.wide_ax, f32[2,16,24,384]{3,2,1,0:T(8,128)S(1)} %get-tuple-element.56.wide_yz, f32[2,24,384]{2,1,0:T(8,128)S(1)} %collective-permute-done.4.high_face.rim_face, ...), custom_call_target="tpu_custom_call" | custom-call | tf_op jit(solution)/shard_map/pallas_call | solution.py:57
  49.8 1.8 %collective-permute-done.13.refs_1_.high_face = f32[1,24,384]{2,1,0:T(8,128)S(1)} collective-permute-done((f32[1,24,384]{2,1,0:T(8,128)S(1)}, f32[1,24,384]{2,1,0:T(8,128)S(1)}, u32[]{:S(2)}, u32[]{:S(2)}) %collective-permute-start.13) | collective-permute-done | bytes 36896 | tf_op jit(solution)/shard_map/ppermute | solution.py:36
  51.9 1.4 %collective-permute-start.16 = (f32[24,384]{1,0:T(8,128)S(1)}, f32[24,384]{1,0:T(8,128)S(1)}, u32[]{:S(2)}, u32[]{:S(2)}) collective-permute-start(f32[24,384]{1,0:T(8,128)S(1)} %get-tuple-element.89), channel_id=1, source_target_pairs={{0,1},{1,2},{2,3},{3,0},{4,5},{5,6},{6,7},{7,4},{8,9},{9,10},{10,1... | collective-permute-start | bytes 110600 | tf_op jit(solution)/shard_map/ppermute | solution.py:36
  53.3 1.2 %shard_map.61 = (f32[16,24,384]{2,1,0:T(8,128)S(1)}, f32[16,24,384]{2,1,0:T(8,128)S(1)}, f32[16,24,256]{2,1,0:T(8,128)S(1)}) custom-call(f32[2,16,24,384]{3,2,1,0:T(8,128)S(1)} %shard_map.54.wide_ax, f32[2,16,24,384]{3,2,1,0:T(8,128)S(1)} %get-tuple-element.56.wide_yz, f32[2,24,384]{2,1,0:T(8,128)S(1)} %collective-permute-done.4.high_face.rim_face, ...), custom_call_target="tpu_custom_call" | custom-call | tf_op jit(solution)/shard_map/pallas_call | solution.py:57
  54.5 2.2 %collective-permute-done.17.refs_1_.high_face = f32[1,24,384]{2,1,0:T(8,128)S(1)} collective-permute-done((f32[1,24,384]{2,1,0:T(8,128)S(1)}, f32[1,24,384]{2,1,0:T(8,128)S(1)}, u32[]{:S(2)}, u32[]{:S(2)}) %collective-permute-start.17) | collective-permute-done | bytes 36896 | tf_op jit(solution)/shard_map/ppermute | solution.py:36
  57.6 1.7 %shard_map.63 = (f32[16,24,256]{2,1,0:T(8,128)S(1)}, f32[16,24,256]{2,1,0:T(8,128)}) custom-call(f32[2,16,24,384]{3,2,1,0:T(8,128)S(1)} %shard_map.54.wide_ax, f32[2,16,24,384]{3,2,1,0:T(8,128)S(1)} %get-tuple-element.56.wide_yz, f32[2,24,384]{2,1,0:T(8,128)S(1)} %collective-permute-done.4.high_face.rim_face, ...), custom_call_target="tpu_custom_call" | custom-call | tf_op jit(solution)/shard_map/pallas_call | solution.py:57
  59.4 1.6 %collective-permute-done.21.high_face = f32[1,24,384]{2,1,0:T(8,128)S(1)} collective-permute-done((f32[1,24,384]{2,1,0:T(8,128)S(1)}, f32[1,24,384]{2,1,0:T(8,128)S(1)}, u32[]{:S(2)}, u32[]{:S(2)}) %collective-permute-start.21) | collective-permute-done | bytes 36896 | tf_op jit(solution)/shard_map/ppermute | solution.py:36
  61.0 0.8 %shard_map.65 = f32[16,24,256]{2,1,0:T(8,128)} custom-call(f32[2,16,24,384]{3,2,1,0:T(8,128)S(1)} %get-tuple-element.56.wide_yz, f32[2,24,384]{2,1,0:T(8,128)S(1)} %collective-permute-done.4.high_face.rim_face, f32[3,16,384]{2,1,0:T(8,128)S(1)} %collective-permute-done.5.ghost_rows.rim_rows, f32[24,384]{1,0:T(8,128)S(1)} %collective-permute-done.20.low_face, ...), custom_call_target="tpu_custom_call" | custom-call | tf_op jit(solution)/shard_map/pallas_call | solution.py:57
  (34 shorter events, 3.2 us)
Async XLA Ops:
  0.6 0.7 %copy-start = (s32[2,1,1]{0,2,1:T(1,128)S(1)}, s32[2,1,1]{0,2,1:T(1,128)}, u32[]{:S(2)}) copy-start(s32[2,1,1]{0,2,1:T(1,128)} %param.5) | copy-start | bytes 28
  3.9 15.2 %collective-permute-start.1 = (f32[72,8,256]{2,1,0:T(8,128)S(1)}, f32[72,8,256]{2,1,0:T(8,128)S(1)}, u32[]{:S(2)}, u32[]{:S(2)}) collective-permute-start(f32[72,8,256]{2,1,0:T(8,128)S(1)} %get-tuple-element.51._), channel_id=1, source_target_pairs={{0,4},{4,0},{1,5},{5,1},{2,6},{6,2},{3,7},{7,3},{8,12},{12,8},{9,1... | collective-permute-start | bytes 1769480 | tf_op jit(solution)/shard_map/ppermute | solution.py:40
  6.7 25.1 %collective-permute-start = (bf16[2,3,8,16,256]{4,3,2,1,0:T(8,128)(2,1)S(1)}, bf16[2,3,8,16,256]{4,3,2,1,0:T(8,128)(2,1)S(1)}, u32[]{:S(2)}, u32[]{:S(2)}) collective-permute-start(bf16[2,3,8,16,256]{4,3,2,1,0:T(8,128)(2,1)S(1)} %shard_map.51._), channel_id=1, source_target_pairs={{0,4},{4,0},{1,5},{5,1},{2,6},{6,2},{3,7},{7,3},{8,12},{12,8},{9,1... | collective-permute-start | bytes 1179656 | tf_op jit(solution)/shard_map/ppermute | solution.py:40
  9.6 15.2 %copy-start.1 = (s32[2,1,1]{0,2,1:T(1,128)S(1)}, s32[2,1,1]{0,2,1:T(1,128)}, u32[]{:S(2)}) copy-start(s32[2,1,1]{0,2,1:T(1,128)} %param.5) | copy-start | bytes 28
  9.6 26.3 %collective-permute-start.6 = (f32[3,16,8,256]{3,2,1,0:T(8,128)S(1)}, f32[3,16,8,256]{3,2,1,0:T(8,128)S(1)}, u32[]{:S(2)}, u32[]{:S(2)}) collective-permute-start(f32[3,16,8,256]{3,2,1,0:T(8,128)S(1)} %get-tuple-element.59), channel_id=1, source_target_pairs={{0,4},{4,0},{1,5},{5,1},{2,6},{6,2},{3,7},{7,3},{8,12},{12,8},{9,1... | collective-permute-start | bytes 1179656 | tf_op jit(solution)/shard_map/ppermute | solution.py:40
  20.1 4.8 %collective-permute-start.2 = (f32[4,3,8,128]{3,2,1,0:T(8,128)S(1)}, f32[4,3,8,128]{3,2,1,0:T(8,128)S(1)}, u32[]{:S(2)}, u32[]{:S(2)}) collective-permute-start(f32[4,3,8,128]{3,2,1,0:T(8,128)S(1)} %get-tuple-element.54.right), channel_id=1, source_target_pairs={{0,8},{8,16},{16,24},{24,0},{1,9},{9,17},{17,25},{25,1},{2,10},{10... | collective-permute-start | bytes 147464 | tf_op jit(solution)/shard_map/ppermute | solution.py:36
  21.4 3.5 %collective-permute-start.3 = (f32[4,3,8,128]{3,2,1,0:T(8,128)S(1)}, f32[4,3,8,128]{3,2,1,0:T(8,128)S(1)}, u32[]{:S(2)}, u32[]{:S(2)}) collective-permute-start(f32[4,3,8,128]{3,2,1,0:T(8,128)S(1)} %get-tuple-element.53.left), channel_id=1, source_target_pairs={{0,24},{8,0},{16,8},{24,16},{1,25},{9,1},{17,9},{25,17},{2,26},{10... | collective-permute-start | bytes 147464 | tf_op jit(solution)/shard_map/ppermute | solution.py:36
  26.1 8.4 %collective-permute-start.4 = (f32[2,24,384]{2,1,0:T(8,128)S(1)}, f32[2,24,384]{2,1,0:T(8,128)S(1)}, u32[]{:S(2)}, u32[]{:S(2)}) collective-permute-start(f32[2,24,384]{2,1,0:T(8,128)S(1)} %get-tuple-element.57.down), channel_id=1, source_target_pairs={{0,3},{1,0},{2,1},{3,2},{4,7},{5,4},{6,5},{7,6},{8,11},{9,8},{10,9... | collective-permute-start | bytes 221192 | tf_op jit(solution)/shard_map/ppermute | solution.py:36
  30.2 7.2 %collective-permute-start.5 = (f32[3,16,384]{2,1,0:T(8,128)S(1)}, f32[3,16,384]{2,1,0:T(8,128)S(1)}, u32[]{:S(2)}, u32[]{:S(2)}) collective-permute-start(f32[3,16,384]{2,1,0:T(8,128)S(1)} %get-tuple-element.58.own_last), channel_id=1, source_target_pairs={{0,4},{4,0},{1,5},{5,1},{2,6},{6,2},{3,7},{7,3},{8,12},{12,8},{9,1... | collective-permute-start | bytes 221192 | tf_op jit(solution)/shard_map/ppermute | solution.py:40
  31.5 16.7 %collective-permute-start.11 = (f32[16,8,256]{2,1,0:T(8,128)S(1)}, f32[16,8,256]{2,1,0:T(8,128)S(1)}, u32[]{:S(2)}, u32[]{:S(2)}) collective-permute-start(f32[16,8,256]{2,1,0:T(8,128)S(1)} %get-tuple-element.78), channel_id=1, source_target_pairs={{0,4},{4,0},{1,5},{5,1},{2,6},{6,2},{3,7},{7,3},{8,12},{12,8},{9,1... | collective-permute-start | bytes 393224 | tf_op jit(solution)/shard_map/ppermute | solution.py:40
  31.7 2.8 %collective-permute-start.7 = (f32[24,384]{1,0:T(8,128)S(1)}, f32[24,384]{1,0:T(8,128)S(1)}, u32[]{:S(2)}, u32[]{:S(2)}) collective-permute-start(f32[24,384]{1,0:T(8,128)S(1)} %get-tuple-element.63.up), channel_id=1, source_target_pairs={{0,1},{1,2},{2,3},{3,0},{4,5},{5,6},{6,7},{7,4},{8,9},{9,10},{10,1... | collective-permute-start | bytes 110600 | tf_op jit(solution)/shard_map/ppermute | solution.py:36
  37.8 8.7 %collective-permute-start.10 = (f32[2,16,384]{2,1,0:T(8,128)S(1)}, f32[2,16,384]{2,1,0:T(8,128)S(1)}, u32[]{:S(2)}, u32[]{:S(2)}) collective-permute-start(f32[2,16,384]{2,1,0:T(8,128)S(1)} %get-tuple-element.77), channel_id=1, source_target_pairs={{0,4},{4,0},{1,5},{5,1},{2,6},{6,2},{3,7},{7,3},{8,12},{12,8},{9,1... | collective-permute-start | bytes 147464 | tf_op jit(solution)/shard_map/ppermute | solution.py:40
  39.0 5.5 %collective-permute-start.8 = (f32[24,384]{1,0:T(8,128)S(1)}, f32[24,384]{1,0:T(8,128)S(1)}, u32[]{:S(2)}, u32[]{:S(2)}) collective-permute-start(f32[24,384]{1,0:T(8,128)S(1)} %get-tuple-element.75), channel_id=1, source_target_pairs={{0,1},{1,2},{2,3},{3,0},{4,5},{5,6},{6,7},{7,4},{8,9},{9,10},{10,1... | collective-permute-start | bytes 110600 | tf_op jit(solution)/shard_map/ppermute | solution.py:36
  43.1 3.4 %collective-permute-start.9 = (f32[1,24,384]{2,1,0:T(8,128)S(1)}, f32[1,24,384]{2,1,0:T(8,128)S(1)}, u32[]{:S(2)}, u32[]{:S(2)}) collective-permute-start(f32[1,24,384]{2,1,0:T(8,128)S(1)} %get-tuple-element.76), channel_id=1, source_target_pairs={{0,3},{1,0},{2,1},{3,2},{4,7},{5,4},{6,5},{7,6},{8,11},{9,8},{10,9... | collective-permute-start | bytes 110600 | tf_op jit(solution)/shard_map/ppermute | solution.py:36
  43.1 10.2 %collective-permute-start.15 = (f32[16,8,256]{2,1,0:T(8,128)S(1)}, f32[16,8,256]{2,1,0:T(8,128)S(1)}, u32[]{:S(2)}, u32[]{:S(2)}) collective-permute-start(f32[16,8,256]{2,1,0:T(8,128)S(1)} %get-tuple-element.85), channel_id=1, source_target_pairs={{0,4},{4,0},{1,5},{5,1},{2,6},{6,2},{3,7},{7,3},{8,12},{12,8},{9,1... | collective-permute-start | bytes 393224 | tf_op jit(solution)/shard_map/ppermute | solution.py:40
  46.5 5.0 %collective-permute-start.14 = (f32[2,16,384]{2,1,0:T(8,128)S(1)}, f32[2,16,384]{2,1,0:T(8,128)S(1)}, u32[]{:S(2)}, u32[]{:S(2)}) collective-permute-start(f32[2,16,384]{2,1,0:T(8,128)S(1)} %get-tuple-element.84), channel_id=1, source_target_pairs={{0,4},{4,0},{1,5},{5,1},{2,6},{6,2},{3,7},{7,3},{8,12},{12,8},{9,1... | collective-permute-start | bytes 147464 | tf_op jit(solution)/shard_map/ppermute | solution.py:40
  47.1 2.6 %collective-permute-start.12 = (f32[24,384]{1,0:T(8,128)S(1)}, f32[24,384]{1,0:T(8,128)S(1)}, u32[]{:S(2)}, u32[]{:S(2)}) collective-permute-start(f32[24,384]{1,0:T(8,128)S(1)} %get-tuple-element.82), channel_id=1, source_target_pairs={{0,1},{1,2},{2,3},{3,0},{4,5},{5,6},{6,7},{7,4},{8,9},{9,10},{10,1... | collective-permute-start | bytes 110600 | tf_op jit(solution)/shard_map/ppermute | solution.py:36
  48.2 3.4 %collective-permute-start.13 = (f32[1,24,384]{2,1,0:T(8,128)S(1)}, f32[1,24,384]{2,1,0:T(8,128)S(1)}, u32[]{:S(2)}, u32[]{:S(2)}) collective-permute-start(f32[1,24,384]{2,1,0:T(8,128)S(1)} %get-tuple-element.83), channel_id=1, source_target_pairs={{0,3},{1,0},{2,1},{3,2},{4,7},{5,4},{6,5},{7,6},{8,11},{9,8},{10,9... | collective-permute-start | bytes 110600 | tf_op jit(solution)/shard_map/ppermute | solution.py:36
  48.2 9.5 %collective-permute-start.19 = (f32[16,8,256]{2,1,0:T(8,128)S(1)}, f32[16,8,256]{2,1,0:T(8,128)S(1)}, u32[]{:S(2)}, u32[]{:S(2)}) collective-permute-start(f32[16,8,256]{2,1,0:T(8,128)S(1)} %get-tuple-element.92), channel_id=1, source_target_pairs={{0,4},{4,0},{1,5},{5,1},{2,6},{6,2},{3,7},{7,3},{8,12},{12,8},{9,1... | collective-permute-start | bytes 393224 | tf_op jit(solution)/shard_map/ppermute | solution.py:40
  51.6 5.1 %collective-permute-start.18 = (f32[2,16,384]{2,1,0:T(8,128)S(1)}, f32[2,16,384]{2,1,0:T(8,128)S(1)}, u32[]{:S(2)}, u32[]{:S(2)}) collective-permute-start(f32[2,16,384]{2,1,0:T(8,128)S(1)} %get-tuple-element.91), channel_id=1, source_target_pairs={{0,4},{4,0},{1,5},{5,1},{2,6},{6,2},{3,7},{7,3},{8,12},{12,8},{9,1... | collective-permute-start | bytes 147464 | tf_op jit(solution)/shard_map/ppermute | solution.py:40
  51.9 2.6 %collective-permute-start.16 = (f32[24,384]{1,0:T(8,128)S(1)}, f32[24,384]{1,0:T(8,128)S(1)}, u32[]{:S(2)}, u32[]{:S(2)}) collective-permute-start(f32[24,384]{1,0:T(8,128)S(1)} %get-tuple-element.89), channel_id=1, source_target_pairs={{0,1},{1,2},{2,3},{3,0},{4,5},{5,6},{6,7},{7,4},{8,9},{9,10},{10,1... | collective-permute-start | bytes 110600 | tf_op jit(solution)/shard_map/ppermute | solution.py:36
  53.3 3.4 %collective-permute-start.17 = (f32[1,24,384]{2,1,0:T(8,128)S(1)}, f32[1,24,384]{2,1,0:T(8,128)S(1)}, u32[]{:S(2)}, u32[]{:S(2)}) collective-permute-start(f32[1,24,384]{2,1,0:T(8,128)S(1)} %get-tuple-element.90), channel_id=1, source_target_pairs={{0,3},{1,0},{2,1},{3,2},{4,7},{5,4},{6,5},{7,6},{8,11},{9,8},{10,9... | collective-permute-start | bytes 110600 | tf_op jit(solution)/shard_map/ppermute | solution.py:36
  56.8 4.2 %collective-permute-start.22 = (f32[2,16,384]{2,1,0:T(8,128)S(1)}, f32[2,16,384]{2,1,0:T(8,128)S(1)}, u32[]{:S(2)}, u32[]{:S(2)}) collective-permute-start(f32[2,16,384]{2,1,0:T(8,128)S(1)} %get-tuple-element.96), channel_id=1, source_target_pairs={{0,4},{4,0},{1,5},{5,1},{2,6},{6,2},{3,7},{7,3},{8,12},{12,8},{9,1... | collective-permute-start | bytes 147464 | tf_op jit(solution)/shard_map/ppermute | solution.py:40
  57.1 2.3 %collective-permute-start.20 = (f32[24,384]{1,0:T(8,128)S(1)}, f32[24,384]{1,0:T(8,128)S(1)}, u32[]{:S(2)}, u32[]{:S(2)}) collective-permute-start(f32[24,384]{1,0:T(8,128)S(1)} %get-tuple-element.94), channel_id=1, source_target_pairs={{0,1},{1,2},{2,3},{3,0},{4,5},{5,6},{6,7},{7,4},{8,9},{9,10},{10,1... | collective-permute-start | bytes 110600 | tf_op jit(solution)/shard_map/ppermute | solution.py:36
  57.6 3.4 %collective-permute-start.21 = (f32[1,24,384]{2,1,0:T(8,128)S(1)}, f32[1,24,384]{2,1,0:T(8,128)S(1)}, u32[]{:S(2)}, u32[]{:S(2)}) collective-permute-start(f32[1,24,384]{2,1,0:T(8,128)S(1)} %get-tuple-element.95), channel_id=1, source_target_pairs={{0,3},{1,0},{2,1},{3,2},{4,7},{5,4},{6,5},{7,6},{8,11},{9,8},{10,9... | collective-permute-start | bytes 110600 | tf_op jit(solution)/shard_map/ppermute | solution.py:36

commit v4 on v3

v4 whole, which is shorter than its diff:
```python
import functools

import jax
import jax.numpy as jnp
from jax import lax
from jax.experimental import pallas as pl
from jax.experimental.pallas import tpu as pltpu
from jax.sharding import PartitionSpec as P

SWEEPS = 4
LANES = 128
STRIP = 8
SHIFT = 4096.0
VMEM_LIMIT = 24 * 1024 * 1024


def chebyshev_weights(count):
    low_bound = 0.25
    high_bound = 2.0
    centre_value = 0.5 * (high_bound + low_bound)
    half_width = 0.5 * (high_bound - low_bound)
    ratio_value = centre_value / half_width
    damping = 1.0 / ratio_value
    first_list = [0.0]
    second_list = [1.0 / centre_value]
    for step_index in range(1, count):
        damping_next = 1.0 / (2.0 * ratio_value - damping)
        first_list.append(damping_next * damping)
        second_list.append(2.0 * damping_next / half_width)
        damping = damping_next
    return (first_list, second_list)


def shifted(value, axis, steps):
    count = lax.axis_size(axis)
    return lax.ppermute(value, axis, [(i, (i + steps) % count) for i in range(count)])


def swapped(value):
    return lax.ppermute(value, "gy", [(i, i ^ 1) for i in range(lax.axis_size("gy"))])


def row_ghosts(rows):
    if lax.axis_size("gy") == 2:
        return swapped(rows)
    return jnp.concatenate([shifted(rows[:1], "gy", 1), shifted(rows[1:], "gy", -1)])


def f32(*shape):
    return jax.ShapeDtypeStruct(shape, jnp.float32)


def call(kernel, outs, *operands, ids=False, sent=False):
    out_specs = [pl.BlockSpec(memory_space=pltpu.VMEM) for _ in outs]
    scratch = []
    if sent:
        out_specs = [pl.BlockSpec(memory_space=pltpu.HBM) for _ in outs]
        scratch = [pltpu.VMEM(out.shape, out.dtype) for out in outs] + [pltpu.SemaphoreType.DMA((4,)) for _ in outs]
    specs = [pl.BlockSpec(memory_space=pltpu.VMEM) for _ in operands]
    if ids:
        specs[0] = pl.BlockSpec(memory_space=pltpu.SMEM)
    return pl.pallas_call(
        kernel,
        out_shape=outs,
        in_specs=specs,
        out_specs=out_specs,
        scratch_shapes=scratch,
        compiler_params=pltpu.CompilerParams(vmem_limit_bytes=VMEM_LIMIT),
    )(*operands)


def lane_of(shape):
    return lax.broadcasted_iota(jnp.int32, shape, 1)


def row_of(shape):
    return lax.broadcasted_iota(jnp.int32, shape, 0)


def units_of(ids, half, numbers=(0, 1, 2)):
    first = 3 * (lax.axis_index("gy") // 2)
    a, b = ids[0] - first, ids[1] - first
    found = []
    for k in numbers:
        unit = (3 * half + k) % 6
        slab = unit // 2
        found.append((jnp.logical_or(a == slab, b == slab), jnp.where(a == slab, 0, 1), unit % 2))
    return found


def field_unit(fields, item, place, z):
    rows = fields.shape[3] // 2
    _, slot, part = place
    return fields[item, slot, z, pl.ds(pl.multiple_of(part * rows, rows), rows), :]


def coef_unit(coef, item, place, z):
    rows = coef.shape[3] // 2
    _, slot, part = place
    both = coef[item, slot, z].astype(jnp.float32)
    return jnp.where(part == 0, both[:rows], both[rows:])


def strips(fields, coef, item, place, planes):
    columns, rows = fields.shape[4], fields.shape[3] // 2
    group = lane_of((rows, LANES)) // STRIP
    low = jnp.zeros((rows, LANES), jnp.float32)
    high = jnp.zeros((rows, LANES), jnp.float32)
    for z in range(planes):
        if item < 2:
            cells = field_unit(fields, item, place, z)
        else:
            cells = coef_unit(coef, 2 * item - 4, place, z) + SHIFT * coef_unit(coef, 2 * item - 3, place, z)
        first, last = cells[:, :LANES], cells[:, columns - LANES :]
        turn = STRIP * z
        low = jnp.where(group == z, pltpu.roll(first, turn, 1) if turn else first, low)
        turn = (STRIP * z + STRIP) % LANES
        high = jnp.where(group == z, pltpu.roll(last, turn, 1) if turn else last, high)
    return low, high


def outer_strips(fields, coef, item, ids, half, planes):
    found = []
    for place in units_of(ids, half, (3, 5)):
        found.append([jnp.where(place[0], side, 0.0) for side in strips(fields, coef, item, place, planes)])
    above = row_of(found[0][0].shape) < found[0][0].shape[0] // 2
    return [jnp.where(above, high, low) for high, low in zip(*found)]


def outer_row(fields, ids, half, z):
    last = fields.shape[3] - 1
    (above_held, above_slot, _), (below_held, below_slot, _) = units_of(ids, half, (3, 5))
    above = jnp.where(above_held, fields[0, above_slot, z, 0:1], 0.0)
    below = jnp.where(below_held, fields[0, below_slot, z, last : last + 1], 0.0)
    return jnp.where(half == 0, below, above)


def brick_rows(ids, half, unit_rows):
    first = 3 * (lax.axis_index("gy") // 2)
    a, b = ids[0] - first, ids[1] - first
    found = []
    for j in range(3):
        slab = jnp.where(half == 0, j // 2, 1 + (j + 1) // 2)
        row = jnp.where((j + half) % 2 == 0, 0, 2 * unit_rows - 1)
        found.append((jnp.logical_or(a == slab, b == slab), jnp.where(a == slab, 0, 1), row))
    return found


def field_row(fields, place, z):
    last = fields.shape[3] - 1
    _, slot, row = place
    return jnp.where(row == 0, fields[0, slot, z, 0:1], fields[0, slot, z, last : last + 1])


PLANES_AT, ROWS_AT = 12, 18
FIRST_PAIRS = 16
NEXT_PAIRS = 45
PIECES = (1, 8, 15)
CODE_BITS = 20
ADDED_AT = (2, 4)


def pieces_at(stage):
    return [number for number, at in enumerate(ADDED_AT) if at == stage]


def power_of_two(number):
    size, result = jnp.abs(number), jnp.ones(number.shape, jnp.float32)
    for bit in range(7):
        factor = jnp.where(number < 0, 2.0 ** -(1 << bit), 2.0 ** (1 << bit))
        result = result * jnp.where((size >> bit) & 1 == 1, factor, 1.0)
    return result


def exponents_of(tops):
    return (jnp.floor(jnp.log2(jnp.maximum(tops, 1e-30)) + 0.001) + 1.0).astype(jnp.int32)


def encoded(tiles, factors, first):
    codes, limit = [], float((1 << CODE_BITS) - 1)
    for j, tile in enumerate(tiles):
        scaled = jnp.floor(tile * factors[:, first + j : first + j + 1] + 0.5)
        codes.append(jnp.clip(scaled, -limit, limit).astype(jnp.int32) + (1 << CODE_BITS))
    a, b, c = codes
    return a | (c & 0x7FF) << 21, b | (c >> 11) << 21


def decoded(words, scales, first):
    a, b = (word & 0x1FFFFF for word in words)
    c = lax.shift_right_logical(words[0], 21) | (lax.shift_right_logical(words[1], 21) << 11)
    tiles = []
    for j, code in enumerate((a, b, c)):
        tiles.append((code - (1 << CODE_BITS)).astype(jnp.float32) * scales[:, first + j : first + j + 1])
    return tiles


def scales_of(exponents):
    return power_of_two(exponents - CODE_BITS)


def piece_rows(piece, scales, number, z):
    at = 2 * (z - PIECES[number])
    if not 0 <= at < piece.shape[0]:
        return 0.0
    return jnp.concatenate(decoded((piece[at], piece[at + 1]), scales, 3 * (z - 1)))


def pair_at(ids, half, number, planes):
    unit = number % (3 * planes)
    part = 2 if number < 3 * planes else 0
    return part, unit // planes, unit % planes, units_of(ids, half)[unit // planes]


def pair_tile(ids, coef, half, number):
    part, _, z, place = pair_at(ids, half, number, coef.shape[2])
    return coef_unit(coef, part, place, z) + SHIFT * coef_unit(coef, part + 1, place, z)


def rim_at(planes, unit_rows):
    planes_at = ROWS_AT + 3 * (planes // unit_rows)
    outer_at = planes_at + 3 + planes // unit_rows
    return planes_at, planes_at + 3, outer_at, outer_at + 2 + 2 * (planes // unit_rows)


def beyond(fields, coef, ids, half, pairs, strip_out, row_out):
    planes = fields.shape[2]
    if pairs > 1:
        return
    for j, item in enumerate((0, 3)):
        strip_out(j, *outer_strips(fields, coef, item, ids, half, planes))
    (above,) = units_of(ids, half, (3,))
    for z in range(planes):
        row_out(0, z, outer_row(fields, ids, half, z))
        row_out(1, z, jnp.where(above[0], first_row(coef, above, z), 0.0))


def first_row(coef, place, z):
    rows = coef.shape[3] // 2
    both = coef[2, place[1], z].astype(jnp.float32)
    return jnp.where(place[2] == 0, both[0:1], both[rows : rows + 1])


def edge_kernel(pairs, ids_in, fields_in, coef_in, fields, coef, out, ids, sems):
    copies = [pltpu.make_async_copy(ids_in, ids, sems.at[0])]
    for item in range(2):
        for slot in range(2):
            at = len(copies)
            copies.append(pltpu.make_async_copy(fields_in.at[item, slot], fields.at[item, slot], sems.at[at]))
    for part in range(4):
        at = len(copies)
        copies.append(pltpu.make_async_copy(coef_in.at[part], coef.at[part], sems.at[at]))
    for copy in copies:
        copy.start()
    planes, unit_rows = fields.shape[2], fields.shape[3] // 2
    half = 1 - lax.axis_index("gy") % 2
    for copy in copies[:5]:
        copy.wait()
    for item in range(4):
        if item == 2:
            for copy in copies[5:]:
                copy.wait()
        for k, place in enumerate(units_of(ids, half)):
            low, high = strips(fields, coef, item, place, planes)
            out[3 * item + k] = jnp.concatenate([low, high], axis=1)
            if item < 2:
                out[PLANES_AT + 3 * item + k] = field_unit(fields, 0, place, item * (planes - 1))
    for j, place in enumerate(brick_rows(ids, half, unit_rows)):
        for z in range(planes):
            at = ROWS_AT + j * (planes // unit_rows) + z // unit_rows
            line = z % unit_rows
            out[at, line : line + 1] = field_row(fields, place, z)
    faces_at, lines_at, beyond_at, pairs_at = rim_at(planes, unit_rows)

    def strip_out(j, low, high):
        out[beyond_at + j] = jnp.concatenate([low, high], axis=1)

    def row_out(j, z, value):
        line = z % unit_rows
        out[beyond_at + 2 + j * (planes // unit_rows) + z // unit_rows, line : line + 1] = value

    beyond(fields, coef, ids, half, pairs, strip_out, row_out)
    places = units_of(ids, half)
    for k, place in enumerate(places):
        out[faces_at + k] = coef_unit(coef, 3, place, 0)
    for z in range(planes):
        line = z % unit_rows
        out[lines_at + z // unit_rows, line : line + 1] = first_row(coef, places[0], z)
    for number in range(FIRST_PAIRS):
        out[pairs_at + number] = pair_tile(ids, coef, half, number)


def coef_kernel(first, ids, coef, _, out):
    for number in range(out.shape[0]):
        out[number] = pair_tile(ids, coef, 1 - lax.axis_index("gy") % 2, first + number)


def outer_at(planes):
    return 6 * planes - FIRST_PAIRS - NEXT_PAIRS


def line_at(planes, unit_rows, edge, z):
    at = outer_at(planes) + 6 + edge * (planes // unit_rows) + z // unit_rows
    return at, slice(z % unit_rows, z % unit_rows + 1)


def partial_kernel(ids, fields, coef, _, out, middle, own, start_own, *refs):
    start_out, partial = refs[:-1], refs[-1]
    _, slots, planes, rows, columns = fields.shape
    lane, row = lane_of((rows, columns)), row_of((rows, columns))
    for slot in range(slots):
        value, lower = fields[0, slot, 0], 0.0
        for z in range(planes):
            alpha, beta_x, beta_y = (coef[part, slot, z].astype(jnp.float32) for part in range(3))
            flux_x = jnp.where(lane == 0, 0.0, beta_x * (value - pltpu.roll(value, 1, 1)))
            flux_y = jnp.where(row == 0, 0.0, beta_y * (value - pltpu.roll(value, 1, 0)))
            image = (
                alpha * value
                + (flux_x - pltpu.roll(flux_x, columns - 1, 1))
                + (flux_y - pltpu.roll(flux_y, rows - 1, 0))
                + lower
            )
            if z + 1 < planes:
                following = fields[0, slot, z + 1]
                lower = coef[3, slot, z + 1].astype(jnp.float32) * (following - value)
                image = image - lower
                value = following
            partial[slot, z] = fields[1, slot, z] - image
    half_rows = rows // 2
    half = lax.axis_index("gy") % 2
    for number in range(outer_at(planes)):
        out[number] = pair_tile(ids, coef, 1 - half, FIRST_PAIRS + NEXT_PAIRS + number)
    places = units_of(ids, half)
    for z in range(planes):
        for k, place in enumerate(places):
            held, slot, part = place
            at = pl.ds(pl.multiple_of(part * half_rows, half_rows), half_rows)
            line = slice(k * half_rows, (k + 1) * half_rows)
            own[z, line] = jnp.where(held, partial[slot, z, at, :], 0.0)
            start_own[z, line] = jnp.where(held, field_unit(fields, 0, place, z), 0.0)
    lane = lane_of((half_rows, columns))
    places = units_of(ids, 1 - half)
    tops = jnp.zeros((half_rows, columns), jnp.float32)
    shares = []
    for z in range(planes):
        lefts, starts = [], []
        for k, place in enumerate(places):
            held, slot, part = place
            at = pl.ds(pl.multiple_of(part * half_rows, half_rows), half_rows)
            lefts.append(jnp.where(held, partial[slot, z, at, :], 0.0))
            starts.append(jnp.where(held, field_unit(fields, 0, place, z), 0.0))
            if k != 1:
                row = 0 if k == 0 else half_rows - 1
                at_line, line_in = line_at(planes, half_rows, k // 2, z)
                out[at_line, line_in] = lefts[k][row : row + 1]
            if z % (planes - 1) == 0:
                out[outer_at(planes) + 3 * (z > 0) + k] = lefts[k]
        if z % (planes - 1) == 0:
            continue
        piece = sum(z >= end for end in PIECES[1:])
        shares.append((lefts, 3 * (z - 1), middle, 2 * (z - 1)))
        shares.append((starts, LANES + 3 * (z - 1), start_out[piece], 2 * (z - PIECES[piece])))
        for tiles, first, _, _ in shares[-2:]:
            for j, tile in enumerate(tiles):
                tops = jnp.where(lane == first + j, jnp.max(jnp.abs(tile), axis=1, keepdims=True), tops)
    exponents = exponents_of(tops)
    factors = power_of_two(CODE_BITS - exponents)
    for tiles, first, target, at in shares:
        target[at], target[at + 1] = encoded(tiles, factors, first)
    middle[2 * (planes - 2)] = exponents


def strip_kernel(pairs, ids, fields, coef, edge_in, left, right, outer_rows):
    planes, unit_rows = fields.shape[2], fields.shape[3] // 2
    half = lax.axis_index("gy") % 2
    for k, place in enumerate(units_of(ids, half)):
        for item in range(4):
            low, high = strips(fields, coef, item, place, planes)
            got = edge_in[3 * item + k]
            left[3 * item + k] = jnp.where(place[0], low, got[:, :LANES])
            right[3 * item + k] = jnp.where(place[0], high, got[:, LANES:])
    beyond_at = rim_at(planes, unit_rows)[2]

    def strip_out(j, low, high):
        got = edge_in[beyond_at + j]
        left[12 + j], right[12 + j] = low + got[:, :LANES], high + got[:, LANES:]

    def row_out(j, z, value):
        line = z % unit_rows
        got = edge_in[beyond_at + 2 + j * (planes // unit_rows) + z // unit_rows, line : line + 1]
        outer_rows[j, z : z + 1] = value + got

    if pairs > 1:
        outer_rows[...] = jnp.zeros_like(outer_rows)
        left[12:14] = jnp.zeros_like(left[12:14])
        right[12:14] = jnp.zeros_like(right[12:14])
    beyond(fields, coef, ids, half, pairs, strip_out, row_out)


def parted(both):
    second = jnp.floor(both * 0.125) * (8.0 / SHIFT)
    return both - SHIFT * second, second


def ghost_columns(from_left, from_right, item, k, z):
    low, high = from_left[3 * item + k], from_right[3 * item + k]
    turn = (LANES - STRIP * z) % LANES
    right = pltpu.roll(high, turn, 1) if turn else high
    turn = (LANES - STRIP - STRIP * z) % LANES
    left = pltpu.roll(low, turn, 1) if turn else low
    return jnp.where(lane_of(low.shape) < LANES // 2, right, left)


def gather_kernel(
    pairs, ids, fields, coef, edge_in, left, right, outer_rows, from_left, from_right,
    edge_start, rhs_ghost, ghosts, own_rows, up, down, rows_out, beyond_rows,
):
    _, _, planes, rows, columns = fields.shape
    rows //= 2
    half = lax.axis_index("gy") % 2
    for k, place in enumerate(units_of(ids, half)):
        at = slice(k * rows, (k + 1) * rows)
        for z in range(planes):
            edge_start[z, at, :LANES] = ghost_columns(right, left, 0, k, z)
            edge_start[z, at, LANES:] = ghost_columns(from_left, from_right, 0, k, z)
            rhs_ghost[z, at] = ghost_columns(from_left, from_right, 1, k, z)
            for item in (2, 3):
                both = ghost_columns(from_left, from_right, item, k, z)
                part = 2 * item - 4
                ghosts[part, z, at], ghosts[part + 1, z, at] = parted(both)
        for e, (z, out) in enumerate(((0, down.at[0]), (planes - 1, up))):
            own = field_unit(fields, 0, place, z)
            out[at, :columns] = jnp.where(place[0], own, edge_in[PLANES_AT + 3 * e + k])
            out[at, columns:] = edge_start[z, at, LANES:]
    faces_at, lines_at, _, _ = rim_at(planes, rows)
    places = units_of(ids, half)
    for k, place in enumerate(places):
        at = slice(k * rows, (k + 1) * rows)
        down[1, at, :columns] = jnp.where(place[0], coef_unit(coef, 3, place, 0), edge_in[faces_at + k])
    down[1, :, columns:] = ghosts[3, 0]
    for j, place in enumerate(brick_rows(ids, half, rows)):
        for z in range(planes):
            at = ROWS_AT + j * (planes // rows) + z // rows
            line = z % rows
            own_rows[j, z : z + 1] = jnp.where(place[0], field_row(fields, place, z), edge_in[at, line : line + 1])
    last = 3 * rows - 1
    for z in range(planes):
        line = slice(z, z + 1)
        for out, row, j, known in ((0, last, 2, half == 1), (1, 0, 0, half == 0)):
            edge = edge_start[z, row : row + 1]
            middle = jnp.concatenate([edge[:, :LANES]] * (columns // LANES), axis=1)
            rows_out[out, line, :columns] = jnp.where(known, own_rows[j, line], middle)
            rows_out[out, line, columns:] = edge[:, LANES:]
        got = edge_in[lines_at + z // rows, z % rows : z % rows + 1]
        rows_out[2, line, :columns] = jnp.where(places[0][0], first_row(coef, places[0], z), got)
        rows_out[2, line, columns:] = ghosts[2, z, 0:1]
        if pairs > 1:
            continue
        own = ghost_columns(right, left, 4, 0, z)
        ghost = ghost_columns(from_left, from_right, 4, 0, z)
        for out, row, known in ((0, rows - 1, half == 0), (1, 0, half == 1)):
            edge = own[row : row + 1]
            middle = jnp.concatenate([edge] * (columns // LANES), axis=1)
            beyond_rows[out, line, :columns] = jnp.where(known, outer_rows[0, line], middle)
            beyond_rows[out, line, columns:] = ghost[row : row + 1]
        beyond_rows[2, line, :columns] = outer_rows[1, line]
        beyond_rows[2, line, columns:] = parted(ghost_columns(from_left, from_right, 4, 1, z)[0:1])[0]
    if pairs > 1:
        beyond_rows[...] = jnp.zeros_like(beyond_rows)


def spread_kernel(ids, coef, edge_in, pairs, more_pairs, ghosts, wide_ax, wide_yz):
    planes, columns, rows = coef.shape[2], coef.shape[4], coef.shape[3] // 2
    pairs_at = rim_at(planes, rows)[3]
    for part in (0, 1):
        wide_ax[part, :, :, columns:] = ghosts[part]
        wide_yz[part, :, :, columns:] = ghosts[2 + part]
    for number in range(6 * planes):
        part, k, z, place = pair_at(ids, lax.axis_index("gy") % 2, number, planes)
        at = slice(k * rows, (k + 1) * rows)
        place_in = number - FIRST_PAIRS
        if place_in < 0:
            got = edge_in[pairs_at + number]
        elif place_in < pairs.shape[0]:
            got = pairs[place_in]
        else:
            got = more_pairs[place_in - pairs.shape[0]]
        for j, value in enumerate(parted(got)):
            out = wide_yz if part else wide_ax
            out[j, z, at, :columns] = jnp.where(place[0], coef_unit(coef, part + j, place, z), value)


def image_plane(value, lower_flux, upper_flux, alpha, beta_x, beta_y, rim_row):
    rows, width = value.shape
    flux_x = beta_x * (value - pltpu.roll(value, 1, 1))
    row = row_of(value.shape)
    before = jnp.where(row == 0, 0.0, pltpu.roll(value, 1, 0))
    flux_y = beta_y * (value - before)
    top = 0.0 if rim_row is None else -rim_row * value[rows - 1 : rows]
    after = jnp.where(row == rows - 1, top, pltpu.roll(flux_y, rows - 1, 0))
    return (
        alpha * value
        + (flux_x - pltpu.roll(flux_x, width - 1, 1))
        + (flux_y - after)
        + (lower_flux - upper_flux)
    )


def images(plane, coef, planes, rim_face, rim_row):
    (value, *others), beta_z = plane(0), coef(3, 0)
    lower = beta_z * value
    for z in range(planes):
        if z + 1 < planes:
            (following, *next_others), next_z = plane(z + 1), coef(3, z + 1)
            upper = next_z * (following - value)
        else:
            following, next_others, next_z = None, None, rim_face
            upper = 0.0 if rim_face is None else -rim_face * value
        image = image_plane(value, lower, upper, coef(0, z), coef(1, z), coef(2, z), rim_row(z))
        yield z, (value, *others), image
        value, others, lower, beta_z = following, next_others, upper, next_z


def edges(value):
    columns = value.shape[1] - LANES
    own = jnp.where(lane_of((value.shape[0], LANES)) < LANES // 2, value[:, :LANES], value[:, columns - LANES : columns])
    return jnp.concatenate([own, value[:, columns:]], axis=1)


def first_kernel(
    wide_ax, wide_yz, edge_start, rhs_ghost, own_rows, down, partial, extra, inverse
):
    planes, rows, width = extra.shape
    columns = width - LANES
    unit_rows = rows // 3
    even = lax.axis_index("gy") % 2 == 0

    def coef(part, z):
        return wide_ax[part, z] if part < 2 else wide_yz[part - 2, z]

    def ring(part, z):
        return edges(coef(part, z))

    lane, row = lane_of((rows, columns)), row_of((rows, columns))
    inner = jnp.where(even, 2 * unit_rows, unit_rows)
    for z, (value,), image in images(
        lambda z: (edge_start[z],),
        ring,
        planes,
        None,
        lambda z: None,
    ):
        flux = ring(1, z) * (value - pltpu.roll(value, 1, 1))
        gain = jnp.where(lane == 0, -flux[:, :columns], 0.0)
        far = jnp.where(lane == columns - 1, pltpu.roll(flux, LANES - 1, 1)[:, :columns], 0.0)
        gain = gain + far
        if z == 0:
            gain = gain - (wide_yz[1, 0] * down[0])[:, :columns]
        beta_y = wide_yz[0, z]
        at = slice(z, z + 1)
        between = jnp.where(even, own_rows[2, at] - own_rows[1, at], own_rows[1, at] - own_rows[0, at])
        beta = jnp.where(even, beta_y[2 * unit_rows : 2 * unit_rows + 1], beta_y[unit_rows : unit_rows + 1])
        between = beta[:, :columns] * between
        gain = gain + jnp.where(row == inner, -between, jnp.where(row == inner - 1, between, 0.0))
        low = jnp.where(even, beta_y[0:1, :columns] * own_rows[0, at], 0.0)
        gain = gain - jnp.where(row == 0, low, 0.0)
        extra[z, :, :columns] = gain + partial[z]
        extra[z, :, columns:] = rhs_ghost[z] - image[:, LANES:]
        beta_x, beta_z = wide_ax[1, z], wide_yz[1, z]
        next_z = wide_yz[1, z + 1] if z + 1 < planes else 0.0
        next_y = jnp.where(row_of((rows, width)) == rows - 1, 0.0, pltpu.roll(beta_y, rows - 1, 0))
        next_x = pltpu.roll(beta_x, width - 1, 1)
        inverse[z] = 1.0 / (wide_ax[0, z] + beta_x + next_x + beta_y + next_y + beta_z + next_z)


def start_rows(
    z, line, known, extra, part_inverse, wide_yz, own_up, own_last, low_face, high_face, ghost_rows
):
    planes, rows, width = extra.shape
    columns = known.shape[1]
    even = lax.axis_index("gy") % 2 == 0
    row = row_of((known.shape[0], width)) + line.start
    ghost = lane_of((1, width)) >= columns
    at = slice(z, z + 1)
    left = extra[z, line] + jnp.concatenate([known, jnp.zeros((known.shape[0], width - columns), jnp.float32)], axis=1)
    factor = part_inverse[z, line]
    if z == 0:
        left = left + wide_yz[1, 0, line] * low_face[line]
    if z == planes - 1:
        rim = high_face[1, line]
        left = left + rim * (high_face[0, line] - own_up[line])
        factor = factor / (1.0 + rim * factor)
    if line.start == 0:
        low = jnp.where(jnp.logical_or(ghost, even), wide_yz[0, z, 0:1] * ghost_rows[0, at], 0.0)
        left = left + jnp.where(row == 0, low, 0.0)
    if line.stop == rows:
        rim = ghost_rows[2, at]
        high = rim * (ghost_rows[1, at] - own_last[0, at])
        high = jnp.where(jnp.logical_and(jnp.logical_not(ghost), even), 0.0, high)
        left = left + jnp.where(row == rows - 1, high, 0.0)
        last = factor[factor.shape[0] - 1 :]
        factor = jnp.where(row == rows - 1, last / (1.0 + rim * last), factor)
    return left, factor


def partner_plane(z, planes, outer, middle=None, scales=None):
    if 0 < z < planes - 1:
        return jnp.concatenate(decoded((middle[2 * z - 2], middle[2 * z - 1]), scales, 3 * (z - 1)))
    return jnp.concatenate([outer[outer_at(planes) + 3 * (z > 0) + k] for k in range(3)])


def start_faces_kernel(second, outer, *refs):
    rest, (up, down, rows_out) = refs[:-3], refs[-3:]
    planes, rows, _ = rest[0].shape

    def step(z, line, known):
        left, factor = start_rows(z, line, known, *rest)
        return second * (factor * left)

    down[0] = step(0, slice(0, rows), partner_plane(0, planes, outer))
    up[...] = step(planes - 1, slice(0, rows), partner_plane(planes - 1, planes, outer))
    for z in range(planes):
        at = slice(z, z + 1)
        if z == 0:
            first, last = down[0, 0:1], down[0, rows - 1 : rows]
        elif z == planes - 1:
            first, last = up[0:1], up[rows - 1 : rows]
        else:
            lines = [outer[line_at(planes, outer.shape[1], edge, z)] for edge in range(2)]
            first, last = step(z, slice(0, 1), lines[0]), step(z, slice(rows - 1, rows), lines[1])
        rows_out[0, at], rows_out[1, at] = last, first


def start_kernel(second, outer, middle, start, *refs):
    own_down, *rest, inverse, residual, direction, total, start_scales = refs
    own_up = rest[3]
    planes, rows, _ = rest[0].shape
    columns = total.shape[2]
    scales = scales_of(middle[2 * (planes - 2)])
    start_scales[...] = scales[:, LANES:]
    for z in range(planes):
        known = partner_plane(z, planes, outer, middle, scales)
        left, factor = start_rows(z, slice(0, rows), known, *rest)
        step = second * (factor * left)
        inverse[z] = factor
        residual[z] = left
        direction[z] = step
        known = {0: own_down, planes - 1: own_up}.get(z)
        total[z] = (start[z] if known is None else known[:, :columns]) + step[:, :columns]


def halo_flux(z, wide_yz, rim_face, rim_rows, low_face, high_face, ghost_rows):
    _, planes, rows, width = wide_yz.shape
    at, row = slice(z, z + 1), row_of((rows, width))
    top = jnp.where(row == rows - 1, rim_rows[2, at] * ghost_rows[1, at], 0.0)
    flux = jnp.where(row == 0, wide_yz[0, z, 0:1] * ghost_rows[0, at], top)
    if z == 0:
        flux = flux + wide_yz[1, 0] * low_face[...]
    if z == planes - 1:
        flux = flux + rim_face[1] * high_face[0]
    return flux


def piecewise(source, target, sems):
    planes, pieces = source.shape[0], sems.shape[0]
    depth = planes // pieces
    copies = []
    for z in range(planes):
        if z % depth == depth - 1:
            at = pl.ds(z + 1 - depth, depth)
            copies.append(pltpu.make_async_copy(source.at[at], target.at[at], sems.at[z // depth]))
            copies[-1].start()
        yield
    for copy in copies:
        copy.wait()


def inner_kernel(weights, stage, wide_ax, wide_yz, rim_face, rim_rows, field, old, inverse, sum_in, *refs):
    before, first, second = weights
    rims = rim_face, rim_rows
    halo = refs[:3]
    if second:
        residual, direction, total = refs[-3:]
    else:
        residual, total = refs[-2:]
    planes, rows, columns = total.shape

    def plane(z):
        if not before:
            return field[z], old[z], sum_in[z]
        flux = halo_flux(z, wide_yz, *rims, *halo)
        step = before * (inverse[z] * flux)
        done = sum_in[z] + step[:, :columns]
        for place, number in enumerate(pieces_at(stage)):
            done = done + piece_rows(refs[4 + place], refs[3], number, z)
        return field[z] + step, old[z] + flux, done

    def coef(part, z):
        return wide_ax[part, z] if part < 2 else wide_yz[part - 2, z]

    for z, (value, left, done), image in images(
        plane, coef, planes, rim_face[1], lambda z: rim_rows[2, z : z + 1]
    ):
        left = left - image
        if second:
            step = first * value + second * (inverse[z] * left)
            residual[z] = left
            direction[z] = step
            total[z] = done + step[:, :columns]
        else:
            residual[z] = left[:, :columns]
            total[z] = done


def faces_kernel(second, wide_yz, rim_face, rim_rows, low_face, high_face, ghost_rows, inverse, direction, up, down, rows_out):
    halo = wide_yz, rim_face, rim_rows, low_face, high_face, ghost_rows
    planes, rows, _ = direction.shape
    for z, out in ((0, down.at[0]), (planes - 1, up)):
        out[...] = direction[z] + second * (inverse[z] * halo_flux(z, *halo))
    for z in range(planes):
        at = slice(z, z + 1)
        for edge, row, out in ((0, 0, 1), (1, rows - 1, 0)):
            line = slice(row, row + 1)
            if z == 0:
                rows_out[out, at] = down[0, line]
            elif z == planes - 1:
                rows_out[out, at] = up[line]
            else:
                beta = rim_rows[2, at] if edge else wide_yz[0, z, line]
                flux = beta * ghost_rows[edge, at]
                rows_out[out, at] = direction[z, line] + second * (inverse[z, line] * flux)


def last_kernel(wide_yz, rim_face, rim_rows, low_face, high_face, ghost_rows, partial, total, *refs):
    total_out, residual_out, whole, residual, total_sems, residual_sems = refs[-6:]
    planes, rows, columns = residual.shape
    copies = piecewise(whole, total_out, total_sems)
    for z in range(planes):
        done = total[z]
        for place, number in enumerate(pieces_at(SWEEPS + 1)):
            done = done + piece_rows(refs[1 + place], refs[0], number, z)
        whole[z] = done
        next(copies)
    more = piecewise(residual, residual_out, residual_sems)
    for z in range(planes):
        flux = halo_flux(z, wide_yz, rim_face, rim_rows, low_face, high_face, ghost_rows)
        residual[z] = partial[z] + flux[:, :columns]
        next(more)
    list(copies)
    list(more)


def local(old_fields, old_coef, held_slabs):
    _, slots, planes, rows, columns = old_fields.shape
    half = rows // 2
    rows = 3 * half
    width = columns + LANES
    full, own = f32(planes, rows, width), f32(planes, rows, columns)
    ids = held_slabs.reshape(2)
    vmem = pl.BlockSpec(memory_space=pltpu.VMEM)
    pairs = lax.axis_size("gy") // 2
    fields, coef, edge_out = pl.pallas_call(
        functools.partial(edge_kernel, pairs),
        out_shape=[
            f32(*old_fields.shape),
            jax.ShapeDtypeStruct(old_coef.shape, old_coef.dtype),
            f32(rim_at(planes, half)[3] + FIRST_PAIRS, half, columns),
        ],
        in_specs=[pl.BlockSpec(memory_space=pltpu.HBM)] * 3,
        out_specs=[vmem] * 3,
        scratch_shapes=[pltpu.SMEM((2,), jnp.int32), pltpu.SemaphoreType.DMA((9,))],
        compiler_params=pltpu.CompilerParams(vmem_limit_bytes=VMEM_LIMIT),
    )(*(pltpu.with_memory_space_constraint(array, pltpu.HBM) for array in (ids, old_fields, old_coef)))
    edge_in = swapped(edge_out)
    (pairs_out,) = call(
        functools.partial(coef_kernel, FIRST_PAIRS), [f32(NEXT_PAIRS, half, columns)], ids, coef, edge_out, ids=True
    )
    pairs_in = swapped(pairs_out)
    outer_out, middle, partial, start_own, *start_out, _ = call(
        partial_kernel,
        [
            f32(outer_at(planes) + 6 + 2 * (planes // half), half, columns),
            jax.ShapeDtypeStruct((2 * (planes - 2) + 1, half, columns), jnp.int32),
            own,
            own,
            *(
                jax.ShapeDtypeStruct((2 * (end - start), half, columns), jnp.int32)
                for start, end in zip(PIECES, PIECES[1:])
            ),
            f32(slots, planes, 2 * half, columns),
        ],
        ids,
        fields,
        coef,
        pairs_out,
        ids=True,
    )
    outer_in, middle_in = swapped(outer_out), swapped(middle)
    strip = f32(14, half, LANES)
    left, right, outer_rows = call(
        functools.partial(strip_kernel, pairs),
        [strip, strip, f32(2, planes, columns)],
        ids,
        fields,
        coef,
        edge_in,
        ids=True,
    )
    from_left, from_right = shifted(right, "gx", 1), shifted(left, "gx", -1)
    coef_full = f32(2, planes, rows, width)
    edge_start, rhs_ghost, ghosts, own_rows, up, down, rows_out, rim_rows = call(
        functools.partial(gather_kernel, pairs),
        [
            f32(planes, rows, 2 * LANES),
            f32(planes, rows, LANES),
            f32(4, planes, rows, LANES),
            f32(3, planes, columns),
            f32(rows, width),
            f32(2, rows, width),
            f32(3, planes, width),
            f32(3, planes, width),
        ],
        ids,
        fields,
        coef,
        edge_in,
        left,
        right,
        outer_rows,
        from_left,
        from_right,
        ids=True,
    )
    low_face, rim_face = shifted(up, "gz", 1), shifted(down, "gz", -1)
    if pairs > 1:
        rim_rows = row_ghosts(rows_out)
    wide_ax, wide_yz = call(
        spread_kernel, [coef_full, coef_full], ids, coef, edge_in, pairs_in, outer_in, ghosts, ids=True
    )
    extra, part_inverse = call(
        first_kernel, [full, full], wide_ax, wide_yz, edge_start, rhs_ghost, own_rows, down, partial
    )
    first_list, second_list = chebyshev_weights(SWEEPS)
    faces = [f32(rows, width), f32(1, rows, width), f32(2, planes, width)]
    down_start = down[0]
    rest = extra, part_inverse, wide_yz, up, rows_out, low_face, rim_face, rim_rows
    up, down, rows_out = call(functools.partial(start_faces_kernel, second_list[0]), faces, outer_in, *rest)
    inverse, residual, direction, total, scales = call(
        functools.partial(start_kernel, second_list[0]), [full, full, full, own, f32(half, LANES)], outer_in, middle_in, start_own, down_start, *rest
    )
    rims, halo, pieces = (rim_face, rim_rows), (), [swapped(units) for units in start_out]
    for stage in range(1, SWEEPS + 1):
        before = second_list[stage - 1] if halo else 0.0
        last = stage == SWEEPS
        weights = (before, 0.0, 0.0) if last else (before, first_list[stage], second_list[stage])
        arrived = (*halo, scales, *(pieces[number] for number in pieces_at(stage))) if halo else ()
        halo = shifted(up, "gz", 1), shifted(down, "gz", -1), row_ghosts(rows_out)
        residual, *state = call(
            functools.partial(inner_kernel, weights, stage),
            [own, own] if last else [full, full, own],
            wide_ax,
            wide_yz,
            *rims,
            direction,
            residual,
            inverse,
            total,
            *arrived,
        )
        if last:
            more = (pieces[number] for number in pieces_at(SWEEPS + 1))
            return tuple(call(last_kernel, [own, own], wide_yz, *rims, *halo, residual, *state, scales, *more, sent=True))
        direction, total = state
        up, down, rows_out = call(
            functools.partial(faces_kernel, second_list[stage]), faces, wide_yz, *rims, *halo, inverse, direction
        )


def solution(mesh):
    in_specs = (
        P(None, "gy", "gz", None, "gx"),
        P(None, "gy", "gz", None, "gx"),
        P("gy", "gz", "gx"),
    )
    out_specs = (P("gz", "gy", "gx"), P("gz", "gy", "gx"))
    return jax.shard_map(local, mesh=mesh, in_specs=in_specs, out_specs=out_specs, check_vma=False)
```

time: 61.9 us -> 57.7 us (0.932)
  waiting for transfers between devices: 19 us -> 13.6 us
  starting transfers between devices: 24.5 us -> 25.5 us
  Pallas kernels: 16.9 us -> 17.7 us
  local copies, waits for them, and re-layouts: 0.65 us -> 0.01 us
    ppermute x11 -> x10, waiting for transfers between devices: 9.68 us -> 4.94 us  [swapped(): lax.ppermute(value, 'gy', [(i, i ^ 1) for i in range(lax.axis_size('gy'))])]
    pallas_call x16 -> x17, Pallas kernels: 16.9 us -> 17.7 us  [the longest x16 15.6 us: call(): pl.pallas_call(kernel, out_shape=outs, in_specs=specs, out_specs=out_spec...]
    ppermute x12, starting transfers between devices: 16.2 us -> 17 us  [shifted(): lax.ppermute(value, axis, [(i, (i + steps) % count) for i in range(count)])]
    unnamed x4 -> x2, local copies, waits for them, and re-layouts: 0.65 us -> 0.01 us
    ppermute x12, waiting for transfers between devices: 9.28 us -> 8.63 us  [shifted(): lax.ppermute(value, axis, [(i, (i + steps) % count) for i in range(count)])]
    ppermute x11 -> x10, starting transfers between devices: 8.26 us -> 8.53 us  [swapped(): lax.ppermute(value, 'gy', [(i, i ^ 1) for i in range(lax.axis_size('gy'))])]
  transfers between devices with their start and end apart: 23 -> 22, of which waited for: 9 -> 7; matrix products, arithmetic and copies ran while one was open for 0% -> 0% of each run, Pallas kernels for 22% -> 25%
where the time goes in v4:
time: 57.7 us; the launch traced here: 57.5 us
  starting transfers between devices  25.5 us (44%)
  Pallas kernels  17.7 us (31%)
  waiting for transfers between devices  13.6 us (24%)
  between operations  0.79 us (1%)
    ppermute x12, starting transfers between devices, shifted(): lax.ppermute(value, axis, [(i, (i + steps) % count) for i in range(count)])  17 us
    pallas_call x16, Pallas kernels, call(): pl.pallas_call(kernel, out_shape=outs, in_specs=specs, out_specs=out_spec...  15.6 us
    ppermute x12, waiting for transfers between devices, shifted(): lax.ppermute(value, axis, [(i, (i + steps) % count) for i in range(count)])  8.63 us
    ppermute x10, starting transfers between devices, swapped(): lax.ppermute(value, 'gy', [(i, i ^ 1) for i in range(lax.axis_size('gy'))])  8.53 us
    ppermute x10, waiting for transfers between devices, swapped(): lax.ppermute(value, 'gy', [(i, i ^ 1) for i in range(lax.axis_size('gy'))])  4.94 us
    pallas_call x1, Pallas kernels, local(): pl.pallas_call(functools.partial(edge_kernel, pairs), out_shape=[f32(*old...  2.08 us
  transfers between devices with their start and end apart: 22, of which 7 were waited for; matrix products, arithmetic and copies ran while one was open for 0% of the time, Pallas kernels for 25%

profile of v4, /device:TPU:1, one launch (start us, length us, event | category | flops | bytes accessed | tf_op | source)
XLA Modules:
  0.0 57.5 jit_solution(8015525344748678709)
XLA Ops:
  0.6 2.1 %shard_map.50 = (f32[2,2,16,16,256]{4,3,2,1,0:T(8,128)S(1)}, bf16[4,2,16,16,256]{4,3,2,1,0:T(8,128)(2,1)S(1)}, f32[51,8,256]{2,1,0:T(8,128)S(1)}) custom-call(s32[2]{0:T(128)} %bitcast.3, f32[2,2,16,16,256]{4,3,2,1,0:T(8,128)} %fields_in.1, bf16[4,2,16,16,256]{4,3,2,1,0:T(8,128)(2,1)} %coef_in.1), custom_call_target="tpu_custom_call" | custom-call | tf_op jit(solution)/shard_map/pallas_call | solution.py:761
  2.7 2.1 %collective-permute-start = (f32[51,8,256]{2,1,0:T(8,128)S(1)}, f32[51,8,256]{2,1,0:T(8,128)S(1)}, u32[]{:S(2)}, u32[]{:S(2)}) collective-permute-start(f32[51,8,256]{2,1,0:T(8,128)S(1)} %get-tuple-element.55._), channel_id=1, source_target_pairs={{0,4},{4,0},{1,5},{5,1},{2,6},{6,2},{3,7},{7,3},{8,12},{12,8},{9,1... | collective-permute-start | bytes 1253384 | tf_op jit(solution)/shard_map/ppermute | solution.py:40
  4.8 0.7 %shard_map.51._ = f32[45,8,256]{2,1,0:T(8,128)S(1)} custom-call(s32[2]{0:T(128)S(1)} %bitcast.4, bf16[4,2,16,16,256]{4,3,2,1,0:T(8,128)(2,1)S(1)} %get-tuple-element.54.coef, f32[51,8,256]{2,1,0:T(8,128)S(1)} %get-tuple-element.55._), custom_call_target="tpu_custom_call" | custom-call | tf_op jit(solution)/shard_map/pallas_call | solution.py:62
  5.6 3.9 %shard_map.52 = (f32[45,8,256]{2,1,0:T(8,128)S(1)}, s32[29,8,256]{2,1,0:T(8,128)S(1)}, f32[16,24,256]{2,1,0:T(8,128)S(1)}, f32[16,24,256]{2,1,0:T(8,128)S(1)}, s...) custom-call(s32[2]{0:T(128)S(1)} %bitcast.5, ...), custom_call_target="tpu_custom_call" | custom-call | tf_op jit(solution)/shard_map/pallas_call | solution.py:62
  9.5 1.4 %collective-permute-start.2 = (f32[45,8,256]{2,1,0:T(8,128)S(1)}, f32[45,8,256]{2,1,0:T(8,128)S(1)}, u32[]{:S(2)}, u32[]{:S(2)}) collective-permute-start(f32[45,8,256]{2,1,0:T(8,128)S(1)} %get-tuple-element.57), channel_id=1, source_target_pairs={{0,4},{4,0},{1,5},{5,1},{2,6},{6,2},{3,7},{7,3},{8,12},{12,8},{9,1... | collective-permute-start | bytes 1105928 | tf_op jit(solution)/shard_map/ppermute | solution.py:40
  10.9 3.3 %collective-permute-done.edge_in = f32[51,8,256]{2,1,0:T(8,128)S(1)} collective-permute-done((f32[51,8,256]{2,1,0:T(8,128)S(1)}, f32[51,8,256]{2,1,0:T(8,128)S(1)}, u32[]{:S(2)}, u32[]{:S(2)}) %collective-permute-start) | collective-permute-done | bytes 417824 | tf_op jit(solution)/shard_map/ppermute | solution.py:40
  14.2 1.2 %shard_map.53 = (f32[14,8,128]{2,1,0:T(8,128)S(1)}, f32[14,8,128]{2,1,0:T(8,128)S(1)}, f32[2,16,256]{2,1,0:T(8,128)S(1)}) custom-call(s32[2]{0:T(128)S(1)} %bitcast.6, f32[2,2,16,16,256]{4,3,2,1,0:T(8,128)S(1)} %get-tuple-element.56.fields, bf16[4,2,16,16,256]{4,3,2,1,0:T(8,128)(2,1)S(1)} %get-tuple-element.54.coef, ...), custom_call_target="tpu_custom_call" | custom-call | tf_op jit(solution)/shard_map/pallas_call | solution.py:62
  15.4 1.3 %collective-permute-start.3 = (f32[14,8,128]{2,1,0:T(8,128)S(1)}, f32[14,8,128]{2,1,0:T(8,128)S(1)}, u32[]{:S(2)}, u32[]{:S(2)}) collective-permute-start(f32[14,8,128]{2,1,0:T(8,128)S(1)} %get-tuple-element.59.right), channel_id=1, source_target_pairs={{0,8},{8,16},{16,24},{24,0},{1,9},{9,17},{17,25},{25,1},{2,10},{10... | collective-permute-start | bytes 172040 | tf_op jit(solution)/shard_map/ppermute | solution.py:36
  16.6 2.1 %collective-permute-start.4 = (f32[14,8,128]{2,1,0:T(8,128)S(1)}, f32[14,8,128]{2,1,0:T(8,128)S(1)}, u32[]{:S(2)}, u32[]{:S(2)}) collective-permute-start(f32[14,8,128]{2,1,0:T(8,128)S(1)} %get-tuple-element.58.left), channel_id=1, source_target_pairs={{0,24},{8,0},{16,8},{24,16},{1,25},{9,1},{17,9},{25,17},{2,26},{10... | collective-permute-start | bytes 172040 | tf_op jit(solution)/shard_map/ppermute | solution.py:36
  18.7 1.6 %collective-permute-done.3.from_left = f32[14,8,128]{2,1,0:T(8,128)S(1)} collective-permute-done((f32[14,8,128]{2,1,0:T(8,128)S(1)}, f32[14,8,128]{2,1,0:T(8,128)S(1)}, u32[]{:S(2)}, u32[]{:S(2)}) %collective-permute-start.3) | collective-permute-done | bytes 57376 | tf_op jit(solution)/shard_map/ppermute | solution.py:36
  20.3 1.2 %shard_map.54 = (f32[16,24,256]{2,1,0:T(8,128)S(1)}, f32[16,24,128]{2,1,0:T(8,128)S(1)}, f32[4,16,24,128]{3,2,1,0:T(8,128)S(1)}, f32[3,16,256]{2,1,0:T(8,128)S(1...) custom-call(s32[2]{0:T(128)S(1)} %bitcast.7, ...), custom_call_target="tpu_custom_call" | custom-call | tf_op jit(solution)/shard_map/pallas_call | solution.py:62
  21.5 4.2 %collective-permute-start.5 = (f32[2,24,384]{2,1,0:T(8,128)S(1)}, f32[2,24,384]{2,1,0:T(8,128)S(1)}, u32[]{:S(2)}, u32[]{:S(2)}) collective-permute-start(f32[2,24,384]{2,1,0:T(8,128)S(1)} %get-tuple-element.63.down), channel_id=1, source_target_pairs={{0,3},{1,0},{2,1},{3,2},{4,7},{5,4},{6,5},{7,6},{8,11},{9,8},{10,9... | collective-permute-start | bytes 221192 | tf_op jit(solution)/shard_map/ppermute | solution.py:36
  25.7 1.2 %collective-permute-start.6 = (f32[24,384]{1,0:T(8,128)S(1)}, f32[24,384]{1,0:T(8,128)S(1)}, u32[]{:S(2)}, u32[]{:S(2)}) collective-permute-start(f32[24,384]{1,0:T(8,128)S(1)} %get-tuple-element.72.refs_3_.refs_4_), channel_id=1, source_target_pairs={{0,1},{1,2},{2,3},{3,0},{4,5},{5,6},{6,7},{7,4},{8,9},{9,10},{10,1... | collective-permute-start | bytes 110600 | tf_op jit(solution)/shard_map/ppermute | solution.py:36
  26.9 1.2 %collective-permute-start.10 = (s32[29,8,256]{2,1,0:T(8,128)S(1)}, s32[29,8,256]{2,1,0:T(8,128)S(1)}, u32[]{:S(2)}, u32[]{:S(2)}) collective-permute-start(s32[29,8,256]{2,1,0:T(8,128)S(1)} %get-tuple-element.77), channel_id=1, source_target_pairs={{0,4},{4,0},{1,5},{5,1},{2,6},{6,2},{3,7},{7,3},{8,12},{12,8},{9,1... | collective-permute-start | bytes 712712 | tf_op jit(solution)/shard_map/ppermute | solution.py:40
  28.4 1.6 %collective-permute-done.2.more_pairs.outer = f32[45,8,256]{2,1,0:T(8,128)S(1)} collective-permute-done((f32[45,8,256]{2,1,0:T(8,128)S(1)}, f32[45,8,256]{2,1,0:T(8,128)S(1)}, u32[]{:S(2)}, u32[]{:S(2)}) %collective-permute-start.2) | collective-permute-done | bytes 368672 | tf_op jit(solution)/shard_map/ppermute | solution.py:40
  30.0 0.9 %shard_map.55 = (f32[2,16,24,384]{3,2,1,0:T(8,128)S(1)}, f32[2,16,24,384]{3,2,1,0:T(8,128)S(1)}) custom-call(s32[2]{0:T(128)S(1)} %bitcast.8, bf16[4,2,16,16,256]{4,3,2,1,0:T(8,128)(2,1)S(1)} %get-tuple-element.54.coef, f32[51,8,256]{2,1,0:T(8,128)S(1)} %collective-permute-done.edge_in, f32[45,8,256]{2,1,0:T(8,128)S(1)} %collective-permute-done.1.pairs, ...), custom_call_target="tpu_custom_call" | custom-call | tf_op jit(solution)/shard_map/pallas_call | solution.py:62
  30.9 1.2 %shard_map.56 = (f32[16,24,384]{2,1,0:T(8,128)S(1)}, f32[16,24,384]{2,1,0:T(8,128)S(1)}) custom-call(f32[2,16,24,384]{3,2,1,0:T(8,128)S(1)} %get-tuple-element.65.wide_ax, f32[2,16,24,384]{3,2,1,0:T(8,128)S(1)} %get-tuple-element.62.wide_yz.refs_2_.refs_3_, f32[16,24,256]{2,1,0:T(8,128)S(1)} %get-tuple-element.66.edge_start, ...), custom_call_target="tpu_custom_call" | custom-call | tf_op jit(solution)/shard_map/pallas_call | solution.py:62
  32.4 3.8 %collective-permute-start.7 = (f32[24,384]{1,0:T(8,128)S(1)}, f32[24,384]{1,0:T(8,128)S(1)}, u32[]{:S(2)}, u32[]{:S(2)}) collective-permute-start(f32[24,384]{1,0:T(8,128)S(1)} %get-tuple-element.74), channel_id=1, source_target_pairs={{0,1},{1,2},{2,3},{3,0},{4,5},{5,6},{6,7},{7,4},{8,9},{9,10},{10,1... | collective-permute-start | bytes 110600 | tf_op jit(solution)/shard_map/ppermute | solution.py:36
  36.2 1.2 %collective-permute-start.9 = (f32[2,16,384]{2,1,0:T(8,128)S(1)}, f32[2,16,384]{2,1,0:T(8,128)S(1)}, u32[]{:S(2)}, u32[]{:S(2)}) collective-permute-start(f32[2,16,384]{2,1,0:T(8,128)S(1)} %get-tuple-element.76), channel_id=1, source_target_pairs={{0,4},{4,0},{1,5},{5,1},{2,6},{6,2},{3,7},{7,3},{8,12},{12,8},{9,1... | collective-permute-start | bytes 147464 | tf_op jit(solution)/shard_map/ppermute | solution.py:40
  37.7 1.1 %shard_map.59 = (f32[16,24,384]{2,1,0:T(8,128)S(1)}, f32[16,24,384]{2,1,0:T(8,128)S(1)}, f32[16,24,256]{2,1,0:T(8,128)S(1)}) custom-call(f32[2,16,24,384]{3,2,1,0:T(8,128)S(1)} %get-tuple-element.65.wide_ax, f32[2,16,24,384]{3,2,1,0:T(8,128)S(1)} %get-tuple-element.62.wide_yz.refs_2_.refs_3_, ...), custom_call_target="tpu_custom_call" | custom-call | tf_op jit(solution)/shard_map/pallas_call | solution.py:62
  38.9 1.0 %collective-permute-done.8.high_face.refs_1_ = f32[1,24,384]{2,1,0:T(8,128)S(1)} collective-permute-done((f32[1,24,384]{2,1,0:T(8,128)S(1)}, f32[1,24,384]{2,1,0:T(8,128)S(1)}, u32[]{:S(2)}, u32[]{:S(2)}) %collective-permute-start.8) | collective-permute-done | bytes 36896 | tf_op jit(solution)/shard_map/ppermute | solution.py:36
  39.9 1.0 %collective-permute-start.13 = (f32[2,16,384]{2,1,0:T(8,128)S(1)}, f32[2,16,384]{2,1,0:T(8,128)S(1)}, u32[]{:S(2)}, u32[]{:S(2)}) collective-permute-start(f32[2,16,384]{2,1,0:T(8,128)S(1)} %get-tuple-element.86), channel_id=1, source_target_pairs={{0,4},{4,0},{1,5},{5,1},{2,6},{6,2},{3,7},{7,3},{8,12},{12,8},{9,1... | collective-permute-start | bytes 147464 | tf_op jit(solution)/shard_map/ppermute | solution.py:40
  40.9 2.7 %collective-permute-start.11 = (f32[24,384]{1,0:T(8,128)S(1)}, f32[24,384]{1,0:T(8,128)S(1)}, u32[]{:S(2)}, u32[]{:S(2)}) collective-permute-start(f32[24,384]{1,0:T(8,128)S(1)} %get-tuple-element.84), channel_id=1, source_target_pairs={{0,1},{1,2},{2,3},{3,0},{4,5},{5,6},{6,7},{7,4},{8,9},{9,10},{10,1... | collective-permute-start | bytes 110600 | tf_op jit(solution)/shard_map/ppermute | solution.py:36
  43.9 1.3 %shard_map.61 = (f32[16,24,384]{2,1,0:T(8,128)S(1)}, f32[16,24,384]{2,1,0:T(8,128)S(1)}, f32[16,24,256]{2,1,0:T(8,128)S(1)}) custom-call(f32[2,16,24,384]{3,2,1,0:T(8,128)S(1)} %get-tuple-element.65.wide_ax, f32[2,16,24,384]{3,2,1,0:T(8,128)S(1)} %get-tuple-element.62.wide_yz.refs_2_.refs_3_, ...), custom_call_target="tpu_custom_call" | custom-call | tf_op jit(solution)/shard_map/pallas_call | solution.py:62
  45.2 1.8 %collective-permute-done.12.high_face.refs_1_ = f32[1,24,384]{2,1,0:T(8,128)S(1)} collective-permute-done((f32[1,24,384]{2,1,0:T(8,128)S(1)}, f32[1,24,384]{2,1,0:T(8,128)S(1)}, u32[]{:S(2)}, u32[]{:S(2)}) %collective-permute-start.12) | collective-permute-done | bytes 36896 | tf_op jit(solution)/shard_map/ppermute | solution.py:36
  47.1 0.6 %collective-permute-start.17 = (f32[2,16,384]{2,1,0:T(8,128)S(1)}, f32[2,16,384]{2,1,0:T(8,128)S(1)}, u32[]{:S(2)}, u32[]{:S(2)}) collective-permute-start(f32[2,16,384]{2,1,0:T(8,128)S(1)} %get-tuple-element.94), channel_id=1, source_target_pairs={{0,4},{4,0},{1,5},{5,1},{2,6},{6,2},{3,7},{7,3},{8,12},{12,8},{9,1... | collective-permute-start | bytes 147464 | tf_op jit(solution)/shard_map/ppermute | solution.py:40
  47.7 1.2 %collective-permute-start.15 = (f32[24,384]{1,0:T(8,128)S(1)}, f32[24,384]{1,0:T(8,128)S(1)}, u32[]{:S(2)}, u32[]{:S(2)}) collective-permute-start(f32[24,384]{1,0:T(8,128)S(1)} %get-tuple-element.92), channel_id=1, source_target_pairs={{0,1},{1,2},{2,3},{3,0},{4,5},{5,6},{6,7},{7,4},{8,9},{9,10},{10,1... | collective-permute-start | bytes 110600 | tf_op jit(solution)/shard_map/ppermute | solution.py:36
  48.9 1.2 %shard_map.63 = (f32[16,24,384]{2,1,0:T(8,128)S(1)}, f32[16,24,384]{2,1,0:T(8,128)S(1)}, f32[16,24,256]{2,1,0:T(8,128)S(1)}) custom-call(f32[2,16,24,384]{3,2,1,0:T(8,128)S(1)} %get-tuple-element.65.wide_ax, f32[2,16,24,384]{3,2,1,0:T(8,128)S(1)} %get-tuple-element.62.wide_yz.refs_2_.refs_3_, ...), custom_call_target="tpu_custom_call" | custom-call | tf_op jit(solution)/shard_map/pallas_call | solution.py:62
  50.2 2.1 %collective-permute-done.16.high_face.refs_1_ = f32[1,24,384]{2,1,0:T(8,128)S(1)} collective-permute-done((f32[1,24,384]{2,1,0:T(8,128)S(1)}, f32[1,24,384]{2,1,0:T(8,128)S(1)}, u32[]{:S(2)}, u32[]{:S(2)}) %collective-permute-start.16) | collective-permute-done | bytes 36896 | tf_op jit(solution)/shard_map/ppermute | solution.py:36
  53.3 1.1 %shard_map.65 = (f32[16,24,256]{2,1,0:T(8,128)S(1)}, f32[16,24,256]{2,1,0:T(8,128)S(1)}) custom-call(f32[2,16,24,384]{3,2,1,0:T(8,128)S(1)} %get-tuple-element.65.wide_ax, f32[2,16,24,384]{3,2,1,0:T(8,128)S(1)} %get-tuple-element.62.wide_yz.refs_2_.refs_3_, f32[2,24,384]{2,1,0:T(8,128)S(1)} %collective-permute-done.5.refs_6_.refs_7_.rim_face, ...), custom_call_target="tpu_custom_call" | custom-call | tf_op jit(solution)/shard_map/pallas_call | solution.py:62
  54.4 2.1 %collective-permute-done.19.high_face = f32[1,24,384]{2,1,0:T(8,128)S(1)} collective-permute-done((f32[1,24,384]{2,1,0:T(8,128)S(1)}, f32[1,24,384]{2,1,0:T(8,128)S(1)}, u32[]{:S(2)}, u32[]{:S(2)}) %collective-permute-start.19) | collective-permute-done | bytes 36896 | tf_op jit(solution)/shard_map/ppermute | solution.py:36
  56.6 0.9 %shard_map.66 = (f32[16,24,256]{2,1,0:T(8,128)}, f32[16,24,256]{2,1,0:T(8,128)}) custom-call(f32[2,16,24,384]{3,2,1,0:T(8,128)S(1)} %get-tuple-element.62.wide_yz.refs_2_.refs_3_, f32[2,24,384]{2,1,0:T(8,128)S(1)} %collective-permute-done.5.refs_6_.refs_7_.rim_face, f32[3,16,384]{2,1,0:T(8,128)S(1)} %get-tuple-element.64.refs_7_.refs_8_.rim_rows, ...), custom_call_target="tpu_custom_call" | custom-call | tf_op jit(solution)/shard_map/pallas_call | solution.py:62
  (32 shorter events, 2.2 us)
Async XLA Ops:
  0.6 4.2 %copy-start = (s32[2,1,1]{0,2,1:T(1,128)S(1)}, s32[2,1,1]{0,2,1:T(1,128)}, u32[]{:S(2)}) copy-start(s32[2,1,1]{0,2,1:T(1,128)} %param.5) | copy-start | bytes 28
  2.7 11.5 %collective-permute-start = (f32[51,8,256]{2,1,0:T(8,128)S(1)}, f32[51,8,256]{2,1,0:T(8,128)S(1)}, u32[]{:S(2)}, u32[]{:S(2)}) collective-permute-start(f32[51,8,256]{2,1,0:T(8,128)S(1)} %get-tuple-element.55._), channel_id=1, source_target_pairs={{0,4},{4,0},{1,5},{5,1},{2,6},{6,2},{3,7},{7,3},{8,12},{12,8},{9,1... | collective-permute-start | bytes 1253384 | tf_op jit(solution)/shard_map/ppermute | solution.py:40
  5.5 22.6 %collective-permute-start.1 = (f32[45,8,256]{2,1,0:T(8,128)S(1)}, f32[45,8,256]{2,1,0:T(8,128)S(1)}, u32[]{:S(2)}, u32[]{:S(2)}) collective-permute-start(f32[45,8,256]{2,1,0:T(8,128)S(1)} %shard_map.51._), channel_id=1, source_target_pairs={{0,4},{4,0},{1,5},{5,1},{2,6},{6,2},{3,7},{7,3},{8,12},{12,8},{9,1... | collective-permute-start | bytes 1105928 | tf_op jit(solution)/shard_map/ppermute | solution.py:40
  9.5 20.5 %collective-permute-start.2 = (f32[45,8,256]{2,1,0:T(8,128)S(1)}, f32[45,8,256]{2,1,0:T(8,128)S(1)}, u32[]{:S(2)}, u32[]{:S(2)}) collective-permute-start(f32[45,8,256]{2,1,0:T(8,128)S(1)} %get-tuple-element.57), channel_id=1, source_target_pairs={{0,4},{4,0},{1,5},{5,1},{2,6},{6,2},{3,7},{7,3},{8,12},{12,8},{9,1... | collective-permute-start | bytes 1105928 | tf_op jit(solution)/shard_map/ppermute | solution.py:40
  15.4 4.9 %collective-permute-start.3 = (f32[14,8,128]{2,1,0:T(8,128)S(1)}, f32[14,8,128]{2,1,0:T(8,128)S(1)}, u32[]{:S(2)}, u32[]{:S(2)}) collective-permute-start(f32[14,8,128]{2,1,0:T(8,128)S(1)} %get-tuple-element.59.right), channel_id=1, source_target_pairs={{0,8},{8,16},{16,24},{24,0},{1,9},{9,17},{17,25},{25,1},{2,10},{10... | collective-permute-start | bytes 172040 | tf_op jit(solution)/shard_map/ppermute | solution.py:36
  16.6 3.6 %collective-permute-start.4 = (f32[14,8,128]{2,1,0:T(8,128)S(1)}, f32[14,8,128]{2,1,0:T(8,128)S(1)}, u32[]{:S(2)}, u32[]{:S(2)}) collective-permute-start(f32[14,8,128]{2,1,0:T(8,128)S(1)} %get-tuple-element.58.left), channel_id=1, source_target_pairs={{0,24},{8,0},{16,8},{24,16},{1,25},{9,1},{17,9},{25,17},{2,26},{10... | collective-permute-start | bytes 172040 | tf_op jit(solution)/shard_map/ppermute | solution.py:36
  21.5 10.7 %collective-permute-start.5 = (f32[2,24,384]{2,1,0:T(8,128)S(1)}, f32[2,24,384]{2,1,0:T(8,128)S(1)}, u32[]{:S(2)}, u32[]{:S(2)}) collective-permute-start(f32[2,24,384]{2,1,0:T(8,128)S(1)} %get-tuple-element.63.down), channel_id=1, source_target_pairs={{0,3},{1,0},{2,1},{3,2},{4,7},{5,4},{6,5},{7,6},{8,11},{9,8},{10,9... | collective-permute-start | bytes 221192 | tf_op jit(solution)/shard_map/ppermute | solution.py:36
  25.7 6.5 %collective-permute-start.6 = (f32[24,384]{1,0:T(8,128)S(1)}, f32[24,384]{1,0:T(8,128)S(1)}, u32[]{:S(2)}, u32[]{:S(2)}) collective-permute-start(f32[24,384]{1,0:T(8,128)S(1)} %get-tuple-element.72.refs_3_.refs_4_), channel_id=1, source_target_pairs={{0,1},{1,2},{2,3},{3,0},{4,5},{5,6},{6,7},{7,4},{8,9},{9,10},{10,1... | collective-permute-start | bytes 110600 | tf_op jit(solution)/shard_map/ppermute | solution.py:36
  26.9 10.5 %collective-permute-start.10 = (s32[29,8,256]{2,1,0:T(8,128)S(1)}, s32[29,8,256]{2,1,0:T(8,128)S(1)}, u32[]{:S(2)}, u32[]{:S(2)}) collective-permute-start(s32[29,8,256]{2,1,0:T(8,128)S(1)} %get-tuple-element.77), channel_id=1, source_target_pairs={{0,4},{4,0},{1,5},{5,1},{2,6},{6,2},{3,7},{7,3},{8,12},{12,8},{9,1... | collective-permute-start | bytes 712712 | tf_op jit(solution)/shard_map/ppermute | solution.py:40
  28.1 15.8 %collective-permute-start.14 = (s32[14,8,256]{2,1,0:T(8,128)S(1)}, s32[14,8,256]{2,1,0:T(8,128)S(1)}, u32[]{:S(2)}, u32[]{:S(2)}) collective-permute-start(s32[14,8,256]{2,1,0:T(8,128)S(1)} %get-tuple-element.90), channel_id=1, source_target_pairs={{0,4},{4,0},{1,5},{5,1},{2,6},{6,2},{3,7},{7,3},{8,12},{12,8},{9,1... | collective-permute-start | bytes 344072 | tf_op jit(solution)/shard_map/ppermute | solution.py:40
  32.4 6.5 %collective-permute-start.7 = (f32[24,384]{1,0:T(8,128)S(1)}, f32[24,384]{1,0:T(8,128)S(1)}, u32[]{:S(2)}, u32[]{:S(2)}) collective-permute-start(f32[24,384]{1,0:T(8,128)S(1)} %get-tuple-element.74), channel_id=1, source_target_pairs={{0,1},{1,2},{2,3},{3,0},{4,5},{5,6},{6,7},{7,4},{8,9},{9,10},{10,1... | collective-permute-start | bytes 110600 | tf_op jit(solution)/shard_map/ppermute | solution.py:36
  36.2 3.7 %collective-permute-start.8 = (f32[1,24,384]{2,1,0:T(8,128)S(1)}, f32[1,24,384]{2,1,0:T(8,128)S(1)}, u32[]{:S(2)}, u32[]{:S(2)}) collective-permute-start(f32[1,24,384]{2,1,0:T(8,128)S(1)} %get-tuple-element.75), channel_id=1, source_target_pairs={{0,3},{1,0},{2,1},{3,2},{4,7},{5,4},{6,5},{7,6},{8,11},{9,8},{10,9... | collective-permute-start | bytes 110600 | tf_op jit(solution)/shard_map/ppermute | solution.py:36
  36.2 3.7 %collective-permute-start.9 = (f32[2,16,384]{2,1,0:T(8,128)S(1)}, f32[2,16,384]{2,1,0:T(8,128)S(1)}, u32[]{:S(2)}, u32[]{:S(2)}) collective-permute-start(f32[2,16,384]{2,1,0:T(8,128)S(1)} %get-tuple-element.76), channel_id=1, source_target_pairs={{0,4},{4,0},{1,5},{5,1},{2,6},{6,2},{3,7},{7,3},{8,12},{12,8},{9,1... | collective-permute-start | bytes 147464 | tf_op jit(solution)/shard_map/ppermute | solution.py:40
  39.9 7.1 %collective-permute-start.13 = (f32[2,16,384]{2,1,0:T(8,128)S(1)}, f32[2,16,384]{2,1,0:T(8,128)S(1)}, u32[]{:S(2)}, u32[]{:S(2)}) collective-permute-start(f32[2,16,384]{2,1,0:T(8,128)S(1)} %get-tuple-element.86), channel_id=1, source_target_pairs={{0,4},{4,0},{1,5},{5,1},{2,6},{6,2},{3,7},{7,3},{8,12},{12,8},{9,1... | collective-permute-start | bytes 147464 | tf_op jit(solution)/shard_map/ppermute | solution.py:40
  40.9 4.3 %collective-permute-start.11 = (f32[24,384]{1,0:T(8,128)S(1)}, f32[24,384]{1,0:T(8,128)S(1)}, u32[]{:S(2)}, u32[]{:S(2)}) collective-permute-start(f32[24,384]{1,0:T(8,128)S(1)} %get-tuple-element.84), channel_id=1, source_target_pairs={{0,1},{1,2},{2,3},{3,0},{4,5},{5,6},{6,7},{7,4},{8,9},{9,10},{10,1... | collective-permute-start | bytes 110600 | tf_op jit(solution)/shard_map/ppermute | solution.py:36
  43.7 3.4 %collective-permute-start.12 = (f32[1,24,384]{2,1,0:T(8,128)S(1)}, f32[1,24,384]{2,1,0:T(8,128)S(1)}, u32[]{:S(2)}, u32[]{:S(2)}) collective-permute-start(f32[1,24,384]{2,1,0:T(8,128)S(1)} %get-tuple-element.85), channel_id=1, source_target_pairs={{0,3},{1,0},{2,1},{3,2},{4,7},{5,4},{6,5},{7,6},{8,11},{9,8},{10,9... | collective-permute-start | bytes 110600 | tf_op jit(solution)/shard_map/ppermute | solution.py:36
  43.7 9.6 %collective-permute-start.21 = (s32[14,8,256]{2,1,0:T(8,128)S(1)}, s32[14,8,256]{2,1,0:T(8,128)S(1)}, u32[]{:S(2)}, u32[]{:S(2)}) collective-permute-start(s32[14,8,256]{2,1,0:T(8,128)S(1)} %get-tuple-element.103), channel_id=1, source_target_pairs={{0,4},{4,0},{1,5},{5,1},{2,6},{6,2},{3,7},{7,3},{8,12},{12,8},{9,1... | collective-permute-start | bytes 344072 | tf_op jit(solution)/shard_map/ppermute | solution.py:40
  47.1 5.2 %collective-permute-start.17 = (f32[2,16,384]{2,1,0:T(8,128)S(1)}, f32[2,16,384]{2,1,0:T(8,128)S(1)}, u32[]{:S(2)}, u32[]{:S(2)}) collective-permute-start(f32[2,16,384]{2,1,0:T(8,128)S(1)} %get-tuple-element.94), channel_id=1, source_target_pairs={{0,4},{4,0},{1,5},{5,1},{2,6},{6,2},{3,7},{7,3},{8,12},{12,8},{9,1... | collective-permute-start | bytes 147464 | tf_op jit(solution)/shard_map/ppermute | solution.py:40
  47.7 2.4 %collective-permute-start.15 = (f32[24,384]{1,0:T(8,128)S(1)}, f32[24,384]{1,0:T(8,128)S(1)}, u32[]{:S(2)}, u32[]{:S(2)}) collective-permute-start(f32[24,384]{1,0:T(8,128)S(1)} %get-tuple-element.92), channel_id=1, source_target_pairs={{0,1},{1,2},{2,3},{3,0},{4,5},{5,6},{6,7},{7,4},{8,9},{9,10},{10,1... | collective-permute-start | bytes 110600 | tf_op jit(solution)/shard_map/ppermute | solution.py:36
  48.9 3.4 %collective-permute-start.16 = (f32[1,24,384]{2,1,0:T(8,128)S(1)}, f32[1,24,384]{2,1,0:T(8,128)S(1)}, u32[]{:S(2)}, u32[]{:S(2)}) collective-permute-start(f32[1,24,384]{2,1,0:T(8,128)S(1)} %get-tuple-element.93), channel_id=1, source_target_pairs={{0,3},{1,0},{2,1},{3,2},{4,7},{5,4},{6,5},{7,6},{8,11},{9,8},{10,9... | collective-permute-start | bytes 110600 | tf_op jit(solution)/shard_map/ppermute | solution.py:36
  52.4 4.2 %collective-permute-start.20 = (f32[2,16,384]{2,1,0:T(8,128)S(1)}, f32[2,16,384]{2,1,0:T(8,128)S(1)}, u32[]{:S(2)}, u32[]{:S(2)}) collective-permute-start(f32[2,16,384]{2,1,0:T(8,128)S(1)} %get-tuple-element.100), channel_id=1, source_target_pairs={{0,4},{4,0},{1,5},{5,1},{2,6},{6,2},{3,7},{7,3},{8,12},{12,8},{9,1... | collective-permute-start | bytes 147464 | tf_op jit(solution)/shard_map/ppermute | solution.py:40
  52.8 1.6 %collective-permute-start.18 = (f32[24,384]{1,0:T(8,128)S(1)}, f32[24,384]{1,0:T(8,128)S(1)}, u32[]{:S(2)}, u32[]{:S(2)}) collective-permute-start(f32[24,384]{1,0:T(8,128)S(1)} %get-tuple-element.98), channel_id=1, source_target_pairs={{0,1},{1,2},{2,3},{3,0},{4,5},{5,6},{6,7},{7,4},{8,9},{9,10},{10,1... | collective-permute-start | bytes 110600 | tf_op jit(solution)/shard_map/ppermute | solution.py:36
  53.2 3.4 %collective-permute-start.19 = (f32[1,24,384]{2,1,0:T(8,128)S(1)}, f32[1,24,384]{2,1,0:T(8,128)S(1)}, u32[]{:S(2)}, u32[]{:S(2)}) collective-permute-start(f32[1,24,384]{2,1,0:T(8,128)S(1)} %get-tuple-element.99), channel_id=1, source_target_pairs={{0,3},{1,0},{2,1},{3,2},{4,7},{5,4},{6,5},{7,6},{8,11},{9,8},{10,9... | collective-permute-start | bytes 110600 | tf_op jit(solution)/shard_map/ppermute | solution.py:36

commit v5 on v4

--- a/solution.py
+++ b/solution.py
@@ -9,7 +9,8 @@
 
 SWEEPS = 4
 LANES = 128
-STRIP = 8
+STRIP = SWEEPS + 1
+STRIPS_AT = (0, 3, 5, 7, 10)
 SHIFT = 4096.0
 VMEM_LIMIT = 24 * 1024 * 1024
 
@@ -101,30 +102,38 @@
     return jnp.where(part == 0, both[:rows], both[rows:])
 
 
-def strips(fields, coef, item, place, planes):
-    columns, rows = fields.shape[4], fields.shape[3] // 2
-    group = lane_of((rows, LANES)) // STRIP
-    low = jnp.zeros((rows, LANES), jnp.float32)
-    high = jnp.zeros((rows, LANES), jnp.float32)
-    for z in range(planes):
+def strip_at(item, k, z, planes):
+    group = k * planes + z
+    return STRIPS_AT[item] + group // (LANES // STRIP), STRIP * (group % (LANES // STRIP))
+
+
+def strips(fields, coef, item, ids, half, pairs, store):
+    planes, columns, rows = fields.shape[2], fields.shape[4], fields.shape[3] // 2
+    lane, row = lane_of((rows, LANES)), row_of((rows, columns))
+    numbers = (0, 1, 2, 3, 5) if pairs == 1 and item in (0, 3) else (0, 1, 2)
+    places = units_of(ids, half, numbers)
+
+    def cells(place, z):
         if item < 2:
-            cells = field_unit(fields, item, place, z)
+            found = field_unit(fields, item, place, z)
         else:
-            cells = coef_unit(coef, 2 * item - 4, place, z) + SHIFT * coef_unit(coef, 2 * item - 3, place, z)
-        first, last = cells[:, :LANES], cells[:, columns - LANES :]
-        turn = STRIP * z
-        low = jnp.where(group == z, pltpu.roll(first, turn, 1) if turn else first, low)
-        turn = (STRIP * z + STRIP) % LANES
-        high = jnp.where(group == z, pltpu.roll(last, turn, 1) if turn else last, high)
-    return low, high
-
-
-def outer_strips(fields, coef, item, ids, half, planes):
-    found = []
-    for place in units_of(ids, half, (3, 5)):
-        found.append([jnp.where(place[0], side, 0.0) for side in strips(fields, coef, item, place, planes)])
-    above = row_of(found[0][0].shape) < found[0][0].shape[0] // 2
-    return [jnp.where(above, high, low) for high, low in zip(*found)]
+            found = coef_unit(coef, 2 * item - 4, place, z) + SHIFT * coef_unit(coef, 2 * item - 3, place, z)
+        return jnp.where(place[0], found, 0.0)
+
+    tiles = {at: [jnp.zeros((rows, LANES), jnp.float32)] * 2 for at in range(STRIPS_AT[item], STRIPS_AT[item + 1])}
+    for k in range(min(len(places), 4)):
+        for z in range(planes):
+            value = cells(places[k], z)
+            if k == 3:
+                value = jnp.where(row < rows // 2, value, cells(places[4], z))
+            at, first = strip_at(item, k, z, planes)
+            inside = jnp.logical_and(lane >= first, lane < first + STRIP)
+            for side, start, turn in ((0, 0, first), (1, columns - LANES, (first + STRIP) % LANES)):
+                part = value[:, start : start + LANES]
+                part = pltpu.roll(part, turn, 1) if turn else part
+                tiles[at][side] = jnp.where(inside, part, tiles[at][side])
+    for at, (low, high) in tiles.items():
+        store(at, low, high)
 
 
 def outer_row(fields, ids, half, z):
@@ -152,10 +161,10 @@
     return jnp.where(row == 0, fields[0, slot, z, 0:1], fields[0, slot, z, last : last + 1])
 
 
-PLANES_AT, ROWS_AT = 12, 18
-FIRST_PAIRS = 16
-NEXT_PAIRS = 45
-PIECES = (1, 8, 15)
+PLANES_AT, ROWS_AT = 10, 16
+FIRST_PAIRS = 20
+NEXT_PAIRS = 43
+PIECES = (1, 7, 15)
 CODE_BITS = 20
 ADDED_AT = (2, 4)
 
@@ -205,31 +214,32 @@
     return jnp.concatenate(decoded((piece[at], piece[at + 1]), scales, 3 * (z - 1)))
 
 
-def pair_at(ids, half, number, planes):
-    unit = number % (3 * planes)
-    part = 2 if number < 3 * planes else 0
-    return part, unit // planes, unit % planes, units_of(ids, half)[unit // planes]
+def pair_order(planes):
+    rest = [(2, k, z) for k in (1, 2) for z in range(1, planes)]
+    return (
+        [(2, 0, z) for z in range(planes)]
+        + [(2, 1, 0), (2, 2, 0)]
+        + rest
+        + [(0, k, z) for k in range(3) for z in range(planes)]
+    )
 
 
 def pair_tile(ids, coef, half, number):
-    part, _, z, place = pair_at(ids, half, number, coef.shape[2])
+    part, k, z = pair_order(coef.shape[2])[number]
+    place = units_of(ids, half)[k]
     return coef_unit(coef, part, place, z) + SHIFT * coef_unit(coef, part + 1, place, z)
 
 
-def rim_at(planes, unit_rows):
-    planes_at = ROWS_AT + 3 * (planes // unit_rows)
-    outer_at = planes_at + 3 + planes // unit_rows
-    return planes_at, planes_at + 3, outer_at, outer_at + 2 + 2 * (planes // unit_rows)
-
-
-def beyond(fields, coef, ids, half, pairs, strip_out, row_out):
-    planes = fields.shape[2]
+def beyond_at(planes, unit_rows):
+    start = ROWS_AT + 3 * (planes // unit_rows)
+    return start, start + 2 * (planes // unit_rows)
+
+
+def beyond(fields, coef, ids, half, pairs, row_out):
     if pairs > 1:
         return
-    for j, item in enumerate((0, 3)):
-        strip_out(j, *outer_strips(fields, coef, item, ids, half, planes))
     (above,) = units_of(ids, half, (3,))
-    for z in range(planes):
+    for z in range(fields.shape[2]):
         row_out(0, z, outer_row(fields, ids, half, z))
         row_out(1, z, jnp.where(above[0], first_row(coef, above, z), 0.0))
 
@@ -255,36 +265,29 @@
     half = 1 - lax.axis_index("gy") % 2
     for copy in copies[:5]:
         copy.wait()
+    def strip_out(at, low, high):
+        out[at] = jnp.concatenate([low, high], axis=1)
+
     for item in range(4):
         if item == 2:
             for copy in copies[5:]:
                 copy.wait()
-        for k, place in enumerate(units_of(ids, half)):
-            low, high = strips(fields, coef, item, place, planes)
-            out[3 * item + k] = jnp.concatenate([low, high], axis=1)
-            if item < 2:
+        strips(fields, coef, item, ids, half, pairs, strip_out)
+        if item < 2:
+            for k, place in enumerate(units_of(ids, half)):
                 out[PLANES_AT + 3 * item + k] = field_unit(fields, 0, place, item * (planes - 1))
     for j, place in enumerate(brick_rows(ids, half, unit_rows)):
         for z in range(planes):
             at = ROWS_AT + j * (planes // unit_rows) + z // unit_rows
             line = z % unit_rows
             out[at, line : line + 1] = field_row(fields, place, z)
-    faces_at, lines_at, beyond_at, pairs_at = rim_at(planes, unit_rows)
-
-    def strip_out(j, low, high):
-        out[beyond_at + j] = jnp.concatenate([low, high], axis=1)
+    rows_at, pairs_at = beyond_at(planes, unit_rows)
 
     def row_out(j, z, value):
         line = z % unit_rows
-        out[beyond_at + 2 + j * (planes // unit_rows) + z // unit_rows, line : line + 1] = value
-
-    beyond(fields, coef, ids, half, pairs, strip_out, row_out)
-    places = units_of(ids, half)
-    for k, place in enumerate(places):
-        out[faces_at + k] = coef_unit(coef, 3, place, 0)
-    for z in range(planes):
-        line = z % unit_rows
-        out[lines_at + z // unit_rows, line : line + 1] = first_row(coef, places[0], z)
+        out[rows_at + j * (planes // unit_rows) + z // unit_rows, line : line + 1] = value
+
+    beyond(fields, coef, ids, half, pairs, row_out)
     for number in range(FIRST_PAIRS):
         out[pairs_at + number] = pair_tile(ids, coef, half, number)
 
@@ -372,28 +375,23 @@
 def strip_kernel(pairs, ids, fields, coef, edge_in, left, right, outer_rows):
     planes, unit_rows = fields.shape[2], fields.shape[3] // 2
     half = lax.axis_index("gy") % 2
-    for k, place in enumerate(units_of(ids, half)):
-        for item in range(4):
-            low, high = strips(fields, coef, item, place, planes)
-            got = edge_in[3 * item + k]
-            left[3 * item + k] = jnp.where(place[0], low, got[:, :LANES])
-            right[3 * item + k] = jnp.where(place[0], high, got[:, LANES:])
-    beyond_at = rim_at(planes, unit_rows)[2]
-
-    def strip_out(j, low, high):
-        got = edge_in[beyond_at + j]
-        left[12 + j], right[12 + j] = low + got[:, :LANES], high + got[:, LANES:]
+
+    def strip_out(at, low, high):
+        got = edge_in[at]
+        left[at], right[at] = low + got[:, :LANES], high + got[:, LANES:]
+
+    for item in range(4):
+        strips(fields, coef, item, ids, half, pairs, strip_out)
+    rows_at, _ = beyond_at(planes, unit_rows)
 
     def row_out(j, z, value):
         line = z % unit_rows
-        got = edge_in[beyond_at + 2 + j * (planes // unit_rows) + z // unit_rows, line : line + 1]
+        got = edge_in[rows_at + j * (planes // unit_rows) + z // unit_rows, line : line + 1]
         outer_rows[j, z : z + 1] = value + got
 
     if pairs > 1:
         outer_rows[...] = jnp.zeros_like(outer_rows)
-        left[12:14] = jnp.zeros_like(left[12:14])
-        right[12:14] = jnp.zeros_like(right[12:14])
-    beyond(fields, coef, ids, half, pairs, strip_out, row_out)
+    beyond(fields, coef, ids, half, pairs, row_out)
 
 
 def parted(both):
@@ -401,13 +399,15 @@
     return both - SHIFT * second, second
 
 
-def ghost_columns(from_left, from_right, item, k, z):
-    low, high = from_left[3 * item + k], from_right[3 * item + k]
-    turn = (LANES - STRIP * z) % LANES
+def ghost_columns(from_left, from_right, item, k, z, planes):
+    at, first = strip_at(item, k, z, planes)
+    low, high = from_left[at], from_right[at]
+    turn = (LANES - first) % LANES
     right = pltpu.roll(high, turn, 1) if turn else high
-    turn = (LANES - STRIP - STRIP * z) % LANES
+    turn = (LANES - STRIP - first) % LANES
     left = pltpu.roll(low, turn, 1) if turn else low
-    return jnp.where(lane_of(low.shape) < LANES // 2, right, left)
+    lane = lane_of(low.shape)
+    return jnp.where(lane < STRIP, right, jnp.where(lane >= LANES - STRIP, left, 1.0))
 
 
 def gather_kernel(
@@ -420,22 +420,24 @@
     for k, place in enumerate(units_of(ids, half)):
         at = slice(k * rows, (k + 1) * rows)
         for z in range(planes):
-            edge_start[z, at, :LANES] = ghost_columns(right, left, 0, k, z)
-            edge_start[z, at, LANES:] = ghost_columns(from_left, from_right, 0, k, z)
-            rhs_ghost[z, at] = ghost_columns(from_left, from_right, 1, k, z)
+            edge_start[z, at, :LANES] = ghost_columns(right, left, 0, k, z, planes)
+            edge_start[z, at, LANES:] = ghost_columns(from_left, from_right, 0, k, z, planes)
+            rhs_ghost[z, at] = ghost_columns(from_left, from_right, 1, k, z, planes)
             for item in (2, 3):
-                both = ghost_columns(from_left, from_right, item, k, z)
+                both = ghost_columns(from_left, from_right, item, k, z, planes)
                 part = 2 * item - 4
                 ghosts[part, z, at], ghosts[part + 1, z, at] = parted(both)
         for e, (z, out) in enumerate(((0, down.at[0]), (planes - 1, up))):
             own = field_unit(fields, 0, place, z)
             out[at, :columns] = jnp.where(place[0], own, edge_in[PLANES_AT + 3 * e + k])
             out[at, columns:] = edge_start[z, at, LANES:]
-    faces_at, lines_at, _, _ = rim_at(planes, rows)
+    _, pairs_at = beyond_at(planes, rows)
     places = units_of(ids, half)
     for k, place in enumerate(places):
         at = slice(k * rows, (k + 1) * rows)
-        down[1, at, :columns] = jnp.where(place[0], coef_unit(coef, 3, place, 0), edge_in[faces_at + k])
+        down[1, at, :columns] = jnp.where(
+            place[0], coef_unit(coef, 3, place, 0), parted(edge_in[pairs_at + (planes - 1 + k if k else 0)])[1]
+        )
     down[1, :, columns:] = ghosts[3, 0]
     for j, place in enumerate(brick_rows(ids, half, rows)):
         for z in range(planes):
@@ -450,32 +452,32 @@
             middle = jnp.concatenate([edge[:, :LANES]] * (columns // LANES), axis=1)
             rows_out[out, line, :columns] = jnp.where(known, own_rows[j, line], middle)
             rows_out[out, line, columns:] = edge[:, LANES:]
-        got = edge_in[lines_at + z // rows, z % rows : z % rows + 1]
+        got = parted(edge_in[pairs_at + z, 0:1])[0]
         rows_out[2, line, :columns] = jnp.where(places[0][0], first_row(coef, places[0], z), got)
         rows_out[2, line, columns:] = ghosts[2, z, 0:1]
         if pairs > 1:
             continue
-        own = ghost_columns(right, left, 4, 0, z)
-        ghost = ghost_columns(from_left, from_right, 4, 0, z)
+        own = ghost_columns(right, left, 0, 3, z, planes)
+        ghost = ghost_columns(from_left, from_right, 0, 3, z, planes)
         for out, row, known in ((0, rows - 1, half == 0), (1, 0, half == 1)):
             edge = own[row : row + 1]
             middle = jnp.concatenate([edge] * (columns // LANES), axis=1)
             beyond_rows[out, line, :columns] = jnp.where(known, outer_rows[0, line], middle)
             beyond_rows[out, line, columns:] = ghost[row : row + 1]
         beyond_rows[2, line, :columns] = outer_rows[1, line]
-        beyond_rows[2, line, columns:] = parted(ghost_columns(from_left, from_right, 4, 1, z)[0:1])[0]
+        beyond_rows[2, line, columns:] = parted(ghost_columns(from_left, from_right, 3, 3, z, planes)[0:1])[0]
     if pairs > 1:
         beyond_rows[...] = jnp.zeros_like(beyond_rows)
 
 
 def spread_kernel(ids, coef, edge_in, pairs, more_pairs, ghosts, wide_ax, wide_yz):
     planes, columns, rows = coef.shape[2], coef.shape[4], coef.shape[3] // 2
-    pairs_at = rim_at(planes, rows)[3]
+    places, pairs_at = units_of(ids, lax.axis_index("gy") % 2), beyond_at(planes, rows)[1]
     for part in (0, 1):
         wide_ax[part, :, :, columns:] = ghosts[part]
         wide_yz[part, :, :, columns:] = ghosts[2 + part]
-    for number in range(6 * planes):
-        part, k, z, place = pair_at(ids, lax.axis_index("gy") % 2, number, planes)
+    for number, (part, k, z) in enumerate(pair_order(planes)):
+        place = places[k]
         at = slice(k * rows, (k + 1) * rows)
         place_in = number - FIRST_PAIRS
         if place_in < 0:
@@ -763,7 +765,7 @@
         out_shape=[
             f32(*old_fields.shape),
             jax.ShapeDtypeStruct(old_coef.shape, old_coef.dtype),
-            f32(rim_at(planes, half)[3] + FIRST_PAIRS, half, columns),
+            f32(beyond_at(planes, half)[1] + FIRST_PAIRS, half, columns),
         ],
         in_specs=[pl.BlockSpec(memory_space=pltpu.HBM)] * 3,
         out_specs=[vmem] * 3,
@@ -795,7 +797,7 @@
         ids=True,
     )
     outer_in, middle_in = swapped(outer_out), swapped(middle)
-    strip = f32(14, half, LANES)
+    strip = f32(STRIPS_AT[-1], half, LANES)
     left, right, outer_rows = call(
         functools.partial(strip_kernel, pairs),
         [strip, strip, f32(2, planes, columns)],

time: 57.7 us -> 56.2 us (0.974)
  waiting for transfers between devices: 13.6 us -> 12.7 us
    ppermute x10, waiting for transfers between devices: 4.94 us -> 3.93 us  [swapped(): lax.ppermute(value, 'gy', [(i, i ^ 1) for i in range(lax.axis_size('gy'))])]
  transfers between devices with their start and end apart: 22 -> 22, of which waited for: 7 -> 7; matrix products, arithmetic and copies ran while one was open for 0% -> 0% of each run, Pallas kernels for 25% -> 26%
where the time goes in v5:
time: 56.2 us; the launch traced here: 56 us
  starting transfers between devices  25 us (44%)
  Pallas kernels  17.5 us (31%)
  waiting for transfers between devices  12.7 us (23%)
  between operations  0.79 us (1%)
    ppermute x12, starting transfers between devices, shifted(): lax.ppermute(value, axis, [(i, (i + steps) % count) for i in range(count)])  16.5 us
    pallas_call x16, Pallas kernels, call(): pl.pallas_call(kernel, out_shape=outs, in_specs=specs, out_specs=out_spec...  15.4 us
    ppermute x12, waiting for transfers between devices, shifted(): lax.ppermute(value, axis, [(i, (i + steps) % count) for i in range(count)])  8.75 us
    ppermute x10, starting transfers between devices, swapped(): lax.ppermute(value, 'gy', [(i, i ^ 1) for i in range(lax.axis_size('gy'))])  8.47 us
    ppermute x10, waiting for transfers between devices, swapped(): lax.ppermute(value, 'gy', [(i, i ^ 1) for i in range(lax.axis_size('gy'))])  3.93 us
    pallas_call x1, Pallas kernels, local(): pl.pallas_call(functools.partial(edge_kernel, pairs), out_shape=[f32(*old...  2.15 us
  transfers between devices with their start and end apart: 22, of which 7 were waited for; matrix products, arithmetic and copies ran while one was open for 0% of the time, Pallas kernels for 26%

profile of v5, /device:TPU:1, one launch (start us, length us, event | category | flops | bytes accessed | tf_op | source)
XLA Modules:
  0.0 56.0 jit_solution(7263772088407376176)
XLA Ops:
  0.6 2.1 %shard_map.50 = (f32[2,2,16,16,256]{4,3,2,1,0:T(8,128)S(1)}, bf16[4,2,16,16,256]{4,3,2,1,0:T(8,128)(2,1)S(1)}, f32[46,8,256]{2,1,0:T(8,128)S(1)}) custom-call(s32[2]{0:T(128)} %bitcast.3, f32[2,2,16,16,256]{4,3,2,1,0:T(8,128)} %fields_in.1, bf16[4,2,16,16,256]{4,3,2,1,0:T(8,128)(2,1)} %coef_in.1), custom_call_target="tpu_custom_call" | custom-call | tf_op jit(solution)/shard_map/pallas_call | solution.py:763
  2.8 2.1 %collective-permute-start = (f32[46,8,256]{2,1,0:T(8,128)S(1)}, f32[46,8,256]{2,1,0:T(8,128)S(1)}, u32[]{:S(2)}, u32[]{:S(2)}) collective-permute-start(f32[46,8,256]{2,1,0:T(8,128)S(1)} %get-tuple-element.55._), channel_id=1, source_target_pairs={{0,4},{4,0},{1,5},{5,1},{2,6},{6,2},{3,7},{7,3},{8,12},{12,8},{9,1... | collective-permute-start | bytes 1130504 | tf_op jit(solution)/shard_map/ppermute | solution.py:41
  4.9 0.7 %shard_map.51._ = f32[43,8,256]{2,1,0:T(8,128)S(1)} custom-call(s32[2]{0:T(128)S(1)} %bitcast.4, bf16[4,2,16,16,256]{4,3,2,1,0:T(8,128)(2,1)S(1)} %get-tuple-element.54.coef, f32[46,8,256]{2,1,0:T(8,128)S(1)} %get-tuple-element.55._), custom_call_target="tpu_custom_call" | custom-call | tf_op jit(solution)/shard_map/pallas_call | solution.py:63
  5.7 3.5 %shard_map.52 = (f32[43,8,256]{2,1,0:T(8,128)S(1)}, s32[29,8,256]{2,1,0:T(8,128)S(1)}, f32[16,24,256]{2,1,0:T(8,128)S(1)}, f32[16,24,256]{2,1,0:T(8,128)S(1)}, s...) custom-call(s32[2]{0:T(128)S(1)} %bitcast.5, ...), custom_call_target="tpu_custom_call" | custom-call | tf_op jit(solution)/shard_map/pallas_call | solution.py:63
  9.2 1.4 %collective-permute-start.2 = (f32[43,8,256]{2,1,0:T(8,128)S(1)}, f32[43,8,256]{2,1,0:T(8,128)S(1)}, u32[]{:S(2)}, u32[]{:S(2)}) collective-permute-start(f32[43,8,256]{2,1,0:T(8,128)S(1)} %get-tuple-element.57), channel_id=1, source_target_pairs={{0,4},{4,0},{1,5},{5,1},{2,6},{6,2},{3,7},{7,3},{8,12},{12,8},{9,1... | collective-permute-start | bytes 1056776 | tf_op jit(solution)/shard_map/ppermute | solution.py:41
  10.6 2.8 %collective-permute-done.edge_in = f32[46,8,256]{2,1,0:T(8,128)S(1)} collective-permute-done((f32[46,8,256]{2,1,0:T(8,128)S(1)}, f32[46,8,256]{2,1,0:T(8,128)S(1)}, u32[]{:S(2)}, u32[]{:S(2)}) %collective-permute-start) | collective-permute-done | bytes 376864 | tf_op jit(solution)/shard_map/ppermute | solution.py:41
  13.4 1.3 %shard_map.53 = (f32[10,8,128]{2,1,0:T(8,128)S(1)}, f32[10,8,128]{2,1,0:T(8,128)S(1)}, f32[2,16,256]{2,1,0:T(8,128)S(1)}) custom-call(s32[2]{0:T(128)S(1)} %bitcast.6, f32[2,2,16,16,256]{4,3,2,1,0:T(8,128)S(1)} %get-tuple-element.56.fields, bf16[4,2,16,16,256]{4,3,2,1,0:T(8,128)(2,1)S(1)} %get-tuple-element.54.coef, ...), custom_call_target="tpu_custom_call" | custom-call | tf_op jit(solution)/shard_map/pallas_call | solution.py:63
  14.7 1.3 %collective-permute-start.3 = (f32[10,8,128]{2,1,0:T(8,128)S(1)}, f32[10,8,128]{2,1,0:T(8,128)S(1)}, u32[]{:S(2)}, u32[]{:S(2)}) collective-permute-start(f32[10,8,128]{2,1,0:T(8,128)S(1)} %get-tuple-element.59.right), channel_id=1, source_target_pairs={{0,8},{8,16},{16,24},{24,0},{1,9},{9,17},{17,25},{25,1},{2,10},{10... | collective-permute-start | bytes 122888 | tf_op jit(solution)/shard_map/ppermute | solution.py:37
  16.0 2.1 %collective-permute-start.4 = (f32[10,8,128]{2,1,0:T(8,128)S(1)}, f32[10,8,128]{2,1,0:T(8,128)S(1)}, u32[]{:S(2)}, u32[]{:S(2)}) collective-permute-start(f32[10,8,128]{2,1,0:T(8,128)S(1)} %get-tuple-element.58.left), channel_id=1, source_target_pairs={{0,24},{8,0},{16,8},{24,16},{1,25},{9,1},{17,9},{25,17},{2,26},{10... | collective-permute-start | bytes 122888 | tf_op jit(solution)/shard_map/ppermute | solution.py:37
  18.0 1.3 %collective-permute-done.3.from_left = f32[10,8,128]{2,1,0:T(8,128)S(1)} collective-permute-done((f32[10,8,128]{2,1,0:T(8,128)S(1)}, f32[10,8,128]{2,1,0:T(8,128)S(1)}, u32[]{:S(2)}, u32[]{:S(2)}) %collective-permute-start.3) | collective-permute-done | bytes 40992 | tf_op jit(solution)/shard_map/ppermute | solution.py:37
  19.4 1.3 %shard_map.54 = (f32[16,24,256]{2,1,0:T(8,128)S(1)}, f32[16,24,128]{2,1,0:T(8,128)S(1)}, f32[4,16,24,128]{3,2,1,0:T(8,128)S(1)}, f32[3,16,256]{2,1,0:T(8,128)S(1...) custom-call(s32[2]{0:T(128)S(1)} %bitcast.7, ...), custom_call_target="tpu_custom_call" | custom-call | tf_op jit(solution)/shard_map/pallas_call | solution.py:63
  20.7 4.0 %collective-permute-start.5 = (f32[2,24,384]{2,1,0:T(8,128)S(1)}, f32[2,24,384]{2,1,0:T(8,128)S(1)}, u32[]{:S(2)}, u32[]{:S(2)}) collective-permute-start(f32[2,24,384]{2,1,0:T(8,128)S(1)} %get-tuple-element.63.down), channel_id=1, source_target_pairs={{0,3},{1,0},{2,1},{3,2},{4,7},{5,4},{6,5},{7,6},{8,11},{9,8},{10,9... | collective-permute-start | bytes 221192 | tf_op jit(solution)/shard_map/ppermute | solution.py:37
  24.7 1.2 %collective-permute-start.6 = (f32[24,384]{1,0:T(8,128)S(1)}, f32[24,384]{1,0:T(8,128)S(1)}, u32[]{:S(2)}, u32[]{:S(2)}) collective-permute-start(f32[24,384]{1,0:T(8,128)S(1)} %get-tuple-element.72.refs_3_.refs_4_), channel_id=1, source_target_pairs={{0,1},{1,2},{2,3},{3,0},{4,5},{5,6},{6,7},{7,4},{8,9},{9,10},{10,1... | collective-permute-start | bytes 110600 | tf_op jit(solution)/shard_map/ppermute | solution.py:37
  25.9 1.2 %collective-permute-start.10 = (s32[29,8,256]{2,1,0:T(8,128)S(1)}, s32[29,8,256]{2,1,0:T(8,128)S(1)}, u32[]{:S(2)}, u32[]{:S(2)}) collective-permute-start(s32[29,8,256]{2,1,0:T(8,128)S(1)} %get-tuple-element.77), channel_id=1, source_target_pairs={{0,4},{4,0},{1,5},{5,1},{2,6},{6,2},{3,7},{7,3},{8,12},{12,8},{9,1... | collective-permute-start | bytes 712712 | tf_op jit(solution)/shard_map/ppermute | solution.py:41
  27.4 1.1 %collective-permute-done.2.more_pairs.outer = f32[43,8,256]{2,1,0:T(8,128)S(1)} collective-permute-done((f32[43,8,256]{2,1,0:T(8,128)S(1)}, f32[43,8,256]{2,1,0:T(8,128)S(1)}, u32[]{:S(2)}, u32[]{:S(2)}) %collective-permute-start.2) | collective-permute-done | bytes 352288 | tf_op jit(solution)/shard_map/ppermute | solution.py:41
  28.5 0.9 %shard_map.55 = (f32[2,16,24,384]{3,2,1,0:T(8,128)S(1)}, f32[2,16,24,384]{3,2,1,0:T(8,128)S(1)}) custom-call(s32[2]{0:T(128)S(1)} %bitcast.8, bf16[4,2,16,16,256]{4,3,2,1,0:T(8,128)(2,1)S(1)} %get-tuple-element.54.coef, f32[46,8,256]{2,1,0:T(8,128)S(1)} %collective-permute-done.edge_in, f32[43,8,256]{2,1,0:T(8,128)S(1)} %collective-permute-done.1.pairs, ...), custom_call_target="tpu_custom_call" | custom-call | tf_op jit(solution)/shard_map/pallas_call | solution.py:63
  29.4 1.2 %shard_map.56 = (f32[16,24,384]{2,1,0:T(8,128)S(1)}, f32[16,24,384]{2,1,0:T(8,128)S(1)}) custom-call(f32[2,16,24,384]{3,2,1,0:T(8,128)S(1)} %get-tuple-element.65.wide_ax, f32[2,16,24,384]{3,2,1,0:T(8,128)S(1)} %get-tuple-element.62.wide_yz.refs_2_.refs_3_, f32[16,24,256]{2,1,0:T(8,128)S(1)} %get-tuple-element.66.edge_start, ...), custom_call_target="tpu_custom_call" | custom-call | tf_op jit(solution)/shard_map/pallas_call | solution.py:63
  30.9 3.8 %collective-permute-start.7 = (f32[24,384]{1,0:T(8,128)S(1)}, f32[24,384]{1,0:T(8,128)S(1)}, u32[]{:S(2)}, u32[]{:S(2)}) collective-permute-start(f32[24,384]{1,0:T(8,128)S(1)} %get-tuple-element.74), channel_id=1, source_target_pairs={{0,1},{1,2},{2,3},{3,0},{4,5},{5,6},{6,7},{7,4},{8,9},{9,10},{10,1... | collective-permute-start | bytes 110600 | tf_op jit(solution)/shard_map/ppermute | solution.py:37
  34.7 1.2 %collective-permute-start.9 = (f32[2,16,384]{2,1,0:T(8,128)S(1)}, f32[2,16,384]{2,1,0:T(8,128)S(1)}, u32[]{:S(2)}, u32[]{:S(2)}) collective-permute-start(f32[2,16,384]{2,1,0:T(8,128)S(1)} %get-tuple-element.76), channel_id=1, source_target_pairs={{0,4},{4,0},{1,5},{5,1},{2,6},{6,2},{3,7},{7,3},{8,12},{12,8},{9,1... | collective-permute-start | bytes 147464 | tf_op jit(solution)/shard_map/ppermute | solution.py:41
  36.3 1.1 %shard_map.59 = (f32[16,24,384]{2,1,0:T(8,128)S(1)}, f32[16,24,384]{2,1,0:T(8,128)S(1)}, f32[16,24,256]{2,1,0:T(8,128)S(1)}) custom-call(f32[2,16,24,384]{3,2,1,0:T(8,128)S(1)} %get-tuple-element.65.wide_ax, f32[2,16,24,384]{3,2,1,0:T(8,128)S(1)} %get-tuple-element.62.wide_yz.refs_2_.refs_3_, ...), custom_call_target="tpu_custom_call" | custom-call | tf_op jit(solution)/shard_map/pallas_call | solution.py:63
  37.4 1.0 %collective-permute-done.8.high_face.refs_1_ = f32[1,24,384]{2,1,0:T(8,128)S(1)} collective-permute-done((f32[1,24,384]{2,1,0:T(8,128)S(1)}, f32[1,24,384]{2,1,0:T(8,128)S(1)}, u32[]{:S(2)}, u32[]{:S(2)}) %collective-permute-start.8) | collective-permute-done | bytes 36896 | tf_op jit(solution)/shard_map/ppermute | solution.py:37
  38.4 1.3 %collective-permute-start.13 = (f32[2,16,384]{2,1,0:T(8,128)S(1)}, f32[2,16,384]{2,1,0:T(8,128)S(1)}, u32[]{:S(2)}, u32[]{:S(2)}) collective-permute-start(f32[2,16,384]{2,1,0:T(8,128)S(1)} %get-tuple-element.86), channel_id=1, source_target_pairs={{0,4},{4,0},{1,5},{5,1},{2,6},{6,2},{3,7},{7,3},{8,12},{12,8},{9,1... | collective-permute-start | bytes 147464 | tf_op jit(solution)/shard_map/ppermute | solution.py:41
  39.7 2.4 %collective-permute-start.11 = (f32[24,384]{1,0:T(8,128)S(1)}, f32[24,384]{1,0:T(8,128)S(1)}, u32[]{:S(2)}, u32[]{:S(2)}) collective-permute-start(f32[24,384]{1,0:T(8,128)S(1)} %get-tuple-element.84), channel_id=1, source_target_pairs={{0,1},{1,2},{2,3},{3,0},{4,5},{5,6},{6,7},{7,4},{8,9},{9,10},{10,1... | collective-permute-start | bytes 110600 | tf_op jit(solution)/shard_map/ppermute | solution.py:37
  42.4 1.3 %shard_map.61 = (f32[16,24,384]{2,1,0:T(8,128)S(1)}, f32[16,24,384]{2,1,0:T(8,128)S(1)}, f32[16,24,256]{2,1,0:T(8,128)S(1)}) custom-call(f32[2,16,24,384]{3,2,1,0:T(8,128)S(1)} %get-tuple-element.65.wide_ax, f32[2,16,24,384]{3,2,1,0:T(8,128)S(1)} %get-tuple-element.62.wide_yz.refs_2_.refs_3_, ...), custom_call_target="tpu_custom_call" | custom-call | tf_op jit(solution)/shard_map/pallas_call | solution.py:63
  43.7 2.1 %collective-permute-done.12.high_face.refs_1_ = f32[1,24,384]{2,1,0:T(8,128)S(1)} collective-permute-done((f32[1,24,384]{2,1,0:T(8,128)S(1)}, f32[1,24,384]{2,1,0:T(8,128)S(1)}, u32[]{:S(2)}, u32[]{:S(2)}) %collective-permute-start.12) | collective-permute-done | bytes 36896 | tf_op jit(solution)/shard_map/ppermute | solution.py:37
  46.2 1.2 %collective-permute-start.15 = (f32[24,384]{1,0:T(8,128)S(1)}, f32[24,384]{1,0:T(8,128)S(1)}, u32[]{:S(2)}, u32[]{:S(2)}) collective-permute-start(f32[24,384]{1,0:T(8,128)S(1)} %get-tuple-element.92), channel_id=1, source_target_pairs={{0,1},{1,2},{2,3},{3,0},{4,5},{5,6},{6,7},{7,4},{8,9},{9,10},{10,1... | collective-permute-start | bytes 110600 | tf_op jit(solution)/shard_map/ppermute | solution.py:37
  47.4 1.2 %shard_map.63 = (f32[16,24,384]{2,1,0:T(8,128)S(1)}, f32[16,24,384]{2,1,0:T(8,128)S(1)}, f32[16,24,256]{2,1,0:T(8,128)S(1)}) custom-call(f32[2,16,24,384]{3,2,1,0:T(8,128)S(1)} %get-tuple-element.65.wide_ax, f32[2,16,24,384]{3,2,1,0:T(8,128)S(1)} %get-tuple-element.62.wide_yz.refs_2_.refs_3_, ...), custom_call_target="tpu_custom_call" | custom-call | tf_op jit(solution)/shard_map/pallas_call | solution.py:63
  48.7 2.1 %collective-permute-done.16.high_face.refs_1_ = f32[1,24,384]{2,1,0:T(8,128)S(1)} collective-permute-done((f32[1,24,384]{2,1,0:T(8,128)S(1)}, f32[1,24,384]{2,1,0:T(8,128)S(1)}, u32[]{:S(2)}, u32[]{:S(2)}) %collective-permute-start.16) | collective-permute-done | bytes 36896 | tf_op jit(solution)/shard_map/ppermute | solution.py:37
  51.2 0.5 collective-permute-start.18
  51.7 1.1 %shard_map.65 = (f32[16,24,256]{2,1,0:T(8,128)S(1)}, f32[16,24,256]{2,1,0:T(8,128)S(1)}) custom-call(f32[2,16,24,384]{3,2,1,0:T(8,128)S(1)} %get-tuple-element.65.wide_ax, f32[2,16,24,384]{3,2,1,0:T(8,128)S(1)} %get-tuple-element.62.wide_yz.refs_2_.refs_3_, f32[2,24,384]{2,1,0:T(8,128)S(1)} %collective-permute-done.5.refs_6_.refs_7_.rim_face, ...), custom_call_target="tpu_custom_call" | custom-call | tf_op jit(solution)/shard_map/pallas_call | solution.py:63
  52.9 2.2 %collective-permute-done.19.high_face = f32[1,24,384]{2,1,0:T(8,128)S(1)} collective-permute-done((f32[1,24,384]{2,1,0:T(8,128)S(1)}, f32[1,24,384]{2,1,0:T(8,128)S(1)}, u32[]{:S(2)}, u32[]{:S(2)}) %collective-permute-start.19) | collective-permute-done | bytes 36896 | tf_op jit(solution)/shard_map/ppermute | solution.py:37
  55.1 0.9 %shard_map.66 = (f32[16,24,256]{2,1,0:T(8,128)}, f32[16,24,256]{2,1,0:T(8,128)}) custom-call(f32[2,16,24,384]{3,2,1,0:T(8,128)S(1)} %get-tuple-element.62.wide_yz.refs_2_.refs_3_, f32[2,24,384]{2,1,0:T(8,128)S(1)} %collective-permute-done.5.refs_6_.refs_7_.rim_face, f32[3,16,384]{2,1,0:T(8,128)S(1)} %get-tuple-element.64.refs_7_.refs_8_.rim_rows, ...), custom_call_target="tpu_custom_call" | custom-call | tf_op jit(solution)/shard_map/pallas_call | solution.py:63
  (32 shorter events, 2.0 us)
Async XLA Ops:
  0.6 4.3 %copy-start = (s32[2,1,1]{0,2,1:T(1,128)S(1)}, s32[2,1,1]{0,2,1:T(1,128)}, u32[]{:S(2)}) copy-start(s32[2,1,1]{0,2,1:T(1,128)} %param.5) | copy-start | bytes 28
  2.8 10.6 %collective-permute-start = (f32[46,8,256]{2,1,0:T(8,128)S(1)}, f32[46,8,256]{2,1,0:T(8,128)S(1)}, u32[]{:S(2)}, u32[]{:S(2)}) collective-permute-start(f32[46,8,256]{2,1,0:T(8,128)S(1)} %get-tuple-element.55._), channel_id=1, source_target_pairs={{0,4},{4,0},{1,5},{5,1},{2,6},{6,2},{3,7},{7,3},{8,12},{12,8},{9,1... | collective-permute-start | bytes 1130504 | tf_op jit(solution)/shard_map/ppermute | solution.py:41
  5.6 21.5 %collective-permute-start.1 = (f32[43,8,256]{2,1,0:T(8,128)S(1)}, f32[43,8,256]{2,1,0:T(8,128)S(1)}, u32[]{:S(2)}, u32[]{:S(2)}) collective-permute-start(f32[43,8,256]{2,1,0:T(8,128)S(1)} %shard_map.51._), channel_id=1, source_target_pairs={{0,4},{4,0},{1,5},{5,1},{2,6},{6,2},{3,7},{7,3},{8,12},{12,8},{9,1... | collective-permute-start | bytes 1056776 | tf_op jit(solution)/shard_map/ppermute | solution.py:41
  9.2 19.3 %collective-permute-start.2 = (f32[43,8,256]{2,1,0:T(8,128)S(1)}, f32[43,8,256]{2,1,0:T(8,128)S(1)}, u32[]{:S(2)}, u32[]{:S(2)}) collective-permute-start(f32[43,8,256]{2,1,0:T(8,128)S(1)} %get-tuple-element.57), channel_id=1, source_target_pairs={{0,4},{4,0},{1,5},{5,1},{2,6},{6,2},{3,7},{7,3},{8,12},{12,8},{9,1... | collective-permute-start | bytes 1056776 | tf_op jit(solution)/shard_map/ppermute | solution.py:41
  14.7 4.7 %collective-permute-start.3 = (f32[10,8,128]{2,1,0:T(8,128)S(1)}, f32[10,8,128]{2,1,0:T(8,128)S(1)}, u32[]{:S(2)}, u32[]{:S(2)}) collective-permute-start(f32[10,8,128]{2,1,0:T(8,128)S(1)} %get-tuple-element.59.right), channel_id=1, source_target_pairs={{0,8},{8,16},{16,24},{24,0},{1,9},{9,17},{17,25},{25,1},{2,10},{10... | collective-permute-start | bytes 122888 | tf_op jit(solution)/shard_map/ppermute | solution.py:37
  16.0 3.4 %collective-permute-start.4 = (f32[10,8,128]{2,1,0:T(8,128)S(1)}, f32[10,8,128]{2,1,0:T(8,128)S(1)}, u32[]{:S(2)}, u32[]{:S(2)}) collective-permute-start(f32[10,8,128]{2,1,0:T(8,128)S(1)} %get-tuple-element.58.left), channel_id=1, source_target_pairs={{0,24},{8,0},{16,8},{24,16},{1,25},{9,1},{17,9},{25,17},{2,26},{10... | collective-permute-start | bytes 122888 | tf_op jit(solution)/shard_map/ppermute | solution.py:37
  20.7 10.0 %collective-permute-start.5 = (f32[2,24,384]{2,1,0:T(8,128)S(1)}, f32[2,24,384]{2,1,0:T(8,128)S(1)}, u32[]{:S(2)}, u32[]{:S(2)}) collective-permute-start(f32[2,24,384]{2,1,0:T(8,128)S(1)} %get-tuple-element.63.down), channel_id=1, source_target_pairs={{0,3},{1,0},{2,1},{3,2},{4,7},{5,4},{6,5},{7,6},{8,11},{9,8},{10,9... | collective-permute-start | bytes 221192 | tf_op jit(solution)/shard_map/ppermute | solution.py:37
  24.7 6.0 %collective-permute-start.6 = (f32[24,384]{1,0:T(8,128)S(1)}, f32[24,384]{1,0:T(8,128)S(1)}, u32[]{:S(2)}, u32[]{:S(2)}) collective-permute-start(f32[24,384]{1,0:T(8,128)S(1)} %get-tuple-element.72.refs_3_.refs_4_), channel_id=1, source_target_pairs={{0,1},{1,2},{2,3},{3,0},{4,5},{5,6},{6,7},{7,4},{8,9},{9,10},{10,1... | collective-permute-start | bytes 110600 | tf_op jit(solution)/shard_map/ppermute | solution.py:37
  25.9 10.0 %collective-permute-start.10 = (s32[29,8,256]{2,1,0:T(8,128)S(1)}, s32[29,8,256]{2,1,0:T(8,128)S(1)}, u32[]{:S(2)}, u32[]{:S(2)}) collective-permute-start(s32[29,8,256]{2,1,0:T(8,128)S(1)} %get-tuple-element.77), channel_id=1, source_target_pairs={{0,4},{4,0},{1,5},{5,1},{2,6},{6,2},{3,7},{7,3},{8,12},{12,8},{9,1... | collective-permute-start | bytes 712712 | tf_op jit(solution)/shard_map/ppermute | solution.py:41
  27.1 15.3 %collective-permute-start.14 = (s32[12,8,256]{2,1,0:T(8,128)S(1)}, s32[12,8,256]{2,1,0:T(8,128)S(1)}, u32[]{:S(2)}, u32[]{:S(2)}) collective-permute-start(s32[12,8,256]{2,1,0:T(8,128)S(1)} %get-tuple-element.90), channel_id=1, source_target_pairs={{0,4},{4,0},{1,5},{5,1},{2,6},{6,2},{3,7},{7,3},{8,12},{12,8},{9,1... | collective-permute-start | bytes 294920 | tf_op jit(solution)/shard_map/ppermute | solution.py:41
  30.9 6.5 %collective-permute-start.7 = (f32[24,384]{1,0:T(8,128)S(1)}, f32[24,384]{1,0:T(8,128)S(1)}, u32[]{:S(2)}, u32[]{:S(2)}) collective-permute-start(f32[24,384]{1,0:T(8,128)S(1)} %get-tuple-element.74), channel_id=1, source_target_pairs={{0,1},{1,2},{2,3},{3,0},{4,5},{5,6},{6,7},{7,4},{8,9},{9,10},{10,1... | collective-permute-start | bytes 110600 | tf_op jit(solution)/shard_map/ppermute | solution.py:37
  34.7 3.7 %collective-permute-start.8 = (f32[1,24,384]{2,1,0:T(8,128)S(1)}, f32[1,24,384]{2,1,0:T(8,128)S(1)}, u32[]{:S(2)}, u32[]{:S(2)}) collective-permute-start(f32[1,24,384]{2,1,0:T(8,128)S(1)} %get-tuple-element.75), channel_id=1, source_target_pairs={{0,3},{1,0},{2,1},{3,2},{4,7},{5,4},{6,5},{7,6},{8,11},{9,8},{10,9... | collective-permute-start | bytes 110600 | tf_op jit(solution)/shard_map/ppermute | solution.py:37
  34.7 3.7 %collective-permute-start.9 = (f32[2,16,384]{2,1,0:T(8,128)S(1)}, f32[2,16,384]{2,1,0:T(8,128)S(1)}, u32[]{:S(2)}, u32[]{:S(2)}) collective-permute-start(f32[2,16,384]{2,1,0:T(8,128)S(1)} %get-tuple-element.76), channel_id=1, source_target_pairs={{0,4},{4,0},{1,5},{5,1},{2,6},{6,2},{3,7},{7,3},{8,12},{12,8},{9,1... | collective-permute-start | bytes 147464 | tf_op jit(solution)/shard_map/ppermute | solution.py:41
  38.4 7.4 %collective-permute-start.13 = (f32[2,16,384]{2,1,0:T(8,128)S(1)}, f32[2,16,384]{2,1,0:T(8,128)S(1)}, u32[]{:S(2)}, u32[]{:S(2)}) collective-permute-start(f32[2,16,384]{2,1,0:T(8,128)S(1)} %get-tuple-element.86), channel_id=1, source_target_pairs={{0,4},{4,0},{1,5},{5,1},{2,6},{6,2},{3,7},{7,3},{8,12},{12,8},{9,1... | collective-permute-start | bytes 147464 | tf_op jit(solution)/shard_map/ppermute | solution.py:41
  39.7 4.0 %collective-permute-start.11 = (f32[24,384]{1,0:T(8,128)S(1)}, f32[24,384]{1,0:T(8,128)S(1)}, u32[]{:S(2)}, u32[]{:S(2)}) collective-permute-start(f32[24,384]{1,0:T(8,128)S(1)} %get-tuple-element.84), channel_id=1, source_target_pairs={{0,1},{1,2},{2,3},{3,0},{4,5},{5,6},{6,7},{7,4},{8,9},{9,10},{10,1... | collective-permute-start | bytes 110600 | tf_op jit(solution)/shard_map/ppermute | solution.py:37
  42.2 3.7 %collective-permute-start.12 = (f32[1,24,384]{2,1,0:T(8,128)S(1)}, f32[1,24,384]{2,1,0:T(8,128)S(1)}, u32[]{:S(2)}, u32[]{:S(2)}) collective-permute-start(f32[1,24,384]{2,1,0:T(8,128)S(1)} %get-tuple-element.85), channel_id=1, source_target_pairs={{0,3},{1,0},{2,1},{3,2},{4,7},{5,4},{6,5},{7,6},{8,11},{9,8},{10,9... | collective-permute-start | bytes 110600 | tf_op jit(solution)/shard_map/ppermute | solution.py:37
  42.2 9.6 %collective-permute-start.21 = (s32[16,8,256]{2,1,0:T(8,128)S(1)}, s32[16,8,256]{2,1,0:T(8,128)S(1)}, u32[]{:S(2)}, u32[]{:S(2)}) collective-permute-start(s32[16,8,256]{2,1,0:T(8,128)S(1)} %get-tuple-element.103), channel_id=1, source_target_pairs={{0,4},{4,0},{1,5},{5,1},{2,6},{6,2},{3,7},{7,3},{8,12},{12,8},{9,1... | collective-permute-start | bytes 393224 | tf_op jit(solution)/shard_map/ppermute | solution.py:41
  45.9 4.9 %collective-permute-start.17 = (f32[2,16,384]{2,1,0:T(8,128)S(1)}, f32[2,16,384]{2,1,0:T(8,128)S(1)}, u32[]{:S(2)}, u32[]{:S(2)}) collective-permute-start(f32[2,16,384]{2,1,0:T(8,128)S(1)} %get-tuple-element.94), channel_id=1, source_target_pairs={{0,4},{4,0},{1,5},{5,1},{2,6},{6,2},{3,7},{7,3},{8,12},{12,8},{9,1... | collective-permute-start | bytes 147464 | tf_op jit(solution)/shard_map/ppermute | solution.py:41
  46.2 2.4 %collective-permute-start.15 = (f32[24,384]{1,0:T(8,128)S(1)}, f32[24,384]{1,0:T(8,128)S(1)}, u32[]{:S(2)}, u32[]{:S(2)}) collective-permute-start(f32[24,384]{1,0:T(8,128)S(1)} %get-tuple-element.92), channel_id=1, source_target_pairs={{0,1},{1,2},{2,3},{3,0},{4,5},{5,6},{6,7},{7,4},{8,9},{9,10},{10,1... | collective-permute-start | bytes 110600 | tf_op jit(solution)/shard_map/ppermute | solution.py:37
  47.4 3.4 %collective-permute-start.16 = (f32[1,24,384]{2,1,0:T(8,128)S(1)}, f32[1,24,384]{2,1,0:T(8,128)S(1)}, u32[]{:S(2)}, u32[]{:S(2)}) collective-permute-start(f32[1,24,384]{2,1,0:T(8,128)S(1)} %get-tuple-element.93), channel_id=1, source_target_pairs={{0,3},{1,0},{2,1},{3,2},{4,7},{5,4},{6,5},{7,6},{8,11},{9,8},{10,9... | collective-permute-start | bytes 110600 | tf_op jit(solution)/shard_map/ppermute | solution.py:37
  50.9 4.2 %collective-permute-start.20 = (f32[2,16,384]{2,1,0:T(8,128)S(1)}, f32[2,16,384]{2,1,0:T(8,128)S(1)}, u32[]{:S(2)}, u32[]{:S(2)}) collective-permute-start(f32[2,16,384]{2,1,0:T(8,128)S(1)} %get-tuple-element.100), channel_id=1, source_target_pairs={{0,4},{4,0},{1,5},{5,1},{2,6},{6,2},{3,7},{7,3},{8,12},{12,8},{9,1... | collective-permute-start | bytes 147464 | tf_op jit(solution)/shard_map/ppermute | solution.py:41
  51.2 1.7 %collective-permute-start.18 = (f32[24,384]{1,0:T(8,128)S(1)}, f32[24,384]{1,0:T(8,128)S(1)}, u32[]{:S(2)}, u32[]{:S(2)}) collective-permute-start(f32[24,384]{1,0:T(8,128)S(1)} %get-tuple-element.98), channel_id=1, source_target_pairs={{0,1},{1,2},{2,3},{3,0},{4,5},{5,6},{6,7},{7,4},{8,9},{9,10},{10,1... | collective-permute-start | bytes 110600 | tf_op jit(solution)/shard_map/ppermute | solution.py:37
  51.7 3.4 %collective-permute-start.19 = (f32[1,24,384]{2,1,0:T(8,128)S(1)}, f32[1,24,384]{2,1,0:T(8,128)S(1)}, u32[]{:S(2)}, u32[]{:S(2)}) collective-permute-start(f32[1,24,384]{2,1,0:T(8,128)S(1)} %get-tuple-element.99), channel_id=1, source_target_pairs={{0,3},{1,0},{2,1},{3,2},{4,7},{5,4},{6,5},{7,6},{8,11},{9,8},{10,9... | collective-permute-start | bytes 110600 | tf_op jit(solution)/shard_map/ppermute | solution.py:37

commit v6 on v5

--- a/solution.py
+++ b/solution.py
@@ -227,7 +227,7 @@
 def pair_tile(ids, coef, half, number):
     part, k, z = pair_order(coef.shape[2])[number]
     place = units_of(ids, half)[k]
-    return coef_unit(coef, part, place, z) + SHIFT * coef_unit(coef, part + 1, place, z)
+    return jnp.where(place[0], coef_unit(coef, part, place, z) + SHIFT * coef_unit(coef, part + 1, place, z), 0.0)
 
 
 def beyond_at(planes, unit_rows):
@@ -470,25 +470,45 @@
         beyond_rows[...] = jnp.zeros_like(beyond_rows)
 
 
-def spread_kernel(ids, coef, edge_in, pairs, more_pairs, ghosts, wide_ax, wide_yz):
+def spread_kernel(
+    ids, coef, edge_in, pairs, ghosts, own_rows, down, partial, middle, wide_yz, own_ax, gain, diagonal, middle_out
+):
     planes, columns, rows = coef.shape[2], coef.shape[4], coef.shape[3] // 2
     places, pairs_at = units_of(ids, lax.axis_index("gy") % 2), beyond_at(planes, rows)[1]
+    even = lax.axis_index("gy") % 2 == 0
+    middle_out[...] = middle[...]
     for part in (0, 1):
-        wide_ax[part, :, :, columns:] = ghosts[part]
         wide_yz[part, :, :, columns:] = ghosts[2 + part]
     for number, (part, k, z) in enumerate(pair_order(planes)):
-        place = places[k]
         at = slice(k * rows, (k + 1) * rows)
-        place_in = number - FIRST_PAIRS
-        if place_in < 0:
-            got = edge_in[pairs_at + number]
-        elif place_in < pairs.shape[0]:
-            got = pairs[place_in]
-        else:
-            got = more_pairs[place_in - pairs.shape[0]]
+        held = places[k][0]
+        own = [coef_unit(coef, part + j, places[k], z) for j in (0, 1)]
+        if part == 0:
+            for j in (0, 1):
+                own_ax[j, z, at] = jnp.where(held, own[j], 0.0)
+            continue
+        got = edge_in[pairs_at + number] if number < FIRST_PAIRS else pairs[number - FIRST_PAIRS]
         for j, value in enumerate(parted(got)):
-            out = wide_yz if part else wide_ax
-            out[j, z, at, :columns] = jnp.where(place[0], coef_unit(coef, part + j, place, z), value)
+            wide_yz[j, z, at, :columns] = jnp.where(held, own[j], value)
+    rows *= 3
+    unit_rows = rows // 3
+    width = wide_yz.shape[3]
+    row = row_of((rows, columns))
+    inner = jnp.where(even, 2 * unit_rows, unit_rows)
+    for z in range(planes):
+        beta_y, beta_z, at = wide_yz[0, z], wide_yz[1, z], slice(z, z + 1)
+        found = partial[z]
+        if z == 0:
+            found = found - (beta_z * down[0])[:, :columns]
+        between = jnp.where(even, own_rows[2, at] - own_rows[1, at], own_rows[1, at] - own_rows[0, at])
+        beta = jnp.where(even, beta_y[2 * unit_rows : 2 * unit_rows + 1], beta_y[unit_rows : unit_rows + 1])
+        between = beta[:, :columns] * between
+        found = found + jnp.where(row == inner, -between, jnp.where(row == inner - 1, between, 0.0))
+        low = jnp.where(even, beta_y[0:1, :columns] * own_rows[0, at], 0.0)
+        gain[z] = found - jnp.where(row == 0, low, 0.0)
+        next_z = wide_yz[1, z + 1] if z + 1 < planes else 0.0
+        next_y = jnp.where(row_of((rows, width)) == rows - 1, 0.0, pltpu.roll(beta_y, rows - 1, 0))
+        diagonal[z] = beta_y + next_y + beta_z + next_z
 
 
 def image_plane(value, lower_flux, upper_flux, alpha, beta_x, beta_y, rim_row):
@@ -529,49 +549,33 @@
 
 
 def first_kernel(
-    wide_ax, wide_yz, edge_start, rhs_ghost, own_rows, down, partial, extra, inverse
+    pairs, more_pairs, own_ax, ghosts, wide_yz, edge_start, rhs_ghost, gain, diagonal, wide_ax, extra, inverse
 ):
     planes, rows, width = extra.shape
     columns = width - LANES
     unit_rows = rows // 3
-    even = lax.axis_index("gy") % 2 == 0
-
-    def coef(part, z):
-        return wide_ax[part, z] if part < 2 else wide_yz[part - 2, z]
+    for part in (0, 1):
+        wide_ax[part, :, :, columns:] = ghosts[part]
+    for number, (part, k, z) in enumerate(pair_order(planes)):
+        if part:
+            continue
+        at, place_in = slice(k * unit_rows, (k + 1) * unit_rows), number - FIRST_PAIRS
+        got = pairs[place_in] if place_in < pairs.shape[0] else more_pairs[place_in - pairs.shape[0]]
+        for j, value in enumerate(parted(got)):
+            wide_ax[j, z, at, :columns] = own_ax[j, z, at] + value
 
     def ring(part, z):
-        return edges(coef(part, z))
-
-    lane, row = lane_of((rows, columns)), row_of((rows, columns))
-    inner = jnp.where(even, 2 * unit_rows, unit_rows)
-    for z, (value,), image in images(
-        lambda z: (edge_start[z],),
-        ring,
-        planes,
-        None,
-        lambda z: None,
-    ):
+        return edges(wide_ax[part, z] if part < 2 else wide_yz[part - 2, z])
+
+    lane = lane_of((rows, columns))
+    for z, (value,), image in images(lambda z: (edge_start[z],), ring, planes, None, lambda z: None):
         flux = ring(1, z) * (value - pltpu.roll(value, 1, 1))
-        gain = jnp.where(lane == 0, -flux[:, :columns], 0.0)
+        near = jnp.where(lane == 0, -flux[:, :columns], 0.0)
         far = jnp.where(lane == columns - 1, pltpu.roll(flux, LANES - 1, 1)[:, :columns], 0.0)
-        gain = gain + far
-        if z == 0:
-            gain = gain - (wide_yz[1, 0] * down[0])[:, :columns]
-        beta_y = wide_yz[0, z]
-        at = slice(z, z + 1)
-        between = jnp.where(even, own_rows[2, at] - own_rows[1, at], own_rows[1, at] - own_rows[0, at])
-        beta = jnp.where(even, beta_y[2 * unit_rows : 2 * unit_rows + 1], beta_y[unit_rows : unit_rows + 1])
-        between = beta[:, :columns] * between
-        gain = gain + jnp.where(row == inner, -between, jnp.where(row == inner - 1, between, 0.0))
-        low = jnp.where(even, beta_y[0:1, :columns] * own_rows[0, at], 0.0)
-        gain = gain - jnp.where(row == 0, low, 0.0)
-        extra[z, :, :columns] = gain + partial[z]
+        extra[z, :, :columns] = gain[z] + near + far
         extra[z, :, columns:] = rhs_ghost[z] - image[:, LANES:]
-        beta_x, beta_z = wide_ax[1, z], wide_yz[1, z]
-        next_z = wide_yz[1, z + 1] if z + 1 < planes else 0.0
-        next_y = jnp.where(row_of((rows, width)) == rows - 1, 0.0, pltpu.roll(beta_y, rows - 1, 0))
-        next_x = pltpu.roll(beta_x, width - 1, 1)
-        inverse[z] = 1.0 / (wide_ax[0, z] + beta_x + next_x + beta_y + next_y + beta_z + next_z)
+        beta_x = wide_ax[1, z]
+        inverse[z] = 1.0 / (wide_ax[0, z] + beta_x + pltpu.roll(beta_x, width - 1, 1) + diagonal[z])
 
 
 def start_rows(
@@ -796,7 +800,7 @@
         pairs_out,
         ids=True,
     )
-    outer_in, middle_in = swapped(outer_out), swapped(middle)
+    outer_in = swapped(outer_out)
     strip = f32(STRIPS_AT[-1], half, LANES)
     left, right, outer_rows = call(
         functools.partial(strip_kernel, pairs),
@@ -835,11 +839,39 @@
     low_face, rim_face = shifted(up, "gz", 1), shifted(down, "gz", -1)
     if pairs > 1:
         rim_rows = row_ghosts(rows_out)
-    wide_ax, wide_yz = call(
-        spread_kernel, [coef_full, coef_full], ids, coef, edge_in, pairs_in, outer_in, ghosts, ids=True
+    wide_yz, own_ax, gain, diagonal, middle = call(
+        spread_kernel,
+        [
+            coef_full,
+            f32(2, planes, rows, columns),
+            own,
+            full,
+            jax.ShapeDtypeStruct(middle.shape, middle.dtype),
+        ],
+        ids,
+        coef,
+        edge_in,
+        pairs_in,
+        ghosts,
+        own_rows,
+        down,
+        partial,
+        middle,
+        ids=True,
     )
-    extra, part_inverse = call(
-        first_kernel, [full, full], wide_ax, wide_yz, edge_start, rhs_ghost, own_rows, down, partial
+    middle_in = swapped(middle)
+    wide_ax, extra, part_inverse = call(
+        first_kernel,
+        [coef_full, full, full],
+        pairs_in,
+        outer_in,
+        own_ax,
+        ghosts,
+        wide_yz,
+        edge_start,
+        rhs_ghost,
+        gain,
+        diagonal,
     )
     first_list, second_list = chebyshev_weights(SWEEPS)
     faces = [f32(rows, width), f32(1, rows, width), f32(2, planes, width)]

time: 56.2 us -> 54.9 us (0.977)
  starting transfers between devices: 25 us -> 24 us
    ppermute x10, waiting for transfers between devices: 3.93 us -> 2.83 us  [swapped(): lax.ppermute(value, 'gy', [(i, i ^ 1) for i in range(lax.axis_size('gy'))])]
    ppermute x12, waiting for transfers between devices: 8.75 us -> 9.61 us  [shifted(): lax.ppermute(value, axis, [(i, (i + steps) % count) for i in range(count)])]
    ppermute x12, starting transfers between devices: 16.5 us -> 15.9 us  [shifted(): lax.ppermute(value, axis, [(i, (i + steps) % count) for i in range(count)])]
where the time goes in v6:
time: 54.9 us; the launch traced here: 54.8 us
  starting transfers between devices  24 us (44%)
  Pallas kernels  17.6 us (32%)
  waiting for transfers between devices  12.4 us (23%)
  between operations  0.79 us (1%)
    ppermute x12, starting transfers between devices, shifted(): lax.ppermute(value, axis, [(i, (i + steps) % count) for i in range(count)])  15.9 us
    pallas_call x16, Pallas kernels, call(): pl.pallas_call(kernel, out_shape=outs, in_specs=specs, out_specs=out_spec...  15.5 us
    ppermute x12, waiting for transfers between devices, shifted(): lax.ppermute(value, axis, [(i, (i + steps) % count) for i in range(count)])  9.61 us
    ppermute x10, starting transfers between devices, swapped(): lax.ppermute(value, 'gy', [(i, i ^ 1) for i in range(lax.axis_size('gy'))])  8.06 us
    ppermute x10, waiting for transfers between devices, swapped(): lax.ppermute(value, 'gy', [(i, i ^ 1) for i in range(lax.axis_size('gy'))])  2.83 us
    pallas_call x1, Pallas kernels, local(): pl.pallas_call(functools.partial(edge_kernel, pairs), out_shape=[f32(*old...  2.15 us
  transfers between devices with their start and end apart: 22, of which 7 were waited for; matrix products, arithmetic and copies ran while one was open for 0% of the time, Pallas kernels for 26%

profile of v6, /device:TPU:1, one launch (start us, length us, event | category | flops | bytes accessed | tf_op | source)
XLA Modules:
  0.0 54.8 jit_solution(3808861506553435144)
XLA Ops:
  0.6 2.2 %shard_map.50 = (f32[2,2,16,16,256]{4,3,2,1,0:T(8,128)S(1)}, bf16[4,2,16,16,256]{4,3,2,1,0:T(8,128)(2,1)S(1)}, f32[46,8,256]{2,1,0:T(8,128)S(1)}) custom-call(s32[2]{0:T(128)} %bitcast.3, f32[2,2,16,16,256]{4,3,2,1,0:T(8,128)} %fields_in.1, bf16[4,2,16,16,256]{4,3,2,1,0:T(8,128)(2,1)} %coef_in.1), custom_call_target="tpu_custom_call" | custom-call | tf_op jit(solution)/shard_map/pallas_call | solution.py:767
  2.8 2.1 %collective-permute-start = (f32[46,8,256]{2,1,0:T(8,128)S(1)}, f32[46,8,256]{2,1,0:T(8,128)S(1)}, u32[]{:S(2)}, u32[]{:S(2)}) collective-permute-start(f32[46,8,256]{2,1,0:T(8,128)S(1)} %get-tuple-element.59._), channel_id=1, source_target_pairs={{0,4},{4,0},{1,5},{5,1},{2,6},{6,2},{3,7},{7,3},{8,12},{12,8},{9,1... | collective-permute-start | bytes 1130504 | tf_op jit(solution)/shard_map/ppermute | solution.py:41
  4.9 0.7 %shard_map.51._ = f32[43,8,256]{2,1,0:T(8,128)S(1)} custom-call(s32[2]{0:T(128)S(1)} %bitcast.4, bf16[4,2,16,16,256]{4,3,2,1,0:T(8,128)(2,1)S(1)} %get-tuple-element.58.coef, f32[46,8,256]{2,1,0:T(8,128)S(1)} %get-tuple-element.59._), custom_call_target="tpu_custom_call" | custom-call | tf_op jit(solution)/shard_map/pallas_call | solution.py:63
  5.7 3.5 %shard_map.54 = (f32[43,8,256]{2,1,0:T(8,128)S(1)}, s32[29,8,256]{2,1,0:T(8,128)S(1)}, f32[16,24,256]{2,1,0:T(8,128)S(1)}, f32[16,24,256]{2,1,0:T(8,128)S(1)}, s...) custom-call(s32[2]{0:T(128)S(1)} %bitcast.5, ...), custom_call_target="tpu_custom_call" | custom-call | tf_op jit(solution)/shard_map/pallas_call | solution.py:63
  9.2 1.4 %collective-permute-start.5 = (f32[43,8,256]{2,1,0:T(8,128)S(1)}, f32[43,8,256]{2,1,0:T(8,128)S(1)}, u32[]{:S(2)}, u32[]{:S(2)}) collective-permute-start(f32[43,8,256]{2,1,0:T(8,128)S(1)} %get-tuple-element.71), channel_id=1, source_target_pairs={{0,4},{4,0},{1,5},{5,1},{2,6},{6,2},{3,7},{7,3},{8,12},{12,8},{9,1... | collective-permute-start | bytes 1056776 | tf_op jit(solution)/shard_map/ppermute | solution.py:41
  10.6 2.8 %collective-permute-done.edge_in = f32[46,8,256]{2,1,0:T(8,128)S(1)} collective-permute-done((f32[46,8,256]{2,1,0:T(8,128)S(1)}, f32[46,8,256]{2,1,0:T(8,128)S(1)}, u32[]{:S(2)}, u32[]{:S(2)}) %collective-permute-start) | collective-permute-done | bytes 376864 | tf_op jit(solution)/shard_map/ppermute | solution.py:41
  13.4 1.3 %shard_map.52 = (f32[10,8,128]{2,1,0:T(8,128)S(1)}, f32[10,8,128]{2,1,0:T(8,128)S(1)}, f32[2,16,256]{2,1,0:T(8,128)S(1)}) custom-call(s32[2]{0:T(128)S(1)} %bitcast.6, f32[2,2,16,16,256]{4,3,2,1,0:T(8,128)S(1)} %get-tuple-element.60.fields, bf16[4,2,16,16,256]{4,3,2,1,0:T(8,128)(2,1)S(1)} %get-tuple-element.58.coef, ...), custom_call_target="tpu_custom_call" | custom-call | tf_op jit(solution)/shard_map/pallas_call | solution.py:63
  14.7 1.3 %collective-permute-start.2 = (f32[10,8,128]{2,1,0:T(8,128)S(1)}, f32[10,8,128]{2,1,0:T(8,128)S(1)}, u32[]{:S(2)}, u32[]{:S(2)}) collective-permute-start(f32[10,8,128]{2,1,0:T(8,128)S(1)} %get-tuple-element.62.right), channel_id=1, source_target_pairs={{0,8},{8,16},{16,24},{24,0},{1,9},{9,17},{17,25},{25,1},{2,10},{10... | collective-permute-start | bytes 122888 | tf_op jit(solution)/shard_map/ppermute | solution.py:37
  16.0 2.1 %collective-permute-start.3 = (f32[10,8,128]{2,1,0:T(8,128)S(1)}, f32[10,8,128]{2,1,0:T(8,128)S(1)}, u32[]{:S(2)}, u32[]{:S(2)}) collective-permute-start(f32[10,8,128]{2,1,0:T(8,128)S(1)} %get-tuple-element.61.left), channel_id=1, source_target_pairs={{0,24},{8,0},{16,8},{24,16},{1,25},{9,1},{17,9},{25,17},{2,26},{10... | collective-permute-start | bytes 122888 | tf_op jit(solution)/shard_map/ppermute | solution.py:37
  18.1 1.3 %collective-permute-done.2.from_left = f32[10,8,128]{2,1,0:T(8,128)S(1)} collective-permute-done((f32[10,8,128]{2,1,0:T(8,128)S(1)}, f32[10,8,128]{2,1,0:T(8,128)S(1)}, u32[]{:S(2)}, u32[]{:S(2)}) %collective-permute-start.2) | collective-permute-done | bytes 40992 | tf_op jit(solution)/shard_map/ppermute | solution.py:37
  19.4 1.3 %shard_map.53 = (f32[16,24,256]{2,1,0:T(8,128)S(1)}, f32[16,24,128]{2,1,0:T(8,128)S(1)}, f32[4,16,24,128]{3,2,1,0:T(8,128)S(1)}, f32[3,16,256]{2,1,0:T(8,128)S(1...) custom-call(s32[2]{0:T(128)S(1)} %bitcast.7, ...), custom_call_target="tpu_custom_call" | custom-call | tf_op jit(solution)/shard_map/pallas_call | solution.py:63
  20.7 4.0 %collective-permute-start.4 = (f32[2,24,384]{2,1,0:T(8,128)S(1)}, f32[2,24,384]{2,1,0:T(8,128)S(1)}, u32[]{:S(2)}, u32[]{:S(2)}) collective-permute-start(f32[2,24,384]{2,1,0:T(8,128)S(1)} %get-tuple-element.66.down), channel_id=1, source_target_pairs={{0,3},{1,0},{2,1},{3,2},{4,7},{5,4},{6,5},{7,6},{8,11},{9,8},{10,9... | collective-permute-start | bytes 221192 | tf_op jit(solution)/shard_map/ppermute | solution.py:37
  24.7 1.2 %collective-permute-start.6 = (f32[24,384]{1,0:T(8,128)S(1)}, f32[24,384]{1,0:T(8,128)S(1)}, u32[]{:S(2)}, u32[]{:S(2)}) collective-permute-start(f32[24,384]{1,0:T(8,128)S(1)} %get-tuple-element.79.refs_3_.refs_4_), channel_id=1, source_target_pairs={{0,1},{1,2},{2,3},{3,0},{4,5},{5,6},{6,7},{7,4},{8,9},{9,10},{10,1... | collective-permute-start | bytes 110600 | tf_op jit(solution)/shard_map/ppermute | solution.py:37
  25.9 1.1 %shard_map.55 = (f32[2,16,24,384]{3,2,1,0:T(8,128)S(1)}, f32[2,16,24,256]{3,2,1,0:T(8,128)S(1)}, f32[16,24,256]{2,1,0:T(8,128)S(1)}, f32[16,24,384]{2,1,0:T(8,128)S(1)}, s32[29,8,256]{2,1,0:T(8,128)S(1)}) custom-call(s32[2]{0:T(128)S(1)} %bitcast.8, bf16[4,2,16,16,256]{4,3,2,1,0:T(8,128)(2,1)S(1)} %get-tuple-element.58.coef, ...), custom_call_target="tpu_custom_call" | custom-call | tf_op jit(solution)/shard_map/pallas_call | solution.py:63
  27.0 1.3 %collective-permute-start.10 = (s32[29,8,256]{2,1,0:T(8,128)S(1)}, s32[29,8,256]{2,1,0:T(8,128)S(1)}, u32[]{:S(2)}, u32[]{:S(2)}) collective-permute-start(s32[29,8,256]{2,1,0:T(8,128)S(1)} %get-tuple-element.84), channel_id=1, source_target_pairs={{0,4},{4,0},{1,5},{5,1},{2,6},{6,2},{3,7},{7,3},{8,12},{12,8},{9,1... | collective-permute-start | bytes 712712 | tf_op jit(solution)/shard_map/ppermute | solution.py:41
  28.5 1.2 %shard_map.56 = (f32[2,16,24,384]{3,2,1,0:T(8,128)S(1)}, f32[16,24,384]{2,1,0:T(8,128)S(1)}, f32[16,24,384]{2,1,0:T(8,128)S(1)}) custom-call(f32[43,8,256]{2,1,0:T(8,128)S(1)} %collective-permute-done.1.pairs, f32[43,8,256]{2,1,0:T(8,128)S(1)} %collective-permute-done.5.more_pairs.outer, f32[2,16,24,256]{3,2,1,0:T(8,128)S(1)} %get-tuple-element.72.own_ax, ...), custom_call_target="tpu_custom_call" | custom-call | tf_op jit(solution)/shard_map/pallas_call | solution.py:63
  30.0 1.3 %collective-permute-start.9 = (f32[2,16,384]{2,1,0:T(8,128)S(1)}, f32[2,16,384]{2,1,0:T(8,128)S(1)}, u32[]{:S(2)}, u32[]{:S(2)}) collective-permute-start(f32[2,16,384]{2,1,0:T(8,128)S(1)} %get-tuple-element.83), channel_id=1, source_target_pairs={{0,4},{4,0},{1,5},{5,1},{2,6},{6,2},{3,7},{7,3},{8,12},{12,8},{9,1... | collective-permute-start | bytes 147464 | tf_op jit(solution)/shard_map/ppermute | solution.py:41
  31.2 3.6 %collective-permute-start.7 = (f32[24,384]{1,0:T(8,128)S(1)}, f32[24,384]{1,0:T(8,128)S(1)}, u32[]{:S(2)}, u32[]{:S(2)}) collective-permute-start(f32[24,384]{1,0:T(8,128)S(1)} %get-tuple-element.81), channel_id=1, source_target_pairs={{0,1},{1,2},{2,3},{3,0},{4,5},{5,6},{6,7},{7,4},{8,9},{9,10},{10,1... | collective-permute-start | bytes 110600 | tf_op jit(solution)/shard_map/ppermute | solution.py:37
  35.2 1.1 %shard_map.59 = (f32[16,24,384]{2,1,0:T(8,128)S(1)}, f32[16,24,384]{2,1,0:T(8,128)S(1)}, f32[16,24,256]{2,1,0:T(8,128)S(1)}) custom-call(f32[2,16,24,384]{3,2,1,0:T(8,128)S(1)} %get-tuple-element.87.wide_ax, f32[2,16,24,384]{3,2,1,0:T(8,128)S(1)} %get-tuple-element.69.wide_yz.refs_2_.refs_3_, ...), custom_call_target="tpu_custom_call" | custom-call | tf_op jit(solution)/shard_map/pallas_call | solution.py:63
  36.4 1.8 %collective-permute-done.8.high_face.refs_1_ = f32[1,24,384]{2,1,0:T(8,128)S(1)} collective-permute-done((f32[1,24,384]{2,1,0:T(8,128)S(1)}, f32[1,24,384]{2,1,0:T(8,128)S(1)}, u32[]{:S(2)}, u32[]{:S(2)}) %collective-permute-start.8) | collective-permute-done | bytes 36896 | tf_op jit(solution)/shard_map/ppermute | solution.py:37
  38.3 0.6 %collective-permute-start.13 = (f32[2,16,384]{2,1,0:T(8,128)S(1)}, f32[2,16,384]{2,1,0:T(8,128)S(1)}, u32[]{:S(2)}, u32[]{:S(2)}) collective-permute-start(f32[2,16,384]{2,1,0:T(8,128)S(1)} %get-tuple-element.94), channel_id=1, source_target_pairs={{0,4},{4,0},{1,5},{5,1},{2,6},{6,2},{3,7},{7,3},{8,12},{12,8},{9,1... | collective-permute-start | bytes 147464 | tf_op jit(solution)/shard_map/ppermute | solution.py:41
  38.9 2.1 %collective-permute-start.11 = (f32[24,384]{1,0:T(8,128)S(1)}, f32[24,384]{1,0:T(8,128)S(1)}, u32[]{:S(2)}, u32[]{:S(2)}) collective-permute-start(f32[24,384]{1,0:T(8,128)S(1)} %get-tuple-element.92), channel_id=1, source_target_pairs={{0,1},{1,2},{2,3},{3,0},{4,5},{5,6},{6,7},{7,4},{8,9},{9,10},{10,1... | collective-permute-start | bytes 110600 | tf_op jit(solution)/shard_map/ppermute | solution.py:37
  41.3 1.3 %shard_map.61 = (f32[16,24,384]{2,1,0:T(8,128)S(1)}, f32[16,24,384]{2,1,0:T(8,128)S(1)}, f32[16,24,256]{2,1,0:T(8,128)S(1)}) custom-call(f32[2,16,24,384]{3,2,1,0:T(8,128)S(1)} %get-tuple-element.87.wide_ax, f32[2,16,24,384]{3,2,1,0:T(8,128)S(1)} %get-tuple-element.69.wide_yz.refs_2_.refs_3_, ...), custom_call_target="tpu_custom_call" | custom-call | tf_op jit(solution)/shard_map/pallas_call | solution.py:63
  42.6 2.1 %collective-permute-done.12.high_face.refs_1_ = f32[1,24,384]{2,1,0:T(8,128)S(1)} collective-permute-done((f32[1,24,384]{2,1,0:T(8,128)S(1)}, f32[1,24,384]{2,1,0:T(8,128)S(1)}, u32[]{:S(2)}, u32[]{:S(2)}) %collective-permute-start.12) | collective-permute-done | bytes 36896 | tf_op jit(solution)/shard_map/ppermute | solution.py:37
  45.1 1.1 %collective-permute-start.15 = (f32[24,384]{1,0:T(8,128)S(1)}, f32[24,384]{1,0:T(8,128)S(1)}, u32[]{:S(2)}, u32[]{:S(2)}) collective-permute-start(f32[24,384]{1,0:T(8,128)S(1)} %get-tuple-element.100), channel_id=1, source_target_pairs={{0,1},{1,2},{2,3},{3,0},{4,5},{5,6},{6,7},{7,4},{8,9},{9,10},{10,1... | collective-permute-start | bytes 110600 | tf_op jit(solution)/shard_map/ppermute | solution.py:37
  46.2 1.2 %shard_map.63 = (f32[16,24,384]{2,1,0:T(8,128)S(1)}, f32[16,24,384]{2,1,0:T(8,128)S(1)}, f32[16,24,256]{2,1,0:T(8,128)S(1)}) custom-call(f32[2,16,24,384]{3,2,1,0:T(8,128)S(1)} %get-tuple-element.87.wide_ax, f32[2,16,24,384]{3,2,1,0:T(8,128)S(1)} %get-tuple-element.69.wide_yz.refs_2_.refs_3_, ...), custom_call_target="tpu_custom_call" | custom-call | tf_op jit(solution)/shard_map/pallas_call | solution.py:63
  47.4 2.2 %collective-permute-done.16.high_face.refs_1_ = f32[1,24,384]{2,1,0:T(8,128)S(1)} collective-permute-done((f32[1,24,384]{2,1,0:T(8,128)S(1)}, f32[1,24,384]{2,1,0:T(8,128)S(1)}, u32[]{:S(2)}, u32[]{:S(2)}) %collective-permute-start.16) | collective-permute-done | bytes 36896 | tf_op jit(solution)/shard_map/ppermute | solution.py:37
  49.7 0.4 collective-permute-start.20
  50.1 0.4 collective-permute-start.18
  50.6 1.1 %shard_map.65 = (f32[16,24,256]{2,1,0:T(8,128)S(1)}, f32[16,24,256]{2,1,0:T(8,128)S(1)}) custom-call(f32[2,16,24,384]{3,2,1,0:T(8,128)S(1)} %get-tuple-element.87.wide_ax, f32[2,16,24,384]{3,2,1,0:T(8,128)S(1)} %get-tuple-element.69.wide_yz.refs_2_.refs_3_, f32[2,24,384]{2,1,0:T(8,128)S(1)} %collective-permute-done.4.refs_6_.refs_7_.rim_face, ...), custom_call_target="tpu_custom_call" | custom-call | tf_op jit(solution)/shard_map/pallas_call | solution.py:63
  51.7 2.1 %collective-permute-done.19.high_face = f32[1,24,384]{2,1,0:T(8,128)S(1)} collective-permute-done((f32[1,24,384]{2,1,0:T(8,128)S(1)}, f32[1,24,384]{2,1,0:T(8,128)S(1)}, u32[]{:S(2)}, u32[]{:S(2)}) %collective-permute-start.19) | collective-permute-done | bytes 36896 | tf_op jit(solution)/shard_map/ppermute | solution.py:37
  53.9 0.9 %shard_map.66 = (f32[16,24,256]{2,1,0:T(8,128)}, f32[16,24,256]{2,1,0:T(8,128)}) custom-call(f32[2,16,24,384]{3,2,1,0:T(8,128)S(1)} %get-tuple-element.69.wide_yz.refs_2_.refs_3_, f32[2,24,384]{2,1,0:T(8,128)S(1)} %collective-permute-done.4.refs_6_.refs_7_.rim_face, f32[3,16,384]{2,1,0:T(8,128)S(1)} %get-tuple-element.70.refs_7_.refs_8_.rim_rows, ...), custom_call_target="tpu_custom_call" | custom-call | tf_op jit(solution)/shard_map/pallas_call | solution.py:63
  (32 shorter events, 1.9 us)
Async XLA Ops:
  0.6 4.3 %copy-start = (s32[2,1,1]{0,2,1:T(1,128)S(1)}, s32[2,1,1]{0,2,1:T(1,128)}, u32[]{:S(2)}) copy-start(s32[2,1,1]{0,2,1:T(1,128)} %param.5) | copy-start | bytes 28
  2.8 10.6 %collective-permute-start = (f32[46,8,256]{2,1,0:T(8,128)S(1)}, f32[46,8,256]{2,1,0:T(8,128)S(1)}, u32[]{:S(2)}, u32[]{:S(2)}) collective-permute-start(f32[46,8,256]{2,1,0:T(8,128)S(1)} %get-tuple-element.59._), channel_id=1, source_target_pairs={{0,4},{4,0},{1,5},{5,1},{2,6},{6,2},{3,7},{7,3},{8,12},{12,8},{9,1... | collective-permute-start | bytes 1130504 | tf_op jit(solution)/shard_map/ppermute | solution.py:41
  5.6 20.3 %collective-permute-start.1 = (f32[43,8,256]{2,1,0:T(8,128)S(1)}, f32[43,8,256]{2,1,0:T(8,128)S(1)}, u32[]{:S(2)}, u32[]{:S(2)}) collective-permute-start(f32[43,8,256]{2,1,0:T(8,128)S(1)} %shard_map.51._), channel_id=1, source_target_pairs={{0,4},{4,0},{1,5},{5,1},{2,6},{6,2},{3,7},{7,3},{8,12},{12,8},{9,1... | collective-permute-start | bytes 1056776 | tf_op jit(solution)/shard_map/ppermute | solution.py:41
  9.2 19.3 %collective-permute-start.5 = (f32[43,8,256]{2,1,0:T(8,128)S(1)}, f32[43,8,256]{2,1,0:T(8,128)S(1)}, u32[]{:S(2)}, u32[]{:S(2)}) collective-permute-start(f32[43,8,256]{2,1,0:T(8,128)S(1)} %get-tuple-element.71), channel_id=1, source_target_pairs={{0,4},{4,0},{1,5},{5,1},{2,6},{6,2},{3,7},{7,3},{8,12},{12,8},{9,1... | collective-permute-start | bytes 1056776 | tf_op jit(solution)/shard_map/ppermute | solution.py:41
  14.7 4.7 %collective-permute-start.2 = (f32[10,8,128]{2,1,0:T(8,128)S(1)}, f32[10,8,128]{2,1,0:T(8,128)S(1)}, u32[]{:S(2)}, u32[]{:S(2)}) collective-permute-start(f32[10,8,128]{2,1,0:T(8,128)S(1)} %get-tuple-element.62.right), channel_id=1, source_target_pairs={{0,8},{8,16},{16,24},{24,0},{1,9},{9,17},{17,25},{25,1},{2,10},{10... | collective-permute-start | bytes 122888 | tf_op jit(solution)/shard_map/ppermute | solution.py:37
  16.0 3.4 %collective-permute-start.3 = (f32[10,8,128]{2,1,0:T(8,128)S(1)}, f32[10,8,128]{2,1,0:T(8,128)S(1)}, u32[]{:S(2)}, u32[]{:S(2)}) collective-permute-start(f32[10,8,128]{2,1,0:T(8,128)S(1)} %get-tuple-element.61.left), channel_id=1, source_target_pairs={{0,24},{8,0},{16,8},{24,16},{1,25},{9,1},{17,9},{25,17},{2,26},{10... | collective-permute-start | bytes 122888 | tf_op jit(solution)/shard_map/ppermute | solution.py:37
  20.7 9.1 %collective-permute-start.4 = (f32[2,24,384]{2,1,0:T(8,128)S(1)}, f32[2,24,384]{2,1,0:T(8,128)S(1)}, u32[]{:S(2)}, u32[]{:S(2)}) collective-permute-start(f32[2,24,384]{2,1,0:T(8,128)S(1)} %get-tuple-element.66.down), channel_id=1, source_target_pairs={{0,3},{1,0},{2,1},{3,2},{4,7},{5,4},{6,5},{7,6},{8,11},{9,8},{10,9... | collective-permute-start | bytes 221192 | tf_op jit(solution)/shard_map/ppermute | solution.py:37
  24.7 5.0 %collective-permute-start.6 = (f32[24,384]{1,0:T(8,128)S(1)}, f32[24,384]{1,0:T(8,128)S(1)}, u32[]{:S(2)}, u32[]{:S(2)}) collective-permute-start(f32[24,384]{1,0:T(8,128)S(1)} %get-tuple-element.79.refs_3_.refs_4_), channel_id=1, source_target_pairs={{0,1},{1,2},{2,3},{3,0},{4,5},{5,6},{6,7},{7,4},{8,9},{9,10},{10,1... | collective-permute-start | bytes 110600 | tf_op jit(solution)/shard_map/ppermute | solution.py:37
  27.0 7.9 %collective-permute-start.10 = (s32[29,8,256]{2,1,0:T(8,128)S(1)}, s32[29,8,256]{2,1,0:T(8,128)S(1)}, u32[]{:S(2)}, u32[]{:S(2)}) collective-permute-start(s32[29,8,256]{2,1,0:T(8,128)S(1)} %get-tuple-element.84), channel_id=1, source_target_pairs={{0,4},{4,0},{1,5},{5,1},{2,6},{6,2},{3,7},{7,3},{8,12},{12,8},{9,1... | collective-permute-start | bytes 712712 | tf_op jit(solution)/shard_map/ppermute | solution.py:41
  28.3 13.0 %collective-permute-start.14 = (s32[12,8,256]{2,1,0:T(8,128)S(1)}, s32[12,8,256]{2,1,0:T(8,128)S(1)}, u32[]{:S(2)}, u32[]{:S(2)}) collective-permute-start(s32[12,8,256]{2,1,0:T(8,128)S(1)} %get-tuple-element.98), channel_id=1, source_target_pairs={{0,4},{4,0},{1,5},{5,1},{2,6},{6,2},{3,7},{7,3},{8,12},{12,8},{9,1... | collective-permute-start | bytes 294920 | tf_op jit(solution)/shard_map/ppermute | solution.py:41
  30.0 8.2 %collective-permute-start.9 = (f32[2,16,384]{2,1,0:T(8,128)S(1)}, f32[2,16,384]{2,1,0:T(8,128)S(1)}, u32[]{:S(2)}, u32[]{:S(2)}) collective-permute-start(f32[2,16,384]{2,1,0:T(8,128)S(1)} %get-tuple-element.83), channel_id=1, source_target_pairs={{0,4},{4,0},{1,5},{5,1},{2,6},{6,2},{3,7},{7,3},{8,12},{12,8},{9,1... | collective-permute-start | bytes 147464 | tf_op jit(solution)/shard_map/ppermute | solution.py:41
  31.2 5.1 %collective-permute-start.7 = (f32[24,384]{1,0:T(8,128)S(1)}, f32[24,384]{1,0:T(8,128)S(1)}, u32[]{:S(2)}, u32[]{:S(2)}) collective-permute-start(f32[24,384]{1,0:T(8,128)S(1)} %get-tuple-element.81), channel_id=1, source_target_pairs={{0,1},{1,2},{2,3},{3,0},{4,5},{5,6},{6,7},{7,4},{8,9},{9,10},{10,1... | collective-permute-start | bytes 110600 | tf_op jit(solution)/shard_map/ppermute | solution.py:37
  34.8 3.4 %collective-permute-start.8 = (f32[1,24,384]{2,1,0:T(8,128)S(1)}, f32[1,24,384]{2,1,0:T(8,128)S(1)}, u32[]{:S(2)}, u32[]{:S(2)}) collective-permute-start(f32[1,24,384]{2,1,0:T(8,128)S(1)} %get-tuple-element.82), channel_id=1, source_target_pairs={{0,3},{1,0},{2,1},{3,2},{4,7},{5,4},{6,5},{7,6},{8,11},{9,8},{10,9... | collective-permute-start | bytes 110600 | tf_op jit(solution)/shard_map/ppermute | solution.py:37
  38.3 6.4 %collective-permute-start.13 = (f32[2,16,384]{2,1,0:T(8,128)S(1)}, f32[2,16,384]{2,1,0:T(8,128)S(1)}, u32[]{:S(2)}, u32[]{:S(2)}) collective-permute-start(f32[2,16,384]{2,1,0:T(8,128)S(1)} %get-tuple-element.94), channel_id=1, source_target_pairs={{0,4},{4,0},{1,5},{5,1},{2,6},{6,2},{3,7},{7,3},{8,12},{12,8},{9,1... | collective-permute-start | bytes 147464 | tf_op jit(solution)/shard_map/ppermute | solution.py:41
  38.9 3.6 %collective-permute-start.11 = (f32[24,384]{1,0:T(8,128)S(1)}, f32[24,384]{1,0:T(8,128)S(1)}, u32[]{:S(2)}, u32[]{:S(2)}) collective-permute-start(f32[24,384]{1,0:T(8,128)S(1)} %get-tuple-element.92), channel_id=1, source_target_pairs={{0,1},{1,2},{2,3},{3,0},{4,5},{5,6},{6,7},{7,4},{8,9},{9,10},{10,1... | collective-permute-start | bytes 110600 | tf_op jit(solution)/shard_map/ppermute | solution.py:37
  41.0 3.7 %collective-permute-start.12 = (f32[1,24,384]{2,1,0:T(8,128)S(1)}, f32[1,24,384]{2,1,0:T(8,128)S(1)}, u32[]{:S(2)}, u32[]{:S(2)}) collective-permute-start(f32[1,24,384]{2,1,0:T(8,128)S(1)} %get-tuple-element.93), channel_id=1, source_target_pairs={{0,3},{1,0},{2,1},{3,2},{4,7},{5,4},{6,5},{7,6},{8,11},{9,8},{10,9... | collective-permute-start | bytes 110600 | tf_op jit(solution)/shard_map/ppermute | solution.py:37
  41.0 9.6 %collective-permute-start.21 = (s32[16,8,256]{2,1,0:T(8,128)S(1)}, s32[16,8,256]{2,1,0:T(8,128)S(1)}, u32[]{:S(2)}, u32[]{:S(2)}) collective-permute-start(s32[16,8,256]{2,1,0:T(8,128)S(1)} %get-tuple-element.111), channel_id=1, source_target_pairs={{0,4},{4,0},{1,5},{5,1},{2,6},{6,2},{3,7},{7,3},{8,12},{12,8},{9,1... | collective-permute-start | bytes 393224 | tf_op jit(solution)/shard_map/ppermute | solution.py:41
  44.7 4.9 %collective-permute-start.17 = (f32[2,16,384]{2,1,0:T(8,128)S(1)}, f32[2,16,384]{2,1,0:T(8,128)S(1)}, u32[]{:S(2)}, u32[]{:S(2)}) collective-permute-start(f32[2,16,384]{2,1,0:T(8,128)S(1)} %get-tuple-element.102), channel_id=1, source_target_pairs={{0,4},{4,0},{1,5},{5,1},{2,6},{6,2},{3,7},{7,3},{8,12},{12,8},{9,1... | collective-permute-start | bytes 147464 | tf_op jit(solution)/shard_map/ppermute | solution.py:41
  45.1 2.3 %collective-permute-start.15 = (f32[24,384]{1,0:T(8,128)S(1)}, f32[24,384]{1,0:T(8,128)S(1)}, u32[]{:S(2)}, u32[]{:S(2)}) collective-permute-start(f32[24,384]{1,0:T(8,128)S(1)} %get-tuple-element.100), channel_id=1, source_target_pairs={{0,1},{1,2},{2,3},{3,0},{4,5},{5,6},{6,7},{7,4},{8,9},{9,10},{10,1... | collective-permute-start | bytes 110600 | tf_op jit(solution)/shard_map/ppermute | solution.py:37
  46.2 3.4 %collective-permute-start.16 = (f32[1,24,384]{2,1,0:T(8,128)S(1)}, f32[1,24,384]{2,1,0:T(8,128)S(1)}, u32[]{:S(2)}, u32[]{:S(2)}) collective-permute-start(f32[1,24,384]{2,1,0:T(8,128)S(1)} %get-tuple-element.101), channel_id=1, source_target_pairs={{0,3},{1,0},{2,1},{3,2},{4,7},{5,4},{6,5},{7,6},{8,11},{9,8},{10,9... | collective-permute-start | bytes 110600 | tf_op jit(solution)/shard_map/ppermute | solution.py:37
  49.7 4.2 %collective-permute-start.20 = (f32[2,16,384]{2,1,0:T(8,128)S(1)}, f32[2,16,384]{2,1,0:T(8,128)S(1)}, u32[]{:S(2)}, u32[]{:S(2)}) collective-permute-start(f32[2,16,384]{2,1,0:T(8,128)S(1)} %get-tuple-element.108), channel_id=1, source_target_pairs={{0,4},{4,0},{1,5},{5,1},{2,6},{6,2},{3,7},{7,3},{8,12},{12,8},{9,1... | collective-permute-start | bytes 147464 | tf_op jit(solution)/shard_map/ppermute | solution.py:41
  50.1 1.6 %collective-permute-start.18 = (f32[24,384]{1,0:T(8,128)S(1)}, f32[24,384]{1,0:T(8,128)S(1)}, u32[]{:S(2)}, u32[]{:S(2)}) collective-permute-start(f32[24,384]{1,0:T(8,128)S(1)} %get-tuple-element.106), channel_id=1, source_target_pairs={{0,1},{1,2},{2,3},{3,0},{4,5},{5,6},{6,7},{7,4},{8,9},{9,10},{10,1... | collective-permute-start | bytes 110600 | tf_op jit(solution)/shard_map/ppermute | solution.py:37
  50.5 3.4 %collective-permute-start.19 = (f32[1,24,384]{2,1,0:T(8,128)S(1)}, f32[1,24,384]{2,1,0:T(8,128)S(1)}, u32[]{:S(2)}, u32[]{:S(2)}) collective-permute-start(f32[1,24,384]{2,1,0:T(8,128)S(1)} %get-tuple-element.107), channel_id=1, source_target_pairs={{0,3},{1,0},{2,1},{3,2},{4,7},{5,4},{6,5},{7,6},{8,11},{9,8},{10,9... | collective-permute-start | bytes 110600 | tf_op jit(solution)/shard_map/ppermute | solution.py:37

commit v7 on v6

--- a/solution.py
+++ b/solution.py
@@ -164,9 +164,9 @@
 PLANES_AT, ROWS_AT = 10, 16
 FIRST_PAIRS = 20
 NEXT_PAIRS = 43
-PIECES = (1, 7, 15)
+PIECES = (1, 4, 11, 15)
 CODE_BITS = 20
-ADDED_AT = (2, 4)
+ADDED_AT = (2, 4, 5)
 
 
 def pieces_at(stage):
@@ -655,14 +655,14 @@
 
 
 def halo_flux(z, wide_yz, rim_face, rim_rows, low_face, high_face, ghost_rows):
-    _, planes, rows, width = wide_yz.shape
-    at, row = slice(z, z + 1), row_of((rows, width))
-    top = jnp.where(row == rows - 1, rim_rows[2, at] * ghost_rows[1, at], 0.0)
-    flux = jnp.where(row == 0, wide_yz[0, z, 0:1] * ghost_rows[0, at], top)
+    planes, (rows, width) = wide_yz.shape[1], low_face.shape
+    at, row, wide = slice(z, z + 1), row_of((rows, width)), slice(0, width)
+    top = jnp.where(row == rows - 1, rim_rows[2, at, wide] * ghost_rows[1, at], 0.0)
+    flux = jnp.where(row == 0, wide_yz[0, z, 0:1, wide] * ghost_rows[0, at], top)
     if z == 0:
-        flux = flux + wide_yz[1, 0] * low_face[...]
+        flux = flux + wide_yz[1, 0, :, wide] * low_face[...]
     if z == planes - 1:
-        flux = flux + rim_face[1] * high_face[0]
+        flux = flux + rim_face[1, :, wide] * high_face[0]
     return flux
 
 
@@ -720,8 +720,9 @@
 def faces_kernel(second, wide_yz, rim_face, rim_rows, low_face, high_face, ghost_rows, inverse, direction, up, down, rows_out):
     halo = wide_yz, rim_face, rim_rows, low_face, high_face, ghost_rows
     planes, rows, _ = direction.shape
+    wide = slice(0, up.shape[1])
     for z, out in ((0, down.at[0]), (planes - 1, up)):
-        out[...] = direction[z] + second * (inverse[z] * halo_flux(z, *halo))
+        out[...] = (direction[z] + second * (inverse[z] * halo_flux(z, *halo)))[:, wide]
     for z in range(planes):
         at = slice(z, z + 1)
         for edge, row, out in ((0, 0, 1), (1, rows - 1, 0)):
@@ -731,9 +732,9 @@
             elif z == planes - 1:
                 rows_out[out, at] = up[line]
             else:
-                beta = rim_rows[2, at] if edge else wide_yz[0, z, line]
-                flux = beta * ghost_rows[edge, at]
-                rows_out[out, at] = direction[z, line] + second * (inverse[z, line] * flux)
+                beta = rim_rows[2, at, wide] if edge else wide_yz[0, z, line, wide]
+                flux = beta * ghost_rows[edge, at, wide]
+                rows_out[out, at] = direction[z, line, wide] + second * (inverse[z, line, wide] * flux)
 
 
 def last_kernel(wide_yz, rim_face, rim_rows, low_face, high_face, ghost_rows, partial, total, *refs):
@@ -904,6 +905,8 @@
             more = (pieces[number] for number in pieces_at(SWEEPS + 1))
             return tuple(call(last_kernel, [own, own], wide_yz, *rims, *halo, residual, *state, scales, *more, sent=True))
         direction, total = state
+        wide = columns if stage == SWEEPS - 1 else width
+        faces = [f32(rows, wide), f32(1, rows, wide), f32(2, planes, wide)]
         up, down, rows_out = call(
             functools.partial(faces_kernel, second_list[stage]), faces, wide_yz, *rims, *halo, inverse, direction
         )

time: 54.9 us -> 54.7 us (level)
    ppermute x10 -> x11, starting transfers between devices: 8.06 us -> 8.59 us  [swapped(): lax.ppermute(value, 'gy', [(i, i ^ 1) for i in range(lax.axis_size('gy'))])]
    ppermute x10 -> x11, waiting for transfers between devices: 2.83 us -> 2.82 us  [swapped(): lax.ppermute(value, 'gy', [(i, i ^ 1) for i in range(lax.axis_size('gy'))])]
  transfers between devices with their start and end apart: 22 -> 23, of which waited for: 7 -> 7; matrix products, arithmetic and copies ran while one was open for 0% -> 0% of each run, Pallas kernels for 26% -> 26%
where the time goes in v7:
time: 54.7 us; the launch traced here: 54.6 us
  starting transfers between devices  24.2 us (44%)
  Pallas kernels  17.5 us (32%)
  waiting for transfers between devices  12 us (22%)
  between operations  0.8 us (1%)
    ppermute x12, starting transfers between devices, shifted(): lax.ppermute(value, axis, [(i, (i + steps) % count) for i in range(count)])  15.6 us
    pallas_call x16, Pallas kernels, call(): pl.pallas_call(kernel, out_shape=outs, in_specs=specs, out_specs=out_spec...  15.4 us
    ppermute x12, waiting for transfers between devices, shifted(): lax.ppermute(value, axis, [(i, (i + steps) % count) for i in range(count)])  9.22 us
    ppermute x11, starting transfers between devices, swapped(): lax.ppermute(value, 'gy', [(i, i ^ 1) for i in range(lax.axis_size('gy'))])  8.59 us
    ppermute x11, waiting for transfers between devices, swapped(): lax.ppermute(value, 'gy', [(i, i ^ 1) for i in range(lax.axis_size('gy'))])  2.82 us
    pallas_call x1, Pallas kernels, local(): pl.pallas_call(functools.partial(edge_kernel, pairs), out_shape=[f32(*old...  2.15 us
  transfers between devices with their start and end apart: 23, of which 7 were waited for; matrix products, arithmetic and copies ran while one was open for 0% of the time, Pallas kernels for 26%

profile of v7, /device:TPU:1, one launch (start us, length us, event | category | flops | bytes accessed | tf_op | source)
XLA Modules:
  0.0 54.6 jit_solution(12770616209886252335)
XLA Ops:
  0.6 2.2 %shard_map.50 = (f32[2,2,16,16,256]{4,3,2,1,0:T(8,128)S(1)}, bf16[4,2,16,16,256]{4,3,2,1,0:T(8,128)(2,1)S(1)}, f32[46,8,256]{2,1,0:T(8,128)S(1)}) custom-call(s32[2]{0:T(128)} %bitcast.3, f32[2,2,16,16,256]{4,3,2,1,0:T(8,128)} %fields_in.1, bf16[4,2,16,16,256]{4,3,2,1,0:T(8,128)(2,1)} %coef_in.1), custom_call_target="tpu_custom_call" | custom-call | tf_op jit(solution)/shard_map/pallas_call | solution.py:768
  2.8 2.1 %collective-permute-start = (f32[46,8,256]{2,1,0:T(8,128)S(1)}, f32[46,8,256]{2,1,0:T(8,128)S(1)}, u32[]{:S(2)}, u32[]{:S(2)}) collective-permute-start(f32[46,8,256]{2,1,0:T(8,128)S(1)} %get-tuple-element.60._), channel_id=1, source_target_pairs={{0,4},{4,0},{1,5},{5,1},{2,6},{6,2},{3,7},{7,3},{8,12},{12,8},{9,1... | collective-permute-start | bytes 1130504 | tf_op jit(solution)/shard_map/ppermute | solution.py:41
  4.9 0.7 %shard_map.51._ = f32[43,8,256]{2,1,0:T(8,128)S(1)} custom-call(s32[2]{0:T(128)S(1)} %bitcast.4, bf16[4,2,16,16,256]{4,3,2,1,0:T(8,128)(2,1)S(1)} %get-tuple-element.59.coef, f32[46,8,256]{2,1,0:T(8,128)S(1)} %get-tuple-element.60._), custom_call_target="tpu_custom_call" | custom-call | tf_op jit(solution)/shard_map/pallas_call | solution.py:63
  5.7 3.5 %shard_map.54 = (f32[43,8,256]{2,1,0:T(8,128)S(1)}, s32[29,8,256]{2,1,0:T(8,128)S(1)}, f32[16,24,256]{2,1,0:T(8,128)S(1)}, f32[16,24,256]{2,1,0:T(8,128)S(1)}, s...) custom-call(s32[2]{0:T(128)S(1)} %bitcast.5, ...), custom_call_target="tpu_custom_call" | custom-call | tf_op jit(solution)/shard_map/pallas_call | solution.py:63
  9.2 1.4 %collective-permute-start.5 = (f32[43,8,256]{2,1,0:T(8,128)S(1)}, f32[43,8,256]{2,1,0:T(8,128)S(1)}, u32[]{:S(2)}, u32[]{:S(2)}) collective-permute-start(f32[43,8,256]{2,1,0:T(8,128)S(1)} %get-tuple-element.72), channel_id=1, source_target_pairs={{0,4},{4,0},{1,5},{5,1},{2,6},{6,2},{3,7},{7,3},{8,12},{12,8},{9,1... | collective-permute-start | bytes 1056776 | tf_op jit(solution)/shard_map/ppermute | solution.py:41
  10.7 2.7 %collective-permute-done.edge_in = f32[46,8,256]{2,1,0:T(8,128)S(1)} collective-permute-done((f32[46,8,256]{2,1,0:T(8,128)S(1)}, f32[46,8,256]{2,1,0:T(8,128)S(1)}, u32[]{:S(2)}, u32[]{:S(2)}) %collective-permute-start) | collective-permute-done | bytes 376864 | tf_op jit(solution)/shard_map/ppermute | solution.py:41
  13.4 1.3 %shard_map.52 = (f32[10,8,128]{2,1,0:T(8,128)S(1)}, f32[10,8,128]{2,1,0:T(8,128)S(1)}, f32[2,16,256]{2,1,0:T(8,128)S(1)}) custom-call(s32[2]{0:T(128)S(1)} %bitcast.6, f32[2,2,16,16,256]{4,3,2,1,0:T(8,128)S(1)} %get-tuple-element.61.fields, bf16[4,2,16,16,256]{4,3,2,1,0:T(8,128)(2,1)S(1)} %get-tuple-element.59.coef, ...), custom_call_target="tpu_custom_call" | custom-call | tf_op jit(solution)/shard_map/pallas_call | solution.py:63
  14.7 1.3 %collective-permute-start.2 = (f32[10,8,128]{2,1,0:T(8,128)S(1)}, f32[10,8,128]{2,1,0:T(8,128)S(1)}, u32[]{:S(2)}, u32[]{:S(2)}) collective-permute-start(f32[10,8,128]{2,1,0:T(8,128)S(1)} %get-tuple-element.63.right), channel_id=1, source_target_pairs={{0,8},{8,16},{16,24},{24,0},{1,9},{9,17},{17,25},{25,1},{2,10},{10... | collective-permute-start | bytes 122888 | tf_op jit(solution)/shard_map/ppermute | solution.py:37
  16.0 2.1 %collective-permute-start.3 = (f32[10,8,128]{2,1,0:T(8,128)S(1)}, f32[10,8,128]{2,1,0:T(8,128)S(1)}, u32[]{:S(2)}, u32[]{:S(2)}) collective-permute-start(f32[10,8,128]{2,1,0:T(8,128)S(1)} %get-tuple-element.62.left), channel_id=1, source_target_pairs={{0,24},{8,0},{16,8},{24,16},{1,25},{9,1},{17,9},{25,17},{2,26},{10... | collective-permute-start | bytes 122888 | tf_op jit(solution)/shard_map/ppermute | solution.py:37
  18.1 1.3 %collective-permute-done.2.from_left = f32[10,8,128]{2,1,0:T(8,128)S(1)} collective-permute-done((f32[10,8,128]{2,1,0:T(8,128)S(1)}, f32[10,8,128]{2,1,0:T(8,128)S(1)}, u32[]{:S(2)}, u32[]{:S(2)}) %collective-permute-start.2) | collective-permute-done | bytes 40992 | tf_op jit(solution)/shard_map/ppermute | solution.py:37
  19.4 1.3 %shard_map.53 = (f32[16,24,256]{2,1,0:T(8,128)S(1)}, f32[16,24,128]{2,1,0:T(8,128)S(1)}, f32[4,16,24,128]{3,2,1,0:T(8,128)S(1)}, f32[3,16,256]{2,1,0:T(8,128)S(1...) custom-call(s32[2]{0:T(128)S(1)} %bitcast.7, ...), custom_call_target="tpu_custom_call" | custom-call | tf_op jit(solution)/shard_map/pallas_call | solution.py:63
  20.7 4.0 %collective-permute-start.4 = (f32[2,24,384]{2,1,0:T(8,128)S(1)}, f32[2,24,384]{2,1,0:T(8,128)S(1)}, u32[]{:S(2)}, u32[]{:S(2)}) collective-permute-start(f32[2,24,384]{2,1,0:T(8,128)S(1)} %get-tuple-element.67.down), channel_id=1, source_target_pairs={{0,3},{1,0},{2,1},{3,2},{4,7},{5,4},{6,5},{7,6},{8,11},{9,8},{10,9... | collective-permute-start | bytes 221192 | tf_op jit(solution)/shard_map/ppermute | solution.py:37
  24.7 1.2 %collective-permute-start.6 = (f32[24,384]{1,0:T(8,128)S(1)}, f32[24,384]{1,0:T(8,128)S(1)}, u32[]{:S(2)}, u32[]{:S(2)}) collective-permute-start(f32[24,384]{1,0:T(8,128)S(1)} %get-tuple-element.80.refs_3_.refs_4_), channel_id=1, source_target_pairs={{0,1},{1,2},{2,3},{3,0},{4,5},{5,6},{6,7},{7,4},{8,9},{9,10},{10,1... | collective-permute-start | bytes 110600 | tf_op jit(solution)/shard_map/ppermute | solution.py:37
  25.9 1.1 %shard_map.55 = (f32[2,16,24,384]{3,2,1,0:T(8,128)S(1)}, f32[2,16,24,256]{3,2,1,0:T(8,128)S(1)}, f32[16,24,256]{2,1,0:T(8,128)S(1)}, f32[16,24,384]{2,1,0:T(8,128)S(1)}, s32[29,8,256]{2,1,0:T(8,128)S(1)}) custom-call(s32[2]{0:T(128)S(1)} %bitcast.8, bf16[4,2,16,16,256]{4,3,2,1,0:T(8,128)(2,1)S(1)} %get-tuple-element.59.coef, ...), custom_call_target="tpu_custom_call" | custom-call | tf_op jit(solution)/shard_map/pallas_call | solution.py:63
  27.0 1.3 %collective-permute-start.10 = (s32[29,8,256]{2,1,0:T(8,128)S(1)}, s32[29,8,256]{2,1,0:T(8,128)S(1)}, u32[]{:S(2)}, u32[]{:S(2)}) collective-permute-start(s32[29,8,256]{2,1,0:T(8,128)S(1)} %get-tuple-element.85), channel_id=1, source_target_pairs={{0,4},{4,0},{1,5},{5,1},{2,6},{6,2},{3,7},{7,3},{8,12},{12,8},{9,1... | collective-permute-start | bytes 712712 | tf_op jit(solution)/shard_map/ppermute | solution.py:41
  28.5 1.2 %shard_map.56 = (f32[2,16,24,384]{3,2,1,0:T(8,128)S(1)}, f32[16,24,384]{2,1,0:T(8,128)S(1)}, f32[16,24,384]{2,1,0:T(8,128)S(1)}) custom-call(f32[43,8,256]{2,1,0:T(8,128)S(1)} %collective-permute-done.1.pairs, f32[43,8,256]{2,1,0:T(8,128)S(1)} %collective-permute-done.5.more_pairs.outer, f32[2,16,24,256]{3,2,1,0:T(8,128)S(1)} %get-tuple-element.73.own_ax, ...), custom_call_target="tpu_custom_call" | custom-call | tf_op jit(solution)/shard_map/pallas_call | solution.py:63
  30.0 1.3 %collective-permute-start.9 = (f32[2,16,384]{2,1,0:T(8,128)S(1)}, f32[2,16,384]{2,1,0:T(8,128)S(1)}, u32[]{:S(2)}, u32[]{:S(2)}) collective-permute-start(f32[2,16,384]{2,1,0:T(8,128)S(1)} %get-tuple-element.84), channel_id=1, source_target_pairs={{0,4},{4,0},{1,5},{5,1},{2,6},{6,2},{3,7},{7,3},{8,12},{12,8},{9,1... | collective-permute-start | bytes 147464 | tf_op jit(solution)/shard_map/ppermute | solution.py:41
  31.2 3.6 %collective-permute-start.7 = (f32[24,384]{1,0:T(8,128)S(1)}, f32[24,384]{1,0:T(8,128)S(1)}, u32[]{:S(2)}, u32[]{:S(2)}) collective-permute-start(f32[24,384]{1,0:T(8,128)S(1)} %get-tuple-element.82), channel_id=1, source_target_pairs={{0,1},{1,2},{2,3},{3,0},{4,5},{5,6},{6,7},{7,4},{8,9},{9,10},{10,1... | collective-permute-start | bytes 110600 | tf_op jit(solution)/shard_map/ppermute | solution.py:37
  35.2 1.1 %shard_map.59 = (f32[16,24,384]{2,1,0:T(8,128)S(1)}, f32[16,24,384]{2,1,0:T(8,128)S(1)}, f32[16,24,256]{2,1,0:T(8,128)S(1)}) custom-call(f32[2,16,24,384]{3,2,1,0:T(8,128)S(1)} %get-tuple-element.88.wide_ax, f32[2,16,24,384]{3,2,1,0:T(8,128)S(1)} %get-tuple-element.70.wide_yz.refs_2_.refs_3_, ...), custom_call_target="tpu_custom_call" | custom-call | tf_op jit(solution)/shard_map/pallas_call | solution.py:63
  36.4 1.8 %collective-permute-done.8.high_face.refs_1_ = f32[1,24,384]{2,1,0:T(8,128)S(1)} collective-permute-done((f32[1,24,384]{2,1,0:T(8,128)S(1)}, f32[1,24,384]{2,1,0:T(8,128)S(1)}, u32[]{:S(2)}, u32[]{:S(2)}) %collective-permute-start.8) | collective-permute-done | bytes 36896 | tf_op jit(solution)/shard_map/ppermute | solution.py:37
  38.6 1.5 %collective-permute-start.11 = (f32[24,384]{1,0:T(8,128)S(1)}, f32[24,384]{1,0:T(8,128)S(1)}, u32[]{:S(2)}, u32[]{:S(2)}) collective-permute-start(f32[24,384]{1,0:T(8,128)S(1)} %get-tuple-element.93), channel_id=1, source_target_pairs={{0,1},{1,2},{2,3},{3,0},{4,5},{5,6},{6,7},{7,4},{8,9},{9,10},{10,1... | collective-permute-start | bytes 110600 | tf_op jit(solution)/shard_map/ppermute | solution.py:37
  40.4 1.2 %shard_map.61 = (f32[16,24,384]{2,1,0:T(8,128)S(1)}, f32[16,24,384]{2,1,0:T(8,128)S(1)}, f32[16,24,256]{2,1,0:T(8,128)S(1)}) custom-call(f32[2,16,24,384]{3,2,1,0:T(8,128)S(1)} %get-tuple-element.88.wide_ax, f32[2,16,24,384]{3,2,1,0:T(8,128)S(1)} %get-tuple-element.70.wide_yz.refs_2_.refs_3_, ...), custom_call_target="tpu_custom_call" | custom-call | tf_op jit(solution)/shard_map/pallas_call | solution.py:63
  41.7 2.1 %collective-permute-done.12.high_face.refs_1_ = f32[1,24,384]{2,1,0:T(8,128)S(1)} collective-permute-done((f32[1,24,384]{2,1,0:T(8,128)S(1)}, f32[1,24,384]{2,1,0:T(8,128)S(1)}, u32[]{:S(2)}, u32[]{:S(2)}) %collective-permute-start.12) | collective-permute-done | bytes 36896 | tf_op jit(solution)/shard_map/ppermute | solution.py:37
  43.8 0.4 collective-permute-start.17
  44.3 1.0 %collective-permute-start.15 = (f32[24,384]{1,0:T(8,128)S(1)}, f32[24,384]{1,0:T(8,128)S(1)}, u32[]{:S(2)}, u32[]{:S(2)}) collective-permute-start(f32[24,384]{1,0:T(8,128)S(1)} %get-tuple-element.101), channel_id=1, source_target_pairs={{0,1},{1,2},{2,3},{3,0},{4,5},{5,6},{6,7},{7,4},{8,9},{9,10},{10,1... | collective-permute-start | bytes 110600 | tf_op jit(solution)/shard_map/ppermute | solution.py:37
  45.2 0.6 %collective-permute-start.22 = (s32[8,8,256]{2,1,0:T(8,128)S(1)}, s32[8,8,256]{2,1,0:T(8,128)S(1)}, u32[]{:S(2)}, u32[]{:S(2)}) collective-permute-start(s32[8,8,256]{2,1,0:T(8,128)S(1)} %get-tuple-element.115), channel_id=1, source_target_pairs={{0,4},{4,0},{1,5},{5,1},{2,6},{6,2},{3,7},{7,3},{8,12},{12,8},{9,1... | collective-permute-start | bytes 196616 | tf_op jit(solution)/shard_map/ppermute | solution.py:41
  45.9 1.2 %shard_map.63 = (f32[16,24,384]{2,1,0:T(8,128)S(1)}, f32[16,24,384]{2,1,0:T(8,128)S(1)}, f32[16,24,256]{2,1,0:T(8,128)S(1)}) custom-call(f32[2,16,24,384]{3,2,1,0:T(8,128)S(1)} %get-tuple-element.88.wide_ax, f32[2,16,24,384]{3,2,1,0:T(8,128)S(1)} %get-tuple-element.70.wide_yz.refs_2_.refs_3_, ...), custom_call_target="tpu_custom_call" | custom-call | tf_op jit(solution)/shard_map/pallas_call | solution.py:63
  47.1 1.8 %collective-permute-done.16.high_face.refs_1_ = f32[1,24,384]{2,1,0:T(8,128)S(1)} collective-permute-done((f32[1,24,384]{2,1,0:T(8,128)S(1)}, f32[1,24,384]{2,1,0:T(8,128)S(1)}, u32[]{:S(2)}, u32[]{:S(2)}) %collective-permute-start.16) | collective-permute-done | bytes 36896 | tf_op jit(solution)/shard_map/ppermute | solution.py:37
  49.4 1.0 %collective-permute-start.18 = (f32[24,256]{1,0:T(8,128)S(1)}, f32[24,256]{1,0:T(8,128)S(1)}, u32[]{:S(2)}, u32[]{:S(2)}) collective-permute-start(f32[24,256]{1,0:T(8,128)S(1)} %get-tuple-element.107), channel_id=1, source_target_pairs={{0,1},{1,2},{2,3},{3,0},{4,5},{5,6},{6,7},{7,4},{8,9},{9,10},{10,1... | collective-permute-start | bytes 73736 | tf_op jit(solution)/shard_map/ppermute | solution.py:37
  50.4 1.1 %shard_map.65 = (f32[16,24,256]{2,1,0:T(8,128)S(1)}, f32[16,24,256]{2,1,0:T(8,128)S(1)}) custom-call(f32[2,16,24,384]{3,2,1,0:T(8,128)S(1)} %get-tuple-element.88.wide_ax, f32[2,16,24,384]{3,2,1,0:T(8,128)S(1)} %get-tuple-element.70.wide_yz.refs_2_.refs_3_, f32[2,24,384]{2,1,0:T(8,128)S(1)} %collective-permute-done.4.refs_6_.refs_7_.rim_face, ...), custom_call_target="tpu_custom_call" | custom-call | tf_op jit(solution)/shard_map/pallas_call | solution.py:63
  51.5 2.1 %collective-permute-done.19.high_face = f32[1,24,256]{2,1,0:T(8,128)S(1)} collective-permute-done((f32[1,24,256]{2,1,0:T(8,128)S(1)}, f32[1,24,256]{2,1,0:T(8,128)S(1)}, u32[]{:S(2)}, u32[]{:S(2)}) %collective-permute-start.19) | collective-permute-done | bytes 24608 | tf_op jit(solution)/shard_map/ppermute | solution.py:37
  53.6 1.0 %shard_map.66 = (f32[16,24,256]{2,1,0:T(8,128)}, f32[16,24,256]{2,1,0:T(8,128)}) custom-call(f32[2,16,24,384]{3,2,1,0:T(8,128)S(1)} %get-tuple-element.70.wide_yz.refs_2_.refs_3_, f32[2,24,384]{2,1,0:T(8,128)S(1)} %collective-permute-done.4.refs_6_.refs_7_.rim_face, f32[3,16,384]{2,1,0:T(8,128)S(1)} %get-tuple-element.71.refs_7_.refs_8_.rim_rows, ...), custom_call_target="tpu_custom_call" | custom-call | tf_op jit(solution)/shard_map/pallas_call | solution.py:63
  (34 shorter events, 2.3 us)
Async XLA Ops:
  0.6 4.3 %copy-start = (s32[2,1,1]{0,2,1:T(1,128)S(1)}, s32[2,1,1]{0,2,1:T(1,128)}, u32[]{:S(2)}) copy-start(s32[2,1,1]{0,2,1:T(1,128)} %param.5) | copy-start | bytes 28
  2.8 10.6 %collective-permute-start = (f32[46,8,256]{2,1,0:T(8,128)S(1)}, f32[46,8,256]{2,1,0:T(8,128)S(1)}, u32[]{:S(2)}, u32[]{:S(2)}) collective-permute-start(f32[46,8,256]{2,1,0:T(8,128)S(1)} %get-tuple-element.60._), channel_id=1, source_target_pairs={{0,4},{4,0},{1,5},{5,1},{2,6},{6,2},{3,7},{7,3},{8,12},{12,8},{9,1... | collective-permute-start | bytes 1130504 | tf_op jit(solution)/shard_map/ppermute | solution.py:41
  5.6 20.3 %collective-permute-start.1 = (f32[43,8,256]{2,1,0:T(8,128)S(1)}, f32[43,8,256]{2,1,0:T(8,128)S(1)}, u32[]{:S(2)}, u32[]{:S(2)}) collective-permute-start(f32[43,8,256]{2,1,0:T(8,128)S(1)} %shard_map.51._), channel_id=1, source_target_pairs={{0,4},{4,0},{1,5},{5,1},{2,6},{6,2},{3,7},{7,3},{8,12},{12,8},{9,1... | collective-permute-start | bytes 1056776 | tf_op jit(solution)/shard_map/ppermute | solution.py:41
  9.2 19.3 %collective-permute-start.5 = (f32[43,8,256]{2,1,0:T(8,128)S(1)}, f32[43,8,256]{2,1,0:T(8,128)S(1)}, u32[]{:S(2)}, u32[]{:S(2)}) collective-permute-start(f32[43,8,256]{2,1,0:T(8,128)S(1)} %get-tuple-element.72), channel_id=1, source_target_pairs={{0,4},{4,0},{1,5},{5,1},{2,6},{6,2},{3,7},{7,3},{8,12},{12,8},{9,1... | collective-permute-start | bytes 1056776 | tf_op jit(solution)/shard_map/ppermute | solution.py:41
  14.7 4.7 %collective-permute-start.2 = (f32[10,8,128]{2,1,0:T(8,128)S(1)}, f32[10,8,128]{2,1,0:T(8,128)S(1)}, u32[]{:S(2)}, u32[]{:S(2)}) collective-permute-start(f32[10,8,128]{2,1,0:T(8,128)S(1)} %get-tuple-element.63.right), channel_id=1, source_target_pairs={{0,8},{8,16},{16,24},{24,0},{1,9},{9,17},{17,25},{25,1},{2,10},{10... | collective-permute-start | bytes 122888 | tf_op jit(solution)/shard_map/ppermute | solution.py:37
  16.0 3.4 %collective-permute-start.3 = (f32[10,8,128]{2,1,0:T(8,128)S(1)}, f32[10,8,128]{2,1,0:T(8,128)S(1)}, u32[]{:S(2)}, u32[]{:S(2)}) collective-permute-start(f32[10,8,128]{2,1,0:T(8,128)S(1)} %get-tuple-element.62.left), channel_id=1, source_target_pairs={{0,24},{8,0},{16,8},{24,16},{1,25},{9,1},{17,9},{25,17},{2,26},{10... | collective-permute-start | bytes 122888 | tf_op jit(solution)/shard_map/ppermute | solution.py:37
  20.7 9.1 %collective-permute-start.4 = (f32[2,24,384]{2,1,0:T(8,128)S(1)}, f32[2,24,384]{2,1,0:T(8,128)S(1)}, u32[]{:S(2)}, u32[]{:S(2)}) collective-permute-start(f32[2,24,384]{2,1,0:T(8,128)S(1)} %get-tuple-element.67.down), channel_id=1, source_target_pairs={{0,3},{1,0},{2,1},{3,2},{4,7},{5,4},{6,5},{7,6},{8,11},{9,8},{10,9... | collective-permute-start | bytes 221192 | tf_op jit(solution)/shard_map/ppermute | solution.py:37
  24.7 5.0 %collective-permute-start.6 = (f32[24,384]{1,0:T(8,128)S(1)}, f32[24,384]{1,0:T(8,128)S(1)}, u32[]{:S(2)}, u32[]{:S(2)}) collective-permute-start(f32[24,384]{1,0:T(8,128)S(1)} %get-tuple-element.80.refs_3_.refs_4_), channel_id=1, source_target_pairs={{0,1},{1,2},{2,3},{3,0},{4,5},{5,6},{6,7},{7,4},{8,9},{9,10},{10,1... | collective-permute-start | bytes 110600 | tf_op jit(solution)/shard_map/ppermute | solution.py:37
  27.0 7.9 %collective-permute-start.10 = (s32[29,8,256]{2,1,0:T(8,128)S(1)}, s32[29,8,256]{2,1,0:T(8,128)S(1)}, u32[]{:S(2)}, u32[]{:S(2)}) collective-permute-start(s32[29,8,256]{2,1,0:T(8,128)S(1)} %get-tuple-element.85), channel_id=1, source_target_pairs={{0,4},{4,0},{1,5},{5,1},{2,6},{6,2},{3,7},{7,3},{8,12},{12,8},{9,1... | collective-permute-start | bytes 712712 | tf_op jit(solution)/shard_map/ppermute | solution.py:41
  28.3 12.2 %collective-permute-start.14 = (s32[6,8,256]{2,1,0:T(8,128)S(1)}, s32[6,8,256]{2,1,0:T(8,128)S(1)}, u32[]{:S(2)}, u32[]{:S(2)}) collective-permute-start(s32[6,8,256]{2,1,0:T(8,128)S(1)} %get-tuple-element.99), channel_id=1, source_target_pairs={{0,4},{4,0},{1,5},{5,1},{2,6},{6,2},{3,7},{7,3},{8,12},{12,8},{9,1... | collective-permute-start | bytes 147464 | tf_op jit(solution)/shard_map/ppermute | solution.py:41
  30.0 8.2 %collective-permute-start.9 = (f32[2,16,384]{2,1,0:T(8,128)S(1)}, f32[2,16,384]{2,1,0:T(8,128)S(1)}, u32[]{:S(2)}, u32[]{:S(2)}) collective-permute-start(f32[2,16,384]{2,1,0:T(8,128)S(1)} %get-tuple-element.84), channel_id=1, source_target_pairs={{0,4},{4,0},{1,5},{5,1},{2,6},{6,2},{3,7},{7,3},{8,12},{12,8},{9,1... | collective-permute-start | bytes 147464 | tf_op jit(solution)/shard_map/ppermute | solution.py:41
  31.2 5.1 %collective-permute-start.7 = (f32[24,384]{1,0:T(8,128)S(1)}, f32[24,384]{1,0:T(8,128)S(1)}, u32[]{:S(2)}, u32[]{:S(2)}) collective-permute-start(f32[24,384]{1,0:T(8,128)S(1)} %get-tuple-element.82), channel_id=1, source_target_pairs={{0,1},{1,2},{2,3},{3,0},{4,5},{5,6},{6,7},{7,4},{8,9},{9,10},{10,1... | collective-permute-start | bytes 110600 | tf_op jit(solution)/shard_map/ppermute | solution.py:37
  34.8 3.4 %collective-permute-start.8 = (f32[1,24,384]{2,1,0:T(8,128)S(1)}, f32[1,24,384]{2,1,0:T(8,128)S(1)}, u32[]{:S(2)}, u32[]{:S(2)}) collective-permute-start(f32[1,24,384]{2,1,0:T(8,128)S(1)} %get-tuple-element.83), channel_id=1, source_target_pairs={{0,3},{1,0},{2,1},{3,2},{4,7},{5,4},{6,5},{7,6},{8,11},{9,8},{10,9... | collective-permute-start | bytes 110600 | tf_op jit(solution)/shard_map/ppermute | solution.py:37
  38.3 5.5 %collective-permute-start.13 = (f32[2,16,384]{2,1,0:T(8,128)S(1)}, f32[2,16,384]{2,1,0:T(8,128)S(1)}, u32[]{:S(2)}, u32[]{:S(2)}) collective-permute-start(f32[2,16,384]{2,1,0:T(8,128)S(1)} %get-tuple-element.95), channel_id=1, source_target_pairs={{0,4},{4,0},{1,5},{5,1},{2,6},{6,2},{3,7},{7,3},{8,12},{12,8},{9,1... | collective-permute-start | bytes 147464 | tf_op jit(solution)/shard_map/ppermute | solution.py:41
  38.6 3.0 %collective-permute-start.11 = (f32[24,384]{1,0:T(8,128)S(1)}, f32[24,384]{1,0:T(8,128)S(1)}, u32[]{:S(2)}, u32[]{:S(2)}) collective-permute-start(f32[24,384]{1,0:T(8,128)S(1)} %get-tuple-element.93), channel_id=1, source_target_pairs={{0,1},{1,2},{2,3},{3,0},{4,5},{5,6},{6,7},{7,4},{8,9},{9,10},{10,1... | collective-permute-start | bytes 110600 | tf_op jit(solution)/shard_map/ppermute | solution.py:37
  40.1 3.7 %collective-permute-start.12 = (f32[1,24,384]{2,1,0:T(8,128)S(1)}, f32[1,24,384]{2,1,0:T(8,128)S(1)}, u32[]{:S(2)}, u32[]{:S(2)}) collective-permute-start(f32[1,24,384]{2,1,0:T(8,128)S(1)} %get-tuple-element.94), channel_id=1, source_target_pairs={{0,3},{1,0},{2,1},{3,2},{4,7},{5,4},{6,5},{7,6},{8,11},{9,8},{10,9... | collective-permute-start | bytes 110600 | tf_op jit(solution)/shard_map/ppermute | solution.py:37
  40.1 10.3 %collective-permute-start.21 = (s32[14,8,256]{2,1,0:T(8,128)S(1)}, s32[14,8,256]{2,1,0:T(8,128)S(1)}, u32[]{:S(2)}, u32[]{:S(2)}) collective-permute-start(s32[14,8,256]{2,1,0:T(8,128)S(1)} %get-tuple-element.112), channel_id=1, source_target_pairs={{0,4},{4,0},{1,5},{5,1},{2,6},{6,2},{3,7},{7,3},{8,12},{12,8},{9,1... | collective-permute-start | bytes 344072 | tf_op jit(solution)/shard_map/ppermute | solution.py:41
  43.8 5.1 %collective-permute-start.17 = (f32[2,16,384]{2,1,0:T(8,128)S(1)}, f32[2,16,384]{2,1,0:T(8,128)S(1)}, u32[]{:S(2)}, u32[]{:S(2)}) collective-permute-start(f32[2,16,384]{2,1,0:T(8,128)S(1)} %get-tuple-element.103), channel_id=1, source_target_pairs={{0,4},{4,0},{1,5},{5,1},{2,6},{6,2},{3,7},{7,3},{8,12},{12,8},{9,1... | collective-permute-start | bytes 147464 | tf_op jit(solution)/shard_map/ppermute | solution.py:41
  44.3 2.8 %collective-permute-start.15 = (f32[24,384]{1,0:T(8,128)S(1)}, f32[24,384]{1,0:T(8,128)S(1)}, u32[]{:S(2)}, u32[]{:S(2)}) collective-permute-start(f32[24,384]{1,0:T(8,128)S(1)} %get-tuple-element.101), channel_id=1, source_target_pairs={{0,1},{1,2},{2,3},{3,0},{4,5},{5,6},{6,7},{7,4},{8,9},{9,10},{10,1... | collective-permute-start | bytes 110600 | tf_op jit(solution)/shard_map/ppermute | solution.py:37
  45.2 3.7 %collective-permute-start.16 = (f32[1,24,384]{2,1,0:T(8,128)S(1)}, f32[1,24,384]{2,1,0:T(8,128)S(1)}, u32[]{:S(2)}, u32[]{:S(2)}) collective-permute-start(f32[1,24,384]{2,1,0:T(8,128)S(1)} %get-tuple-element.102), channel_id=1, source_target_pairs={{0,3},{1,0},{2,1},{3,2},{4,7},{5,4},{6,5},{7,6},{8,11},{9,8},{10,9... | collective-permute-start | bytes 110600 | tf_op jit(solution)/shard_map/ppermute | solution.py:37
  45.2 6.3 %collective-permute-start.22 = (s32[8,8,256]{2,1,0:T(8,128)S(1)}, s32[8,8,256]{2,1,0:T(8,128)S(1)}, u32[]{:S(2)}, u32[]{:S(2)}) collective-permute-start(s32[8,8,256]{2,1,0:T(8,128)S(1)} %get-tuple-element.115), channel_id=1, source_target_pairs={{0,4},{4,0},{1,5},{5,1},{2,6},{6,2},{3,7},{7,3},{8,12},{12,8},{9,1... | collective-permute-start | bytes 196616 | tf_op jit(solution)/shard_map/ppermute | solution.py:41
  49.0 4.6 %collective-permute-start.20 = (f32[2,16,256]{2,1,0:T(8,128)S(1)}, f32[2,16,256]{2,1,0:T(8,128)S(1)}, u32[]{:S(2)}, u32[]{:S(2)}) collective-permute-start(f32[2,16,256]{2,1,0:T(8,128)S(1)} %get-tuple-element.109), channel_id=1, source_target_pairs={{0,4},{4,0},{1,5},{5,1},{2,6},{6,2},{3,7},{7,3},{8,12},{12,8},{9,1... | collective-permute-start | bytes 98312 | tf_op jit(solution)/shard_map/ppermute | solution.py:41
  49.4 2.1 %collective-permute-start.18 = (f32[24,256]{1,0:T(8,128)S(1)}, f32[24,256]{1,0:T(8,128)S(1)}, u32[]{:S(2)}, u32[]{:S(2)}) collective-permute-start(f32[24,256]{1,0:T(8,128)S(1)} %get-tuple-element.107), channel_id=1, source_target_pairs={{0,1},{1,2},{2,3},{3,0},{4,5},{5,6},{6,7},{7,4},{8,9},{9,10},{10,1... | collective-permute-start | bytes 73736 | tf_op jit(solution)/shard_map/ppermute | solution.py:37
  50.4 3.3 %collective-permute-start.19 = (f32[1,24,256]{2,1,0:T(8,128)S(1)}, f32[1,24,256]{2,1,0:T(8,128)S(1)}, u32[]{:S(2)}, u32[]{:S(2)}) collective-permute-start(f32[1,24,256]{2,1,0:T(8,128)S(1)} %get-tuple-element.108), channel_id=1, source_target_pairs={{0,3},{1,0},{2,1},{3,2},{4,7},{5,4},{6,5},{7,6},{8,11},{9,8},{10,9... | collective-permute-start | bytes 73736 | tf_op jit(solution)/shard_map/ppermute | solution.py:37
